TPU v7x, 32 devices: a whole 2x2x4 slice. The times are simulated.
32 devices in a mesh: row: 8 (over z, y), col: 4 (over x, core).
Axes of the slice: x: 2, y: 2, z: 4, core: 2. Of those that a mesh axis runs over, the one named last changes fastest.
Arguments:
- a_blocks: bfloat16 [512, 4, 128, 128], P('row', 'col'), may hold values from -4 to 4
- p_tiles: bfloat16 [512, 128, 128], P(('row', 'col')), may hold values from -0.5 to 0.5
- owner: int32 [512, 1], P('row'), may hold values from 0 to 7; in each aligned block of 64 rows (0 to 63, 64 to 127, ...) at most 16 rows name the same one
- agg_local: int32 [512], P('row'), may hold values from 0 to 1
- a_cols: int32 [512, 4], P('row', 'col'), may hold values from 0 to 511, as said below
Outputs:
- coarse: float32 [16, 16, 128, 128], P('row', 'col')
Inputs may be any that keep to these rules, and one draw needn't show every extreme that they name: Column c of a_cols names a tile g with (g // 16) % 4 == c. Among the 64 tiles of one row slab at most 16 name the same owner, and in every draw some owner is named exactly 16 times by some slab.
All inputs are finite; a program needn't handle non-finite values.
Results may differ from a plain program's by a relative error of at most 0.0029.
Values may be sent and summed in bfloat16 or wider, within the bound.
No kernel may reach another device: no remote copies, remote signals or barrier semaphores. Data moves between devices by JAX's collectives and lax.ppermute only.
A program may use at most 192 MiB of HBM per device.

v0:
```python
import jax
import jax.numpy as jnp
from jax import lax
from jax.sharding import PartitionSpec as P

OWN = 2


def shards(a_blocks, p_tiles, owner, agg_local, a_cols):
    tile_count = p_tiles.shape[0]
    tile_side = p_tiles.shape[1]
    slab_rows = a_blocks.shape[0]
    row_count = lax.axis_size("row")
    col_count = lax.axis_size("col")
    col_index = lax.axis_index("col")
    coarse_count = OWN * row_count
    aggregate = owner[:, 0] * OWN + agg_local
    own_aggs = lax.dynamic_slice_in_dim(aggregate, col_index * tile_count, tile_count)
    panel, panel_aggs = (
        lax.all_gather(p_tiles, "row", axis=0, tiled=True),
        lax.all_gather(own_aggs, "row", axis=0, tiled=True),
    )
    own_rows = lax.all_gather(p_tiles, "col", axis=0, tiled=True)
    column_tiles = a_cols[:, 0]
    panel_index = column_tiles // (col_count * tile_count) * tile_count + column_tiles % tile_count
    dest_block = agg_local * coarse_count + panel_aggs[panel_index]
    owner_hot = (owner == jnp.arange(row_count, dtype=jnp.int32)[None, :]).astype(jnp.int32)
    position = jnp.sum((jnp.cumsum(owner_hot, 0) - owner_hot) * owner_hot, 1)
    capacity = 2 * slab_rows // row_count
    slot_range = jnp.arange(capacity, dtype=jnp.int32)
    matches = (owner_hot[:, :, None] == 1) & (position[:, None, None] == slot_range[None, None, :])
    filled = jnp.any(matches, 0)
    tile_range = jnp.arange(slab_rows, dtype=jnp.int32)
    source_tile = jnp.sum(jnp.where(matches, tile_range[:, None, None], 0), 0)
    pairs = jnp.stack([a_blocks[:, 0], own_rows], 1)
    outgoing = jnp.where(
        filled[:, :, None, None, None], pairs[source_tile], jnp.zeros((), jnp.bfloat16)
    )
    indices = jnp.stack([panel_index[source_tile], dest_block[source_tile]], -1)
    tile_pair = lax.all_to_all(outgoing, "row", split_axis=0, concat_axis=0, tiled=True)
    tile_index = lax.all_to_all(indices, "row", split_axis=0, concat_axis=0, tiled=True)
    column_side = panel[tile_index[..., 0]]
    product = jnp.einsum(
        "rnij,rnjk->rnik", tile_pair[:, :, 0], column_side, preferred_element_type=jnp.float32
    ).astype(jnp.bfloat16)
    result = jnp.einsum(
        "rnji,rnjk->rnik", tile_pair[:, :, 1], product, preferred_element_type=jnp.float32
    )
    landing = tile_index[..., 1]
    partial_sum = jnp.zeros((OWN * coarse_count, tile_side, tile_side), jnp.float32)
    partial_sum = partial_sum.at[landing.reshape(-1)].add(result.reshape(-1, tile_side, tile_side))
    partial_sum = partial_sum.reshape(OWN, coarse_count, tile_side, tile_side)
    return lax.psum_scatter(partial_sum, "col", scatter_dimension=1, tiled=True)


def solution(mesh):
    in_specs = (
        P("row", "col", None, None),
        P(("row", "col"), None, None),
        P("row", None),
        P("row"),
        P("row", "col"),
    )
    out_specs = P("row", "col", None, None)
    return jax.shard_map(shards, mesh=mesh, in_specs=in_specs, out_specs=out_specs, check_vma=False)
```

profile of v0, /device:TPU:0, one launch (start us, length us, event | category | flops | bytes accessed | tf_op | source)
XLA Modules:
  0.0 394.0 jit_solution(4738700040105961249)
XLA Ops:
  7.4 0.0 all-gather.3.cloned.1.call-start
  7.4 0.7 all-gather.3.cloned.1.call-update
  8.1 0.7 fusion.5
  8.8 0.1 reduce_window_sum.11
  8.9 0.1 copy.16
  9.0 0.8 select_reduce_fusion
  9.9 0.2 fusion.3
  10.1 0.1 reshape.98
  10.2 1.2 dynamic-slice
  12.1 0.7 multiply_add_fusion
  12.8 0.2 dynamic-slice_dynamic-update-slice_fusion
  12.9 13.1 %all-reduce = s32[128]{0:T(128)S(1)} all-reduce(s32[128]{0:T(128)S(1)} %dynamic-slice_dynamic-update-slice_fusion), channel_id=1, replica_groups=mesh['row'=8,'col'=4] {'row'}, use_global_device_ids=true, to_apply=%add | all-reduce | flops 128 | bytes 1024
  26.0 0.7 fusion.8
  26.7 0.8 gather_fusion.1
  27.4 0.7 multiply_add_fusion.1
  28.1 1.2 gather_fusion.2
  29.3 0.1 stack.16
  29.4 0.0 copy-done.2
  29.4 1.2 gather_fusion
  30.7 0.1 stack.15
  30.8 0.6 copy.17
  31.4 3.3 all-to-all-start
  34.7 0.2 and_reduce_fusion
  34.9 0.1 all-gather.3.cloned.1.call-done
  35.1 0.0 copy-done.1
  35.1 3.9 %pad_maximum_fusion = bf16[64,2,128,128]{3,2,0,1:T(8,128)(2,1)} fusion(bf16[64,1,128,128]{3,2,0,1:T(8,128)(2,1)} %bitcast.57, bf16[64,1,128,128]{3,2,0,1:T(8,128)(2,1)S(1)} %bitcast.56), kind=kLoop, calls=%fused_computation.11 | loop fusion | flops 2097152 | bytes 8388608 | tf_op jit(solution)/shard_map/stack | solution.py:35
  39.0 8.6 %gather_fusion.3 = bf16[128,2,128,128]{3,2,1,0:T(8,128)(2,1)} fusion(bf16[64,2,128,128]{3,2,0,1:T(8,128)(2,1)} %pad_maximum_fusion, s32[1024]{0:T(1024)S(1)} %pad_clamp_fusion.2), kind=kCustom, calls=%fused_computation.3 | custom fusion | bytes 16777728 | tf_op jit(solution)/shard_map/gather | solution.py:37
  47.6 11.4 %copy.19 = bf16[8,16,2,128,128]{3,4,1,2,0:T(8,128)(2,1)} copy(bf16[8,16,2,128,128]{4,3,2,1,0:T(8,128)(2,1)} %bitcast.53) | data formatting | bytes 16777216 | tf_op jit(solution)/shard_map/gather | solution.py:37
  59.0 7.2 %broadcast_select_fusion = bf16[8,16,2,128,128]{3,4,1,2,0:T(8,128)(2,1)} fusion(bf16[8,16,2,128,128]{3,4,1,2,0:T(8,128)(2,1)} %copy.19, pred[8,16]{1,0:T(8,128)(4,1)S(1)} %and_reduce_fusion), kind=kLoop, calls=%fused_computation.6 | loop fusion | flops 4194304 | bytes 16777344 | tf_op jit(solution)/shard_map/jit(_where)/select_n | solution.py:36
  66.3 0.0 all-to-all-done
  66.3 5.8 %all-to-all-start.1 = ((bf16[8,16,2,128,128]{3,4,1,2,0:T(8,128)(2,1)}), bf16[8,16,2,128,128]{3,4,1,2,0:T(8,128)(2,1)}, u32[]{:S(2)}, u32[]{:S(2)}) async-start(bf16[8,16,2,128,128]{3,4,1,2,0:T(8,128)(2,1)} %broadcast_select_fusion), calls=%async_computation.1 | async-start | bytes 16777216 | tf_op jit(solution)/shard_map/all_to_all | solution.py:40
  72.1 0.0 all-gather.5.cloned.1.call-start
  72.2 0.5 all-gather.5.cloned.1.call-update
  72.7 0.0 all-reduce.4.cloned.1.call-start
  72.8 0.1 reshape.130
  72.9 0.1 reshape_squeeze.3
  73.0 206.4 %all-gather.5.cloned.1.call-done = bf16[128,128,128]{2,1,0:T(8,128)(2,1)} async-done(((bf16[16,128,128]{2,1,0:T(8,128)(2,1)}), bf16[128,128,128]{2,1,0:T(8,128)(2,1)}) %all-gather.5.cloned.1.call-update) | async-done | bytes 4194320 | tf_op jit(solution)/shard_map/all_gather | solution.py:20
  279.4 5.2 %gather_fusion.4 = bf16[128,128,128]{2,1,0:T(8,128)(2,1)} fusion(bf16[128,128,128]{2,1,0:T(8,128)(2,1)} %all-gather.5.cloned.1.call-done, s32[1024]{0:T(1024)S(1)} %pad_clamp_fusion), kind=kCustom, calls=%fused_computation.4 | custom fusion | bytes 8389120 | tf_op jit(solution)/shard_map/gather | solution.py:42
  284.6 21.4 %all-to-all-done.1 = bf16[8,16,2,128,128]{3,4,1,2,0:T(8,128)(2,1)} async-done(((bf16[8,16,2,128,128]{3,4,1,2,0:T(8,128)(2,1)}), bf16[8,16,2,128,128]{3,4,1,2,0:T(8,128)(2,1)}, u32[]{:S(2)}, u32[]{:S(2)}) %all-to-all-start.1) | async-done | bytes 8388640 | tf_op jit(solution)/shard_map/all_to_all | solution.py:40
  306.0 10.5 %fusion.1 = f32[8,16,128,128]{3,2,1,0:T(8,128)} fusion(bf16[8,16,2,128,128]{3,4,1,2,0:T(8,128)(2,1)} %all-to-all-done.1, bf16[8,16,128,128]{3,2,1,0:T(8,128)(2,1)} %bitcast.55), kind=kOutput, calls=%fused_computation.10 | convolution fusion | flops 1075838976 | bytes 20971520 | tf_op jit(solution)/shard_map/rnji,rnjk->rnik/dot_general | solution.py:46
  316.5 0.2 broadcast_in_dim.26
  316.7 0.0 copy-start.3
  316.7 17.0 %scatter_fusion = f32[32,128,128]{2,1,0:T(8,128)S(1)} fusion(f32[32,128,128]{2,1,0:T(8,128)S(1)} %broadcast_in_dim.26, s32[128]{0:T(128)S(1)} %fusion.9, f32[128,128,128]{2,1,0:T(8,128)} %bitcast.54), kind=kCustom, calls=%fused_computation.5 | custom fusion | flops 2097152 | bytes 25166336 | tf_op jit(solution)/shard_map/scatter-add | solution.py:51
  333.7 1.3 copy-done
  335.0 0.0 all-reduce.4.cloned.1.call-update
  335.1 0.6 dynamic-slice.1
  336.3 48.3 %all-reduce.4.cloned.1.call-done = f32[2,16,128,128]{3,2,1,0:T(8,128)} async-done(((f32[2,16,128,128]{3,2,1,0:T(8,128)}), f32[2,16,128,128]{3,2,1,0:T(8,128)}) %all-reduce.4.cloned.1.call-update) | async-done | bytes 2097168
  384.6 1.9 constant_dynamic-slice_fusion
  (15 shorter events, 0.1 us)
Async XLA Ops:
  7.4 22.0 %copy-start.2 = (s32[64,1]{0,1:T(1,128)S(1)}, s32[64,1]{0,1:T(1,128)}, u32[]{:S(2)}) copy-start(s32[64,1]{0,1:T(1,128)} %param.9) | copy-start | bytes 772
  7.4 27.7 %all-gather.3.cloned.1.call-start = ((), (), s32[]{:S(2)}) async-start(), calls=%async_computation.2 | async-start | bytes 2621440 | tf_op jit(solution)/shard_map/all_gather | solution.py:23
  28.1 7.0 %copy-start.1 = (bf16[64,1,128,128]{3,2,1,0:T(8,128)(2,1)S(1)}, bf16[64,1,128,128]{3,2,1,0:T(8,128)(2,1)}, u32[]{:S(2)}) copy-start(bf16[64,1,128,128]{3,2,1,0:T(8,128)(2,1)} %param.5) | copy-start | bytes 6291460
  31.4 34.9 %all-to-all-start = ((s32[8,16,2]{1,2,0:T(2,128)}), s32[8,16,2]{1,2,0:T(2,128)S(1)}, u32[]{:S(2)}, u32[]{:S(2)}) async-start(s32[8,16,2]{1,2,0:T(2,128)} %copy.17), calls=%async_computation | async-start | bytes 16384 | tf_op jit(solution)/shard_map/all_to_all | solution.py:41
  66.3 239.7 %all-to-all-start.1 = ((bf16[8,16,2,128,128]{3,4,1,2,0:T(8,128)(2,1)}), bf16[8,16,2,128,128]{3,4,1,2,0:T(8,128)(2,1)}, u32[]{:S(2)}, u32[]{:S(2)}) async-start(bf16[8,16,2,128,128]{3,4,1,2,0:T(8,128)(2,1)} %broadcast_select_fusion), calls=%async_computation.1 | async-start | bytes 16777216 | tf_op jit(solution)/shard_map/all_to_all | solution.py:40
  72.1 207.3 %all-gather.5.cloned.1.call-start = ((), (), s32[]{:S(2)}) async-start(), calls=%async_computation.3 | async-start | bytes 4718592 | tf_op jit(solution)/shard_map/all_gather | solution.py:20
  72.7 312.0 %all-reduce.4.cloned.1.call-start = ((), (), s32[]{:S(2)}) async-start(), calls=%async_computation.4 | async-start | bytes 4194304
  316.7 18.4 %copy-start.3 = (u32[32]{0:T(128)S(1)}, u32[32]{0:T(128)}, u32[]{:S(2)}) copy-start(u32[32]{0:T(128)} %constant.72) | copy-start | bytes 388
  333.7 1.3 copy-start
Sparse Core Ops, SparseCore 0:
  9.8 25.2 all-gather.2
  335.2 49.4 all-reduce.3
Sparse Core Ops, SparseCore 1:
  74.7 204.6 all-gather.4
where the time goes:
time: 395 us; the launch traced here: 394 us
  waiting for transfers between devices  278 us (70%)
  local copies, waits for them, and re-layouts  34.9 us (9%)
  other arithmetic  32.4 us (8%)
  between operations  16.3 us (4%)
  blocking collectives  13.1 us (3%)
  matrix products  10.5 us (3%)
  starting transfers between devices  9.26 us (2%)
    all_gather x1, waiting for transfers between devices, shards(): lax.all_gather(p_tiles, 'row', axis=0, tiled=True)  206 us
    unnamed x4, waiting for transfers between devices  49.6 us
    all_to_all x1, waiting for transfers between devices, shards(): lax.all_to_all(outgoing, 'row', split_axis=0, concat_axis=0, tiled=True)  21.4 us
    gather x2, local copies, waits for them, and re-layouts, shards(): pairs[source_tile]  20 us
    scatter-add x1, other arithmetic, shards(): partial_sum.at[landing.reshape(-1)]  17 us
    unnamed x1, blocking collectives  13.1 us
    dot_general x1, matrix products, shards(): jnp.einsum('rnji,rnjk->rnik', tile_pair[:, :, 1], product, preferred_elem...  10.5 us
  transfers between devices with their start and end apart: 5, of which 4 were waited for; matrix products, arithmetic and copies ran while one was open for 12% of the time, Pallas kernels for 0%

commit v1 on v0

v1 whole, which is shorter than its diff:
```python
import functools
import math

import jax
import jax.numpy as jnp
from jax import lax
from jax.experimental import pallas as pl
from jax.experimental.pallas import tpu as pltpu
from jax.sharding import PartitionSpec as P

OWN = 2
UNROLL = 8
GROUPS = 4


def ring_order(count):
    return list(range(0, count, 2)) + list(range(1, count, 2))[::-1]


def swap(value, axis, bit):
    size = lax.axis_size(axis)
    return lax.ppermute(value, axis, [(i, i ^ bit) for i in range(size)])


def log2(size):
    power = size.bit_length() - 1
    assert size == 1 << power
    return power


class Sizes:
    def __init__(self, rows, cols, tiles, side):
        self.rows, self.cols, self.tiles, self.side = rows, cols, tiles, side
        self.slab = cols * tiles
        self.pairs = 2 * self.slab
        self.width = OWN * rows // cols
        self.per = OWN * self.width
        self.his = rows // 4
        self.buckets = 2 * self.his
        self.slots = self.pairs + self.buckets * UNROLL
        self.half = rows // 2
        self.early = (rows - 1, rows - 3)
        self.near = sum(self.early) * tiles
        cells = 2 * cols * self.per
        self.fields, shift = [], 0
        for size in (self.pairs, 2 * rows * tiles, self.slab, cells):
            self.fields.append((shift, size - 1))
            shift += log2(size)
        assert shift <= 31


def field(s, entry, k):
    shift, mask = s.fields[k]
    return (entry >> shift) & mask


def plan_kernel(s, cols_ref, aggs_ref, plan_ref, starts_ref, info, counts):
    row = lax.axis_index("row")
    col = lax.axis_index("col")

    def ring_place(index):
        return jnp.where((index & 1) == 0, index >> 1, s.rows - 1 - (index >> 1))

    here = ring_place(row)
    for b in range(s.buckets):
        counts[b] = 0

    def blank(k, carry):
        plan_ref[k] = -1
        return carry

    lax.fori_loop(0, s.slots + 1, blank, 0, unroll=8)

    def sort(i, carry):
        tile = i & (s.slab - 1)
        side = i >> log2(s.slab)
        other = cols_ref[i]
        other_row = other >> log2(s.slab)
        i_agg = aggs_ref[tile]
        j_agg = aggs_ref[((other_row ^ row) << log2(s.slab)) + (other & (s.slab - 1))]
        rel_col = (j_agg >> log2(s.width)) ^ col
        rel_row = (i_agg >> log2(OWN)) ^ row
        turn = ring_place(other_row) - here
        away = jnp.where(((col ^ side) & 1) == 0, turn, -turn) & (s.rows - 1)
        reach = jnp.abs(away - s.half)
        late = jnp.where(reach <= side, 1, 0)
        order = away - jnp.where(away > s.half, 1 + 2 * side, 0) + side * s.early[0]
        last = jnp.where(side == 0, 0, 2 + away - s.half)
        piece = jnp.where(late == 1, last, order)
        panel_at = (piece << log2(s.tiles)) + (other & (s.tiles - 1))
        rel_part = (tile >> log2(s.tiles)) ^ col
        part = (rel_part & 1) * (s.cols // 2) + (rel_part >> 1)
        rows_at = (part << log2(s.tiles)) + (tile & (s.tiles - 1))
        cell = (rel_row & 3) * (s.cols // 2) + (rel_col >> 1)
        cell = (cell << log2(OWN)) + (i_agg & (OWN - 1))
        cell = (cell << log2(s.width)) + (j_agg & (s.width - 1))
        bucket = (rel_row >> 2) * 2 + late
        mine = (rel_col & 1) == 0
        rank = counts[bucket]
        counts[bucket] = rank + jnp.where(mine, 1, 0)
        info[i * 2] = jnp.where(mine, rank * s.buckets + bucket, -1)
        entry = i
        for k, value in enumerate((panel_at, rows_at, cell)):
            entry = entry + (value << s.fields[k + 1][0])
        info[i * 2 + 1] = entry
        return carry

    lax.fori_loop(0, s.pairs, sort, 0, unroll=4)

    start = jnp.int32(0)
    for b in range(s.buckets):
        starts_ref[b] = start
        start = start + ((counts[b] + UNROLL - 1) & ~(UNROLL - 1))
    starts_ref[s.buckets] = start

    def place(i, carry):
        key = info[i * 2]
        slot = starts_ref[key & (s.buckets - 1)] + (key >> log2(s.buckets))
        plan_ref[jnp.where(key >= 0, slot, s.slots)] = info[i * 2 + 1]
        return carry

    lax.fori_loop(0, s.pairs, place, 0, unroll=4)


def room(*shapes):
    total = sum(math.prod(shape) * jnp.dtype(dtype).itemsize for shape, dtype in shapes)
    return total + (2 << 20)


def make_plan(s, cols, aggs):
    smem = pl.BlockSpec(memory_space=pltpu.SMEM)
    return pl.pallas_call(
        functools.partial(plan_kernel, s),
        in_specs=[smem, smem],
        out_specs=[smem, smem],
        out_shape=[
            jax.ShapeDtypeStruct((s.slots + 1,), jnp.int32),
            jax.ShapeDtypeStruct((s.buckets + 1,), jnp.int32),
        ],
        scratch_shapes=[
            pltpu.SMEM((s.pairs * 2,), jnp.int32),
            pltpu.SMEM((s.buckets,), jnp.int32),
        ],
        compiler_params=pltpu.CompilerParams(vmem_limit_bytes=room()),
        cost_estimate=pl.CostEstimate(flops=1 << 20, bytes_accessed=1 << 20, transcendentals=0),
    )(cols, aggs)


def product_kernel(s, plan_ref, starts_ref, *refs):
    slots_ref, rows_ref, a_buf, panel, rows_buf, sems = refs[-6:]
    copies = []
    for k in range(2):
        copies.append((refs[k], a_buf.at[pl.ds(k * s.slab, s.slab)]))
    for k in range(s.cols):
        copies.append((refs[2 + k], rows_buf.at[pl.ds(k * s.tiles, s.tiles)]))
    for k in range(sum(s.early)):
        source = refs[2] if k == 0 else refs[1 + s.cols + k]
        copies.append((source, panel.at[pl.ds(k * s.tiles, s.tiles)]))
    copies = [pltpu.make_async_copy(src, dst, sems.at[k]) for k, (src, dst) in enumerate(copies)]
    for copy in copies:
        copy.start()
    for copy in copies:
        copy.wait()

    def turn(k, carry):
        rows_ref[k] = rows_buf[k].T
        return carry

    lax.fori_loop(0, s.slab, turn, 0, unroll=4)

    for hi in range(s.his):
        begin = starts_ref[2 * hi] // UNROLL
        middle = starts_ref[2 * hi + 1] // UNROLL
        end = starts_ref[2 * hi + 2] // UNROLL

        def near(group, carry):
            for u in range(UNROLL):
                n = group * UNROLL + u
                entry = jnp.maximum(plan_ref[n], 0)
                slots_ref[n] = jnp.dot(
                    a_buf[field(s, entry, 0)],
                    panel[field(s, entry, 1)],
                    preferred_element_type=jnp.float32,
                ).astype(jnp.bfloat16)
            return carry

        def far(group, carry):
            for u in range(UNROLL):
                n = group * UNROLL + u
                slots_ref[n] = a_buf[field(s, jnp.maximum(plan_ref[n], 0), 0)]
            return carry

        lax.fori_loop(begin, middle, near, 0)
        lax.fori_loop(middle, end, far, 0)


def make_products(s, plan, starts, a_own, a_other, near, rows):
    smem = pl.BlockSpec(memory_space=pltpu.SMEM)
    vmem = pl.BlockSpec(memory_space=pltpu.VMEM)
    anywhere = pl.BlockSpec(memory_space=pl.ANY)
    shapes = [
        ((count, s.side, s.side), jnp.bfloat16)
        for count in (s.slots, s.slab, s.pairs, s.near, s.slab)
    ]
    hbm = pl.BlockSpec(memory_space=pltpu.HBM)
    a_own, own = (pltpu.with_memory_space_constraint(x, pltpu.HBM) for x in (a_own, rows[0]))
    operands = [a_own, a_other, own, *rows[1:], *near[1:]]
    return pl.pallas_call(
        functools.partial(product_kernel, s),
        in_specs=[smem, smem, hbm, anywhere, hbm] + [anywhere] * (len(operands) - 3),
        out_specs=[vmem, vmem],
        out_shape=[jax.ShapeDtypeStruct(*shape) for shape in shapes[:2]],
        scratch_shapes=[pltpu.VMEM(*shape) for shape in shapes[2:]]
        + [pltpu.SemaphoreType.DMA((len(operands) + 1,))],
        compiler_params=pltpu.CompilerParams(vmem_limit_bytes=room(*shapes)),
        cost_estimate=pl.CostEstimate(
            flops=s.pairs * s.side**3, bytes_accessed=16 << 20, transcendentals=0
        ),
    )(plan, starts, *operands)


def sum_kernel(
    s, plan_ref, starts_ref, slots_ref, rows_ref, far0, far1, far2, far3,
    send0, keep0, send1, keep1, send2, keep2, send3, keep3, total, far_buf, sems,
):
    hi = pl.program_id(0)
    copies = [
        pltpu.make_async_copy(ref, far_buf.at[pl.ds(k * s.tiles, s.tiles)], sems.at[k])
        for k, ref in enumerate((far0, far1, far2, far3))
    ]

    @pl.when(hi == 0)
    def _():
        for copy in copies:
            copy.start()

    cells = total.shape[0]

    def clear(k, carry):
        total[pl.ds(k * 8, 8)] = jnp.zeros((8,) + total.shape[1:], jnp.float32)
        return carry

    lax.fori_loop(0, cells // 8, clear, 0)

    def add(n, product):
        entry = plan_ref[n]
        known = jnp.maximum(entry, 0)
        term = jnp.dot(
            rows_ref[field(s, known, 2)], product, preferred_element_type=jnp.float32
        )
        total[field(s, known, 3)] += jnp.where(entry >= 0, term, 0.0)

    def near(group, carry):
        for u in range(UNROLL):
            n = group * UNROLL + u
            add(n, slots_ref[n])
        return carry

    def far(group, carry):
        for u in range(UNROLL):
            n = group * UNROLL + u
            piece = far_buf[field(s, jnp.maximum(plan_ref[n], 0), 1)]
            product = jnp.dot(slots_ref[n], piece, preferred_element_type=jnp.float32)
            add(n, product.astype(jnp.bfloat16))
        return carry

    begin = starts_ref[2 * hi] // UNROLL
    middle = starts_ref[2 * hi + 1] // UNROLL
    end = starts_ref[2 * hi + 2] // UNROLL
    lax.fori_loop(begin, middle, near, 0)

    @pl.when(hi == 0)
    def _():
        for copy in copies:
            copy.wait()

    lax.fori_loop(middle, end, far, 0)

    xh = s.cols // 4
    tall = s.side // GROUPS

    for z1 in range(2):
        for y in range(2):
            for x in range(xh):
                for x1 in range(2):
                    base = (((z1 * 2 + y) * xh + x) * 2 + x1) * s.per
                    part = [
                        total[pl.ds(base, s.per), k * tall:(k + 1) * tall, :]
                        for k in range(GROUPS)
                    ]
                    for k, (bit, send, keep, at) in enumerate((
                        (z1, send0, keep0, (y, 0, x1)),
                        (y, send1, keep1, (0, x1, z1)),
                        (x1, send2, keep2, (y, z1, 0)),
                        (z1, send3, keep3, (x1, 0, y)),
                    )):
                        if bit:
                            send[(*at, 0, x)] = part[k].astype(jnp.bfloat16)
                        else:
                            keep[(*at, 0, x)] = part[k]


def make_sums(s, plan, starts, slots, rows_t, far):
    smem = pl.BlockSpec(memory_space=pltpu.SMEM)
    vmem = pl.BlockSpec(memory_space=pltpu.VMEM)
    anywhere = pl.BlockSpec(memory_space=pl.ANY)
    last = (s.cols // 4, s.per, s.side // GROUPS, s.side)
    blocks = [
        ((2, 1, 2), lambda h: (0, h & 1, 0, h >> 1, 0, 0, 0, 0)),
        ((1, 2, 2), lambda h: (h & 1, 0, 0, h >> 1, 0, 0, 0, 0)),
        ((2, 2, 1), lambda h: (0, 0, h & 1, h >> 1, 0, 0, 0, 0)),
        ((2, 1, 2), lambda h: (0, h & 1, 0, h >> 1, 0, 0, 0, 0)),
    ]
    shapes = [
        ((s.slots + s.slab + 4 * s.tiles, s.side, s.side), jnp.bfloat16),
        ((2 * s.cols * s.per, s.side, s.side), jnp.float32),
    ]
    out_shape, out_specs = [], []
    for block, index in blocks:
        for dtype in (jnp.bfloat16, jnp.float32):
            out_shape.append(jax.ShapeDtypeStruct((2, 2, 2, s.his // 2) + last, dtype))
            out_specs.append(pl.BlockSpec(block + (1,) + last, index))
            shapes.append(((2,) + block + last, dtype))
    return pl.pallas_call(
        functools.partial(sum_kernel, s),
        grid=(s.his,),
        in_specs=[smem, smem, vmem, vmem] + [anywhere] * 4,
        out_specs=out_specs,
        out_shape=out_shape,
        scratch_shapes=[
            pltpu.VMEM((2 * s.cols * s.per, s.side, s.side), jnp.float32),
            pltpu.VMEM((4 * s.tiles, s.side, s.side), jnp.bfloat16),
            pltpu.SemaphoreType.DMA((4,)),
        ],
        compiler_params=pltpu.CompilerParams(vmem_limit_bytes=room(*shapes)),
        cost_estimate=pl.CostEstimate(
            flops=s.pairs * s.side**3, bytes_accessed=16 << 20, transcendentals=0
        ),
    )(plan, starts, slots, rows_t, *far)


def shards(a_blocks, p_tiles, owner, agg_local, a_cols):
    s = Sizes(
        lax.axis_size("row"), lax.axis_size("col"), p_tiles.shape[0], p_tiles.shape[1]
    )
    order = ring_order(s.rows)
    barrier = lax.optimization_barrier

    def ring(value, stream):
        moves = []
        for k in range(s.rows):
            for c in range(s.cols):
                step = 1 if (stream + c) % 2 == 0 else -1
                to = order[(k + step) % s.rows]
                moves.append((order[k] * s.cols + c, to * s.cols + c))
        return lax.ppermute(value, ("row", "col"), moves)

    first, second = ring(p_tiles, 0), ring(p_tiles, 1)
    rows = [p_tiles]
    bit = 2
    while bit < s.cols:
        rows += [swap(piece, "col", bit) for piece in rows]
        bit *= 2
    p_other = swap(p_tiles, "col", 1)
    cols = a_cols[:, 0]
    cols_other = swap(cols, "col", 1)
    aggs = owner[:, 0] * OWN + agg_local
    first, second, p_other, cols_other, aggs, *rows[1:] = barrier(
        (first, second, p_other, cols_other, aggs, *rows[1:])
    )
    own_near = {0: p_tiles, s.rows - 1: first, 1: second}
    other_near = {0: p_other}

    aggs = [aggs] + [swap(aggs, "row", mask) for mask in (1, 2, 3)]
    aggs = jnp.concatenate(aggs, 0)
    held = [1, s.rows - 1]
    for step in range(2, s.half):
        first, second = barrier((ring(first, 0), ring(second, 1)))
        if step == 2:
            came, aggs, a_own, *rest = barrier((first, aggs, a_blocks[:, 0], *rows[1:]))
            bit = 4
            while bit < s.rows:
                aggs = jnp.concatenate([aggs, swap(aggs, "row", bit)], 0)
                bit *= 2
            a_other = swap(a_own, "col", 1)
            rows += [p_other] + [swap(piece, "col", 1) for piece in rest]
        else:
            came, *rest = barrier((first, *(own_near[away] for away in held)))
            for away, piece in zip(held, rest):
                other_near[away] = swap(piece, "col", 1)
            held = []
        own_near[s.rows - step], own_near[step] = came, second
        held += [step, s.rows - step]

    far = ring(first, 0)
    last_other = [swap(own_near[away], "col", 1) for away in (s.half - 1, s.half + 1)]
    plan, starts = make_plan(s, jnp.concatenate([cols, cols_other], 0), aggs)
    near = [own_near[k] for k in sorted(own_near)]
    near += [other_near[k] for k in sorted(other_near)]
    slots, rows_t = make_products(s, plan, starts, a_blocks[:, 0], a_other, near, rows)
    far, slots, rows_t = barrier((far, slots, rows_t))
    far_other = swap(far, "col", 1)
    parts = make_sums(s, plan, starts, slots, rows_t, [far, last_other[0], far_other, last_other[1]])

    y, z1, z2, x1 = ("row", 1), ("row", 2), ("row", 4), ("col", 2)
    orders = [[z1, y, z2, x1], [y, z2, x1, z1], [x1, y, z1, z2], [z1, x1, z2, y]]
    sends, keeps, steps = list(parts[0::2]), list(parts[1::2]), [0] * GROUPS
    moving = [swap(sends[k], *orders[k][0]) for k in range(GROUPS)]
    for k in list(range(GROUPS)) * 4:
        got = moving[k]
        steps[k] += 1
        if steps[k] < 4:
            send = (keeps[k][1] + got[1].astype(jnp.float32)).astype(jnp.bfloat16)
            moving[k] = swap(send, *orders[k][steps[k]])
            keeps[k] = keeps[k][0] + got[0].astype(jnp.float32)
        else:
            keeps[k] = keeps[k] + got.astype(jnp.float32)
    total = jnp.concatenate(keeps, -2)
    tail = [("row", 1 << k) for k in range(3, log2(s.rows))][::-1]
    tail += [("col", 1 << k) for k in range(2, log2(s.cols))][::-1]
    total = total.reshape((2,) * len(tail) + total.shape[-3:])
    for axis in tail:
        got = swap(total[1].astype(jnp.bfloat16), *axis)
        total = total[0] + got.astype(jnp.float32)
    return total.reshape(OWN, s.width, s.side, s.side)


def solution(mesh):
    in_specs = (
        P("row", "col", None, None),
        P(("row", "col"), None, None),
        P("row", None),
        P("row"),
        P("row", "col"),
    )
    out_specs = P("row", "col", None, None)
    return jax.shard_map(shards, mesh=mesh, in_specs=in_specs, out_specs=out_specs, check_vma=False)
```

time: 395 us -> 128 us (0.32)
  waiting for transfers between devices: 278 us -> 71.8 us
  local copies, waits for them, and re-layouts: 34.9 us -> 0 us
  other arithmetic: 32.4 us -> 3.36 us
  starting transfers between devices: 9.26 us -> 36 us
  Pallas kernels: 0 us -> 16.4 us
  between operations: 16.3 us -> 0.24 us
  blocking collectives: 13.1 us -> 0 us
  matrix products: 10.5 us -> 0 us
    all_gather x2 -> x0, waiting for transfers between devices: 207 us -> none  [the longest x1 206 us: shards(): lax.all_gather(p_tiles, 'row', axis=0, tiled=True)]
    ppermute x0 -> x39, waiting for transfers between devices: none -> 71.8 us  [the longest x32 50.4 us: swap(): return lax.ppermute(value, axis, [(i, i ^ bit) for i in range(size)])]
    unnamed x4 -> x0, waiting for transfers between devices: 49.6 us -> none
    ppermute x0 -> x39, starting transfers between devices: none -> 36 us  [the longest x32 27.7 us: swap(): return lax.ppermute(value, axis, [(i, i ^ bit) for i in range(size)])]
    gather x6 -> x0, local copies, waits for them, and re-layouts: 28.4 us -> none  [the longest x2 20 us: shards(): pairs[source_tile]]
    all_to_all x2 -> x0, waiting for transfers between devices: 21.4 us -> none  [the longest x1 21.4 us: shards(): lax.all_to_all(outgoing, 'row', split_axis=0, concat_axis=0, tiled=True)]
    scatter-add x1 -> x0, other arithmetic: 17 us -> none  [shards(): partial_sum.at[landing.reshape(-1)]]
    pallas_call x0 -> x3, Pallas kernels: none -> 16.4 us  [the longest x1 6.28 us: make_products(): pl.pallas_call(functools.partial(product_kernel, s), in_specs=[smem, smem...]
  transfers between devices with their start and end apart: 5 -> 39, of which waited for: 4 -> 16; matrix products, arithmetic and copies ran while one was open for 12% -> 2% of each run, Pallas kernels for 0% -> 9%
where the time goes in v1:
time: 128 us
  waiting for transfers between devices  71.8 us (56%)
  starting transfers between devices  36 us (28%)
  Pallas kernels  16.4 us (13%)
  other arithmetic  3.36 us (3%)
    ppermute x32, waiting for transfers between devices, swap(): return lax.ppermute(value, axis, [(i, i ^ bit) for i in range(size)])  50.4 us
    ppermute x32, starting transfers between devices, swap(): return lax.ppermute(value, axis, [(i, i ^ bit) for i in range(size)])  27.7 us
    ppermute x7, waiting for transfers between devices, ring(): return lax.ppermute(value, ('row', 'col'), moves)  21.4 us
    ppermute x7, starting transfers between devices, ring(): return lax.ppermute(value, ('row', 'col'), moves)  8.26 us
    pallas_call x1, Pallas kernels, make_products(): pl.pallas_call(functools.partial(product_kernel, s), in_specs=[smem, smem...  6.28 us
    pallas_call x1, Pallas kernels, make_plan(): pl.pallas_call(functools.partial(plan_kernel, s), in_specs=[smem, smem],...  5.2 us
    pallas_call x1, Pallas kernels, make_sums(): pl.pallas_call(functools.partial(sum_kernel, s), grid=(s.his,), in_specs=...  4.97 us
  transfers between devices with their start and end apart: 39, of which 16 were waited for; matrix products, arithmetic and copies ran while one was open for 2% of the time, Pallas kernels for 9%

profile of v1, /device:TPU:0, one launch (start us, length us, event | category | flops | bytes accessed | tf_op | source)
XLA Modules:
  0.0 127.9 jit_solution(4600283400526504068)
XLA Ops:
  0.0 3.0 %collective-permute-start = (bf16[16,128,128]{2,1,0:T(8,128)(2,1)}, bf16[16,128,128]{2,1,0:T(8,128)(2,1)S(1)}, u32[]{:S(2)}, u32[]{:S(2)}) collective-permute-start(bf16[16,128,128]{2,1,0:T(8,128)(2,1)} %refs_2_.1), channel_id=1, source_target_pairs={{0,8},{1,5},{2,10},{3,7},{8,16},{9,1},{10,18},{11,3},{16,24},{17,9... | collective-permute-start | bytes 1572872 | tf_op jit(solution)/shard_map/ppermute | solution.py:356
  3.0 1.9 %collective-permute-start.4 = (bf16[16,128,128]{2,1,0:T(8,128)(2,1)}, bf16[16,128,128]{2,1,0:T(8,128)(2,1)S(1)}, u32[]{:S(2)}, u32[]{:S(2)}) collective-permute-start(bf16[16,128,128]{2,1,0:T(8,128)(2,1)} %refs_2_.1), channel_id=1, source_target_pairs={{0,2},{1,3},{2,0},{3,1},{4,6},{5,7},{6,4},{7,5},{8,10},{9,11},{10,... | collective-permute-start | bytes 1572872 | tf_op jit(solution)/shard_map/ppermute | solution.py:22
  5.0 0.2 collective-permute-start.3
  5.2 0.7 bitcast_add_fusion
  5.9 0.4 collective-permute-done.3
  6.2 9.2 %collective-permute-done.refs_11_ = bf16[16,128,128]{2,1,0:T(8,128)(2,1)S(1)} collective-permute-done((bf16[16,128,128]{2,1,0:T(8,128)(2,1)}, bf16[16,128,128]{2,1,0:T(8,128)(2,1)S(1)}, u32[]{:S(2)}, u32[]{:S(2)}) %collective-permute-start) | collective-permute-done | bytes 524320 | tf_op jit(solution)/shard_map/ppermute | solution.py:356
  15.4 2.4 %collective-permute-done.4.refs_3_ = bf16[16,128,128]{2,1,0:T(8,128)(2,1)S(1)} collective-permute-done((bf16[16,128,128]{2,1,0:T(8,128)(2,1)}, bf16[16,128,128]{2,1,0:T(8,128)(2,1)S(1)}, u32[]{:S(2)}, u32[]{:S(2)}) %collective-permute-start.4) | collective-permute-done | bytes 524320 | tf_op jit(solution)/shard_map/ppermute | solution.py:22
  17.8 1.8 %collective-permute-start.5 = (bf16[16,128,128]{2,1,0:T(8,128)(2,1)S(1)}, bf16[16,128,128]{2,1,0:T(8,128)(2,1)S(1)}, u32[]{:S(2)}, u32[]{:S(2)}) collective-permute-start(bf16[16,128,128]{2,1,0:T(8,128)(2,1)S(1)} %collective-permute-done.refs_11_), channel_id=1, source_target_pairs={{0,8},{1,5},{2,10},{3,7},{8,16},{9,1},{10,18},{11,3},{16,24},{17,9... | collective-permute-start | bytes 1572872 | tf_op jit(solution)/shard_map/ppermute | solution.py:356
  19.8 1.8 %collective-permute-start.7 = (s32[64]{0:T(128)S(1)}, s32[64]{0:T(128)S(1)}, u32[]{:S(2)}, u32[]{:S(2)}) collective-permute-start(s32[64]{0:T(128)S(1)} %bitcast_add_fusion), channel_id=1, source_target_pairs={{0,4},{4,0},{8,12},{12,8},{16,20},{20,16},{24,28},{28,24},{1,5},{5... | collective-permute-start | bytes 776 | tf_op jit(solution)/shard_map/ppermute | solution.py:22
  21.6 1.6 %collective-permute-start.8 = (s32[64]{0:T(128)S(1)}, s32[64]{0:T(128)S(1)}, u32[]{:S(2)}, u32[]{:S(2)}) collective-permute-start(s32[64]{0:T(128)S(1)} %bitcast_add_fusion), channel_id=1, source_target_pairs={{0,8},{4,12},{8,0},{12,4},{16,24},{20,28},{24,16},{28,20},{1,9},{5... | collective-permute-start | bytes 776 | tf_op jit(solution)/shard_map/ppermute | solution.py:22
  23.3 9.1 %collective-permute-done.7 = s32[64]{0:T(128)S(1)} collective-permute-done((s32[64]{0:T(128)S(1)}, s32[64]{0:T(128)S(1)}, u32[]{:S(2)}, u32[]{:S(2)}) %collective-permute-start.7) | collective-permute-done | bytes 288 | tf_op jit(solution)/shard_map/ppermute | solution.py:22
  32.4 1.3 %collective-permute-done.9 = s32[64]{0:T(128)S(1)} collective-permute-done((s32[64]{0:T(128)S(1)}, s32[64]{0:T(128)S(1)}, u32[]{:S(2)}, u32[]{:S(2)}) %collective-permute-start.9) | collective-permute-done | bytes 288 | tf_op jit(solution)/shard_map/ppermute | solution.py:22
  33.9 0.7 collective-permute-start.12
  34.6 1.4 %collective-permute-start.11 = (bf16[16,128,128]{2,1,0:T(8,128)(2,1)S(1)}, bf16[16,128,128]{2,1,0:T(8,128)(2,1)S(1)}, u32[]{:S(2)}, u32[]{:S(2)}) collective-permute-start(bf16[16,128,128]{2,1,0:T(8,128)(2,1)S(1)} %collective-permute-done.5.refs_10_), channel_id=1, source_target_pairs={{0,8},{1,5},{2,10},{3,7},{8,16},{9,1},{10,18},{11,3},{16,24},{17,9... | collective-permute-start | bytes 1572872 | tf_op jit(solution)/shard_map/ppermute | solution.py:356
  36.0 12.2 %collective-permute-done.12.refs_8_ = bf16[16,128,128]{2,1,0:T(8,128)(2,1)S(1)} collective-permute-done((bf16[16,128,128]{2,1,0:T(8,128)(2,1)S(1)}, bf16[16,128,128]{2,1,0:T(8,128)(2,1)S(1)}, u32[]{:S(2)}, u32[]{:S(2)}) %collective-permute-start.12) | collective-permute-done | bytes 524320 | tf_op jit(solution)/shard_map/ppermute | solution.py:356
  48.2 0.3 collective-permute-start.16
  48.6 2.4 %collective-permute-start.10 = (s32[256]{0:T(256)S(1)}, s32[256]{0:T(256)S(1)}, u32[]{:S(2)}, u32[]{:S(2)}) collective-permute-start(s32[256]{0:T(256)S(1)} %pad_add_fusion.1), channel_id=1, source_target_pairs={{0,16},{4,20},{8,24},{12,28},{16,0},{20,4},{24,8},{28,12},{1,17},{... | collective-permute-start | bytes 3080 | tf_op jit(solution)/shard_map/ppermute | solution.py:22
  50.9 0.2 collective-permute-start.17
  51.1 1.9 %collective-permute-done.10 = s32[256]{0:T(256)S(1)} collective-permute-done((s32[256]{0:T(256)S(1)}, s32[256]{0:T(256)S(1)}, u32[]{:S(2)}, u32[]{:S(2)}) %collective-permute-start.10) | collective-permute-done | bytes 1056 | tf_op jit(solution)/shard_map/ppermute | solution.py:22
  53.0 0.5 collective-permute-start.19
  53.5 1.1 collective-permute-start.13
  54.7 0.7 pad_add_fusion.2.cols_ref
  55.4 5.2 %shard_map.55 = (s32[161]{0:T(256)S(1)}, s32[5]{0:T(128)S(1)}) custom-call(s32[128]{0:T(128)S(1)} %pad_add_fusion.2.cols_ref, s32[512]{0:T(512)S(1)} %pad_add_fusion.aggs_ref), custom_call_target="tpu_custom_call" | custom-call | flops 1048576 | bytes 1048576 | tf_op jit(solution)/shard_map/pallas_call | solution.py:132
  60.7 0.5 collective-permute-start.20
  61.2 6.3 %shard_map.56 = (bf16[160,128,128]{2,1,0:T(8,128)(2,1)S(1)}, bf16[64,128,128]{2,1,0:T(8,128)(2,1)S(1)}) custom-call(s32[161]{0:T(256)S(1)} %get-tuple-element.46.plan_ref, s32[5]{0:T(128)S(1)} %get-tuple-element.47.starts_ref, bf16[64,128,128]{2,1,0:T(8,128)(2,1)} %bitcast.203, bf16[64,128,128]{2,1,0:T(8,128)(2,1)S(1)} %collective-permute-done.14.refs_1_, ...), custom_call_target="tpu_custom_call" | custom-call | flops 268435456 | bytes 16777216 | tf_op jit(solution)/shard_map/pallas_call | solution.py:208
  67.6 1.9 %collective-permute-done.21.far2 = bf16[16,128,128]{2,1,0:T(8,128)(2,1)S(1)} collective-permute-done((bf16[16,128,128]{2,1,0:T(8,128)(2,1)S(1)}, bf16[16,128,128]{2,1,0:T(8,128)(2,1)S(1)}, u32[]{:S(2)}, u32[]{:S(2)}) %collective-permute-start.21) | collective-permute-done | bytes 524320 | tf_op jit(solution)/shard_map/ppermute | solution.py:22
  69.5 5.0 %shard_map.57 = (bf16[2,2,2,1,1,8,32,128]{7,6,5,4,3,2,1,0:T(8,128)(2,1)S(1)}, f32[2,2,2,1,1,8,32,128]{7,6,5,4,3,2,1,0:T(8,128)S(1)}, bf16[2,2,2,1,1,8,32,128]{7,...) custom-call(s32[161]{0:T(256)S(1)} %get-tuple-element.46.plan_ref, ...), custom_call_target="tpu_custom_call" | custom-call | flops 268435456 | bytes 16777216 | tf_op jit(solution)/shard_map/pallas_call | solution.py:324
  74.5 2.3 %collective-permute-start.23 = (bf16[2,2,2,1,1,8,32,128]{7,6,5,2,4,3,1,0:T(8,128)(2,1)S(1)}, bf16[2,2,2,1,1,8,32,128]{7,6,5,2,4,3,1,0:T(8,128)(2,1)S(1)}, u32[]{:S(2)}, u32[]{:S(2)}) collective-permute-start(bf16[2,2,2,1,1,8,32,128]{7,6,5,2,4,3,1,0:T(8,128)(2,1)S(1)} %bitcast.201), channel_id=1, source_target_pairs={{0,8},{4,12},{8,0},{12,4},{16,24},{20,28},{24,16},{28,20},{1,9},{5... | collective-permute-start | bytes 1572872 | tf_op jit(solution)/shard_map/ppermute | solution.py:22
  76.7 1.3 %collective-permute-start.31 = (bf16[2,2,2,1,1,8,32,128]{7,6,5,2,4,3,1,0:T(8,128)(2,1)S(1)}, bf16[2,2,2,1,1,8,32,128]{7,6,5,2,4,3,1,0:T(8,128)(2,1)S(1)}, u32[]{:S(2)}, u32[]{:S(2)}) collective-permute-start(bf16[2,2,2,1,1,8,32,128]{7,6,5,2,4,3,1,0:T(8,128)(2,1)S(1)} %bitcast.199), channel_id=1, source_target_pairs={{0,2},{1,3},{2,0},{3,1},{4,6},{5,7},{6,4},{7,5},{8,10},{9,11},{10,... | collective-permute-start | bytes 1572872 | tf_op jit(solution)/shard_map/ppermute | solution.py:22
  78.0 0.9 collective-permute-start.35
  78.9 10.6 %collective-permute-done.23 = bf16[2,2,2,1,1,8,32,128]{7,6,5,2,4,3,1,0:T(8,128)(2,1)S(1)} collective-permute-done((bf16[2,2,2,1,1,8,32,128]{7,6,5,2,4,3,1,0:T(8,128)(2,1)S(1)}, bf16[2,2,2,1,1,8,32,128]{7,6,5,2,4,3,1,0:T(8,128)(2,1)S(1)}, u32[]{:S(2)}, u32[]{:S(2)}) %collective-permute-start.23) | collective-permute-done | bytes 524320 | tf_op jit(solution)/shard_map/ppermute | solution.py:22
  89.7 0.7 collective-permute-start.24
  90.6 1.6 %collective-permute-start.28 = (bf16[2,2,1,1,8,32,128]{6,5,4,3,2,1,0:T(8,128)(2,1)S(1)}, bf16[2,2,1,1,8,32,128]{6,5,4,3,2,1,0:T(8,128)(2,1)S(1)}, u32[]{:S(2)}, u32[]{:S(2)}) collective-permute-start(bf16[2,2,1,1,8,32,128]{6,5,4,3,2,1,0:T(8,128)(2,1)S(1)} %get-tuple-element.75), channel_id=1, source_target_pairs={{0,16},{4,20},{8,24},{12,28},{16,0},{20,4},{24,8},{28,12},{1,17},{... | collective-permute-start | bytes 786440 | tf_op jit(solution)/shard_map/ppermute | solution.py:22
  92.3 1.3 %collective-permute-start.32 = (bf16[2,2,1,1,8,32,128]{6,5,4,3,2,1,0:T(8,128)(2,1)S(1)}, bf16[2,2,1,1,8,32,128]{6,5,4,3,2,1,0:T(8,128)(2,1)S(1)}, u32[]{:S(2)}, u32[]{:S(2)}) collective-permute-start(bf16[2,2,1,1,8,32,128]{6,5,4,3,2,1,0:T(8,128)(2,1)S(1)} %get-tuple-element.77), channel_id=1, source_target_pairs={{0,4},{4,0},{8,12},{12,8},{16,20},{20,16},{24,28},{28,24},{1,5},{5... | collective-permute-start | bytes 786440 | tf_op jit(solution)/shard_map/ppermute | solution.py:22
  93.6 11.7 %collective-permute-done.35 = bf16[2,2,2,1,1,8,32,128]{7,6,5,2,4,3,1,0:T(8,128)(2,1)S(1)} collective-permute-done((bf16[2,2,2,1,1,8,32,128]{7,6,5,2,4,3,1,0:T(8,128)(2,1)S(1)}, bf16[2,2,2,1,1,8,32,128]{7,6,5,2,4,3,1,0:T(8,128)(2,1)S(1)}, u32[]{:S(2)}, u32[]{:S(2)}) %collective-permute-start.35) | collective-permute-done | bytes 524320 | tf_op jit(solution)/shard_map/ppermute | solution.py:22
  105.4 1.1 collective-permute-start.36
  106.7 0.9 collective-permute-start.25
  107.6 0.5 collective-permute-start.29
  108.2 2.5 %collective-permute-start.33 = (bf16[2,1,1,8,32,128]{5,4,3,2,1,0:T(8,128)(2,1)S(1)}, bf16[2,1,1,8,32,128]{5,4,3,2,1,0:T(8,128)(2,1)S(1)}, u32[]{:S(2)}, u32[]{:S(2)}) collective-permute-start(bf16[2,1,1,8,32,128]{5,4,3,2,1,0:T(8,128)(2,1)S(1)} %get-tuple-element.83), channel_id=1, source_target_pairs={{0,8},{4,12},{8,0},{12,4},{16,24},{20,28},{24,16},{28,20},{1,9},{5... | collective-permute-start | bytes 393224 | tf_op jit(solution)/shard_map/ppermute | solution.py:22
  110.7 3.3 %collective-permute-done.36 = bf16[2,2,1,1,8,32,128]{6,5,4,1,0,3,2:T(8,128)(2,1)S(1)} collective-permute-done((bf16[2,2,1,1,8,32,128]{6,5,4,1,0,3,2:T(8,128)(2,1)S(1)}, bf16[2,2,1,1,8,32,128]{6,5,4,1,0,3,2:T(8,128)(2,1)S(1)}, u32[]{:S(2)}, u32[]{:S(2)}) %collective-permute-start.36) | collective-permute-done | bytes 262176 | tf_op jit(solution)/shard_map/ppermute | solution.py:22
  114.1 0.9 collective-permute-start.37
  115.0 0.4 collective-permute-done.25
  115.4 1.3 %collective-permute-start.26 = (bf16[1,1,8,32,128]{4,3,2,1,0:T(8,128)(2,1)S(1)}, bf16[1,1,8,32,128]{4,3,2,1,0:T(8,128)(2,1)S(1)}, u32[]{:S(2)}, u32[]{:S(2)}) collective-permute-start(bf16[1,1,8,32,128]{4,3,2,1,0:T(8,128)(2,1)S(1)} %fusion.44), channel_id=1, source_target_pairs={{0,2},{1,3},{2,0},{3,1},{4,6},{5,7},{6,4},{7,5},{8,10},{9,11},{10,... | collective-permute-start | bytes 196616 | tf_op jit(solution)/shard_map/ppermute | solution.py:22
  116.7 2.6 %collective-permute-start.30 = (bf16[1,1,8,32,128]{4,3,2,1,0:T(8,128)(2,1)S(1)}, bf16[1,1,8,32,128]{4,3,2,1,0:T(8,128)(2,1)S(1)}, u32[]{:S(2)}, u32[]{:S(2)}) collective-permute-start(bf16[1,1,8,32,128]{4,3,2,1,0:T(8,128)(2,1)S(1)} %fusion.45), channel_id=1, source_target_pairs={{0,8},{4,12},{8,0},{12,4},{16,24},{20,28},{24,16},{28,20},{1,9},{5... | collective-permute-start | bytes 196616 | tf_op jit(solution)/shard_map/ppermute | solution.py:22
  119.4 3.3 %collective-permute-done.37 = bf16[2,1,1,8,32,128]{5,4,3,0,2,1:T(8,128)(2,1)S(1)} collective-permute-done((bf16[2,1,1,8,32,128]{5,4,3,0,2,1:T(8,128)(2,1)S(1)}, bf16[2,1,1,8,32,128]{5,4,3,0,2,1:T(8,128)(2,1)S(1)}, u32[]{:S(2)}, u32[]{:S(2)}) %collective-permute-start.37) | collective-permute-done | bytes 131104 | tf_op jit(solution)/shard_map/ppermute | solution.py:22
  122.9 1.7 %collective-permute-done.34 = bf16[1,1,8,32,128]{4,3,2,1,0:T(8,128)(2,1)S(1)} collective-permute-done((bf16[1,1,8,32,128]{4,3,2,1,0:T(8,128)(2,1)S(1)}, bf16[1,1,8,32,128]{4,3,2,1,0:T(8,128)(2,1)S(1)}, u32[]{:S(2)}, u32[]{:S(2)}) %collective-permute-start.34) | collective-permute-done | bytes 65568 | tf_op jit(solution)/shard_map/ppermute | solution.py:22
  124.7 2.3 %collective-permute-done.38 = bf16[1,1,8,32,128]{4,3,2,1,0:T(8,128)(2,1)S(1)} collective-permute-done((bf16[1,1,8,32,128]{4,3,2,1,0:T(8,128)(2,1)S(1)}, bf16[1,1,8,32,128]{4,3,2,1,0:T(8,128)(2,1)S(1)}, u32[]{:S(2)}, u32[]{:S(2)}) %collective-permute-start.38) | collective-permute-done | bytes 65568 | tf_op jit(solution)/shard_map/ppermute | solution.py:22
  127.0 0.8 pad_maximum_fusion
  (56 shorter events, 2.0 us)
Async XLA Ops:
  0.0 15.4 %collective-permute-start = (bf16[16,128,128]{2,1,0:T(8,128)(2,1)}, bf16[16,128,128]{2,1,0:T(8,128)(2,1)S(1)}, u32[]{:S(2)}, u32[]{:S(2)}) collective-permute-start(bf16[16,128,128]{2,1,0:T(8,128)(2,1)} %refs_2_.1), channel_id=1, source_target_pairs={{0,8},{1,5},{2,10},{3,7},{8,16},{9,1},{10,18},{11,3},{16,24},{17,9... | collective-permute-start | bytes 1572872 | tf_op jit(solution)/shard_map/ppermute | solution.py:356
  3.0 12.4 %collective-permute-start.1 = (bf16[16,128,128]{2,1,0:T(8,128)(2,1)}, bf16[16,128,128]{2,1,0:T(8,128)(2,1)S(1)}, u32[]{:S(2)}, u32[]{:S(2)}) collective-permute-start(bf16[16,128,128]{2,1,0:T(8,128)(2,1)} %refs_2_.1), channel_id=1, source_target_pairs={{0,4},{1,9},{2,6},{3,11},{8,0},{9,17},{10,2},{11,19},{16,8},{17,25... | collective-permute-start | bytes 1572872 | tf_op jit(solution)/shard_map/ppermute | solution.py:356
  3.0 12.4 %collective-permute-start.2 = (bf16[16,128,128]{2,1,0:T(8,128)(2,1)}, bf16[16,128,128]{2,1,0:T(8,128)(2,1)S(1)}, u32[]{:S(2)}, u32[]{:S(2)}) collective-permute-start(bf16[16,128,128]{2,1,0:T(8,128)(2,1)} %refs_2_.1), channel_id=1, source_target_pairs={{0,1},{1,0},{2,3},{3,2},{4,5},{5,4},{6,7},{7,6},{8,9},{9,8},{10,11... | collective-permute-start | bytes 1572872 | tf_op jit(solution)/shard_map/ppermute | solution.py:22
  3.0 14.7 %collective-permute-start.4 = (bf16[16,128,128]{2,1,0:T(8,128)(2,1)}, bf16[16,128,128]{2,1,0:T(8,128)(2,1)S(1)}, u32[]{:S(2)}, u32[]{:S(2)}) collective-permute-start(bf16[16,128,128]{2,1,0:T(8,128)(2,1)} %refs_2_.1), channel_id=1, source_target_pairs={{0,2},{1,3},{2,0},{3,1},{4,6},{5,7},{6,4},{7,5},{8,10},{9,11},{10,... | collective-permute-start | bytes 1572872 | tf_op jit(solution)/shard_map/ppermute | solution.py:22
  5.0 1.3 collective-permute-start.3
  17.8 16.0 %collective-permute-start.5 = (bf16[16,128,128]{2,1,0:T(8,128)(2,1)S(1)}, bf16[16,128,128]{2,1,0:T(8,128)(2,1)S(1)}, u32[]{:S(2)}, u32[]{:S(2)}) collective-permute-start(bf16[16,128,128]{2,1,0:T(8,128)(2,1)S(1)} %collective-permute-done.refs_11_), channel_id=1, source_target_pairs={{0,8},{1,5},{2,10},{3,7},{8,16},{9,1},{10,18},{11,3},{16,24},{17,9... | collective-permute-start | bytes 1572872 | tf_op jit(solution)/shard_map/ppermute | solution.py:356
  19.6 14.2 %collective-permute-start.6 = (bf16[16,128,128]{2,1,0:T(8,128)(2,1)S(1)}, bf16[16,128,128]{2,1,0:T(8,128)(2,1)S(1)}, u32[]{:S(2)}, u32[]{:S(2)}) collective-permute-start(bf16[16,128,128]{2,1,0:T(8,128)(2,1)S(1)} %collective-permute-done.1.refs_6_), channel_id=1, source_target_pairs={{0,4},{1,9},{2,6},{3,11},{8,0},{9,17},{10,2},{11,19},{16,8},{17,25... | collective-permute-start | bytes 1572872 | tf_op jit(solution)/shard_map/ppermute | solution.py:356
  19.8 12.6 %collective-permute-start.7 = (s32[64]{0:T(128)S(1)}, s32[64]{0:T(128)S(1)}, u32[]{:S(2)}, u32[]{:S(2)}) collective-permute-start(s32[64]{0:T(128)S(1)} %bitcast_add_fusion), channel_id=1, source_target_pairs={{0,4},{4,0},{8,12},{12,8},{16,20},{20,16},{24,28},{28,24},{1,5},{5... | collective-permute-start | bytes 776 | tf_op jit(solution)/shard_map/ppermute | solution.py:22
  21.6 10.8 %collective-permute-start.8 = (s32[64]{0:T(128)S(1)}, s32[64]{0:T(128)S(1)}, u32[]{:S(2)}, u32[]{:S(2)}) collective-permute-start(s32[64]{0:T(128)S(1)} %bitcast_add_fusion), channel_id=1, source_target_pairs={{0,8},{4,12},{8,0},{12,4},{16,24},{20,28},{24,16},{28,20},{1,9},{5... | collective-permute-start | bytes 776 | tf_op jit(solution)/shard_map/ppermute | solution.py:22
  23.1 10.6 %collective-permute-start.9 = (s32[64]{0:T(128)S(1)}, s32[64]{0:T(128)S(1)}, u32[]{:S(2)}, u32[]{:S(2)}) collective-permute-start(s32[64]{0:T(128)S(1)} %bitcast_add_fusion), channel_id=1, source_target_pairs={{0,12},{4,8},{8,4},{12,0},{16,28},{20,24},{24,20},{28,16},{1,13},{... | collective-permute-start | bytes 776 | tf_op jit(solution)/shard_map/ppermute | solution.py:22
  33.8 27.4 %collective-permute-start.14 = (bf16[64,128,128]{2,1,0:T(8,128)(2,1)}, bf16[64,128,128]{2,1,0:T(8,128)(2,1)S(1)}, u32[]{:S(2)}, u32[]{:S(2)}) collective-permute-start(bf16[64,128,128]{2,1,0:T(8,128)(2,1)} %bitcast.202), channel_id=1, source_target_pairs={{0,1},{1,0},{2,3},{3,2},{4,5},{5,4},{6,7},{7,6},{8,9},{9,8},{10,11... | collective-permute-start | bytes 6291464 | tf_op jit(solution)/shard_map/ppermute | solution.py:22
  33.9 14.3 %collective-permute-start.12 = (bf16[16,128,128]{2,1,0:T(8,128)(2,1)S(1)}, bf16[16,128,128]{2,1,0:T(8,128)(2,1)S(1)}, u32[]{:S(2)}, u32[]{:S(2)}) collective-permute-start(bf16[16,128,128]{2,1,0:T(8,128)(2,1)S(1)} %collective-permute-done.6.refs_7_), channel_id=1, source_target_pairs={{0,4},{1,9},{2,6},{3,11},{8,0},{9,17},{10,2},{11,19},{16,8},{17,25... | collective-permute-start | bytes 1572872 | tf_op jit(solution)/shard_map/ppermute | solution.py:356
  34.6 13.6 %collective-permute-start.11 = (bf16[16,128,128]{2,1,0:T(8,128)(2,1)S(1)}, bf16[16,128,128]{2,1,0:T(8,128)(2,1)S(1)}, u32[]{:S(2)}, u32[]{:S(2)}) collective-permute-start(bf16[16,128,128]{2,1,0:T(8,128)(2,1)S(1)} %collective-permute-done.5.refs_10_), channel_id=1, source_target_pairs={{0,8},{1,5},{2,10},{3,7},{8,16},{9,1},{10,18},{11,3},{16,24},{17,9... | collective-permute-start | bytes 1572872 | tf_op jit(solution)/shard_map/ppermute | solution.py:356
  36.0 17.1 %collective-permute-start.15 = (bf16[16,128,128]{2,1,0:T(8,128)(2,1)S(1)}, bf16[16,128,128]{2,1,0:T(8,128)(2,1)S(1)}, u32[]{:S(2)}, u32[]{:S(2)}) collective-permute-start(bf16[16,128,128]{2,1,0:T(8,128)(2,1)S(1)} %collective-permute-done.4.refs_3_), channel_id=1, source_target_pairs={{0,1},{1,0},{2,3},{3,2},{4,5},{5,4},{6,7},{7,6},{8,9},{9,8},{10,11... | collective-permute-start | bytes 1572872 | tf_op jit(solution)/shard_map/ppermute | solution.py:22
  48.2 5.3 %collective-permute-start.16 = (bf16[16,128,128]{2,1,0:T(8,128)(2,1)S(1)}, bf16[16,128,128]{2,1,0:T(8,128)(2,1)S(1)}, u32[]{:S(2)}, u32[]{:S(2)}) collective-permute-start(bf16[16,128,128]{2,1,0:T(8,128)(2,1)S(1)} %collective-permute-done.1.refs_6_), channel_id=1, source_target_pairs={{0,1},{1,0},{2,3},{3,2},{4,5},{5,4},{6,7},{7,6},{8,9},{9,8},{10,11... | collective-permute-start | bytes 1572872 | tf_op jit(solution)/shard_map/ppermute | solution.py:22
  48.6 4.5 %collective-permute-start.10 = (s32[256]{0:T(256)S(1)}, s32[256]{0:T(256)S(1)}, u32[]{:S(2)}, u32[]{:S(2)}) collective-permute-start(s32[256]{0:T(256)S(1)} %pad_add_fusion.1), channel_id=1, source_target_pairs={{0,16},{4,20},{8,24},{12,28},{16,0},{20,4},{24,8},{28,12},{1,17},{... | collective-permute-start | bytes 3080 | tf_op jit(solution)/shard_map/ppermute | solution.py:22
  50.9 9.7 %collective-permute-start.17 = (bf16[16,128,128]{2,1,0:T(8,128)(2,1)S(1)}, bf16[16,128,128]{2,1,0:T(8,128)(2,1)S(1)}, u32[]{:S(2)}, u32[]{:S(2)}) collective-permute-start(bf16[16,128,128]{2,1,0:T(8,128)(2,1)S(1)} %collective-permute-done.6.refs_7_), channel_id=1, source_target_pairs={{0,1},{1,0},{2,3},{3,2},{4,5},{5,4},{6,7},{7,6},{8,9},{9,8},{10,11... | collective-permute-start | bytes 1572872 | tf_op jit(solution)/shard_map/ppermute | solution.py:22
  53.0 7.7 %collective-permute-start.18 = (bf16[16,128,128]{2,1,0:T(8,128)(2,1)S(1)}, bf16[16,128,128]{2,1,0:T(8,128)(2,1)S(1)}, u32[]{:S(2)}, u32[]{:S(2)}) collective-permute-start(bf16[16,128,128]{2,1,0:T(8,128)(2,1)S(1)} %collective-permute-done.5.refs_10_), channel_id=1, source_target_pairs={{0,1},{1,0},{2,3},{3,2},{4,5},{5,4},{6,7},{7,6},{8,9},{9,8},{10,11... | collective-permute-start | bytes 1572872 | tf_op jit(solution)/shard_map/ppermute | solution.py:22
  53.0 8.2 %collective-permute-start.19 = (bf16[16,128,128]{2,1,0:T(8,128)(2,1)S(1)}, bf16[16,128,128]{2,1,0:T(8,128)(2,1)S(1)}, u32[]{:S(2)}, u32[]{:S(2)}) collective-permute-start(bf16[16,128,128]{2,1,0:T(8,128)(2,1)S(1)} %collective-permute-done.refs_11_), channel_id=1, source_target_pairs={{0,1},{1,0},{2,3},{3,2},{4,5},{5,4},{6,7},{7,6},{8,9},{9,8},{10,11... | collective-permute-start | bytes 1572872 | tf_op jit(solution)/shard_map/ppermute | solution.py:22
  53.5 14.0 %collective-permute-start.13 = (bf16[16,128,128]{2,1,0:T(8,128)(2,1)S(1)}, bf16[16,128,128]{2,1,0:T(8,128)(2,1)S(1)}, u32[]{:S(2)}, u32[]{:S(2)}) collective-permute-start(bf16[16,128,128]{2,1,0:T(8,128)(2,1)S(1)} %collective-permute-done.11.refs_9_), channel_id=1, source_target_pairs={{0,8},{1,5},{2,10},{3,7},{8,16},{9,1},{10,18},{11,3},{16,24},{17,9... | collective-permute-start | bytes 1572872 | tf_op jit(solution)/shard_map/ppermute | solution.py:356
  60.6 7.0 %collective-permute-start.22 = (bf16[16,128,128]{2,1,0:T(8,128)(2,1)S(1)}, bf16[16,128,128]{2,1,0:T(8,128)(2,1)S(1)}, u32[]{:S(2)}, u32[]{:S(2)}) collective-permute-start(bf16[16,128,128]{2,1,0:T(8,128)(2,1)S(1)} %collective-permute-done.11.refs_9_), channel_id=1, source_target_pairs={{0,1},{1,0},{2,3},{3,2},{4,5},{5,4},{6,7},{7,6},{8,9},{9,8},{10,11... | collective-permute-start | bytes 1572872 | tf_op jit(solution)/shard_map/ppermute | solution.py:22
  60.7 6.9 %collective-permute-start.20 = (bf16[16,128,128]{2,1,0:T(8,128)(2,1)S(1)}, bf16[16,128,128]{2,1,0:T(8,128)(2,1)S(1)}, u32[]{:S(2)}, u32[]{:S(2)}) collective-permute-start(bf16[16,128,128]{2,1,0:T(8,128)(2,1)S(1)} %collective-permute-done.12.refs_8_), channel_id=1, source_target_pairs={{0,1},{1,0},{2,3},{3,2},{4,5},{5,4},{6,7},{7,6},{8,9},{9,8},{10,11... | collective-permute-start | bytes 1572872 | tf_op jit(solution)/shard_map/ppermute | solution.py:22
  67.5 2.0 %collective-permute-start.21 = (bf16[16,128,128]{2,1,0:T(8,128)(2,1)S(1)}, bf16[16,128,128]{2,1,0:T(8,128)(2,1)S(1)}, u32[]{:S(2)}, u32[]{:S(2)}) collective-permute-start(bf16[16,128,128]{2,1,0:T(8,128)(2,1)S(1)} %collective-permute-done.13.far0), channel_id=1, source_target_pairs={{0,1},{1,0},{2,3},{3,2},{4,5},{5,4},{6,7},{7,6},{8,9},{9,8},{10,11... | collective-permute-start | bytes 1572872 | tf_op jit(solution)/shard_map/ppermute | solution.py:22
  74.5 15.1 %collective-permute-start.23 = (bf16[2,2,2,1,1,8,32,128]{7,6,5,2,4,3,1,0:T(8,128)(2,1)S(1)}, bf16[2,2,2,1,1,8,32,128]{7,6,5,2,4,3,1,0:T(8,128)(2,1)S(1)}, u32[]{:S(2)}, u32[]{:S(2)}) collective-permute-start(bf16[2,2,2,1,1,8,32,128]{7,6,5,2,4,3,1,0:T(8,128)(2,1)S(1)} %bitcast.201), channel_id=1, source_target_pairs={{0,8},{4,12},{8,0},{12,4},{16,24},{20,28},{24,16},{28,20},{1,9},{5... | collective-permute-start | bytes 1572872 | tf_op jit(solution)/shard_map/ppermute | solution.py:22
  76.7 13.7 %collective-permute-start.27 = (bf16[2,2,2,1,1,8,32,128]{7,6,5,2,4,3,1,0:T(8,128)(2,1)S(1)}, bf16[2,2,2,1,1,8,32,128]{7,6,5,2,4,3,1,0:T(8,128)(2,1)S(1)}, u32[]{:S(2)}, u32[]{:S(2)}) collective-permute-start(bf16[2,2,2,1,1,8,32,128]{7,6,5,2,4,3,1,0:T(8,128)(2,1)S(1)} %bitcast.200), channel_id=1, source_target_pairs={{0,4},{4,0},{8,12},{12,8},{16,20},{20,16},{24,28},{28,24},{1,5},{5... | collective-permute-start | bytes 1572872 | tf_op jit(solution)/shard_map/ppermute | solution.py:22
  76.7 15.4 %collective-permute-start.31 = (bf16[2,2,2,1,1,8,32,128]{7,6,5,2,4,3,1,0:T(8,128)(2,1)S(1)}, bf16[2,2,2,1,1,8,32,128]{7,6,5,2,4,3,1,0:T(8,128)(2,1)S(1)}, u32[]{:S(2)}, u32[]{:S(2)}) collective-permute-start(bf16[2,2,2,1,1,8,32,128]{7,6,5,2,4,3,1,0:T(8,128)(2,1)S(1)} %bitcast.199), channel_id=1, source_target_pairs={{0,2},{1,3},{2,0},{3,1},{4,6},{5,7},{6,4},{7,5},{8,10},{9,11},{10,... | collective-permute-start | bytes 1572872 | tf_op jit(solution)/shard_map/ppermute | solution.py:22
  78.0 27.3 %collective-permute-start.35 = (bf16[2,2,2,1,1,8,32,128]{7,6,5,2,4,3,1,0:T(8,128)(2,1)S(1)}, bf16[2,2,2,1,1,8,32,128]{7,6,5,2,4,3,1,0:T(8,128)(2,1)S(1)}, u32[]{:S(2)}, u32[]{:S(2)}) collective-permute-start(bf16[2,2,2,1,1,8,32,128]{7,6,5,2,4,3,1,0:T(8,128)(2,1)S(1)} %bitcast.198), channel_id=1, source_target_pairs={{0,8},{4,12},{8,0},{12,4},{16,24},{20,28},{24,16},{28,20},{1,9},{5... | collective-permute-start | bytes 1572872 | tf_op jit(solution)/shard_map/ppermute | solution.py:22
  89.7 16.9 %collective-permute-start.24 = (bf16[2,2,1,1,8,32,128]{6,5,4,3,2,1,0:T(8,128)(2,1)S(1)}, bf16[2,2,1,1,8,32,128]{6,5,4,3,2,1,0:T(8,128)(2,1)S(1)}, u32[]{:S(2)}, u32[]{:S(2)}) collective-permute-start(bf16[2,2,1,1,8,32,128]{6,5,4,3,2,1,0:T(8,128)(2,1)S(1)} %get-tuple-element.73), channel_id=1, source_target_pairs={{0,4},{4,0},{8,12},{12,8},{16,20},{20,16},{24,28},{28,24},{1,5},{5... | collective-permute-start | bytes 786440 | tf_op jit(solution)/shard_map/ppermute | solution.py:22
  90.6 16.9 %collective-permute-start.28 = (bf16[2,2,1,1,8,32,128]{6,5,4,3,2,1,0:T(8,128)(2,1)S(1)}, bf16[2,2,1,1,8,32,128]{6,5,4,3,2,1,0:T(8,128)(2,1)S(1)}, u32[]{:S(2)}, u32[]{:S(2)}) collective-permute-start(bf16[2,2,1,1,8,32,128]{6,5,4,3,2,1,0:T(8,128)(2,1)S(1)} %get-tuple-element.75), channel_id=1, source_target_pairs={{0,16},{4,20},{8,24},{12,28},{16,0},{20,4},{24,8},{28,12},{1,17},{... | collective-permute-start | bytes 786440 | tf_op jit(solution)/shard_map/ppermute | solution.py:22
  92.3 15.8 %collective-permute-start.32 = (bf16[2,2,1,1,8,32,128]{6,5,4,3,2,1,0:T(8,128)(2,1)S(1)}, bf16[2,2,1,1,8,32,128]{6,5,4,3,2,1,0:T(8,128)(2,1)S(1)}, u32[]{:S(2)}, u32[]{:S(2)}) collective-permute-start(bf16[2,2,1,1,8,32,128]{6,5,4,3,2,1,0:T(8,128)(2,1)S(1)} %get-tuple-element.77), channel_id=1, source_target_pairs={{0,4},{4,0},{8,12},{12,8},{16,20},{20,16},{24,28},{28,24},{1,5},{5... | collective-permute-start | bytes 786440 | tf_op jit(solution)/shard_map/ppermute | solution.py:22
  105.4 8.7 %collective-permute-start.36 = (bf16[2,2,1,1,8,32,128]{6,5,4,1,0,3,2:T(8,128)(2,1)S(1)}, bf16[2,2,1,1,8,32,128]{6,5,4,1,0,3,2:T(8,128)(2,1)S(1)}, u32[]{:S(2)}, u32[]{:S(2)}) collective-permute-start(bf16[2,2,1,1,8,32,128]{6,5,4,1,0,3,2:T(8,128)(2,1)S(1)} %fusion.4), channel_id=1, source_target_pairs={{0,2},{1,3},{2,0},{3,1},{4,6},{5,7},{6,4},{7,5},{8,10},{9,11},{10,... | collective-permute-start | bytes 786440 | tf_op jit(solution)/shard_map/ppermute | solution.py:22
  106.7 8.7 %collective-permute-start.25 = (bf16[2,1,1,8,32,128]{5,4,3,2,1,0:T(8,128)(2,1)S(1)}, bf16[2,1,1,8,32,128]{5,4,3,2,1,0:T(8,128)(2,1)S(1)}, u32[]{:S(2)}, u32[]{:S(2)}) collective-permute-start(bf16[2,1,1,8,32,128]{5,4,3,2,1,0:T(8,128)(2,1)S(1)} %get-tuple-element.79), channel_id=1, source_target_pairs={{0,16},{4,20},{8,24},{12,28},{16,0},{20,4},{24,8},{28,12},{1,17},{... | collective-permute-start | bytes 393224 | tf_op jit(solution)/shard_map/ppermute | solution.py:22
  107.6 9.1 %collective-permute-start.29 = (bf16[2,1,1,8,32,128]{5,4,3,2,1,0:T(8,128)(2,1)S(1)}, bf16[2,1,1,8,32,128]{5,4,3,2,1,0:T(8,128)(2,1)S(1)}, u32[]{:S(2)}, u32[]{:S(2)}) collective-permute-start(bf16[2,1,1,8,32,128]{5,4,3,2,1,0:T(8,128)(2,1)S(1)} %get-tuple-element.81), channel_id=1, source_target_pairs={{0,2},{1,3},{2,0},{3,1},{4,6},{5,7},{6,4},{7,5},{8,10},{9,11},{10,... | collective-permute-start | bytes 393224 | tf_op jit(solution)/shard_map/ppermute | solution.py:22
  108.2 11.1 %collective-permute-start.33 = (bf16[2,1,1,8,32,128]{5,4,3,2,1,0:T(8,128)(2,1)S(1)}, bf16[2,1,1,8,32,128]{5,4,3,2,1,0:T(8,128)(2,1)S(1)}, u32[]{:S(2)}, u32[]{:S(2)}) collective-permute-start(bf16[2,1,1,8,32,128]{5,4,3,2,1,0:T(8,128)(2,1)S(1)} %get-tuple-element.83), channel_id=1, source_target_pairs={{0,8},{4,12},{8,0},{12,4},{16,24},{20,28},{24,16},{28,20},{1,9},{5... | collective-permute-start | bytes 393224 | tf_op jit(solution)/shard_map/ppermute | solution.py:22
  114.1 8.6 %collective-permute-start.37 = (bf16[2,1,1,8,32,128]{5,4,3,0,2,1:T(8,128)(2,1)S(1)}, bf16[2,1,1,8,32,128]{5,4,3,0,2,1:T(8,128)(2,1)S(1)}, u32[]{:S(2)}, u32[]{:S(2)}) collective-permute-start(bf16[2,1,1,8,32,128]{5,4,3,0,2,1:T(8,128)(2,1)S(1)} %fusion.23), channel_id=1, source_target_pairs={{0,16},{4,20},{8,24},{12,28},{16,0},{20,4},{24,8},{28,12},{1,17},{... | collective-permute-start | bytes 393224 | tf_op jit(solution)/shard_map/ppermute | solution.py:22
  115.4 7.4 %collective-permute-start.26 = (bf16[1,1,8,32,128]{4,3,2,1,0:T(8,128)(2,1)S(1)}, bf16[1,1,8,32,128]{4,3,2,1,0:T(8,128)(2,1)S(1)}, u32[]{:S(2)}, u32[]{:S(2)}) collective-permute-start(bf16[1,1,8,32,128]{4,3,2,1,0:T(8,128)(2,1)S(1)} %fusion.44), channel_id=1, source_target_pairs={{0,2},{1,3},{2,0},{3,1},{4,6},{5,7},{6,4},{7,5},{8,10},{9,11},{10,... | collective-permute-start | bytes 196616 | tf_op jit(solution)/shard_map/ppermute | solution.py:22
  116.7 6.2 %collective-permute-start.30 = (bf16[1,1,8,32,128]{4,3,2,1,0:T(8,128)(2,1)S(1)}, bf16[1,1,8,32,128]{4,3,2,1,0:T(8,128)(2,1)S(1)}, u32[]{:S(2)}, u32[]{:S(2)}) collective-permute-start(bf16[1,1,8,32,128]{4,3,2,1,0:T(8,128)(2,1)S(1)} %fusion.45), channel_id=1, source_target_pairs={{0,8},{4,12},{8,0},{12,4},{16,24},{20,28},{24,16},{28,20},{1,9},{5... | collective-permute-start | bytes 196616 | tf_op jit(solution)/shard_map/ppermute | solution.py:22
  119.3 5.4 %collective-permute-start.34 = (bf16[1,1,8,32,128]{4,3,2,1,0:T(8,128)(2,1)S(1)}, bf16[1,1,8,32,128]{4,3,2,1,0:T(8,128)(2,1)S(1)}, u32[]{:S(2)}, u32[]{:S(2)}) collective-permute-start(bf16[1,1,8,32,128]{4,3,2,1,0:T(8,128)(2,1)S(1)} %fusion.46), channel_id=1, source_target_pairs={{0,16},{4,20},{8,24},{12,28},{16,0},{20,4},{24,8},{28,12},{1,17},{... | collective-permute-start | bytes 196616 | tf_op jit(solution)/shard_map/ppermute | solution.py:22
  122.7 4.3 %collective-permute-start.38 = (bf16[1,1,8,32,128]{4,3,2,1,0:T(8,128)(2,1)S(1)}, bf16[1,1,8,32,128]{4,3,2,1,0:T(8,128)(2,1)S(1)}, u32[]{:S(2)}, u32[]{:S(2)}) collective-permute-start(bf16[1,1,8,32,128]{4,3,2,1,0:T(8,128)(2,1)S(1)} %fusion.47), channel_id=1, source_target_pairs={{0,4},{4,0},{8,12},{12,8},{16,20},{20,16},{24,28},{28,24},{1,5},{5... | collective-permute-start | bytes 196616 | tf_op jit(solution)/shard_map/ppermute | solution.py:22

commit v2 on v1

--- a/solution.py
+++ b/solution.py
@@ -39,8 +39,8 @@
         self.buckets = 2 * self.his
         self.slots = self.pairs + self.buckets * UNROLL
         self.half = rows // 2
-        self.early = (rows - 1, rows - 3)
-        self.near = sum(self.early) * tiles
+        self.early = rows - 1
+        self.near = 2 * self.early * tiles
         cells = 2 * cols * self.per
         self.fields, shift = [], 0
         for size in (self.pairs, 2 * rows * tiles, self.slab, cells):
@@ -82,11 +82,9 @@
         rel_row = (i_agg >> log2(OWN)) ^ row
         turn = ring_place(other_row) - here
         away = jnp.where(((col ^ side) & 1) == 0, turn, -turn) & (s.rows - 1)
-        reach = jnp.abs(away - s.half)
-        late = jnp.where(reach <= side, 1, 0)
-        order = away - jnp.where(away > s.half, 1 + 2 * side, 0) + side * s.early[0]
-        last = jnp.where(side == 0, 0, 2 + away - s.half)
-        piece = jnp.where(late == 1, last, order)
+        late = jnp.where(away == s.half, 1, 0)
+        order = away - jnp.where(away > s.half, 1, 0) + side * s.early
+        piece = jnp.where(late == 1, side, order)
         panel_at = (piece << log2(s.tiles)) + (other & (s.tiles - 1))
         rel_part = (tile >> log2(s.tiles)) ^ col
         part = (rel_part & 1) * (s.cols // 2) + (rel_part >> 1)
@@ -142,7 +140,7 @@
             pltpu.SMEM((s.buckets,), jnp.int32),
         ],
         compiler_params=pltpu.CompilerParams(vmem_limit_bytes=room()),
-        cost_estimate=pl.CostEstimate(flops=1 << 20, bytes_accessed=1 << 20, transcendentals=0),
+        cost_estimate=pl.CostEstimate(flops=1 << 20, bytes_accessed=16 << 20, transcendentals=0),
     )(cols, aggs)
 
 
@@ -153,7 +151,7 @@
         copies.append((refs[k], a_buf.at[pl.ds(k * s.slab, s.slab)]))
     for k in range(s.cols):
         copies.append((refs[2 + k], rows_buf.at[pl.ds(k * s.tiles, s.tiles)]))
-    for k in range(sum(s.early)):
+    for k in range(2 * s.early):
         source = refs[2] if k == 0 else refs[1 + s.cols + k]
         copies.append((source, panel.at[pl.ds(k * s.tiles, s.tiles)]))
     copies = [pltpu.make_async_copy(src, dst, sems.at[k]) for k, (src, dst) in enumerate(copies)]
@@ -214,19 +212,19 @@
         + [pltpu.SemaphoreType.DMA((len(operands) + 1,))],
         compiler_params=pltpu.CompilerParams(vmem_limit_bytes=room(*shapes)),
         cost_estimate=pl.CostEstimate(
-            flops=s.pairs * s.side**3, bytes_accessed=16 << 20, transcendentals=0
+            flops=s.pairs * s.side**3, bytes_accessed=1 << 20, transcendentals=0
         ),
     )(plan, starts, *operands)
 
 
 def sum_kernel(
-    s, plan_ref, starts_ref, slots_ref, rows_ref, far0, far1, far2, far3,
+    s, plan_ref, starts_ref, slots_ref, rows_ref, far0, far1,
     send0, keep0, send1, keep1, send2, keep2, send3, keep3, total, far_buf, sems,
 ):
     hi = pl.program_id(0)
     copies = [
         pltpu.make_async_copy(ref, far_buf.at[pl.ds(k * s.tiles, s.tiles)], sems.at[k])
-        for k, ref in enumerate((far0, far1, far2, far3))
+        for k, ref in enumerate((far0, far1))
     ]
 
     @pl.when(hi == 0)
@@ -312,7 +310,7 @@
         ((2, 1, 2), lambda h: (0, h & 1, 0, h >> 1, 0, 0, 0, 0)),
     ]
     shapes = [
-        ((s.slots + s.slab + 4 * s.tiles, s.side, s.side), jnp.bfloat16),
+        ((s.slots + s.slab + 2 * s.tiles, s.side, s.side), jnp.bfloat16),
         ((2 * s.cols * s.per, s.side, s.side), jnp.float32),
     ]
     out_shape, out_specs = [], []
@@ -324,13 +322,13 @@
     return pl.pallas_call(
         functools.partial(sum_kernel, s),
         grid=(s.his,),
-        in_specs=[smem, smem, vmem, vmem] + [anywhere] * 4,
+        in_specs=[smem, smem, vmem, vmem, anywhere, anywhere],
         out_specs=out_specs,
         out_shape=out_shape,
         scratch_shapes=[
             pltpu.VMEM((2 * s.cols * s.per, s.side, s.side), jnp.float32),
-            pltpu.VMEM((4 * s.tiles, s.side, s.side), jnp.bfloat16),
-            pltpu.SemaphoreType.DMA((4,)),
+            pltpu.VMEM((2 * s.tiles, s.side, s.side), jnp.bfloat16),
+            pltpu.SemaphoreType.DMA((2,)),
         ],
         compiler_params=pltpu.CompilerParams(vmem_limit_bytes=room(*shapes)),
         cost_estimate=pl.CostEstimate(
@@ -355,52 +353,62 @@
                 moves.append((order[k] * s.cols + c, to * s.cols + c))
         return lax.ppermute(value, ("row", "col"), moves)
 
-    first, second = ring(p_tiles, 0), ring(p_tiles, 1)
-    rows = [p_tiles]
+    first = ring(p_tiles, 0)
+    cols = a_cols[:, 0]
+    cols_other = swap(cols, "col", 1)
+    cols_other, mine = barrier((cols_other, p_tiles))
+    second = ring(mine, 1)
+    a_other, p_other = swap(a_blocks[:, 0], "col", 1), swap(p_tiles, "col", 1)
+
+    aggs = owner[:, 0] * OWN + agg_local
+    came, aggs, a_other, p_other = barrier((first, aggs, a_other, p_other))
+    first = ring(first, 0)
+    aggs = [aggs] + [swap(aggs, "row", mask) for mask in (1, 2, 3)]
+    own_near, other_near = {0: p_tiles, s.rows - 1: came, 1: second}, {0: p_other}
+    second = ring(second, 1)
+    aggs, mine = barrier((jnp.concatenate(aggs, 0), p_tiles))
+    bit = 4
+    while bit < s.rows:
+        aggs = jnp.concatenate([aggs, swap(aggs, "row", bit)], 0)
+        bit *= 2
+    rows = [mine]
     bit = 2
     while bit < s.cols:
         rows += [swap(piece, "col", bit) for piece in rows]
         bit *= 2
-    p_other = swap(p_tiles, "col", 1)
-    cols = a_cols[:, 0]
-    cols_other = swap(cols, "col", 1)
-    aggs = owner[:, 0] * OWN + agg_local
-    first, second, p_other, cols_other, aggs, *rows[1:] = barrier(
-        (first, second, p_other, cols_other, aggs, *rows[1:])
-    )
-    own_near = {0: p_tiles, s.rows - 1: first, 1: second}
-    other_near = {0: p_other}
-
-    aggs = [aggs] + [swap(aggs, "row", mask) for mask in (1, 2, 3)]
-    aggs = jnp.concatenate(aggs, 0)
+    plan, starts = make_plan(s, jnp.concatenate([cols, cols_other], 0), aggs)
+
     held = [1, s.rows - 1]
-    for step in range(2, s.half):
-        first, second = barrier((ring(first, 0), ring(second, 1)))
+    for step in range(2, s.half - 1):
+        came, *rest = barrier((second, *(own_near[away] for away in held), *rows[1:]))
+        for away, piece in zip(held, rest):
+            other_near[away] = swap(piece, "col", 1)
         if step == 2:
-            came, aggs, a_own, *rest = barrier((first, aggs, a_blocks[:, 0], *rows[1:]))
-            bit = 4
-            while bit < s.rows:
-                aggs = jnp.concatenate([aggs, swap(aggs, "row", bit)], 0)
-                bit *= 2
-            a_other = swap(a_own, "col", 1)
-            rows += [p_other] + [swap(piece, "col", 1) for piece in rest]
-        else:
-            came, *rest = barrier((first, *(own_near[away] for away in held)))
-            for away, piece in zip(held, rest):
-                other_near[away] = swap(piece, "col", 1)
-            held = []
-        own_near[s.rows - step], own_near[step] = came, second
-        held += [step, s.rows - step]
-
+            rows += [p_other] + [swap(piece, "col", 1) for piece in rest[len(held):]]
+        own_near[s.rows - step], own_near[step] = first, came
+        first, second = ring(first, 0), ring(second, 1)
+        held = [step, s.rows - step]
+
+    others = sorted(set(other_near) - {0})
+    tie = (first, second, plan, starts, *rows[s.cols // 2 + 1:])
+    tie += (*(own_near[away] for away in held), *(other_near[away] for away in others))
+    first, second, plan, starts, *rest = barrier(tie)
+    rows[s.cols // 2 + 1:] = rest[:s.cols // 2 - 1]
+    rest = rest[s.cols // 2 - 1:]
+    for away, piece in zip(others, rest[len(held):]):
+        other_near[away] = piece
     far = ring(first, 0)
-    last_other = [swap(own_near[away], "col", 1) for away in (s.half - 1, s.half + 1)]
-    plan, starts = make_plan(s, jnp.concatenate([cols, cols_other], 0), aggs)
+    own_near[s.half + 1], own_near[s.half - 1] = first, second
+    for away, piece in zip(held, rest):
+        other_near[away] = swap(piece, "col", 1)
+    for away in (s.half + 1, s.half - 1):
+        other_near[away] = swap(own_near[away], "col", 1)
     near = [own_near[k] for k in sorted(own_near)]
     near += [other_near[k] for k in sorted(other_near)]
     slots, rows_t = make_products(s, plan, starts, a_blocks[:, 0], a_other, near, rows)
     far, slots, rows_t = barrier((far, slots, rows_t))
     far_other = swap(far, "col", 1)
-    parts = make_sums(s, plan, starts, slots, rows_t, [far, last_other[0], far_other, last_other[1]])
+    parts = make_sums(s, plan, starts, slots, rows_t, [far, far_other])
 
     y, z1, z2, x1 = ("row", 1), ("row", 2), ("row", 4), ("col", 2)
     orders = [[z1, y, z2, x1], [y, z2, x1, z1], [x1, y, z1, z2], [z1, x1, z2, y]]

time: 128 us -> 114 us (0.89)
  waiting for transfers between devices: 71.8 us -> 49.1 us
  starting transfers between devices: 36 us -> 46.1 us
    ppermute x32, waiting for transfers between devices: 50.4 us -> 33.6 us  [swap(): return lax.ppermute(value, axis, [(i, i ^ bit) for i in range(size)])]
    ppermute x32, starting transfers between devices: 27.7 us -> 34.4 us  [swap(): return lax.ppermute(value, axis, [(i, i ^ bit) for i in range(size)])]
    ppermute x7, waiting for transfers between devices: 21.4 us -> 15.5 us  [ring(): return lax.ppermute(value, ('row', 'col'), moves)]
    ppermute x7, starting transfers between devices: 8.26 us -> 11.6 us  [ring(): return lax.ppermute(value, ('row', 'col'), moves)]
where the time goes in v2:
time: 114 us
  waiting for transfers between devices  49.1 us (43%)
  starting transfers between devices  46.1 us (40%)
  Pallas kernels  15.2 us (13%)
  other arithmetic  3.35 us (3%)
    ppermute x32, starting transfers between devices, swap(): return lax.ppermute(value, axis, [(i, i ^ bit) for i in range(size)])  34.4 us
    ppermute x32, waiting for transfers between devices, swap(): return lax.ppermute(value, axis, [(i, i ^ bit) for i in range(size)])  33.6 us
    ppermute x7, waiting for transfers between devices, ring(): return lax.ppermute(value, ('row', 'col'), moves)  15.5 us
    ppermute x7, starting transfers between devices, ring(): return lax.ppermute(value, ('row', 'col'), moves)  11.6 us
    pallas_call x1, Pallas kernels, make_products(): pl.pallas_call(functools.partial(product_kernel, s), in_specs=[smem, smem...  5.66 us
    pallas_call x1, Pallas kernels, make_plan(): pl.pallas_call(functools.partial(plan_kernel, s), in_specs=[smem, smem],...  4.94 us
    pallas_call x1, Pallas kernels, make_sums(): pl.pallas_call(functools.partial(sum_kernel, s), grid=(s.his,), in_specs=...  4.59 us
  transfers between devices with their start and end apart: 39, of which 16 were waited for; matrix products, arithmetic and copies ran while one was open for 2% of the time, Pallas kernels for 9%

profile of v2, /device:TPU:0, one launch (start us, length us, event | category | flops | bytes accessed | tf_op | source)
XLA Modules:
  0.0 113.9 jit_solution(17615017699462295550)
XLA Ops:
  0.0 0.5 collective-permute-start.7
  0.5 3.0 %collective-permute-start = (bf16[16,128,128]{2,1,0:T(8,128)(2,1)}, bf16[16,128,128]{2,1,0:T(8,128)(2,1)S(1)}, u32[]{:S(2)}, u32[]{:S(2)}) collective-permute-start(bf16[16,128,128]{2,1,0:T(8,128)(2,1)} %refs_2_), channel_id=1, source_target_pairs={{0,8},{1,5},{2,10},{3,7},{8,16},{9,1},{10,18},{11,3},{16,24},{17,9... | collective-permute-start | bytes 1572872 | tf_op jit(solution)/shard_map/ppermute | solution.py:354
  3.5 0.9 collective-permute-done.3
  4.5 2.9 %collective-permute-start.4 = (bf16[16,128,128]{2,1,0:T(8,128)(2,1)}, bf16[16,128,128]{2,1,0:T(8,128)(2,1)S(1)}, u32[]{:S(2)}, u32[]{:S(2)}) collective-permute-start(bf16[16,128,128]{2,1,0:T(8,128)(2,1)} %refs_2_), channel_id=1, source_target_pairs={{0,4},{1,9},{2,6},{3,11},{8,0},{9,17},{10,2},{11,19},{16,8},{17,25... | collective-permute-start | bytes 1572872 | tf_op jit(solution)/shard_map/ppermute | solution.py:354
  7.3 0.7 bitcast_add_fusion
  8.0 5.1 %collective-permute-done.refs_11_ = bf16[16,128,128]{2,1,0:T(8,128)(2,1)S(1)} collective-permute-done((bf16[16,128,128]{2,1,0:T(8,128)(2,1)}, bf16[16,128,128]{2,1,0:T(8,128)(2,1)S(1)}, u32[]{:S(2)}, u32[]{:S(2)}) %collective-permute-start) | collective-permute-done | bytes 524320 | tf_op jit(solution)/shard_map/ppermute | solution.py:354
  13.1 3.3 %collective-permute-start.11 = (s32[64]{0:T(128)S(1)}, s32[64]{0:T(128)S(1)}, u32[]{:S(2)}, u32[]{:S(2)}) collective-permute-start(s32[64]{0:T(128)S(1)} %bitcast_add_fusion), channel_id=1, source_target_pairs={{0,12},{4,8},{8,4},{12,0},{16,28},{20,24},{24,20},{28,16},{1,13},{... | collective-permute-start | bytes 776 | tf_op jit(solution)/shard_map/ppermute | solution.py:22
  16.4 0.4 collective-permute-start.10
  17.1 1.9 %collective-permute-start.1 = (bf16[16,128,128]{2,1,0:T(8,128)(2,1)S(1)}, bf16[16,128,128]{2,1,0:T(8,128)(2,1)S(1)}, u32[]{:S(2)}, u32[]{:S(2)}) collective-permute-start(bf16[16,128,128]{2,1,0:T(8,128)(2,1)S(1)} %collective-permute-done.refs_11_), channel_id=1, source_target_pairs={{0,8},{1,5},{2,10},{3,7},{8,16},{9,1},{10,18},{11,3},{16,24},{17,9... | collective-permute-start | bytes 1572872 | tf_op jit(solution)/shard_map/ppermute | solution.py:354
  19.1 0.9 collective-permute-done.10
  20.5 1.5 %collective-permute-start.13 = (bf16[16,128,128]{2,1,0:T(8,128)(2,1)}, bf16[16,128,128]{2,1,0:T(8,128)(2,1)S(1)}, u32[]{:S(2)}, u32[]{:S(2)}) collective-permute-start(bf16[16,128,128]{2,1,0:T(8,128)(2,1)} %refs_2_), channel_id=1, source_target_pairs={{0,2},{1,3},{2,0},{3,1},{4,6},{5,7},{6,4},{7,5},{8,10},{9,11},{10,... | collective-permute-start | bytes 1572872 | tf_op jit(solution)/shard_map/ppermute | solution.py:22
  22.0 2.6 %collective-permute-start.12 = (s32[256]{0:T(256)S(1)}, s32[256]{0:T(256)S(1)}, u32[]{:S(2)}, u32[]{:S(2)}) collective-permute-start(s32[256]{0:T(256)S(1)} %pad_add_fusion.1), channel_id=1, source_target_pairs={{0,16},{4,20},{8,24},{12,28},{16,0},{20,4},{24,8},{28,12},{1,17},{... | collective-permute-start | bytes 3080 | tf_op jit(solution)/shard_map/ppermute | solution.py:22
  24.6 5.8 %collective-permute-done.1.refs_10_ = bf16[16,128,128]{2,1,0:T(8,128)(2,1)S(1)} collective-permute-done((bf16[16,128,128]{2,1,0:T(8,128)(2,1)S(1)}, bf16[16,128,128]{2,1,0:T(8,128)(2,1)S(1)}, u32[]{:S(2)}, u32[]{:S(2)}) %collective-permute-start.1) | collective-permute-done | bytes 524320 | tf_op jit(solution)/shard_map/ppermute | solution.py:354
  30.4 1.8 %collective-permute-start.2 = (bf16[16,128,128]{2,1,0:T(8,128)(2,1)S(1)}, bf16[16,128,128]{2,1,0:T(8,128)(2,1)S(1)}, u32[]{:S(2)}, u32[]{:S(2)}) collective-permute-start(bf16[16,128,128]{2,1,0:T(8,128)(2,1)S(1)} %collective-permute-done.1.refs_10_), channel_id=1, source_target_pairs={{0,8},{1,5},{2,10},{3,7},{8,16},{9,1},{10,18},{11,3},{16,24},{17,9... | collective-permute-start | bytes 1572872 | tf_op jit(solution)/shard_map/ppermute | solution.py:354
  32.4 0.5 collective-permute-start.15
  33.0 0.7 pad_add_fusion.2.cols_ref
  33.7 4.9 %shard_map.55 = (s32[161]{0:T(256)S(1)}, s32[5]{0:T(128)S(1)}) custom-call(s32[128]{0:T(128)S(1)} %pad_add_fusion.2.cols_ref, s32[512]{0:T(512)S(1)} %pad_add_fusion.aggs_ref), custom_call_target="tpu_custom_call" | custom-call | flops 1048576 | bytes 16777216 | tf_op jit(solution)/shard_map/pallas_call | solution.py:130
  38.6 4.2 %collective-permute-done.2.refs_9_ = bf16[16,128,128]{2,1,0:T(8,128)(2,1)S(1)} collective-permute-done((bf16[16,128,128]{2,1,0:T(8,128)(2,1)S(1)}, bf16[16,128,128]{2,1,0:T(8,128)(2,1)S(1)}, u32[]{:S(2)}, u32[]{:S(2)}) %collective-permute-start.2) | collective-permute-done | bytes 524320 | tf_op jit(solution)/shard_map/ppermute | solution.py:354
  42.9 0.5 collective-permute-start.21
  43.5 0.4 collective-permute-start.20
  43.9 1.7 %collective-permute-start.17 = (bf16[16,128,128]{2,1,0:T(8,128)(2,1)S(1)}, bf16[16,128,128]{2,1,0:T(8,128)(2,1)S(1)}, u32[]{:S(2)}, u32[]{:S(2)}) collective-permute-start(bf16[16,128,128]{2,1,0:T(8,128)(2,1)S(1)} %collective-permute-done.2.refs_9_), channel_id=1, source_target_pairs={{0,8},{1,5},{2,10},{3,7},{8,16},{9,1},{10,18},{11,3},{16,24},{17,9... | collective-permute-start | bytes 1572872 | tf_op jit(solution)/shard_map/ppermute | solution.py:354
  45.6 0.7 collective-permute-done.19.refs_15_
  46.3 0.7 collective-permute-done.20.refs_16_
  47.1 5.7 %shard_map.56 = (bf16[160,128,128]{2,1,0:T(8,128)(2,1)S(1)}, bf16[64,128,128]{2,1,0:T(8,128)(2,1)S(1)}) custom-call(s32[161]{0:T(256)S(1)} %get-tuple-element.53.plan_ref, s32[5]{0:T(128)S(1)} %get-tuple-element.54.starts_ref, bf16[64,128,128]{2,1,0:T(8,128)(2,1)} %bitcast.203, bf16[64,128,128]{2,1,0:T(8,128)(2,1)S(1)} %collective-permute-done.7.refs_1_, ...), custom_call_target="tpu_custom_call" | custom-call | flops 268435456 | bytes 1048576 | tf_op jit(solution)/shard_map/pallas_call | solution.py:206
  53.4 1.7 %collective-permute-done.22.far1 = bf16[16,128,128]{2,1,0:T(8,128)(2,1)S(1)} collective-permute-done((bf16[16,128,128]{2,1,0:T(8,128)(2,1)S(1)}, bf16[16,128,128]{2,1,0:T(8,128)(2,1)S(1)}, u32[]{:S(2)}, u32[]{:S(2)}) %collective-permute-start.22) | collective-permute-done | bytes 524320 | tf_op jit(solution)/shard_map/ppermute | solution.py:22
  55.0 4.6 %shard_map.57 = (bf16[2,2,2,1,1,8,32,128]{7,6,5,4,3,2,1,0:T(8,128)(2,1)S(1)}, f32[2,2,2,1,1,8,32,128]{7,6,5,4,3,2,1,0:T(8,128)S(1)}, bf16[2,2,2,1,1,8,32,128]{7,...) custom-call(s32[161]{0:T(256)S(1)} %get-tuple-element.53.plan_ref, ...), custom_call_target="tpu_custom_call" | custom-call | flops 268435456 | bytes 16777216 | tf_op jit(solution)/shard_map/pallas_call | solution.py:322
  59.6 1.9 %collective-permute-start.23 = (bf16[2,2,2,1,1,8,32,128]{7,6,5,2,4,3,1,0:T(8,128)(2,1)S(1)}, bf16[2,2,2,1,1,8,32,128]{7,6,5,2,4,3,1,0:T(8,128)(2,1)S(1)}, u32[]{:S(2)}, u32[]{:S(2)}) collective-permute-start(bf16[2,2,2,1,1,8,32,128]{7,6,5,2,4,3,1,0:T(8,128)(2,1)S(1)} %bitcast.201), channel_id=1, source_target_pairs={{0,8},{4,12},{8,0},{12,4},{16,24},{20,28},{24,16},{28,20},{1,9},{5... | collective-permute-start | bytes 1572872 | tf_op jit(solution)/shard_map/ppermute | solution.py:22
  61.6 1.9 %collective-permute-start.27 = (bf16[2,2,2,1,1,8,32,128]{7,6,5,2,4,3,1,0:T(8,128)(2,1)S(1)}, bf16[2,2,2,1,1,8,32,128]{7,6,5,2,4,3,1,0:T(8,128)(2,1)S(1)}, u32[]{:S(2)}, u32[]{:S(2)}) collective-permute-start(bf16[2,2,2,1,1,8,32,128]{7,6,5,2,4,3,1,0:T(8,128)(2,1)S(1)} %bitcast.200), channel_id=1, source_target_pairs={{0,4},{4,0},{8,12},{12,8},{16,20},{20,16},{24,28},{28,24},{1,5},{5... | collective-permute-start | bytes 1572872 | tf_op jit(solution)/shard_map/ppermute | solution.py:22
  63.5 1.1 collective-permute-start.31
  64.6 0.4 collective-permute-start.35
  65.0 9.5 %collective-permute-done.23 = bf16[2,2,2,1,1,8,32,128]{7,6,5,2,4,3,1,0:T(8,128)(2,1)S(1)} collective-permute-done((bf16[2,2,2,1,1,8,32,128]{7,6,5,2,4,3,1,0:T(8,128)(2,1)S(1)}, bf16[2,2,2,1,1,8,32,128]{7,6,5,2,4,3,1,0:T(8,128)(2,1)S(1)}, u32[]{:S(2)}, u32[]{:S(2)}) %collective-permute-start.23) | collective-permute-done | bytes 524320 | tf_op jit(solution)/shard_map/ppermute | solution.py:22
  74.6 1.8 %collective-permute-start.24 = (bf16[2,2,1,1,8,32,128]{6,5,4,3,2,1,0:T(8,128)(2,1)S(1)}, bf16[2,2,1,1,8,32,128]{6,5,4,3,2,1,0:T(8,128)(2,1)S(1)}, u32[]{:S(2)}, u32[]{:S(2)}) collective-permute-start(bf16[2,2,1,1,8,32,128]{6,5,4,3,2,1,0:T(8,128)(2,1)S(1)} %get-tuple-element.77), channel_id=1, source_target_pairs={{0,4},{4,0},{8,12},{12,8},{16,20},{20,16},{24,28},{28,24},{1,5},{5... | collective-permute-start | bytes 786440 | tf_op jit(solution)/shard_map/ppermute | solution.py:22
  76.6 2.7 %collective-permute-start.28 = (bf16[2,2,1,1,8,32,128]{6,5,4,3,2,1,0:T(8,128)(2,1)S(1)}, bf16[2,2,1,1,8,32,128]{6,5,4,3,2,1,0:T(8,128)(2,1)S(1)}, u32[]{:S(2)}, u32[]{:S(2)}) collective-permute-start(bf16[2,2,1,1,8,32,128]{6,5,4,3,2,1,0:T(8,128)(2,1)S(1)} %get-tuple-element.79), channel_id=1, source_target_pairs={{0,16},{4,20},{8,24},{12,28},{16,0},{20,4},{24,8},{28,12},{1,17},{... | collective-permute-start | bytes 786440 | tf_op jit(solution)/shard_map/ppermute | solution.py:22
  79.5 1.3 %collective-permute-start.32 = (bf16[2,2,1,1,8,32,128]{6,5,4,3,2,1,0:T(8,128)(2,1)S(1)}, bf16[2,2,1,1,8,32,128]{6,5,4,3,2,1,0:T(8,128)(2,1)S(1)}, u32[]{:S(2)}, u32[]{:S(2)}) collective-permute-start(bf16[2,2,1,1,8,32,128]{6,5,4,3,2,1,0:T(8,128)(2,1)S(1)} %get-tuple-element.81), channel_id=1, source_target_pairs={{0,4},{4,0},{8,12},{12,8},{16,20},{20,16},{24,28},{28,24},{1,5},{5... | collective-permute-start | bytes 786440 | tf_op jit(solution)/shard_map/ppermute | solution.py:22
  80.8 10.3 %collective-permute-done.35 = bf16[2,2,2,1,1,8,32,128]{7,6,5,2,4,3,1,0:T(8,128)(2,1)S(1)} collective-permute-done((bf16[2,2,2,1,1,8,32,128]{7,6,5,2,4,3,1,0:T(8,128)(2,1)S(1)}, bf16[2,2,2,1,1,8,32,128]{7,6,5,2,4,3,1,0:T(8,128)(2,1)S(1)}, u32[]{:S(2)}, u32[]{:S(2)}) %collective-permute-start.35) | collective-permute-done | bytes 524320 | tf_op jit(solution)/shard_map/ppermute | solution.py:22
  91.1 1.8 %collective-permute-start.36 = (bf16[2,2,1,1,8,32,128]{6,5,4,1,0,3,2:T(8,128)(2,1)S(1)}, bf16[2,2,1,1,8,32,128]{6,5,4,1,0,3,2:T(8,128)(2,1)S(1)}, u32[]{:S(2)}, u32[]{:S(2)}) collective-permute-start(bf16[2,2,1,1,8,32,128]{6,5,4,1,0,3,2:T(8,128)(2,1)S(1)} %fusion.4), channel_id=1, source_target_pairs={{0,2},{1,3},{2,0},{3,1},{4,6},{5,7},{6,4},{7,5},{8,10},{9,11},{10,... | collective-permute-start | bytes 786440 | tf_op jit(solution)/shard_map/ppermute | solution.py:22
  93.1 0.8 collective-permute-start.25
  94.0 1.1 collective-permute-start.29
  95.1 2.5 %collective-permute-start.33 = (bf16[2,1,1,8,32,128]{5,4,3,2,1,0:T(8,128)(2,1)S(1)}, bf16[2,1,1,8,32,128]{5,4,3,2,1,0:T(8,128)(2,1)S(1)}, u32[]{:S(2)}, u32[]{:S(2)}) collective-permute-start(bf16[2,1,1,8,32,128]{5,4,3,2,1,0:T(8,128)(2,1)S(1)} %get-tuple-element.87), channel_id=1, source_target_pairs={{0,8},{4,12},{8,0},{12,4},{16,24},{20,28},{24,16},{28,20},{1,9},{5... | collective-permute-start | bytes 393224 | tf_op jit(solution)/shard_map/ppermute | solution.py:22
  97.7 2.7 %collective-permute-done.36 = bf16[2,2,1,1,8,32,128]{6,5,4,1,0,3,2:T(8,128)(2,1)S(1)} collective-permute-done((bf16[2,2,1,1,8,32,128]{6,5,4,1,0,3,2:T(8,128)(2,1)S(1)}, bf16[2,2,1,1,8,32,128]{6,5,4,1,0,3,2:T(8,128)(2,1)S(1)}, u32[]{:S(2)}, u32[]{:S(2)}) %collective-permute-start.36) | collective-permute-done | bytes 262176 | tf_op jit(solution)/shard_map/ppermute | solution.py:22
  100.4 1.5 %collective-permute-start.37 = (bf16[2,1,1,8,32,128]{5,4,3,0,2,1:T(8,128)(2,1)S(1)}, bf16[2,1,1,8,32,128]{5,4,3,0,2,1:T(8,128)(2,1)S(1)}, u32[]{:S(2)}, u32[]{:S(2)}) collective-permute-start(bf16[2,1,1,8,32,128]{5,4,3,0,2,1:T(8,128)(2,1)S(1)} %fusion.23), channel_id=1, source_target_pairs={{0,16},{4,20},{8,24},{12,28},{16,0},{20,4},{24,8},{28,12},{1,17},{... | collective-permute-start | bytes 393224 | tf_op jit(solution)/shard_map/ppermute | solution.py:22
  102.0 1.0 collective-permute-start.26
  103.0 2.6 %collective-permute-start.30 = (bf16[1,1,8,32,128]{4,3,2,1,0:T(8,128)(2,1)S(1)}, bf16[1,1,8,32,128]{4,3,2,1,0:T(8,128)(2,1)S(1)}, u32[]{:S(2)}, u32[]{:S(2)}) collective-permute-start(bf16[1,1,8,32,128]{4,3,2,1,0:T(8,128)(2,1)S(1)} %fusion.45), channel_id=1, source_target_pairs={{0,8},{4,12},{8,0},{12,4},{16,24},{20,28},{24,16},{28,20},{1,9},{5... | collective-permute-start | bytes 196616 | tf_op jit(solution)/shard_map/ppermute | solution.py:22
  106.0 2.7 %collective-permute-done.37 = bf16[2,1,1,8,32,128]{5,4,3,0,2,1:T(8,128)(2,1)S(1)} collective-permute-done((bf16[2,1,1,8,32,128]{5,4,3,0,2,1:T(8,128)(2,1)S(1)}, bf16[2,1,1,8,32,128]{5,4,3,0,2,1:T(8,128)(2,1)S(1)}, u32[]{:S(2)}, u32[]{:S(2)}) %collective-permute-start.37) | collective-permute-done | bytes 131104 | tf_op jit(solution)/shard_map/ppermute | solution.py:22
  108.7 1.2 %collective-permute-start.38 = (bf16[1,1,8,32,128]{4,3,2,1,0:T(8,128)(2,1)S(1)}, bf16[1,1,8,32,128]{4,3,2,1,0:T(8,128)(2,1)S(1)}, u32[]{:S(2)}, u32[]{:S(2)}) collective-permute-start(bf16[1,1,8,32,128]{4,3,2,1,0:T(8,128)(2,1)S(1)} %fusion.47), channel_id=1, source_target_pairs={{0,4},{4,0},{8,12},{12,8},{16,20},{20,16},{24,28},{28,24},{1,5},{5... | collective-permute-start | bytes 196616 | tf_op jit(solution)/shard_map/ppermute | solution.py:22
  110.0 1.0 collective-permute-done.34
  111.0 2.0 %collective-permute-done.38 = bf16[1,1,8,32,128]{4,3,2,1,0:T(8,128)(2,1)S(1)} collective-permute-done((bf16[1,1,8,32,128]{4,3,2,1,0:T(8,128)(2,1)S(1)}, bf16[1,1,8,32,128]{4,3,2,1,0:T(8,128)(2,1)S(1)}, u32[]{:S(2)}, u32[]{:S(2)}) %collective-permute-start.38) | collective-permute-done | bytes 65568 | tf_op jit(solution)/shard_map/ppermute | solution.py:22
  113.1 0.8 pad_maximum_fusion
  (56 shorter events, 3.4 us)
Async XLA Ops:
  0.0 13.1 %collective-permute-start.7 = (bf16[64,128,128]{2,1,0:T(8,128)(2,1)}, bf16[64,128,128]{2,1,0:T(8,128)(2,1)S(1)}, u32[]{:S(2)}, u32[]{:S(2)}) collective-permute-start(bf16[64,128,128]{2,1,0:T(8,128)(2,1)} %bitcast.202), channel_id=1, source_target_pairs={{0,1},{1,0},{2,3},{3,2},{4,5},{5,4},{6,7},{7,6},{8,9},{9,8},{10,11... | collective-permute-start | bytes 6291464 | tf_op jit(solution)/shard_map/ppermute | solution.py:22
  0.5 4.0 %collective-permute-start.3 = (s32[64]{0:T(128)}, s32[64]{0:T(128)S(1)}, u32[]{:S(2)}, u32[]{:S(2)}) collective-permute-start(s32[64]{0:T(128)} %bitcast.206), channel_id=1, source_target_pairs={{0,1},{1,0},{2,3},{3,2},{4,5},{5,4},{6,7},{7,6},{8,9},{9,8},{10,11... | collective-permute-start | bytes 776 | tf_op jit(solution)/shard_map/ppermute | solution.py:22
  0.5 12.6 %collective-permute-start = (bf16[16,128,128]{2,1,0:T(8,128)(2,1)}, bf16[16,128,128]{2,1,0:T(8,128)(2,1)S(1)}, u32[]{:S(2)}, u32[]{:S(2)}) collective-permute-start(bf16[16,128,128]{2,1,0:T(8,128)(2,1)} %refs_2_), channel_id=1, source_target_pairs={{0,8},{1,5},{2,10},{3,7},{8,16},{9,1},{10,18},{11,3},{16,24},{17,9... | collective-permute-start | bytes 1572872 | tf_op jit(solution)/shard_map/ppermute | solution.py:354
  3.5 9.6 %collective-permute-start.8 = (bf16[16,128,128]{2,1,0:T(8,128)(2,1)}, bf16[16,128,128]{2,1,0:T(8,128)(2,1)S(1)}, u32[]{:S(2)}, u32[]{:S(2)}) collective-permute-start(bf16[16,128,128]{2,1,0:T(8,128)(2,1)} %refs_2_), channel_id=1, source_target_pairs={{0,1},{1,0},{2,3},{3,2},{4,5},{5,4},{6,7},{7,6},{8,9},{9,8},{10,11... | collective-permute-start | bytes 1572872 | tf_op jit(solution)/shard_map/ppermute | solution.py:22
  4.5 14.5 %collective-permute-start.4 = (bf16[16,128,128]{2,1,0:T(8,128)(2,1)}, bf16[16,128,128]{2,1,0:T(8,128)(2,1)S(1)}, u32[]{:S(2)}, u32[]{:S(2)}) collective-permute-start(bf16[16,128,128]{2,1,0:T(8,128)(2,1)} %refs_2_), channel_id=1, source_target_pairs={{0,4},{1,9},{2,6},{3,11},{8,0},{9,17},{10,2},{11,19},{16,8},{17,25... | collective-permute-start | bytes 1572872 | tf_op jit(solution)/shard_map/ppermute | solution.py:354
  13.1 6.0 %collective-permute-start.11 = (s32[64]{0:T(128)S(1)}, s32[64]{0:T(128)S(1)}, u32[]{:S(2)}, u32[]{:S(2)}) collective-permute-start(s32[64]{0:T(128)S(1)} %bitcast_add_fusion), channel_id=1, source_target_pairs={{0,12},{4,8},{8,4},{12,0},{16,28},{20,24},{24,20},{28,16},{1,13},{... | collective-permute-start | bytes 776 | tf_op jit(solution)/shard_map/ppermute | solution.py:22
  16.4 3.6 %collective-permute-start.10 = (s32[64]{0:T(128)S(1)}, s32[64]{0:T(128)S(1)}, u32[]{:S(2)}, u32[]{:S(2)}) collective-permute-start(s32[64]{0:T(128)S(1)} %bitcast_add_fusion), channel_id=1, source_target_pairs={{0,8},{4,12},{8,0},{12,4},{16,24},{20,28},{24,16},{28,20},{1,9},{5... | collective-permute-start | bytes 776 | tf_op jit(solution)/shard_map/ppermute | solution.py:22
  16.9 3.6 %collective-permute-start.9 = (s32[64]{0:T(128)S(1)}, s32[64]{0:T(128)S(1)}, u32[]{:S(2)}, u32[]{:S(2)}) collective-permute-start(s32[64]{0:T(128)S(1)} %bitcast_add_fusion), channel_id=1, source_target_pairs={{0,4},{4,0},{8,12},{12,8},{16,20},{20,16},{24,28},{28,24},{1,5},{5... | collective-permute-start | bytes 776 | tf_op jit(solution)/shard_map/ppermute | solution.py:22
  17.1 13.3 %collective-permute-start.1 = (bf16[16,128,128]{2,1,0:T(8,128)(2,1)S(1)}, bf16[16,128,128]{2,1,0:T(8,128)(2,1)S(1)}, u32[]{:S(2)}, u32[]{:S(2)}) collective-permute-start(bf16[16,128,128]{2,1,0:T(8,128)(2,1)S(1)} %collective-permute-done.refs_11_), channel_id=1, source_target_pairs={{0,8},{1,5},{2,10},{3,7},{8,16},{9,1},{10,18},{11,3},{16,24},{17,9... | collective-permute-start | bytes 1572872 | tf_op jit(solution)/shard_map/ppermute | solution.py:354
  19.0 13.3 %collective-permute-start.5 = (bf16[16,128,128]{2,1,0:T(8,128)(2,1)S(1)}, bf16[16,128,128]{2,1,0:T(8,128)(2,1)S(1)}, u32[]{:S(2)}, u32[]{:S(2)}) collective-permute-start(bf16[16,128,128]{2,1,0:T(8,128)(2,1)S(1)} %collective-permute-done.4.refs_6_), channel_id=1, source_target_pairs={{0,4},{1,9},{2,6},{3,11},{8,0},{9,17},{10,2},{11,19},{16,8},{17,25... | collective-permute-start | bytes 1572872 | tf_op jit(solution)/shard_map/ppermute | solution.py:354
  20.5 11.9 %collective-permute-start.13 = (bf16[16,128,128]{2,1,0:T(8,128)(2,1)}, bf16[16,128,128]{2,1,0:T(8,128)(2,1)S(1)}, u32[]{:S(2)}, u32[]{:S(2)}) collective-permute-start(bf16[16,128,128]{2,1,0:T(8,128)(2,1)} %refs_2_), channel_id=1, source_target_pairs={{0,2},{1,3},{2,0},{3,1},{4,6},{5,7},{6,4},{7,5},{8,10},{9,11},{10,... | collective-permute-start | bytes 1572872 | tf_op jit(solution)/shard_map/ppermute | solution.py:22
  22.0 11.0 %collective-permute-start.12 = (s32[256]{0:T(256)S(1)}, s32[256]{0:T(256)S(1)}, u32[]{:S(2)}, u32[]{:S(2)}) collective-permute-start(s32[256]{0:T(256)S(1)} %pad_add_fusion.1), channel_id=1, source_target_pairs={{0,16},{4,20},{8,24},{12,28},{16,0},{20,4},{24,8},{28,12},{1,17},{... | collective-permute-start | bytes 3080 | tf_op jit(solution)/shard_map/ppermute | solution.py:22
  30.4 12.4 %collective-permute-start.2 = (bf16[16,128,128]{2,1,0:T(8,128)(2,1)S(1)}, bf16[16,128,128]{2,1,0:T(8,128)(2,1)S(1)}, u32[]{:S(2)}, u32[]{:S(2)}) collective-permute-start(bf16[16,128,128]{2,1,0:T(8,128)(2,1)S(1)} %collective-permute-done.1.refs_10_), channel_id=1, source_target_pairs={{0,8},{1,5},{2,10},{3,7},{8,16},{9,1},{10,18},{11,3},{16,24},{17,9... | collective-permute-start | bytes 1572872 | tf_op jit(solution)/shard_map/ppermute | solution.py:354
  32.2 10.6 %collective-permute-start.6 = (bf16[16,128,128]{2,1,0:T(8,128)(2,1)S(1)}, bf16[16,128,128]{2,1,0:T(8,128)(2,1)S(1)}, u32[]{:S(2)}, u32[]{:S(2)}) collective-permute-start(bf16[16,128,128]{2,1,0:T(8,128)(2,1)S(1)} %collective-permute-done.5.refs_7_), channel_id=1, source_target_pairs={{0,4},{1,9},{2,6},{3,11},{8,0},{9,17},{10,2},{11,19},{16,8},{17,25... | collective-permute-start | bytes 1572872 | tf_op jit(solution)/shard_map/ppermute | solution.py:354
  32.4 10.4 %collective-permute-start.14 = (bf16[16,128,128]{2,1,0:T(8,128)(2,1)S(1)}, bf16[16,128,128]{2,1,0:T(8,128)(2,1)S(1)}, u32[]{:S(2)}, u32[]{:S(2)}) collective-permute-start(bf16[16,128,128]{2,1,0:T(8,128)(2,1)S(1)} %collective-permute-done.13.refs_3_), channel_id=1, source_target_pairs={{0,1},{1,0},{2,3},{3,2},{4,5},{5,4},{6,7},{7,6},{8,9},{9,8},{10,11... | collective-permute-start | bytes 1572872 | tf_op jit(solution)/shard_map/ppermute | solution.py:22
  32.4 10.4 %collective-permute-start.15 = (bf16[16,128,128]{2,1,0:T(8,128)(2,1)S(1)}, bf16[16,128,128]{2,1,0:T(8,128)(2,1)S(1)}, u32[]{:S(2)}, u32[]{:S(2)}) collective-permute-start(bf16[16,128,128]{2,1,0:T(8,128)(2,1)S(1)} %collective-permute-done.4.refs_6_), channel_id=1, source_target_pairs={{0,1},{1,0},{2,3},{3,2},{4,5},{5,4},{6,7},{7,6},{8,9},{9,8},{10,11... | collective-permute-start | bytes 1572872 | tf_op jit(solution)/shard_map/ppermute | solution.py:22
  32.9 9.9 %collective-permute-start.16 = (bf16[16,128,128]{2,1,0:T(8,128)(2,1)S(1)}, bf16[16,128,128]{2,1,0:T(8,128)(2,1)S(1)}, u32[]{:S(2)}, u32[]{:S(2)}) collective-permute-start(bf16[16,128,128]{2,1,0:T(8,128)(2,1)S(1)} %collective-permute-done.refs_11_), channel_id=1, source_target_pairs={{0,1},{1,0},{2,3},{3,2},{4,5},{5,4},{6,7},{7,6},{8,9},{9,8},{10,11... | collective-permute-start | bytes 1572872 | tf_op jit(solution)/shard_map/ppermute | solution.py:22
  42.9 2.8 %collective-permute-start.18 = (bf16[16,128,128]{2,1,0:T(8,128)(2,1)S(1)}, bf16[16,128,128]{2,1,0:T(8,128)(2,1)S(1)}, u32[]{:S(2)}, u32[]{:S(2)}) collective-permute-start(bf16[16,128,128]{2,1,0:T(8,128)(2,1)S(1)} %collective-permute-done.5.refs_7_), channel_id=1, source_target_pairs={{0,1},{1,0},{2,3},{3,2},{4,5},{5,4},{6,7},{7,6},{8,9},{9,8},{10,11... | collective-permute-start | bytes 1572872 | tf_op jit(solution)/shard_map/ppermute | solution.py:22
  42.9 2.7 %collective-permute-start.21 = (bf16[16,128,128]{2,1,0:T(8,128)(2,1)S(1)}, bf16[16,128,128]{2,1,0:T(8,128)(2,1)S(1)}, u32[]{:S(2)}, u32[]{:S(2)}) collective-permute-start(bf16[16,128,128]{2,1,0:T(8,128)(2,1)S(1)} %collective-permute-done.1.refs_10_), channel_id=1, source_target_pairs={{0,1},{1,0},{2,3},{3,2},{4,5},{5,4},{6,7},{7,6},{8,9},{9,8},{10,11... | collective-permute-start | bytes 1572872 | tf_op jit(solution)/shard_map/ppermute | solution.py:22
  43.4 2.9 %collective-permute-start.19 = (bf16[16,128,128]{2,1,0:T(8,128)(2,1)S(1)}, bf16[16,128,128]{2,1,0:T(8,128)(2,1)S(1)}, u32[]{:S(2)}, u32[]{:S(2)}) collective-permute-start(bf16[16,128,128]{2,1,0:T(8,128)(2,1)S(1)} %collective-permute-done.6.refs_8_), channel_id=1, source_target_pairs={{0,1},{1,0},{2,3},{3,2},{4,5},{5,4},{6,7},{7,6},{8,9},{9,8},{10,11... | collective-permute-start | bytes 1572872 | tf_op jit(solution)/shard_map/ppermute | solution.py:22
  43.5 3.6 %collective-permute-start.20 = (bf16[16,128,128]{2,1,0:T(8,128)(2,1)S(1)}, bf16[16,128,128]{2,1,0:T(8,128)(2,1)S(1)}, u32[]{:S(2)}, u32[]{:S(2)}) collective-permute-start(bf16[16,128,128]{2,1,0:T(8,128)(2,1)S(1)} %collective-permute-done.2.refs_9_), channel_id=1, source_target_pairs={{0,1},{1,0},{2,3},{3,2},{4,5},{5,4},{6,7},{7,6},{8,9},{9,8},{10,11... | collective-permute-start | bytes 1572872 | tf_op jit(solution)/shard_map/ppermute | solution.py:22
  43.9 9.2 %collective-permute-start.17 = (bf16[16,128,128]{2,1,0:T(8,128)(2,1)S(1)}, bf16[16,128,128]{2,1,0:T(8,128)(2,1)S(1)}, u32[]{:S(2)}, u32[]{:S(2)}) collective-permute-start(bf16[16,128,128]{2,1,0:T(8,128)(2,1)S(1)} %collective-permute-done.2.refs_9_), channel_id=1, source_target_pairs={{0,8},{1,5},{2,10},{3,7},{8,16},{9,1},{10,18},{11,3},{16,24},{17,9... | collective-permute-start | bytes 1572872 | tf_op jit(solution)/shard_map/ppermute | solution.py:354
  53.1 1.9 %collective-permute-start.22 = (bf16[16,128,128]{2,1,0:T(8,128)(2,1)S(1)}, bf16[16,128,128]{2,1,0:T(8,128)(2,1)S(1)}, u32[]{:S(2)}, u32[]{:S(2)}) collective-permute-start(bf16[16,128,128]{2,1,0:T(8,128)(2,1)S(1)} %collective-permute-done.17.far0), channel_id=1, source_target_pairs={{0,1},{1,0},{2,3},{3,2},{4,5},{5,4},{6,7},{7,6},{8,9},{9,8},{10,11... | collective-permute-start | bytes 1572872 | tf_op jit(solution)/shard_map/ppermute | solution.py:22
  59.6 14.9 %collective-permute-start.23 = (bf16[2,2,2,1,1,8,32,128]{7,6,5,2,4,3,1,0:T(8,128)(2,1)S(1)}, bf16[2,2,2,1,1,8,32,128]{7,6,5,2,4,3,1,0:T(8,128)(2,1)S(1)}, u32[]{:S(2)}, u32[]{:S(2)}) collective-permute-start(bf16[2,2,2,1,1,8,32,128]{7,6,5,2,4,3,1,0:T(8,128)(2,1)S(1)} %bitcast.201), channel_id=1, source_target_pairs={{0,8},{4,12},{8,0},{12,4},{16,24},{20,28},{24,16},{28,20},{1,9},{5... | collective-permute-start | bytes 1572872 | tf_op jit(solution)/shard_map/ppermute | solution.py:22
  61.6 14.9 %collective-permute-start.27 = (bf16[2,2,2,1,1,8,32,128]{7,6,5,2,4,3,1,0:T(8,128)(2,1)S(1)}, bf16[2,2,2,1,1,8,32,128]{7,6,5,2,4,3,1,0:T(8,128)(2,1)S(1)}, u32[]{:S(2)}, u32[]{:S(2)}) collective-permute-start(bf16[2,2,2,1,1,8,32,128]{7,6,5,2,4,3,1,0:T(8,128)(2,1)S(1)} %bitcast.200), channel_id=1, source_target_pairs={{0,4},{4,0},{8,12},{12,8},{16,20},{20,16},{24,28},{28,24},{1,5},{5... | collective-permute-start | bytes 1572872 | tf_op jit(solution)/shard_map/ppermute | solution.py:22
  63.5 15.8 %collective-permute-start.31 = (bf16[2,2,2,1,1,8,32,128]{7,6,5,2,4,3,1,0:T(8,128)(2,1)S(1)}, bf16[2,2,2,1,1,8,32,128]{7,6,5,2,4,3,1,0:T(8,128)(2,1)S(1)}, u32[]{:S(2)}, u32[]{:S(2)}) collective-permute-start(bf16[2,2,2,1,1,8,32,128]{7,6,5,2,4,3,1,0:T(8,128)(2,1)S(1)} %bitcast.199), channel_id=1, source_target_pairs={{0,2},{1,3},{2,0},{3,1},{4,6},{5,7},{6,4},{7,5},{8,10},{9,11},{10,... | collective-permute-start | bytes 1572872 | tf_op jit(solution)/shard_map/ppermute | solution.py:22
  64.6 26.5 %collective-permute-start.35 = (bf16[2,2,2,1,1,8,32,128]{7,6,5,2,4,3,1,0:T(8,128)(2,1)S(1)}, bf16[2,2,2,1,1,8,32,128]{7,6,5,2,4,3,1,0:T(8,128)(2,1)S(1)}, u32[]{:S(2)}, u32[]{:S(2)}) collective-permute-start(bf16[2,2,2,1,1,8,32,128]{7,6,5,2,4,3,1,0:T(8,128)(2,1)S(1)} %bitcast.198), channel_id=1, source_target_pairs={{0,8},{4,12},{8,0},{12,4},{16,24},{20,28},{24,16},{28,20},{1,9},{5... | collective-permute-start | bytes 1572872 | tf_op jit(solution)/shard_map/ppermute | solution.py:22
  74.6 18.4 %collective-permute-start.24 = (bf16[2,2,1,1,8,32,128]{6,5,4,3,2,1,0:T(8,128)(2,1)S(1)}, bf16[2,2,1,1,8,32,128]{6,5,4,3,2,1,0:T(8,128)(2,1)S(1)}, u32[]{:S(2)}, u32[]{:S(2)}) collective-permute-start(bf16[2,2,1,1,8,32,128]{6,5,4,3,2,1,0:T(8,128)(2,1)S(1)} %get-tuple-element.77), channel_id=1, source_target_pairs={{0,4},{4,0},{8,12},{12,8},{16,20},{20,16},{24,28},{28,24},{1,5},{5... | collective-permute-start | bytes 786440 | tf_op jit(solution)/shard_map/ppermute | solution.py:22
  76.6 17.3 %collective-permute-start.28 = (bf16[2,2,1,1,8,32,128]{6,5,4,3,2,1,0:T(8,128)(2,1)S(1)}, bf16[2,2,1,1,8,32,128]{6,5,4,3,2,1,0:T(8,128)(2,1)S(1)}, u32[]{:S(2)}, u32[]{:S(2)}) collective-permute-start(bf16[2,2,1,1,8,32,128]{6,5,4,3,2,1,0:T(8,128)(2,1)S(1)} %get-tuple-element.79), channel_id=1, source_target_pairs={{0,16},{4,20},{8,24},{12,28},{16,0},{20,4},{24,8},{28,12},{1,17},{... | collective-permute-start | bytes 786440 | tf_op jit(solution)/shard_map/ppermute | solution.py:22
  79.5 15.6 %collective-permute-start.32 = (bf16[2,2,1,1,8,32,128]{6,5,4,3,2,1,0:T(8,128)(2,1)S(1)}, bf16[2,2,1,1,8,32,128]{6,5,4,3,2,1,0:T(8,128)(2,1)S(1)}, u32[]{:S(2)}, u32[]{:S(2)}) collective-permute-start(bf16[2,2,1,1,8,32,128]{6,5,4,3,2,1,0:T(8,128)(2,1)S(1)} %get-tuple-element.81), channel_id=1, source_target_pairs={{0,4},{4,0},{8,12},{12,8},{16,20},{20,16},{24,28},{28,24},{1,5},{5... | collective-permute-start | bytes 786440 | tf_op jit(solution)/shard_map/ppermute | solution.py:22
  91.1 9.3 %collective-permute-start.36 = (bf16[2,2,1,1,8,32,128]{6,5,4,1,0,3,2:T(8,128)(2,1)S(1)}, bf16[2,2,1,1,8,32,128]{6,5,4,1,0,3,2:T(8,128)(2,1)S(1)}, u32[]{:S(2)}, u32[]{:S(2)}) collective-permute-start(bf16[2,2,1,1,8,32,128]{6,5,4,1,0,3,2:T(8,128)(2,1)S(1)} %fusion.4), channel_id=1, source_target_pairs={{0,2},{1,3},{2,0},{3,1},{4,6},{5,7},{6,4},{7,5},{8,10},{9,11},{10,... | collective-permute-start | bytes 786440 | tf_op jit(solution)/shard_map/ppermute | solution.py:22
  93.1 8.9 %collective-permute-start.25 = (bf16[2,1,1,8,32,128]{5,4,3,2,1,0:T(8,128)(2,1)S(1)}, bf16[2,1,1,8,32,128]{5,4,3,2,1,0:T(8,128)(2,1)S(1)}, u32[]{:S(2)}, u32[]{:S(2)}) collective-permute-start(bf16[2,1,1,8,32,128]{5,4,3,2,1,0:T(8,128)(2,1)S(1)} %get-tuple-element.83), channel_id=1, source_target_pairs={{0,16},{4,20},{8,24},{12,28},{16,0},{20,4},{24,8},{28,12},{1,17},{... | collective-permute-start | bytes 393224 | tf_op jit(solution)/shard_map/ppermute | solution.py:22
  94.0 9.0 %collective-permute-start.29 = (bf16[2,1,1,8,32,128]{5,4,3,2,1,0:T(8,128)(2,1)S(1)}, bf16[2,1,1,8,32,128]{5,4,3,2,1,0:T(8,128)(2,1)S(1)}, u32[]{:S(2)}, u32[]{:S(2)}) collective-permute-start(bf16[2,1,1,8,32,128]{5,4,3,2,1,0:T(8,128)(2,1)S(1)} %get-tuple-element.85), channel_id=1, source_target_pairs={{0,2},{1,3},{2,0},{3,1},{4,6},{5,7},{6,4},{7,5},{8,10},{9,11},{10,... | collective-permute-start | bytes 393224 | tf_op jit(solution)/shard_map/ppermute | solution.py:22
  95.1 10.5 %collective-permute-start.33 = (bf16[2,1,1,8,32,128]{5,4,3,2,1,0:T(8,128)(2,1)S(1)}, bf16[2,1,1,8,32,128]{5,4,3,2,1,0:T(8,128)(2,1)S(1)}, u32[]{:S(2)}, u32[]{:S(2)}) collective-permute-start(bf16[2,1,1,8,32,128]{5,4,3,2,1,0:T(8,128)(2,1)S(1)} %get-tuple-element.87), channel_id=1, source_target_pairs={{0,8},{4,12},{8,0},{12,4},{16,24},{20,28},{24,16},{28,20},{1,9},{5... | collective-permute-start | bytes 393224 | tf_op jit(solution)/shard_map/ppermute | solution.py:22
  100.4 8.3 %collective-permute-start.37 = (bf16[2,1,1,8,32,128]{5,4,3,0,2,1:T(8,128)(2,1)S(1)}, bf16[2,1,1,8,32,128]{5,4,3,0,2,1:T(8,128)(2,1)S(1)}, u32[]{:S(2)}, u32[]{:S(2)}) collective-permute-start(bf16[2,1,1,8,32,128]{5,4,3,0,2,1:T(8,128)(2,1)S(1)} %fusion.23), channel_id=1, source_target_pairs={{0,16},{4,20},{8,24},{12,28},{16,0},{20,4},{24,8},{28,12},{1,17},{... | collective-permute-start | bytes 393224 | tf_op jit(solution)/shard_map/ppermute | solution.py:22
  102.0 7.9 %collective-permute-start.26 = (bf16[1,1,8,32,128]{4,3,2,1,0:T(8,128)(2,1)S(1)}, bf16[1,1,8,32,128]{4,3,2,1,0:T(8,128)(2,1)S(1)}, u32[]{:S(2)}, u32[]{:S(2)}) collective-permute-start(bf16[1,1,8,32,128]{4,3,2,1,0:T(8,128)(2,1)S(1)} %fusion.44), channel_id=1, source_target_pairs={{0,2},{1,3},{2,0},{3,1},{4,6},{5,7},{6,4},{7,5},{8,10},{9,11},{10,... | collective-permute-start | bytes 196616 | tf_op jit(solution)/shard_map/ppermute | solution.py:22
  103.0 6.9 %collective-permute-start.30 = (bf16[1,1,8,32,128]{4,3,2,1,0:T(8,128)(2,1)S(1)}, bf16[1,1,8,32,128]{4,3,2,1,0:T(8,128)(2,1)S(1)}, u32[]{:S(2)}, u32[]{:S(2)}) collective-permute-start(bf16[1,1,8,32,128]{4,3,2,1,0:T(8,128)(2,1)S(1)} %fusion.45), channel_id=1, source_target_pairs={{0,8},{4,12},{8,0},{12,4},{16,24},{20,28},{24,16},{28,20},{1,9},{5... | collective-permute-start | bytes 196616 | tf_op jit(solution)/shard_map/ppermute | solution.py:22
  105.6 5.4 %collective-permute-start.34 = (bf16[1,1,8,32,128]{4,3,2,1,0:T(8,128)(2,1)S(1)}, bf16[1,1,8,32,128]{4,3,2,1,0:T(8,128)(2,1)S(1)}, u32[]{:S(2)}, u32[]{:S(2)}) collective-permute-start(bf16[1,1,8,32,128]{4,3,2,1,0:T(8,128)(2,1)S(1)} %fusion.46), channel_id=1, source_target_pairs={{0,16},{4,20},{8,24},{12,28},{16,0},{20,4},{24,8},{28,12},{1,17},{... | collective-permute-start | bytes 196616 | tf_op jit(solution)/shard_map/ppermute | solution.py:22
  108.7 4.3 %collective-permute-start.38 = (bf16[1,1,8,32,128]{4,3,2,1,0:T(8,128)(2,1)S(1)}, bf16[1,1,8,32,128]{4,3,2,1,0:T(8,128)(2,1)S(1)}, u32[]{:S(2)}, u32[]{:S(2)}) collective-permute-start(bf16[1,1,8,32,128]{4,3,2,1,0:T(8,128)(2,1)S(1)} %fusion.47), channel_id=1, source_target_pairs={{0,4},{4,0},{8,12},{12,8},{16,20},{20,16},{24,28},{28,24},{1,5},{5... | collective-permute-start | bytes 196616 | tf_op jit(solution)/shard_map/ppermute | solution.py:22

commit v3 on v2

--- a/solution.py
+++ b/solution.py
@@ -1,4 +1,5 @@
 import functools
+import itertools
 import math
 
 import jax
@@ -10,7 +11,8 @@
 
 OWN = 2
 UNROLL = 8
-GROUPS = 4
+ORDERS = (("1x2y", "x1y2"), ("xy12", "yx21"), ("y1x2", "2xy1"))
+LINKS = {"x": ("col", 2), "y": ("row", 1), "1": ("row", 2), "2": ("row", 4)}
 
 
 def ring_order(count):
@@ -20,6 +22,17 @@
 def swap(value, axis, bit):
     size = lax.axis_size(axis)
     return lax.ppermute(value, axis, [(i, i ^ bit) for i in range(size)])
+
+
+def exchange(value, links):
+    rows, cols = lax.axis_size("row"), lax.axis_size("col")
+    moves = []
+    for r in range(rows):
+        for c in range(cols):
+            axis, bit = LINKS[links[c % 2]]
+            to = (r ^ bit, c) if axis == "row" else (r, c ^ bit)
+            moves.append((r * cols + c, to[0] * cols + to[1]))
+    return lax.ppermute(value, ("row", "col"), moves)
 
 
 def log2(size):
@@ -35,15 +48,17 @@
         self.pairs = 2 * self.slab
         self.width = OWN * rows // cols
         self.per = OWN * self.width
-        self.his = rows // 4
+        self.his = rows // 8
+        self.blocks, self.tall = 4 * cols, self.per * side
+        third = self.tall // 16 // 3 * 16
+        self.splits = (0, third, 2 * third, self.tall)
         self.buckets = 2 * self.his
         self.slots = self.pairs + self.buckets * UNROLL
         self.half = rows // 2
         self.early = rows - 1
         self.near = 2 * self.early * tiles
-        cells = 2 * cols * self.per
         self.fields, shift = [], 0
-        for size in (self.pairs, 2 * rows * tiles, self.slab, cells):
+        for size in (self.pairs, 2 * rows * tiles, self.blocks * self.per):
             self.fields.append((shift, size - 1))
             shift += log2(size)
         assert shift <= 31
@@ -86,19 +101,16 @@
         order = away - jnp.where(away > s.half, 1, 0) + side * s.early
         piece = jnp.where(late == 1, side, order)
         panel_at = (piece << log2(s.tiles)) + (other & (s.tiles - 1))
-        rel_part = (tile >> log2(s.tiles)) ^ col
-        part = (rel_part & 1) * (s.cols // 2) + (rel_part >> 1)
-        rows_at = (part << log2(s.tiles)) + (tile & (s.tiles - 1))
-        cell = (rel_row & 3) * (s.cols // 2) + (rel_col >> 1)
+        cell = (rel_row & 7) * (s.cols // 2) + (rel_col >> 1)
         cell = (cell << log2(OWN)) + (i_agg & (OWN - 1))
         cell = (cell << log2(s.width)) + (j_agg & (s.width - 1))
-        bucket = (rel_row >> 2) * 2 + late
+        bucket = (rel_row >> 3) * 2 + late
         mine = (rel_col & 1) == 0
         rank = counts[bucket]
         counts[bucket] = rank + jnp.where(mine, 1, 0)
         info[i * 2] = jnp.where(mine, rank * s.buckets + bucket, -1)
         entry = i
-        for k, value in enumerate((panel_at, rows_at, cell)):
+        for k, value in enumerate((panel_at, cell)):
             entry = entry + (value << s.fields[k + 1][0])
         info[i * 2 + 1] = entry
         return carry
@@ -160,8 +172,12 @@
     for copy in copies:
         copy.wait()
 
+    col = lax.axis_index("col")
+
     def turn(k, carry):
-        rows_ref[k] = rows_buf[k].T
+        part = k >> log2(s.tiles)
+        rel = (part & (s.cols // 2 - 1)) * 2 + (part >> log2(s.cols // 2))
+        rows_ref[((rel ^ col) << log2(s.tiles)) + (k & (s.tiles - 1))] = rows_buf[k].T
         return carry
 
     lax.fori_loop(0, s.slab, turn, 0, unroll=4)
@@ -219,7 +235,7 @@
 
 def sum_kernel(
     s, plan_ref, starts_ref, slots_ref, rows_ref, far0, far1,
-    send0, keep0, send1, keep1, send2, keep2, send3, keep3, total, far_buf, sems,
+    send0, keep0, send1, keep1, send2, keep2, total, far_buf, sems,
 ):
     hi = pl.program_id(0)
     copies = [
@@ -232,21 +248,21 @@
         for copy in copies:
             copy.start()
 
-    cells = total.shape[0]
-
     def clear(k, carry):
-        total[pl.ds(k * 8, 8)] = jnp.zeros((8,) + total.shape[1:], jnp.float32)
-        return carry
-
-    lax.fori_loop(0, cells // 8, clear, 0)
+        total[k] = jnp.zeros(total.shape[1:], jnp.float32)
+        return carry
+
+    lax.fori_loop(0, s.blocks, clear, 0)
 
     def add(n, product):
         entry = plan_ref[n]
         known = jnp.maximum(entry, 0)
         term = jnp.dot(
-            rows_ref[field(s, known, 2)], product, preferred_element_type=jnp.float32
+            rows_ref[known & (s.slab - 1)], product, preferred_element_type=jnp.float32
         )
-        total[field(s, known, 3)] += jnp.where(entry >= 0, term, 0.0)
+        cell = field(s, known, 2)
+        at = pl.ds(pl.multiple_of((cell & (s.per - 1)) * s.side, s.side), s.side)
+        total[cell >> log2(s.per), at, :] += jnp.where(entry >= 0, term, 0.0)
 
     def near(group, carry):
         for u in range(UNROLL):
@@ -274,51 +290,41 @@
 
     lax.fori_loop(middle, end, far, 0)
 
-    xh = s.cols // 4
-    tall = s.side // GROUPS
-
-    for z1 in range(2):
-        for y in range(2):
-            for x in range(xh):
-                for x1 in range(2):
-                    base = (((z1 * 2 + y) * xh + x) * 2 + x1) * s.per
-                    part = [
-                        total[pl.ds(base, s.per), k * tall:(k + 1) * tall, :]
-                        for k in range(GROUPS)
-                    ]
-                    for k, (bit, send, keep, at) in enumerate((
-                        (z1, send0, keep0, (y, 0, x1)),
-                        (y, send1, keep1, (0, x1, z1)),
-                        (x1, send2, keep2, (y, z1, 0)),
-                        (z1, send3, keep3, (x1, 0, y)),
-                    )):
-                        if bit:
-                            send[(*at, 0, x)] = part[k].astype(jnp.bfloat16)
-                        else:
-                            keep[(*at, 0, x)] = part[k]
+    half = s.cols // 2
+    weight = {"x": 1, "y": half, "1": 2 * half, "2": 4 * half}
+    core = lax.axis_index("col") & 1
+    outs = ((send0, keep0), (send1, keep1), (send2, keep2))
+    for k, (send, keep) in enumerate(outs):
+        for bits in itertools.product(range(2), repeat=4):
+            base = [
+                sum(weight[link] * bit for link, bit in zip(order, bits)) for order in ORDERS[k]
+            ]
+            base = jnp.where(core == 0, *base)
+            for x in range(half // 2):
+                part = total[base + 2 * x, s.splits[k]:s.splits[k + 1], :]
+                if bits[0]:
+                    send[(*bits[1:], 0, x)] = part.astype(jnp.bfloat16)
+                else:
+                    keep[(*bits[1:], 0, x)] = part
 
 
 def make_sums(s, plan, starts, slots, rows_t, far):
     smem = pl.BlockSpec(memory_space=pltpu.SMEM)
     vmem = pl.BlockSpec(memory_space=pltpu.VMEM)
     anywhere = pl.BlockSpec(memory_space=pl.ANY)
-    last = (s.cols // 4, s.per, s.side // GROUPS, s.side)
-    blocks = [
-        ((2, 1, 2), lambda h: (0, h & 1, 0, h >> 1, 0, 0, 0, 0)),
-        ((1, 2, 2), lambda h: (h & 1, 0, 0, h >> 1, 0, 0, 0, 0)),
-        ((2, 2, 1), lambda h: (0, 0, h & 1, h >> 1, 0, 0, 0, 0)),
-        ((2, 1, 2), lambda h: (0, h & 1, 0, h >> 1, 0, 0, 0, 0)),
-    ]
     shapes = [
         ((s.slots + s.slab + 2 * s.tiles, s.side, s.side), jnp.bfloat16),
-        ((2 * s.cols * s.per, s.side, s.side), jnp.float32),
+        ((s.blocks, s.tall, s.side), jnp.float32),
     ]
     out_shape, out_specs = [], []
-    for block, index in blocks:
+    for k in range(len(ORDERS)):
+        last = (s.cols // 4, s.splits[k + 1] - s.splits[k], s.side)
         for dtype in (jnp.bfloat16, jnp.float32):
-            out_shape.append(jax.ShapeDtypeStruct((2, 2, 2, s.his // 2) + last, dtype))
-            out_specs.append(pl.BlockSpec(block + (1,) + last, index))
-            shapes.append(((2,) + block + last, dtype))
+            out_shape.append(jax.ShapeDtypeStruct((2, 2, 2, s.his) + last, dtype))
+            out_specs.append(
+                pl.BlockSpec((2, 2, 2, 1) + last, lambda h: (0, 0, 0, h, 0, 0, 0))
+            )
+            shapes.append(((2 if s.his > 1 else 1, 8) + last, dtype))
     return pl.pallas_call(
         functools.partial(sum_kernel, s),
         grid=(s.his,),
@@ -326,7 +332,7 @@
         out_specs=out_specs,
         out_shape=out_shape,
         scratch_shapes=[
-            pltpu.VMEM((2 * s.cols * s.per, s.side, s.side), jnp.float32),
+            pltpu.VMEM((s.blocks, s.tall, s.side), jnp.float32),
             pltpu.VMEM((2 * s.tiles, s.side, s.side), jnp.bfloat16),
             pltpu.SemaphoreType.DMA((2,)),
         ],
@@ -361,20 +367,21 @@
     a_other, p_other = swap(a_blocks[:, 0], "col", 1), swap(p_tiles, "col", 1)
 
     aggs = owner[:, 0] * OWN + agg_local
-    came, aggs, a_other, p_other = barrier((first, aggs, a_other, p_other))
-    first = ring(first, 0)
+    aggs, a_other, p_other, one, two, mine = barrier(
+        (aggs, a_other, p_other, first, second, p_tiles)
+    )
+    own_near, other_near = {0: p_tiles, s.rows - 1: one, 1: two}, {0: p_other}
+    first, second = ring(first, 0), ring(second, 1)
     aggs = [aggs] + [swap(aggs, "row", mask) for mask in (1, 2, 3)]
-    own_near, other_near = {0: p_tiles, s.rows - 1: came, 1: second}, {0: p_other}
-    second = ring(second, 1)
-    aggs, mine = barrier((jnp.concatenate(aggs, 0), p_tiles))
-    bit = 4
-    while bit < s.rows:
-        aggs = jnp.concatenate([aggs, swap(aggs, "row", bit)], 0)
-        bit *= 2
+    second, aggs = barrier((second, jnp.concatenate(aggs, 0)))
     rows = [mine]
     bit = 2
     while bit < s.cols:
         rows += [swap(piece, "col", bit) for piece in rows]
+        bit *= 2
+    bit = 4
+    while bit < s.rows:
+        aggs = jnp.concatenate([aggs, swap(aggs, "row", bit)], 0)
         bit *= 2
     plan, starts = make_plan(s, jnp.concatenate([cols, cols_other], 0), aggs)
 
@@ -390,11 +397,9 @@
         held = [step, s.rows - step]
 
     others = sorted(set(other_near) - {0})
-    tie = (first, second, plan, starts, *rows[s.cols // 2 + 1:])
+    tie = (first, second, plan, starts)
     tie += (*(own_near[away] for away in held), *(other_near[away] for away in others))
     first, second, plan, starts, *rest = barrier(tie)
-    rows[s.cols // 2 + 1:] = rest[:s.cols // 2 - 1]
-    rest = rest[s.cols // 2 - 1:]
     for away, piece in zip(others, rest[len(held):]):
         other_near[away] = piece
     far = ring(first, 0)
@@ -410,23 +415,22 @@
     far_other = swap(far, "col", 1)
     parts = make_sums(s, plan, starts, slots, rows_t, [far, far_other])
 
-    y, z1, z2, x1 = ("row", 1), ("row", 2), ("row", 4), ("col", 2)
-    orders = [[z1, y, z2, x1], [y, z2, x1, z1], [x1, y, z1, z2], [z1, x1, z2, y]]
-    sends, keeps, steps = list(parts[0::2]), list(parts[1::2]), [0] * GROUPS
-    moving = [swap(sends[k], *orders[k][0]) for k in range(GROUPS)]
-    for k in list(range(GROUPS)) * 4:
-        got = moving[k]
-        steps[k] += 1
-        if steps[k] < 4:
-            send = (keeps[k][1] + got[1].astype(jnp.float32)).astype(jnp.bfloat16)
-            moving[k] = swap(send, *orders[k][steps[k]])
-            keeps[k] = keeps[k][0] + got[0].astype(jnp.float32)
-        else:
-            keeps[k] = keeps[k] + got.astype(jnp.float32)
+    sends, keeps = list(parts[0::2]), list(parts[1::2])
+    groups = range(len(ORDERS))
+    moving = [exchange(sends[k], [order[0] for order in ORDERS[k]]) for k in groups]
+    for step in range(1, 5):
+        for k in groups:
+            got = moving[k]
+            if step < 4:
+                send = (keeps[k][1] + got[1].astype(jnp.float32)).astype(jnp.bfloat16)
+                moving[k] = exchange(send, [order[step] for order in ORDERS[k]])
+                keeps[k] = keeps[k][0] + got[0].astype(jnp.float32)
+            else:
+                keeps[k] = keeps[k] + got.astype(jnp.float32)
     total = jnp.concatenate(keeps, -2)
     tail = [("row", 1 << k) for k in range(3, log2(s.rows))][::-1]
     tail += [("col", 1 << k) for k in range(2, log2(s.cols))][::-1]
-    total = total.reshape((2,) * len(tail) + total.shape[-3:])
+    total = total.reshape((2,) * len(tail) + total.shape[-2:])
     for axis in tail:
         got = swap(total[1].astype(jnp.bfloat16), *axis)
         total = total[0] + got.astype(jnp.float32)

time: 114 us -> 115 us (level)
  waiting for transfers between devices: 49.1 us -> 50.5 us
    ppermute x0 -> x12, waiting for transfers between devices: none -> 28.2 us  [exchange(): return lax.ppermute(value, ('row', 'col'), moves)]
    ppermute x32 -> x16, starting transfers between devices: 34.4 us -> 11.4 us  [swap(): return lax.ppermute(value, axis, [(i, i ^ bit) for i in range(size)])]
    ppermute x0 -> x12, starting transfers between devices: none -> 20 us  [exchange(): return lax.ppermute(value, ('row', 'col'), moves)]
    ppermute x32 -> x16, waiting for transfers between devices: 33.6 us -> 14.6 us  [swap(): return lax.ppermute(value, axis, [(i, i ^ bit) for i in range(size)])]
    ppermute x7, waiting for transfers between devices: 15.5 us -> 7.71 us  [ring(): return lax.ppermute(value, ('row', 'col'), moves)]
    ppermute x7, starting transfers between devices: 11.6 us -> 15 us  [ring(): return lax.ppermute(value, ('row', 'col'), moves)]
  transfers between devices with their start and end apart: 39 -> 35, of which waited for: 16 -> 15; matrix products, arithmetic and copies ran while one was open for 2% -> 2% of each run, Pallas kernels for 9% -> 9%
where the time goes in v3:
time: 115 us
  waiting for transfers between devices  50.5 us (44%)
  starting transfers between devices  46.4 us (40%)
  Pallas kernels  14.8 us (13%)
  other arithmetic  3.16 us (3%)
    ppermute x12, waiting for transfers between devices, exchange(): return lax.ppermute(value, ('row', 'col'), moves)  28.2 us
    ppermute x12, starting transfers between devices, exchange(): return lax.ppermute(value, ('row', 'col'), moves)  20 us
    ppermute x7, starting transfers between devices, ring(): return lax.ppermute(value, ('row', 'col'), moves)  15 us
    ppermute x16, waiting for transfers between devices, swap(): return lax.ppermute(value, axis, [(i, i ^ bit) for i in range(size)])  14.6 us
    ppermute x16, starting transfers between devices, swap(): return lax.ppermute(value, axis, [(i, i ^ bit) for i in range(size)])  11.4 us
    ppermute x7, waiting for transfers between devices, ring(): return lax.ppermute(value, ('row', 'col'), moves)  7.71 us
    pallas_call x1, Pallas kernels, make_products(): pl.pallas_call(functools.partial(product_kernel, s), in_specs=[smem, smem...  6.32 us
    pallas_call x1, Pallas kernels, make_plan(): pl.pallas_call(functools.partial(plan_kernel, s), in_specs=[smem, smem],...  4.54 us
  transfers between devices with their start and end apart: 35, of which 15 were waited for; matrix products, arithmetic and copies ran while one was open for 2% of the time, Pallas kernels for 9%

profile of v3, /device:TPU:0, one launch (start us, length us, event | category | flops | bytes accessed | tf_op | source)
XLA Modules:
  0.0 115.1 jit_solution(7090126686036529172)
XLA Ops:
  0.0 0.5 collective-permute-start.6
  0.5 2.6 %collective-permute-start = (bf16[16,128,128]{2,1,0:T(8,128)(2,1)}, bf16[16,128,128]{2,1,0:T(8,128)(2,1)S(1)}, u32[]{:S(2)}, u32[]{:S(2)}) collective-permute-start(bf16[16,128,128]{2,1,0:T(8,128)(2,1)} %refs_2_), channel_id=1, source_target_pairs={{0,8},{1,5},{2,10},{3,7},{8,16},{9,1},{10,18},{11,3},{16,24},{17,9... | collective-permute-start | bytes 1572872 | tf_op jit(solution)/shard_map/ppermute | solution.py:360
  3.0 0.2 collective-permute-start.3
  3.2 1.3 %collective-permute-done.3 = s32[64]{0:T(128)S(1)} collective-permute-done((s32[64]{0:T(128)}, s32[64]{0:T(128)S(1)}, u32[]{:S(2)}, u32[]{:S(2)}) %collective-permute-start.3) | collective-permute-done | bytes 288 | tf_op jit(solution)/shard_map/ppermute | solution.py:24
  4.5 2.9 %collective-permute-start.4 = (bf16[16,128,128]{2,1,0:T(8,128)(2,1)}, bf16[16,128,128]{2,1,0:T(8,128)(2,1)S(1)}, u32[]{:S(2)}, u32[]{:S(2)}) collective-permute-start(bf16[16,128,128]{2,1,0:T(8,128)(2,1)} %refs_2_), channel_id=1, source_target_pairs={{0,4},{1,9},{2,6},{3,11},{8,0},{9,17},{10,2},{11,19},{16,8},{17,25... | collective-permute-start | bytes 1572872 | tf_op jit(solution)/shard_map/ppermute | solution.py:360
  7.3 4.7 %collective-permute-done.refs_11_ = bf16[16,128,128]{2,1,0:T(8,128)(2,1)S(1)} collective-permute-done((bf16[16,128,128]{2,1,0:T(8,128)(2,1)}, bf16[16,128,128]{2,1,0:T(8,128)(2,1)S(1)}, u32[]{:S(2)}, u32[]{:S(2)}) %collective-permute-start) | collective-permute-done | bytes 524320 | tf_op jit(solution)/shard_map/ppermute | solution.py:360
  12.1 2.4 %collective-permute-start.1 = (bf16[16,128,128]{2,1,0:T(8,128)(2,1)S(1)}, bf16[16,128,128]{2,1,0:T(8,128)(2,1)S(1)}, u32[]{:S(2)}, u32[]{:S(2)}) collective-permute-start(bf16[16,128,128]{2,1,0:T(8,128)(2,1)S(1)} %collective-permute-done.refs_11_), channel_id=1, source_target_pairs={{0,8},{1,5},{2,10},{3,7},{8,16},{9,1},{10,18},{11,3},{16,24},{17,9... | collective-permute-start | bytes 1572872 | tf_op jit(solution)/shard_map/ppermute | solution.py:360
  14.4 0.7 bitcast_add_fusion
  15.1 2.6 %collective-permute-done.4.refs_6_ = bf16[16,128,128]{2,1,0:T(8,128)(2,1)S(1)} collective-permute-done((bf16[16,128,128]{2,1,0:T(8,128)(2,1)}, bf16[16,128,128]{2,1,0:T(8,128)(2,1)S(1)}, u32[]{:S(2)}, u32[]{:S(2)}) %collective-permute-start.4) | collective-permute-done | bytes 524320 | tf_op jit(solution)/shard_map/ppermute | solution.py:360
  17.7 2.0 %collective-permute-start.5 = (bf16[16,128,128]{2,1,0:T(8,128)(2,1)S(1)}, bf16[16,128,128]{2,1,0:T(8,128)(2,1)S(1)}, u32[]{:S(2)}, u32[]{:S(2)}) collective-permute-start(bf16[16,128,128]{2,1,0:T(8,128)(2,1)S(1)} %collective-permute-done.4.refs_6_), channel_id=1, source_target_pairs={{0,4},{1,9},{2,6},{3,11},{8,0},{9,17},{10,2},{11,19},{16,8},{17,25... | collective-permute-start | bytes 1572872 | tf_op jit(solution)/shard_map/ppermute | solution.py:360
  19.6 1.5 %collective-permute-start.13 = (bf16[16,128,128]{2,1,0:T(8,128)(2,1)}, bf16[16,128,128]{2,1,0:T(8,128)(2,1)S(1)}, u32[]{:S(2)}, u32[]{:S(2)}) collective-permute-start(bf16[16,128,128]{2,1,0:T(8,128)(2,1)} %refs_2_), channel_id=1, source_target_pairs={{0,2},{1,3},{2,0},{3,1},{4,6},{5,7},{6,4},{7,5},{8,10},{9,11},{10,... | collective-permute-start | bytes 1572872 | tf_op jit(solution)/shard_map/ppermute | solution.py:24
  21.1 2.6 %collective-permute-start.10 = (s32[64]{0:T(128)S(1)}, s32[64]{0:T(128)S(1)}, u32[]{:S(2)}, u32[]{:S(2)}) collective-permute-start(s32[64]{0:T(128)S(1)} %bitcast_add_fusion), channel_id=1, source_target_pairs={{0,12},{4,8},{8,4},{12,0},{16,28},{20,24},{24,20},{28,16},{1,13},{... | collective-permute-start | bytes 776 | tf_op jit(solution)/shard_map/ppermute | solution.py:24
  23.7 0.4 collective-permute-done.1.refs_10_
  24.1 2.4 %collective-permute-start.9 = (s32[64]{0:T(128)S(1)}, s32[64]{0:T(128)S(1)}, u32[]{:S(2)}, u32[]{:S(2)}) collective-permute-start(s32[64]{0:T(128)S(1)} %bitcast_add_fusion), channel_id=1, source_target_pairs={{0,8},{4,12},{8,0},{12,4},{16,24},{20,28},{24,16},{28,20},{1,9},{5... | collective-permute-start | bytes 776 | tf_op jit(solution)/shard_map/ppermute | solution.py:24
  26.5 3.3 %collective-permute-start.2 = (bf16[16,128,128]{2,1,0:T(8,128)(2,1)S(1)}, bf16[16,128,128]{2,1,0:T(8,128)(2,1)S(1)}, u32[]{:S(2)}, u32[]{:S(2)}) collective-permute-start(bf16[16,128,128]{2,1,0:T(8,128)(2,1)S(1)} %collective-permute-done.1.refs_10_), channel_id=1, source_target_pairs={{0,8},{1,5},{2,10},{3,7},{8,16},{9,1},{10,18},{11,3},{16,24},{17,9... | collective-permute-start | bytes 1572872 | tf_op jit(solution)/shard_map/ppermute | solution.py:360
  30.1 1.9 %collective-permute-done.13.refs_3_ = bf16[16,128,128]{2,1,0:T(8,128)(2,1)S(1)} collective-permute-done((bf16[16,128,128]{2,1,0:T(8,128)(2,1)}, bf16[16,128,128]{2,1,0:T(8,128)(2,1)S(1)}, u32[]{:S(2)}, u32[]{:S(2)}) %collective-permute-start.13) | collective-permute-done | bytes 524320 | tf_op jit(solution)/shard_map/ppermute | solution.py:24
  31.9 0.5 collective-permute-start.15
  32.4 2.6 %collective-permute-start.12 = (s32[256]{0:T(256)S(1)}, s32[256]{0:T(256)S(1)}, u32[]{:S(2)}, u32[]{:S(2)}) collective-permute-start(s32[256]{0:T(256)S(1)} %pad_add_fusion.1), channel_id=1, source_target_pairs={{0,16},{4,20},{8,24},{12,28},{16,0},{20,4},{24,8},{28,12},{1,17},{... | collective-permute-start | bytes 3080 | tf_op jit(solution)/shard_map/ppermute | solution.py:24
  35.0 8.1 %collective-permute-done.12 = s32[256]{0:T(256)S(1)} collective-permute-done((s32[256]{0:T(256)S(1)}, s32[256]{0:T(256)S(1)}, u32[]{:S(2)}, u32[]{:S(2)}) %collective-permute-start.12) | collective-permute-done | bytes 1056 | tf_op jit(solution)/shard_map/ppermute | solution.py:24
  43.2 0.7 pad_add_fusion.2.cols_ref
  43.9 4.5 %shard_map.55 = (s32[145]{0:T(256)S(1)}, s32[3]{0:T(128)S(1)}) custom-call(s32[128]{0:T(128)S(1)} %pad_add_fusion.2.cols_ref, s32[512]{0:T(512)S(1)} %pad_add_fusion.aggs_ref), custom_call_target="tpu_custom_call" | custom-call | flops 1048576 | bytes 16777216 | tf_op jit(solution)/shard_map/pallas_call | solution.py:142
  48.5 0.6 collective-permute-start.18
  49.1 0.4 collective-permute-start.20
  49.6 1.7 %collective-permute-start.16 = (bf16[16,128,128]{2,1,0:T(8,128)(2,1)S(1)}, bf16[16,128,128]{2,1,0:T(8,128)(2,1)S(1)}, u32[]{:S(2)}, u32[]{:S(2)}) collective-permute-start(bf16[16,128,128]{2,1,0:T(8,128)(2,1)S(1)} %collective-permute-done.2.refs_9_), channel_id=1, source_target_pairs={{0,8},{1,5},{2,10},{3,7},{8,16},{9,1},{10,18},{11,3},{16,24},{17,9... | collective-permute-start | bytes 1572872 | tf_op jit(solution)/shard_map/ppermute | solution.py:360
  51.4 0.7 collective-permute-done.20.refs_16_
  52.1 0.7 collective-permute-done.21.refs_17_
  52.8 6.3 %shard_map.56 = (bf16[144,128,128]{2,1,0:T(8,128)(2,1)S(1)}, bf16[64,128,128]{2,1,0:T(8,128)(2,1)S(1)}) custom-call(s32[145]{0:T(256)S(1)} %get-tuple-element.53.plan_ref, s32[3]{0:T(128)S(1)} %get-tuple-element.54.starts_ref, bf16[64,128,128]{2,1,0:T(8,128)(2,1)} %bitcast.155, bf16[64,128,128]{2,1,0:T(8,128)(2,1)S(1)} %collective-permute-done.6.refs_1_, ...), custom_call_target="tpu_custom_call" | custom-call | flops 268435456 | bytes 1048576 | tf_op jit(solution)/shard_map/pallas_call | solution.py:222
  59.3 1.9 %collective-permute-done.22.far1 = bf16[16,128,128]{2,1,0:T(8,128)(2,1)S(1)} collective-permute-done((bf16[16,128,128]{2,1,0:T(8,128)(2,1)S(1)}, bf16[16,128,128]{2,1,0:T(8,128)(2,1)S(1)}, u32[]{:S(2)}, u32[]{:S(2)}) %collective-permute-start.22) | collective-permute-done | bytes 524320 | tf_op jit(solution)/shard_map/ppermute | solution.py:24
  61.2 4.0 %shard_map.57 = (bf16[2,2,2,1,1,336,128]{6,5,4,3,2,1,0:T(8,128)(2,1)S(1)}, f32[2,2,2,1,1,336,128]{6,5,4,3,2,1,0:T(8,128)S(1)}, bf16[2,2,2,1,1,336,128]{6,5,4,3,2...) custom-call(s32[145]{0:T(256)S(1)} %get-tuple-element.53.plan_ref, ...), custom_call_target="tpu_custom_call" | custom-call | flops 268435456 | bytes 16777216 | tf_op jit(solution)/shard_map/pallas_call | solution.py:328
  65.2 1.8 %collective-permute-start.23 = (bf16[2,2,2,1,1,336,128]{6,5,2,4,3,1,0:T(8,128)(2,1)S(1)}, bf16[2,2,2,1,1,336,128]{6,5,2,4,3,1,0:T(8,128)(2,1)S(1)}, u32[]{:S(2)}, u32[]{:S(2)}) collective-permute-start(bf16[2,2,2,1,1,336,128]{6,5,2,4,3,1,0:T(8,128)(2,1)S(1)} %bitcast.153), channel_id=1, source_target_pairs={{0,8},{1,3},{2,10},{3,1},{4,12},{5,7},{6,14},{7,5},{8,0},{9,11},{1... | collective-permute-start | bytes 2064392 | tf_op jit(solution)/shard_map/ppermute | solution.py:35
  66.9 1.0 collective-permute-start.27
  68.0 1.4 %collective-permute-start.31 = (bf16[2,2,2,1,1,352,128]{6,5,2,4,3,1,0:T(8,128)(2,1)S(1)}, bf16[2,2,2,1,1,352,128]{6,5,2,4,3,1,0:T(8,128)(2,1)S(1)}, u32[]{:S(2)}, u32[]{:S(2)}) collective-permute-start(bf16[2,2,2,1,1,352,128]{6,5,2,4,3,1,0:T(8,128)(2,1)S(1)} %bitcast.151), channel_id=1, source_target_pairs={{0,4},{1,17},{2,6},{3,19},{4,0},{5,21},{6,2},{7,23},{8,12},{9,25},... | collective-permute-start | bytes 2162696 | tf_op jit(solution)/shard_map/ppermute | solution.py:35
  69.3 13.0 %collective-permute-done.23 = bf16[2,2,2,1,1,336,128]{6,5,2,4,3,1,0:T(8,128)(2,1)S(1)} collective-permute-done((bf16[2,2,2,1,1,336,128]{6,5,2,4,3,1,0:T(8,128)(2,1)S(1)}, bf16[2,2,2,1,1,336,128]{6,5,2,4,3,1,0:T(8,128)(2,1)S(1)}, u32[]{:S(2)}, u32[]{:S(2)}) %collective-permute-start.23) | collective-permute-done | bytes 688160 | tf_op jit(solution)/shard_map/ppermute | solution.py:35
  82.4 1.6 %collective-permute-start.24 = (bf16[2,2,1,1,336,128]{5,4,3,2,1,0:T(8,128)(2,1)S(1)}, bf16[2,2,1,1,336,128]{5,4,3,2,1,0:T(8,128)(2,1)S(1)}, u32[]{:S(2)}, u32[]{:S(2)}) collective-permute-start(bf16[2,2,1,1,336,128]{5,4,3,2,1,0:T(8,128)(2,1)S(1)} %get-tuple-element.75), channel_id=1, source_target_pairs={{0,2},{1,9},{2,0},{3,11},{4,6},{5,13},{6,4},{7,15},{8,10},{9,1},{1... | collective-permute-start | bytes 1032200 | tf_op jit(solution)/shard_map/ppermute | solution.py:35
  84.2 1.2 %collective-permute-start.28 = (bf16[2,2,1,1,336,128]{5,4,3,2,1,0:T(8,128)(2,1)S(1)}, bf16[2,2,1,1,336,128]{5,4,3,2,1,0:T(8,128)(2,1)S(1)}, u32[]{:S(2)}, u32[]{:S(2)}) collective-permute-start(bf16[2,2,1,1,336,128]{5,4,3,2,1,0:T(8,128)(2,1)S(1)} %get-tuple-element.77), channel_id=1, source_target_pairs={{0,4},{1,3},{2,6},{3,1},{4,0},{5,7},{6,2},{7,5},{8,12},{9,11},{10,... | collective-permute-start | bytes 1032200 | tf_op jit(solution)/shard_map/ppermute | solution.py:35
  85.4 0.5 collective-permute-done.31
  85.9 2.1 %collective-permute-start.32 = (bf16[2,2,1,1,352,128]{5,4,1,0,3,2:T(8,128)(2,1)S(1)}, bf16[2,2,1,1,352,128]{5,4,1,0,3,2:T(8,128)(2,1)S(1)}, u32[]{:S(2)}, u32[]{:S(2)}) collective-permute-start(bf16[2,2,1,1,352,128]{5,4,1,0,3,2:T(8,128)(2,1)S(1)} %fusion.3), channel_id=1, source_target_pairs={{0,8},{1,3},{2,10},{3,1},{4,12},{5,7},{6,14},{7,5},{8,0},{9,11},{1... | collective-permute-start | bytes 1081352 | tf_op jit(solution)/shard_map/ppermute | solution.py:35
  88.1 3.7 %collective-permute-done.24 = bf16[2,2,1,1,336,128]{5,4,3,2,1,0:T(8,128)(2,1)S(1)} collective-permute-done((bf16[2,2,1,1,336,128]{5,4,3,2,1,0:T(8,128)(2,1)S(1)}, bf16[2,2,1,1,336,128]{5,4,3,2,1,0:T(8,128)(2,1)S(1)}, u32[]{:S(2)}, u32[]{:S(2)}) %collective-permute-start.24) | collective-permute-done | bytes 344096 | tf_op jit(solution)/shard_map/ppermute | solution.py:35
  91.9 3.4 %collective-permute-start.25 = (bf16[2,1,1,336,128]{4,3,2,1,0:T(8,128)(2,1)S(1)}, bf16[2,1,1,336,128]{4,3,2,1,0:T(8,128)(2,1)S(1)}, u32[]{:S(2)}, u32[]{:S(2)}) collective-permute-start(bf16[2,1,1,336,128]{4,3,2,1,0:T(8,128)(2,1)S(1)} %get-tuple-element.79), channel_id=1, source_target_pairs={{0,16},{1,5},{2,18},{3,7},{4,20},{5,1},{6,22},{7,3},{8,24},{9,13},... | collective-permute-start | bytes 516104 | tf_op jit(solution)/shard_map/ppermute | solution.py:35
  95.4 0.9 collective-permute-start.29
  96.3 1.7 %collective-permute-start.33 = (bf16[2,1,1,352,128]{4,3,0,2,1:T(8,128)(2,1)S(1)}, bf16[2,1,1,352,128]{4,3,0,2,1:T(8,128)(2,1)S(1)}, u32[]{:S(2)}, u32[]{:S(2)}) collective-permute-start(bf16[2,1,1,352,128]{4,3,0,2,1:T(8,128)(2,1)S(1)} %fusion.15), channel_id=1, source_target_pairs={{0,2},{1,5},{2,0},{3,7},{4,6},{5,1},{6,4},{7,3},{8,10},{9,13},{10,... | collective-permute-start | bytes 540680 | tf_op jit(solution)/shard_map/ppermute | solution.py:35
  98.0 6.2 %collective-permute-done.25 = bf16[2,1,1,336,128]{4,3,2,1,0:T(8,128)(2,1)S(1)} collective-permute-done((bf16[2,1,1,336,128]{4,3,2,1,0:T(8,128)(2,1)S(1)}, bf16[2,1,1,336,128]{4,3,2,1,0:T(8,128)(2,1)S(1)}, u32[]{:S(2)}, u32[]{:S(2)}) %collective-permute-start.25) | collective-permute-done | bytes 172064 | tf_op jit(solution)/shard_map/ppermute | solution.py:35
  104.3 2.0 %collective-permute-start.26 = (bf16[1,1,336,128]{3,2,1,0:T(8,128)(2,1)S(1)}, bf16[1,1,336,128]{3,2,1,0:T(8,128)(2,1)S(1)}, u32[]{:S(2)}, u32[]{:S(2)}) collective-permute-start(bf16[1,1,336,128]{3,2,1,0:T(8,128)(2,1)S(1)} %fusion.34), channel_id=1, source_target_pairs={{0,4},{1,17},{2,6},{3,19},{4,0},{5,21},{6,2},{7,23},{8,12},{9,25},... | collective-permute-start | bytes 258056 | tf_op jit(solution)/shard_map/ppermute | solution.py:35
  106.3 0.4 collective-permute-start.30
  106.7 2.7 %collective-permute-start.34 = (bf16[1,1,352,128]{3,2,1,0:T(8,128)(2,1)S(1)}, bf16[1,1,352,128]{3,2,1,0:T(8,128)(2,1)S(1)}, u32[]{:S(2)}, u32[]{:S(2)}) collective-permute-start(bf16[1,1,352,128]{3,2,1,0:T(8,128)(2,1)S(1)} %fusion.33), channel_id=1, source_target_pairs={{0,16},{1,9},{2,18},{3,11},{4,20},{5,13},{6,22},{7,15},{8,24},{9,1... | collective-permute-start | bytes 270344 | tf_op jit(solution)/shard_map/ppermute | solution.py:35
  109.4 2.9 %collective-permute-done.30 = bf16[1,1,336,128]{3,2,1,0:T(8,128)(2,1)S(1)} collective-permute-done((bf16[1,1,336,128]{3,2,1,0:T(8,128)(2,1)S(1)}, bf16[1,1,336,128]{3,2,1,0:T(8,128)(2,1)S(1)}, u32[]{:S(2)}, u32[]{:S(2)}) %collective-permute-start.30) | collective-permute-done | bytes 86048 | tf_op jit(solution)/shard_map/ppermute | solution.py:35
  112.4 1.9 %collective-permute-done.34 = bf16[1,1,352,128]{3,2,1,0:T(8,128)(2,1)S(1)} collective-permute-done((bf16[1,1,352,128]{3,2,1,0:T(8,128)(2,1)S(1)}, bf16[1,1,352,128]{3,2,1,0:T(8,128)(2,1)S(1)}, u32[]{:S(2)}, u32[]{:S(2)}) %collective-permute-start.34) | collective-permute-done | bytes 90144 | tf_op jit(solution)/shard_map/ppermute | solution.py:35
  114.3 0.8 pad_maximum_fusion
  (44 shorter events, 1.4 us)
Async XLA Ops:
  0.0 19.6 %collective-permute-start.6 = (bf16[64,128,128]{2,1,0:T(8,128)(2,1)}, bf16[64,128,128]{2,1,0:T(8,128)(2,1)S(1)}, u32[]{:S(2)}, u32[]{:S(2)}) collective-permute-start(bf16[64,128,128]{2,1,0:T(8,128)(2,1)} %bitcast.154), channel_id=1, source_target_pairs={{0,1},{1,0},{2,3},{3,2},{4,5},{5,4},{6,7},{7,6},{8,9},{9,8},{10,11... | collective-permute-start | bytes 6291464 | tf_op jit(solution)/shard_map/ppermute | solution.py:24
  0.5 11.6 %collective-permute-start = (bf16[16,128,128]{2,1,0:T(8,128)(2,1)}, bf16[16,128,128]{2,1,0:T(8,128)(2,1)S(1)}, u32[]{:S(2)}, u32[]{:S(2)}) collective-permute-start(bf16[16,128,128]{2,1,0:T(8,128)(2,1)} %refs_2_), channel_id=1, source_target_pairs={{0,8},{1,5},{2,10},{3,7},{8,16},{9,1},{10,18},{11,3},{16,24},{17,9... | collective-permute-start | bytes 1572872 | tf_op jit(solution)/shard_map/ppermute | solution.py:360
  3.0 1.4 %collective-permute-start.3 = (s32[64]{0:T(128)}, s32[64]{0:T(128)S(1)}, u32[]{:S(2)}, u32[]{:S(2)}) collective-permute-start(s32[64]{0:T(128)} %bitcast.158), channel_id=1, source_target_pairs={{0,1},{1,0},{2,3},{3,2},{4,5},{5,4},{6,7},{7,6},{8,9},{9,8},{10,11... | collective-permute-start | bytes 776 | tf_op jit(solution)/shard_map/ppermute | solution.py:24
  4.5 13.2 %collective-permute-start.4 = (bf16[16,128,128]{2,1,0:T(8,128)(2,1)}, bf16[16,128,128]{2,1,0:T(8,128)(2,1)S(1)}, u32[]{:S(2)}, u32[]{:S(2)}) collective-permute-start(bf16[16,128,128]{2,1,0:T(8,128)(2,1)} %refs_2_), channel_id=1, source_target_pairs={{0,4},{1,9},{2,6},{3,11},{8,0},{9,17},{10,2},{11,19},{16,8},{17,25... | collective-permute-start | bytes 1572872 | tf_op jit(solution)/shard_map/ppermute | solution.py:360
  7.3 12.3 %collective-permute-start.7 = (bf16[16,128,128]{2,1,0:T(8,128)(2,1)}, bf16[16,128,128]{2,1,0:T(8,128)(2,1)S(1)}, u32[]{:S(2)}, u32[]{:S(2)}) collective-permute-start(bf16[16,128,128]{2,1,0:T(8,128)(2,1)} %refs_2_), channel_id=1, source_target_pairs={{0,1},{1,0},{2,3},{3,2},{4,5},{5,4},{6,7},{7,6},{8,9},{9,8},{10,11... | collective-permute-start | bytes 1572872 | tf_op jit(solution)/shard_map/ppermute | solution.py:24
  12.1 12.1 %collective-permute-start.1 = (bf16[16,128,128]{2,1,0:T(8,128)(2,1)S(1)}, bf16[16,128,128]{2,1,0:T(8,128)(2,1)S(1)}, u32[]{:S(2)}, u32[]{:S(2)}) collective-permute-start(bf16[16,128,128]{2,1,0:T(8,128)(2,1)S(1)} %collective-permute-done.refs_11_), channel_id=1, source_target_pairs={{0,8},{1,5},{2,10},{3,7},{8,16},{9,1},{10,18},{11,3},{16,24},{17,9... | collective-permute-start | bytes 1572872 | tf_op jit(solution)/shard_map/ppermute | solution.py:360
  17.7 12.2 %collective-permute-start.5 = (bf16[16,128,128]{2,1,0:T(8,128)(2,1)S(1)}, bf16[16,128,128]{2,1,0:T(8,128)(2,1)S(1)}, u32[]{:S(2)}, u32[]{:S(2)}) collective-permute-start(bf16[16,128,128]{2,1,0:T(8,128)(2,1)S(1)} %collective-permute-done.4.refs_6_), channel_id=1, source_target_pairs={{0,4},{1,9},{2,6},{3,11},{8,0},{9,17},{10,2},{11,19},{16,8},{17,25... | collective-permute-start | bytes 1572872 | tf_op jit(solution)/shard_map/ppermute | solution.py:360
  19.6 12.3 %collective-permute-start.13 = (bf16[16,128,128]{2,1,0:T(8,128)(2,1)}, bf16[16,128,128]{2,1,0:T(8,128)(2,1)S(1)}, u32[]{:S(2)}, u32[]{:S(2)}) collective-permute-start(bf16[16,128,128]{2,1,0:T(8,128)(2,1)} %refs_2_), channel_id=1, source_target_pairs={{0,2},{1,3},{2,0},{3,1},{4,6},{5,7},{6,4},{7,5},{8,10},{9,11},{10,... | collective-permute-start | bytes 1572872 | tf_op jit(solution)/shard_map/ppermute | solution.py:24
  21.1 5.4 %collective-permute-start.10 = (s32[64]{0:T(128)S(1)}, s32[64]{0:T(128)S(1)}, u32[]{:S(2)}, u32[]{:S(2)}) collective-permute-start(s32[64]{0:T(128)S(1)} %bitcast_add_fusion), channel_id=1, source_target_pairs={{0,12},{4,8},{8,4},{12,0},{16,28},{20,24},{24,20},{28,16},{1,13},{... | collective-permute-start | bytes 776 | tf_op jit(solution)/shard_map/ppermute | solution.py:24
  23.7 6.1 %collective-permute-start.8 = (s32[64]{0:T(128)S(1)}, s32[64]{0:T(128)S(1)}, u32[]{:S(2)}, u32[]{:S(2)}) collective-permute-start(s32[64]{0:T(128)S(1)} %bitcast_add_fusion), channel_id=1, source_target_pairs={{0,4},{4,0},{8,12},{12,8},{16,20},{20,16},{24,28},{28,24},{1,5},{5... | collective-permute-start | bytes 776 | tf_op jit(solution)/shard_map/ppermute | solution.py:24
  24.1 5.7 %collective-permute-start.9 = (s32[64]{0:T(128)S(1)}, s32[64]{0:T(128)S(1)}, u32[]{:S(2)}, u32[]{:S(2)}) collective-permute-start(s32[64]{0:T(128)S(1)} %bitcast_add_fusion), channel_id=1, source_target_pairs={{0,8},{4,12},{8,0},{12,4},{16,24},{20,28},{24,16},{28,20},{1,9},{5... | collective-permute-start | bytes 776 | tf_op jit(solution)/shard_map/ppermute | solution.py:24
  26.5 21.9 %collective-permute-start.2 = (bf16[16,128,128]{2,1,0:T(8,128)(2,1)S(1)}, bf16[16,128,128]{2,1,0:T(8,128)(2,1)S(1)}, u32[]{:S(2)}, u32[]{:S(2)}) collective-permute-start(bf16[16,128,128]{2,1,0:T(8,128)(2,1)S(1)} %collective-permute-done.1.refs_10_), channel_id=1, source_target_pairs={{0,8},{1,5},{2,10},{3,7},{8,16},{9,1},{10,18},{11,3},{16,24},{17,9... | collective-permute-start | bytes 1572872 | tf_op jit(solution)/shard_map/ppermute | solution.py:360
  29.9 18.6 %collective-permute-start.11 = (bf16[16,128,128]{2,1,0:T(8,128)(2,1)S(1)}, bf16[16,128,128]{2,1,0:T(8,128)(2,1)S(1)}, u32[]{:S(2)}, u32[]{:S(2)}) collective-permute-start(bf16[16,128,128]{2,1,0:T(8,128)(2,1)S(1)} %collective-permute-done.5.refs_7_), channel_id=1, source_target_pairs={{0,4},{1,9},{2,6},{3,11},{8,0},{9,17},{10,2},{11,19},{16,8},{17,25... | collective-permute-start | bytes 1572872 | tf_op jit(solution)/shard_map/ppermute | solution.py:360
  31.9 16.5 %collective-permute-start.14 = (bf16[16,128,128]{2,1,0:T(8,128)(2,1)S(1)}, bf16[16,128,128]{2,1,0:T(8,128)(2,1)S(1)}, u32[]{:S(2)}, u32[]{:S(2)}) collective-permute-start(bf16[16,128,128]{2,1,0:T(8,128)(2,1)S(1)} %collective-permute-done.4.refs_6_), channel_id=1, source_target_pairs={{0,1},{1,0},{2,3},{3,2},{4,5},{5,4},{6,7},{7,6},{8,9},{9,8},{10,11... | collective-permute-start | bytes 1572872 | tf_op jit(solution)/shard_map/ppermute | solution.py:24
  31.9 16.6 %collective-permute-start.15 = (bf16[16,128,128]{2,1,0:T(8,128)(2,1)S(1)}, bf16[16,128,128]{2,1,0:T(8,128)(2,1)S(1)}, u32[]{:S(2)}, u32[]{:S(2)}) collective-permute-start(bf16[16,128,128]{2,1,0:T(8,128)(2,1)S(1)} %collective-permute-done.refs_11_), channel_id=1, source_target_pairs={{0,1},{1,0},{2,3},{3,2},{4,5},{5,4},{6,7},{7,6},{8,9},{9,8},{10,11... | collective-permute-start | bytes 1572872 | tf_op jit(solution)/shard_map/ppermute | solution.py:24
  32.4 10.7 %collective-permute-start.12 = (s32[256]{0:T(256)S(1)}, s32[256]{0:T(256)S(1)}, u32[]{:S(2)}, u32[]{:S(2)}) collective-permute-start(s32[256]{0:T(256)S(1)} %pad_add_fusion.1), channel_id=1, source_target_pairs={{0,16},{4,20},{8,24},{12,28},{16,0},{20,4},{24,8},{28,12},{1,17},{... | collective-permute-start | bytes 3080 | tf_op jit(solution)/shard_map/ppermute | solution.py:24
  43.2 6.5 %collective-permute-start.17 = (bf16[16,128,128]{2,1,0:T(8,128)(2,1)S(1)}, bf16[16,128,128]{2,1,0:T(8,128)(2,1)S(1)}, u32[]{:S(2)}, u32[]{:S(2)}) collective-permute-start(bf16[16,128,128]{2,1,0:T(8,128)(2,1)S(1)} %collective-permute-done.13.refs_3_), channel_id=1, source_target_pairs={{0,1},{1,0},{2,3},{3,2},{4,5},{5,4},{6,7},{7,6},{8,9},{9,8},{10,11... | collective-permute-start | bytes 1572872 | tf_op jit(solution)/shard_map/ppermute | solution.py:24
  48.5 2.9 %collective-permute-start.18 = (bf16[16,128,128]{2,1,0:T(8,128)(2,1)S(1)}, bf16[16,128,128]{2,1,0:T(8,128)(2,1)S(1)}, u32[]{:S(2)}, u32[]{:S(2)}) collective-permute-start(bf16[16,128,128]{2,1,0:T(8,128)(2,1)S(1)} %collective-permute-done.5.refs_7_), channel_id=1, source_target_pairs={{0,1},{1,0},{2,3},{3,2},{4,5},{5,4},{6,7},{7,6},{8,9},{9,8},{10,11... | collective-permute-start | bytes 1572872 | tf_op jit(solution)/shard_map/ppermute | solution.py:24
  49.1 2.3 %collective-permute-start.19 = (bf16[16,128,128]{2,1,0:T(8,128)(2,1)S(1)}, bf16[16,128,128]{2,1,0:T(8,128)(2,1)S(1)}, u32[]{:S(2)}, u32[]{:S(2)}) collective-permute-start(bf16[16,128,128]{2,1,0:T(8,128)(2,1)S(1)} %collective-permute-done.11.refs_8_), channel_id=1, source_target_pairs={{0,1},{1,0},{2,3},{3,2},{4,5},{5,4},{6,7},{7,6},{8,9},{9,8},{10,11... | collective-permute-start | bytes 1572872 | tf_op jit(solution)/shard_map/ppermute | solution.py:24
  49.1 3.0 %collective-permute-start.20 = (bf16[16,128,128]{2,1,0:T(8,128)(2,1)S(1)}, bf16[16,128,128]{2,1,0:T(8,128)(2,1)S(1)}, u32[]{:S(2)}, u32[]{:S(2)}) collective-permute-start(bf16[16,128,128]{2,1,0:T(8,128)(2,1)S(1)} %collective-permute-done.2.refs_9_), channel_id=1, source_target_pairs={{0,1},{1,0},{2,3},{3,2},{4,5},{5,4},{6,7},{7,6},{8,9},{9,8},{10,11... | collective-permute-start | bytes 1572872 | tf_op jit(solution)/shard_map/ppermute | solution.py:24
  49.6 3.3 %collective-permute-start.21 = (bf16[16,128,128]{2,1,0:T(8,128)(2,1)S(1)}, bf16[16,128,128]{2,1,0:T(8,128)(2,1)S(1)}, u32[]{:S(2)}, u32[]{:S(2)}) collective-permute-start(bf16[16,128,128]{2,1,0:T(8,128)(2,1)S(1)} %collective-permute-done.1.refs_10_), channel_id=1, source_target_pairs={{0,1},{1,0},{2,3},{3,2},{4,5},{5,4},{6,7},{7,6},{8,9},{9,8},{10,11... | collective-permute-start | bytes 1572872 | tf_op jit(solution)/shard_map/ppermute | solution.py:24
  49.6 9.5 %collective-permute-start.16 = (bf16[16,128,128]{2,1,0:T(8,128)(2,1)S(1)}, bf16[16,128,128]{2,1,0:T(8,128)(2,1)S(1)}, u32[]{:S(2)}, u32[]{:S(2)}) collective-permute-start(bf16[16,128,128]{2,1,0:T(8,128)(2,1)S(1)} %collective-permute-done.2.refs_9_), channel_id=1, source_target_pairs={{0,8},{1,5},{2,10},{3,7},{8,16},{9,1},{10,18},{11,3},{16,24},{17,9... | collective-permute-start | bytes 1572872 | tf_op jit(solution)/shard_map/ppermute | solution.py:360
  59.2 2.0 %collective-permute-start.22 = (bf16[16,128,128]{2,1,0:T(8,128)(2,1)S(1)}, bf16[16,128,128]{2,1,0:T(8,128)(2,1)S(1)}, u32[]{:S(2)}, u32[]{:S(2)}) collective-permute-start(bf16[16,128,128]{2,1,0:T(8,128)(2,1)S(1)} %collective-permute-done.16.far0), channel_id=1, source_target_pairs={{0,1},{1,0},{2,3},{3,2},{4,5},{5,4},{6,7},{7,6},{8,9},{9,8},{10,11... | collective-permute-start | bytes 1572872 | tf_op jit(solution)/shard_map/ppermute | solution.py:24
  65.2 17.1 %collective-permute-start.23 = (bf16[2,2,2,1,1,336,128]{6,5,2,4,3,1,0:T(8,128)(2,1)S(1)}, bf16[2,2,2,1,1,336,128]{6,5,2,4,3,1,0:T(8,128)(2,1)S(1)}, u32[]{:S(2)}, u32[]{:S(2)}) collective-permute-start(bf16[2,2,2,1,1,336,128]{6,5,2,4,3,1,0:T(8,128)(2,1)S(1)} %bitcast.153), channel_id=1, source_target_pairs={{0,8},{1,3},{2,10},{3,1},{4,12},{5,7},{6,14},{7,5},{8,0},{9,11},{1... | collective-permute-start | bytes 2064392 | tf_op jit(solution)/shard_map/ppermute | solution.py:35
  66.9 17.1 %collective-permute-start.27 = (bf16[2,2,2,1,1,336,128]{6,5,2,4,3,1,0:T(8,128)(2,1)S(1)}, bf16[2,2,2,1,1,336,128]{6,5,2,4,3,1,0:T(8,128)(2,1)S(1)}, u32[]{:S(2)}, u32[]{:S(2)}) collective-permute-start(bf16[2,2,2,1,1,336,128]{6,5,2,4,3,1,0:T(8,128)(2,1)S(1)} %bitcast.152), channel_id=1, source_target_pairs={{0,2},{1,5},{2,0},{3,7},{4,6},{5,1},{6,4},{7,3},{8,10},{9,13},{10,... | collective-permute-start | bytes 2064392 | tf_op jit(solution)/shard_map/ppermute | solution.py:35
  68.0 17.9 %collective-permute-start.31 = (bf16[2,2,2,1,1,352,128]{6,5,2,4,3,1,0:T(8,128)(2,1)S(1)}, bf16[2,2,2,1,1,352,128]{6,5,2,4,3,1,0:T(8,128)(2,1)S(1)}, u32[]{:S(2)}, u32[]{:S(2)}) collective-permute-start(bf16[2,2,2,1,1,352,128]{6,5,2,4,3,1,0:T(8,128)(2,1)S(1)} %bitcast.151), channel_id=1, source_target_pairs={{0,4},{1,17},{2,6},{3,19},{4,0},{5,21},{6,2},{7,23},{8,12},{9,25},... | collective-permute-start | bytes 2162696 | tf_op jit(solution)/shard_map/ppermute | solution.py:35
  82.4 9.4 %collective-permute-start.24 = (bf16[2,2,1,1,336,128]{5,4,3,2,1,0:T(8,128)(2,1)S(1)}, bf16[2,2,1,1,336,128]{5,4,3,2,1,0:T(8,128)(2,1)S(1)}, u32[]{:S(2)}, u32[]{:S(2)}) collective-permute-start(bf16[2,2,1,1,336,128]{5,4,3,2,1,0:T(8,128)(2,1)S(1)} %get-tuple-element.75), channel_id=1, source_target_pairs={{0,2},{1,9},{2,0},{3,11},{4,6},{5,13},{6,4},{7,15},{8,10},{9,1},{1... | collective-permute-start | bytes 1032200 | tf_op jit(solution)/shard_map/ppermute | solution.py:35
  84.2 11.1 %collective-permute-start.28 = (bf16[2,2,1,1,336,128]{5,4,3,2,1,0:T(8,128)(2,1)S(1)}, bf16[2,2,1,1,336,128]{5,4,3,2,1,0:T(8,128)(2,1)S(1)}, u32[]{:S(2)}, u32[]{:S(2)}) collective-permute-start(bf16[2,2,1,1,336,128]{5,4,3,2,1,0:T(8,128)(2,1)S(1)} %get-tuple-element.77), channel_id=1, source_target_pairs={{0,4},{1,3},{2,6},{3,1},{4,0},{5,7},{6,2},{7,5},{8,12},{9,11},{10,... | collective-permute-start | bytes 1032200 | tf_op jit(solution)/shard_map/ppermute | solution.py:35
  85.9 10.3 %collective-permute-start.32 = (bf16[2,2,1,1,352,128]{5,4,1,0,3,2:T(8,128)(2,1)S(1)}, bf16[2,2,1,1,352,128]{5,4,1,0,3,2:T(8,128)(2,1)S(1)}, u32[]{:S(2)}, u32[]{:S(2)}) collective-permute-start(bf16[2,2,1,1,352,128]{5,4,1,0,3,2:T(8,128)(2,1)S(1)} %fusion.3), channel_id=1, source_target_pairs={{0,8},{1,3},{2,10},{3,1},{4,12},{5,7},{6,14},{7,5},{8,0},{9,11},{1... | collective-permute-start | bytes 1081352 | tf_op jit(solution)/shard_map/ppermute | solution.py:35
  91.9 12.3 %collective-permute-start.25 = (bf16[2,1,1,336,128]{4,3,2,1,0:T(8,128)(2,1)S(1)}, bf16[2,1,1,336,128]{4,3,2,1,0:T(8,128)(2,1)S(1)}, u32[]{:S(2)}, u32[]{:S(2)}) collective-permute-start(bf16[2,1,1,336,128]{4,3,2,1,0:T(8,128)(2,1)S(1)} %get-tuple-element.79), channel_id=1, source_target_pairs={{0,16},{1,5},{2,18},{3,7},{4,20},{5,1},{6,22},{7,3},{8,24},{9,13},... | collective-permute-start | bytes 516104 | tf_op jit(solution)/shard_map/ppermute | solution.py:35
  95.4 10.9 %collective-permute-start.29 = (bf16[2,1,1,336,128]{4,3,2,1,0:T(8,128)(2,1)S(1)}, bf16[2,1,1,336,128]{4,3,2,1,0:T(8,128)(2,1)S(1)}, u32[]{:S(2)}, u32[]{:S(2)}) collective-permute-start(bf16[2,1,1,336,128]{4,3,2,1,0:T(8,128)(2,1)S(1)} %get-tuple-element.81), channel_id=1, source_target_pairs={{0,8},{1,17},{2,10},{3,19},{4,12},{5,21},{6,14},{7,23},{8,0},{9,25... | collective-permute-start | bytes 516104 | tf_op jit(solution)/shard_map/ppermute | solution.py:35
  96.3 10.4 %collective-permute-start.33 = (bf16[2,1,1,352,128]{4,3,0,2,1:T(8,128)(2,1)S(1)}, bf16[2,1,1,352,128]{4,3,0,2,1:T(8,128)(2,1)S(1)}, u32[]{:S(2)}, u32[]{:S(2)}) collective-permute-start(bf16[2,1,1,352,128]{4,3,0,2,1:T(8,128)(2,1)S(1)} %fusion.15), channel_id=1, source_target_pairs={{0,2},{1,5},{2,0},{3,7},{4,6},{5,1},{6,4},{7,3},{8,10},{9,13},{10,... | collective-permute-start | bytes 540680 | tf_op jit(solution)/shard_map/ppermute | solution.py:35
  104.3 5.1 %collective-permute-start.26 = (bf16[1,1,336,128]{3,2,1,0:T(8,128)(2,1)S(1)}, bf16[1,1,336,128]{3,2,1,0:T(8,128)(2,1)S(1)}, u32[]{:S(2)}, u32[]{:S(2)}) collective-permute-start(bf16[1,1,336,128]{3,2,1,0:T(8,128)(2,1)S(1)} %fusion.34), channel_id=1, source_target_pairs={{0,4},{1,17},{2,6},{3,19},{4,0},{5,21},{6,2},{7,23},{8,12},{9,25},... | collective-permute-start | bytes 258056 | tf_op jit(solution)/shard_map/ppermute | solution.py:35
  106.3 6.0 %collective-permute-start.30 = (bf16[1,1,336,128]{3,2,1,0:T(8,128)(2,1)S(1)}, bf16[1,1,336,128]{3,2,1,0:T(8,128)(2,1)S(1)}, u32[]{:S(2)}, u32[]{:S(2)}) collective-permute-start(bf16[1,1,336,128]{3,2,1,0:T(8,128)(2,1)S(1)} %fusion.35), channel_id=1, source_target_pairs={{0,16},{1,9},{2,18},{3,11},{4,20},{5,13},{6,22},{7,15},{8,24},{9,1... | collective-permute-start | bytes 258056 | tf_op jit(solution)/shard_map/ppermute | solution.py:35
  106.7 7.5 %collective-permute-start.34 = (bf16[1,1,352,128]{3,2,1,0:T(8,128)(2,1)S(1)}, bf16[1,1,352,128]{3,2,1,0:T(8,128)(2,1)S(1)}, u32[]{:S(2)}, u32[]{:S(2)}) collective-permute-start(bf16[1,1,352,128]{3,2,1,0:T(8,128)(2,1)S(1)} %fusion.33), channel_id=1, source_target_pairs={{0,16},{1,9},{2,18},{3,11},{4,20},{5,13},{6,22},{7,15},{8,24},{9,1... | collective-permute-start | bytes 270344 | tf_op jit(solution)/shard_map/ppermute | solution.py:35

commit v4 on v3

--- a/solution.py
+++ b/solution.py
@@ -367,21 +367,20 @@
     a_other, p_other = swap(a_blocks[:, 0], "col", 1), swap(p_tiles, "col", 1)
 
     aggs = owner[:, 0] * OWN + agg_local
-    aggs, a_other, p_other, one, two, mine = barrier(
-        (aggs, a_other, p_other, first, second, p_tiles)
-    )
-    own_near, other_near = {0: p_tiles, s.rows - 1: one, 1: two}, {0: p_other}
-    first, second = ring(first, 0), ring(second, 1)
+    came, aggs, a_other, p_other = barrier((first, aggs, a_other, p_other))
+    first = ring(first, 0)
     aggs = [aggs] + [swap(aggs, "row", mask) for mask in (1, 2, 3)]
-    second, aggs = barrier((second, jnp.concatenate(aggs, 0)))
+    own_near, other_near = {0: p_tiles, s.rows - 1: came, 1: second}, {0: p_other}
+    second = ring(second, 1)
+    aggs, mine = barrier((jnp.concatenate(aggs, 0), p_tiles))
+    bit = 4
+    while bit < s.rows:
+        aggs = jnp.concatenate([aggs, swap(aggs, "row", bit)], 0)
+        bit *= 2
     rows = [mine]
     bit = 2
     while bit < s.cols:
         rows += [swap(piece, "col", bit) for piece in rows]
-        bit *= 2
-    bit = 4
-    while bit < s.rows:
-        aggs = jnp.concatenate([aggs, swap(aggs, "row", bit)], 0)
         bit *= 2
     plan, starts = make_plan(s, jnp.concatenate([cols, cols_other], 0), aggs)
 
@@ -397,9 +396,11 @@
         held = [step, s.rows - step]
 
     others = sorted(set(other_near) - {0})
-    tie = (first, second, plan, starts)
+    tie = (first, second, plan, starts, *rows[s.cols // 2 + 1:])
     tie += (*(own_near[away] for away in held), *(other_near[away] for away in others))
     first, second, plan, starts, *rest = barrier(tie)
+    rows[s.cols // 2 + 1:] = rest[:s.cols // 2 - 1]
+    rest = rest[s.cols // 2 - 1:]
     for away, piece in zip(others, rest[len(held):]):
         other_near[away] = piece
     far = ring(first, 0)

time: 115 us -> 110 us (0.957)
  starting transfers between devices: 46.4 us -> 43.5 us
  waiting for transfers between devices: 50.5 us -> 49.1 us
    ppermute x16, waiting for transfers between devices: 14.6 us -> 5.28 us  [swap(): return lax.ppermute(value, axis, [(i, i ^ bit) for i in range(size)])]
    ppermute x7, waiting for transfers between devices: 7.71 us -> 15.9 us  [ring(): return lax.ppermute(value, ('row', 'col'), moves)]
    ppermute x7, starting transfers between devices: 15 us -> 11.6 us  [ring(): return lax.ppermute(value, ('row', 'col'), moves)]
    ppermute x12, starting transfers between devices: 20 us -> 21.3 us  [exchange(): return lax.ppermute(value, ('row', 'col'), moves)]
  transfers between devices with their start and end apart: 35 -> 35, of which waited for: 15 -> 16; matrix products, arithmetic and copies ran while one was open for 2% -> 2% of each run, Pallas kernels for 9% -> 9%
where the time goes in v4:
time: 110 us
  waiting for transfers between devices  49.1 us (45%)
  starting transfers between devices  43.5 us (40%)
  Pallas kernels  13.9 us (13%)
  other arithmetic  3.19 us (3%)
    ppermute x12, waiting for transfers between devices, exchange(): return lax.ppermute(value, ('row', 'col'), moves)  27.9 us
    ppermute x12, starting transfers between devices, exchange(): return lax.ppermute(value, ('row', 'col'), moves)  21.3 us
    ppermute x7, waiting for transfers between devices, ring(): return lax.ppermute(value, ('row', 'col'), moves)  15.9 us
    ppermute x7, starting transfers between devices, ring(): return lax.ppermute(value, ('row', 'col'), moves)  11.6 us
    ppermute x16, starting transfers between devices, swap(): return lax.ppermute(value, axis, [(i, i ^ bit) for i in range(size)])  10.6 us
    pallas_call x1, Pallas kernels, make_products(): pl.pallas_call(functools.partial(product_kernel, s), in_specs=[smem, smem...  5.67 us
    ppermute x16, waiting for transfers between devices, swap(): return lax.ppermute(value, axis, [(i, i ^ bit) for i in range(size)])  5.28 us
    pallas_call x1, Pallas kernels, make_plan(): pl.pallas_call(functools.partial(plan_kernel, s), in_specs=[smem, smem],...  4.54 us
  transfers between devices with their start and end apart: 35, of which 16 were waited for; matrix products, arithmetic and copies ran while one was open for 2% of the time, Pallas kernels for 9%

profile of v4, /device:TPU:0, one launch (start us, length us, event | category | flops | bytes accessed | tf_op | source)
XLA Modules:
  0.0 109.9 jit_solution(13939777223603939807)
XLA Ops:
  0.0 0.5 collective-permute-start.7
  0.5 3.0 %collective-permute-start = (bf16[16,128,128]{2,1,0:T(8,128)(2,1)}, bf16[16,128,128]{2,1,0:T(8,128)(2,1)S(1)}, u32[]{:S(2)}, u32[]{:S(2)}) collective-permute-start(bf16[16,128,128]{2,1,0:T(8,128)(2,1)} %refs_2_), channel_id=1, source_target_pairs={{0,8},{1,5},{2,10},{3,7},{8,16},{9,1},{10,18},{11,3},{16,24},{17,9... | collective-permute-start | bytes 1572872 | tf_op jit(solution)/shard_map/ppermute | solution.py:360
  3.5 0.9 collective-permute-done.3
  4.5 2.9 %collective-permute-start.4 = (bf16[16,128,128]{2,1,0:T(8,128)(2,1)}, bf16[16,128,128]{2,1,0:T(8,128)(2,1)S(1)}, u32[]{:S(2)}, u32[]{:S(2)}) collective-permute-start(bf16[16,128,128]{2,1,0:T(8,128)(2,1)} %refs_2_), channel_id=1, source_target_pairs={{0,4},{1,9},{2,6},{3,11},{8,0},{9,17},{10,2},{11,19},{16,8},{17,25... | collective-permute-start | bytes 1572872 | tf_op jit(solution)/shard_map/ppermute | solution.py:360
  7.3 0.7 bitcast_add_fusion
  8.0 5.1 %collective-permute-done.refs_11_ = bf16[16,128,128]{2,1,0:T(8,128)(2,1)S(1)} collective-permute-done((bf16[16,128,128]{2,1,0:T(8,128)(2,1)}, bf16[16,128,128]{2,1,0:T(8,128)(2,1)S(1)}, u32[]{:S(2)}, u32[]{:S(2)}) %collective-permute-start) | collective-permute-done | bytes 524320 | tf_op jit(solution)/shard_map/ppermute | solution.py:360
  13.1 3.3 %collective-permute-start.11 = (s32[64]{0:T(128)S(1)}, s32[64]{0:T(128)S(1)}, u32[]{:S(2)}, u32[]{:S(2)}) collective-permute-start(s32[64]{0:T(128)S(1)} %bitcast_add_fusion), channel_id=1, source_target_pairs={{0,12},{4,8},{8,4},{12,0},{16,28},{20,24},{24,20},{28,16},{1,13},{... | collective-permute-start | bytes 776 | tf_op jit(solution)/shard_map/ppermute | solution.py:24
  16.4 0.4 collective-permute-start.10
  16.9 0.2 collective-permute-start.9
  17.1 1.9 %collective-permute-start.1 = (bf16[16,128,128]{2,1,0:T(8,128)(2,1)S(1)}, bf16[16,128,128]{2,1,0:T(8,128)(2,1)S(1)}, u32[]{:S(2)}, u32[]{:S(2)}) collective-permute-start(bf16[16,128,128]{2,1,0:T(8,128)(2,1)S(1)} %collective-permute-done.refs_11_), channel_id=1, source_target_pairs={{0,8},{1,5},{2,10},{3,7},{8,16},{9,1},{10,18},{11,3},{16,24},{17,9... | collective-permute-start | bytes 1572872 | tf_op jit(solution)/shard_map/ppermute | solution.py:360
  19.1 0.9 collective-permute-done.10
  20.0 0.4 collective-permute-done.9
  20.5 1.5 %collective-permute-start.13 = (bf16[16,128,128]{2,1,0:T(8,128)(2,1)}, bf16[16,128,128]{2,1,0:T(8,128)(2,1)S(1)}, u32[]{:S(2)}, u32[]{:S(2)}) collective-permute-start(bf16[16,128,128]{2,1,0:T(8,128)(2,1)} %refs_2_), channel_id=1, source_target_pairs={{0,2},{1,3},{2,0},{3,1},{4,6},{5,7},{6,4},{7,5},{8,10},{9,11},{10,... | collective-permute-start | bytes 1572872 | tf_op jit(solution)/shard_map/ppermute | solution.py:24
  22.0 2.6 %collective-permute-start.12 = (s32[256]{0:T(256)S(1)}, s32[256]{0:T(256)S(1)}, u32[]{:S(2)}, u32[]{:S(2)}) collective-permute-start(s32[256]{0:T(256)S(1)} %pad_add_fusion.1), channel_id=1, source_target_pairs={{0,16},{4,20},{8,24},{12,28},{16,0},{20,4},{24,8},{28,12},{1,17},{... | collective-permute-start | bytes 3080 | tf_op jit(solution)/shard_map/ppermute | solution.py:24
  24.6 5.8 %collective-permute-done.1.refs_10_ = bf16[16,128,128]{2,1,0:T(8,128)(2,1)S(1)} collective-permute-done((bf16[16,128,128]{2,1,0:T(8,128)(2,1)S(1)}, bf16[16,128,128]{2,1,0:T(8,128)(2,1)S(1)}, u32[]{:S(2)}, u32[]{:S(2)}) %collective-permute-start.1) | collective-permute-done | bytes 524320 | tf_op jit(solution)/shard_map/ppermute | solution.py:360
  30.4 1.8 %collective-permute-start.2 = (bf16[16,128,128]{2,1,0:T(8,128)(2,1)S(1)}, bf16[16,128,128]{2,1,0:T(8,128)(2,1)S(1)}, u32[]{:S(2)}, u32[]{:S(2)}) collective-permute-start(bf16[16,128,128]{2,1,0:T(8,128)(2,1)S(1)} %collective-permute-done.1.refs_10_), channel_id=1, source_target_pairs={{0,8},{1,5},{2,10},{3,7},{8,16},{9,1},{10,18},{11,3},{16,24},{17,9... | collective-permute-start | bytes 1572872 | tf_op jit(solution)/shard_map/ppermute | solution.py:360
  32.2 0.2 collective-permute-start.6
  32.4 0.5 collective-permute-start.15
  33.0 0.7 pad_add_fusion.2.cols_ref
  33.7 4.5 %shard_map.55 = (s32[145]{0:T(256)S(1)}, s32[3]{0:T(128)S(1)}) custom-call(s32[128]{0:T(128)S(1)} %pad_add_fusion.2.cols_ref, s32[512]{0:T(512)S(1)} %pad_add_fusion.aggs_ref), custom_call_target="tpu_custom_call" | custom-call | flops 1048576 | bytes 16777216 | tf_op jit(solution)/shard_map/pallas_call | solution.py:142
  38.2 4.6 %collective-permute-done.2.refs_9_ = bf16[16,128,128]{2,1,0:T(8,128)(2,1)S(1)} collective-permute-done((bf16[16,128,128]{2,1,0:T(8,128)(2,1)S(1)}, bf16[16,128,128]{2,1,0:T(8,128)(2,1)S(1)}, u32[]{:S(2)}, u32[]{:S(2)}) %collective-permute-start.2) | collective-permute-done | bytes 524320 | tf_op jit(solution)/shard_map/ppermute | solution.py:360
  42.9 0.5 collective-permute-start.21
  43.5 0.4 collective-permute-start.20
  43.9 1.7 %collective-permute-start.17 = (bf16[16,128,128]{2,1,0:T(8,128)(2,1)S(1)}, bf16[16,128,128]{2,1,0:T(8,128)(2,1)S(1)}, u32[]{:S(2)}, u32[]{:S(2)}) collective-permute-start(bf16[16,128,128]{2,1,0:T(8,128)(2,1)S(1)} %collective-permute-done.2.refs_9_), channel_id=1, source_target_pairs={{0,8},{1,5},{2,10},{3,7},{8,16},{9,1},{10,18},{11,3},{16,24},{17,9... | collective-permute-start | bytes 1572872 | tf_op jit(solution)/shard_map/ppermute | solution.py:360
  45.6 0.7 collective-permute-done.19.refs_15_
  46.3 0.7 collective-permute-done.20.refs_16_
  47.1 5.7 %shard_map.56 = (bf16[144,128,128]{2,1,0:T(8,128)(2,1)S(1)}, bf16[64,128,128]{2,1,0:T(8,128)(2,1)S(1)}) custom-call(s32[145]{0:T(256)S(1)} %get-tuple-element.51.plan_ref, s32[3]{0:T(128)S(1)} %get-tuple-element.52.starts_ref, bf16[64,128,128]{2,1,0:T(8,128)(2,1)} %bitcast.155, bf16[64,128,128]{2,1,0:T(8,128)(2,1)S(1)} %collective-permute-done.7.refs_1_, ...), custom_call_target="tpu_custom_call" | custom-call | flops 268435456 | bytes 1048576 | tf_op jit(solution)/shard_map/pallas_call | solution.py:222
  52.8 0.4 collective-permute-done.17.far0
  53.1 0.5 collective-permute-start.22
  53.6 1.5 %collective-permute-done.22.far1 = bf16[16,128,128]{2,1,0:T(8,128)(2,1)S(1)} collective-permute-done((bf16[16,128,128]{2,1,0:T(8,128)(2,1)S(1)}, bf16[16,128,128]{2,1,0:T(8,128)(2,1)S(1)}, u32[]{:S(2)}, u32[]{:S(2)}) %collective-permute-start.22) | collective-permute-done | bytes 524320 | tf_op jit(solution)/shard_map/ppermute | solution.py:24
  55.2 3.7 %shard_map.57 = (bf16[2,2,2,1,1,336,128]{6,5,4,3,2,1,0:T(8,128)(2,1)S(1)}, f32[2,2,2,1,1,336,128]{6,5,4,3,2,1,0:T(8,128)S(1)}, bf16[2,2,2,1,1,336,128]{6,5,4,3,2...) custom-call(s32[145]{0:T(256)S(1)} %get-tuple-element.51.plan_ref, ...), custom_call_target="tpu_custom_call" | custom-call | flops 268435456 | bytes 16777216 | tf_op jit(solution)/shard_map/pallas_call | solution.py:328
  58.9 1.4 %collective-permute-start.23 = (bf16[2,2,2,1,1,336,128]{6,5,2,4,3,1,0:T(8,128)(2,1)S(1)}, bf16[2,2,2,1,1,336,128]{6,5,2,4,3,1,0:T(8,128)(2,1)S(1)}, u32[]{:S(2)}, u32[]{:S(2)}) collective-permute-start(bf16[2,2,2,1,1,336,128]{6,5,2,4,3,1,0:T(8,128)(2,1)S(1)} %bitcast.153), channel_id=1, source_target_pairs={{0,8},{1,3},{2,10},{3,1},{4,12},{5,7},{6,14},{7,5},{8,0},{9,11},{1... | collective-permute-start | bytes 2064392 | tf_op jit(solution)/shard_map/ppermute | solution.py:35
  60.3 1.8 %collective-permute-start.27 = (bf16[2,2,2,1,1,336,128]{6,5,2,4,3,1,0:T(8,128)(2,1)S(1)}, bf16[2,2,2,1,1,336,128]{6,5,2,4,3,1,0:T(8,128)(2,1)S(1)}, u32[]{:S(2)}, u32[]{:S(2)}) collective-permute-start(bf16[2,2,2,1,1,336,128]{6,5,2,4,3,1,0:T(8,128)(2,1)S(1)} %bitcast.152), channel_id=1, source_target_pairs={{0,2},{1,5},{2,0},{3,7},{4,6},{5,1},{6,4},{7,3},{8,10},{9,13},{10,... | collective-permute-start | bytes 2064392 | tf_op jit(solution)/shard_map/ppermute | solution.py:35
  62.1 2.0 %collective-permute-start.31 = (bf16[2,2,2,1,1,352,128]{6,5,2,4,3,1,0:T(8,128)(2,1)S(1)}, bf16[2,2,2,1,1,352,128]{6,5,2,4,3,1,0:T(8,128)(2,1)S(1)}, u32[]{:S(2)}, u32[]{:S(2)}) collective-permute-start(bf16[2,2,2,1,1,352,128]{6,5,2,4,3,1,0:T(8,128)(2,1)S(1)} %bitcast.151), channel_id=1, source_target_pairs={{0,4},{1,17},{2,6},{3,19},{4,0},{5,21},{6,2},{7,23},{8,12},{9,25},... | collective-permute-start | bytes 2162696 | tf_op jit(solution)/shard_map/ppermute | solution.py:35
  64.1 11.6 %collective-permute-done.23 = bf16[2,2,2,1,1,336,128]{6,5,2,4,3,1,0:T(8,128)(2,1)S(1)} collective-permute-done((bf16[2,2,2,1,1,336,128]{6,5,2,4,3,1,0:T(8,128)(2,1)S(1)}, bf16[2,2,2,1,1,336,128]{6,5,2,4,3,1,0:T(8,128)(2,1)S(1)}, u32[]{:S(2)}, u32[]{:S(2)}) %collective-permute-start.23) | collective-permute-done | bytes 688160 | tf_op jit(solution)/shard_map/ppermute | solution.py:35
  75.8 1.3 %collective-permute-start.24 = (bf16[2,2,1,1,336,128]{5,4,3,2,1,0:T(8,128)(2,1)S(1)}, bf16[2,2,1,1,336,128]{5,4,3,2,1,0:T(8,128)(2,1)S(1)}, u32[]{:S(2)}, u32[]{:S(2)}) collective-permute-start(bf16[2,2,1,1,336,128]{5,4,3,2,1,0:T(8,128)(2,1)S(1)} %get-tuple-element.73), channel_id=1, source_target_pairs={{0,2},{1,9},{2,0},{3,11},{4,6},{5,13},{6,4},{7,15},{8,10},{9,1},{1... | collective-permute-start | bytes 1032200 | tf_op jit(solution)/shard_map/ppermute | solution.py:35
  77.1 0.2 collective-permute-done.27
  77.5 2.9 %collective-permute-start.28 = (bf16[2,2,1,1,336,128]{5,4,3,2,1,0:T(8,128)(2,1)S(1)}, bf16[2,2,1,1,336,128]{5,4,3,2,1,0:T(8,128)(2,1)S(1)}, u32[]{:S(2)}, u32[]{:S(2)}) collective-permute-start(bf16[2,2,1,1,336,128]{5,4,3,2,1,0:T(8,128)(2,1)S(1)} %get-tuple-element.75), channel_id=1, source_target_pairs={{0,4},{1,3},{2,6},{3,1},{4,0},{5,7},{6,2},{7,5},{8,12},{9,11},{10,... | collective-permute-start | bytes 1032200 | tf_op jit(solution)/shard_map/ppermute | solution.py:35
  80.5 1.1 collective-permute-start.32
  81.7 4.3 %collective-permute-done.24 = bf16[2,2,1,1,336,128]{5,4,3,2,1,0:T(8,128)(2,1)S(1)} collective-permute-done((bf16[2,2,1,1,336,128]{5,4,3,2,1,0:T(8,128)(2,1)S(1)}, bf16[2,2,1,1,336,128]{5,4,3,2,1,0:T(8,128)(2,1)S(1)}, u32[]{:S(2)}, u32[]{:S(2)}) %collective-permute-start.24) | collective-permute-done | bytes 344096 | tf_op jit(solution)/shard_map/ppermute | solution.py:35
  86.0 2.1 %collective-permute-start.25 = (bf16[2,1,1,336,128]{4,3,2,1,0:T(8,128)(2,1)S(1)}, bf16[2,1,1,336,128]{4,3,2,1,0:T(8,128)(2,1)S(1)}, u32[]{:S(2)}, u32[]{:S(2)}) collective-permute-start(bf16[2,1,1,336,128]{4,3,2,1,0:T(8,128)(2,1)S(1)} %get-tuple-element.77), channel_id=1, source_target_pairs={{0,16},{1,5},{2,18},{3,7},{4,20},{5,1},{6,22},{7,3},{8,24},{9,13},... | collective-permute-start | bytes 516104 | tf_op jit(solution)/shard_map/ppermute | solution.py:35
  88.3 2.5 %collective-permute-start.33 = (bf16[2,1,1,352,128]{4,3,0,2,1:T(8,128)(2,1)S(1)}, bf16[2,1,1,352,128]{4,3,0,2,1:T(8,128)(2,1)S(1)}, u32[]{:S(2)}, u32[]{:S(2)}) collective-permute-start(bf16[2,1,1,352,128]{4,3,0,2,1:T(8,128)(2,1)S(1)} %fusion.15), channel_id=1, source_target_pairs={{0,2},{1,5},{2,0},{3,7},{4,6},{5,1},{6,4},{7,3},{8,10},{9,13},{10,... | collective-permute-start | bytes 540680 | tf_op jit(solution)/shard_map/ppermute | solution.py:35
  90.9 7.8 %collective-permute-done.25 = bf16[2,1,1,336,128]{4,3,2,1,0:T(8,128)(2,1)S(1)} collective-permute-done((bf16[2,1,1,336,128]{4,3,2,1,0:T(8,128)(2,1)S(1)}, bf16[2,1,1,336,128]{4,3,2,1,0:T(8,128)(2,1)S(1)}, u32[]{:S(2)}, u32[]{:S(2)}) %collective-permute-start.25) | collective-permute-done | bytes 172064 | tf_op jit(solution)/shard_map/ppermute | solution.py:35
  98.7 3.1 %collective-permute-start.26 = (bf16[1,1,336,128]{3,2,1,0:T(8,128)(2,1)S(1)}, bf16[1,1,336,128]{3,2,1,0:T(8,128)(2,1)S(1)}, u32[]{:S(2)}, u32[]{:S(2)}) collective-permute-start(bf16[1,1,336,128]{3,2,1,0:T(8,128)(2,1)S(1)} %fusion.34), channel_id=1, source_target_pairs={{0,4},{1,17},{2,6},{3,19},{4,0},{5,21},{6,2},{7,23},{8,12},{9,25},... | collective-permute-start | bytes 258056 | tf_op jit(solution)/shard_map/ppermute | solution.py:35
  101.9 3.0 %collective-permute-start.34 = (bf16[1,1,352,128]{3,2,1,0:T(8,128)(2,1)S(1)}, bf16[1,1,352,128]{3,2,1,0:T(8,128)(2,1)S(1)}, u32[]{:S(2)}, u32[]{:S(2)}) collective-permute-start(bf16[1,1,352,128]{3,2,1,0:T(8,128)(2,1)S(1)} %fusion.33), channel_id=1, source_target_pairs={{0,16},{1,9},{2,18},{3,11},{4,20},{5,13},{6,22},{7,15},{8,24},{9,1... | collective-permute-start | bytes 270344 | tf_op jit(solution)/shard_map/ppermute | solution.py:35
  104.9 3.1 %collective-permute-done.30 = bf16[1,1,336,128]{3,2,1,0:T(8,128)(2,1)S(1)} collective-permute-done((bf16[1,1,336,128]{3,2,1,0:T(8,128)(2,1)S(1)}, bf16[1,1,336,128]{3,2,1,0:T(8,128)(2,1)S(1)}, u32[]{:S(2)}, u32[]{:S(2)}) %collective-permute-start.30) | collective-permute-done | bytes 86048 | tf_op jit(solution)/shard_map/ppermute | solution.py:35
  108.1 0.9 collective-permute-done.34
  109.1 0.8 pad_maximum_fusion
  (44 shorter events, 1.5 us)
Async XLA Ops:
  0.0 13.1 %collective-permute-start.7 = (bf16[64,128,128]{2,1,0:T(8,128)(2,1)}, bf16[64,128,128]{2,1,0:T(8,128)(2,1)S(1)}, u32[]{:S(2)}, u32[]{:S(2)}) collective-permute-start(bf16[64,128,128]{2,1,0:T(8,128)(2,1)} %bitcast.154), channel_id=1, source_target_pairs={{0,1},{1,0},{2,3},{3,2},{4,5},{5,4},{6,7},{7,6},{8,9},{9,8},{10,11... | collective-permute-start | bytes 6291464 | tf_op jit(solution)/shard_map/ppermute | solution.py:24
  0.5 4.0 %collective-permute-start.3 = (s32[64]{0:T(128)}, s32[64]{0:T(128)S(1)}, u32[]{:S(2)}, u32[]{:S(2)}) collective-permute-start(s32[64]{0:T(128)} %bitcast.158), channel_id=1, source_target_pairs={{0,1},{1,0},{2,3},{3,2},{4,5},{5,4},{6,7},{7,6},{8,9},{9,8},{10,11... | collective-permute-start | bytes 776 | tf_op jit(solution)/shard_map/ppermute | solution.py:24
  0.5 12.6 %collective-permute-start = (bf16[16,128,128]{2,1,0:T(8,128)(2,1)}, bf16[16,128,128]{2,1,0:T(8,128)(2,1)S(1)}, u32[]{:S(2)}, u32[]{:S(2)}) collective-permute-start(bf16[16,128,128]{2,1,0:T(8,128)(2,1)} %refs_2_), channel_id=1, source_target_pairs={{0,8},{1,5},{2,10},{3,7},{8,16},{9,1},{10,18},{11,3},{16,24},{17,9... | collective-permute-start | bytes 1572872 | tf_op jit(solution)/shard_map/ppermute | solution.py:360
  3.5 9.6 %collective-permute-start.8 = (bf16[16,128,128]{2,1,0:T(8,128)(2,1)}, bf16[16,128,128]{2,1,0:T(8,128)(2,1)S(1)}, u32[]{:S(2)}, u32[]{:S(2)}) collective-permute-start(bf16[16,128,128]{2,1,0:T(8,128)(2,1)} %refs_2_), channel_id=1, source_target_pairs={{0,1},{1,0},{2,3},{3,2},{4,5},{5,4},{6,7},{7,6},{8,9},{9,8},{10,11... | collective-permute-start | bytes 1572872 | tf_op jit(solution)/shard_map/ppermute | solution.py:24
  4.5 14.5 %collective-permute-start.4 = (bf16[16,128,128]{2,1,0:T(8,128)(2,1)}, bf16[16,128,128]{2,1,0:T(8,128)(2,1)S(1)}, u32[]{:S(2)}, u32[]{:S(2)}) collective-permute-start(bf16[16,128,128]{2,1,0:T(8,128)(2,1)} %refs_2_), channel_id=1, source_target_pairs={{0,4},{1,9},{2,6},{3,11},{8,0},{9,17},{10,2},{11,19},{16,8},{17,25... | collective-permute-start | bytes 1572872 | tf_op jit(solution)/shard_map/ppermute | solution.py:360
  13.1 6.0 %collective-permute-start.11 = (s32[64]{0:T(128)S(1)}, s32[64]{0:T(128)S(1)}, u32[]{:S(2)}, u32[]{:S(2)}) collective-permute-start(s32[64]{0:T(128)S(1)} %bitcast_add_fusion), channel_id=1, source_target_pairs={{0,12},{4,8},{8,4},{12,0},{16,28},{20,24},{24,20},{28,16},{1,13},{... | collective-permute-start | bytes 776 | tf_op jit(solution)/shard_map/ppermute | solution.py:24
  16.4 3.6 %collective-permute-start.10 = (s32[64]{0:T(128)S(1)}, s32[64]{0:T(128)S(1)}, u32[]{:S(2)}, u32[]{:S(2)}) collective-permute-start(s32[64]{0:T(128)S(1)} %bitcast_add_fusion), channel_id=1, source_target_pairs={{0,8},{4,12},{8,0},{12,4},{16,24},{20,28},{24,16},{28,20},{1,9},{5... | collective-permute-start | bytes 776 | tf_op jit(solution)/shard_map/ppermute | solution.py:24
  16.9 3.6 %collective-permute-start.9 = (s32[64]{0:T(128)S(1)}, s32[64]{0:T(128)S(1)}, u32[]{:S(2)}, u32[]{:S(2)}) collective-permute-start(s32[64]{0:T(128)S(1)} %bitcast_add_fusion), channel_id=1, source_target_pairs={{0,4},{4,0},{8,12},{12,8},{16,20},{20,16},{24,28},{28,24},{1,5},{5... | collective-permute-start | bytes 776 | tf_op jit(solution)/shard_map/ppermute | solution.py:24
  17.1 13.3 %collective-permute-start.1 = (bf16[16,128,128]{2,1,0:T(8,128)(2,1)S(1)}, bf16[16,128,128]{2,1,0:T(8,128)(2,1)S(1)}, u32[]{:S(2)}, u32[]{:S(2)}) collective-permute-start(bf16[16,128,128]{2,1,0:T(8,128)(2,1)S(1)} %collective-permute-done.refs_11_), channel_id=1, source_target_pairs={{0,8},{1,5},{2,10},{3,7},{8,16},{9,1},{10,18},{11,3},{16,24},{17,9... | collective-permute-start | bytes 1572872 | tf_op jit(solution)/shard_map/ppermute | solution.py:360
  19.0 13.3 %collective-permute-start.5 = (bf16[16,128,128]{2,1,0:T(8,128)(2,1)S(1)}, bf16[16,128,128]{2,1,0:T(8,128)(2,1)S(1)}, u32[]{:S(2)}, u32[]{:S(2)}) collective-permute-start(bf16[16,128,128]{2,1,0:T(8,128)(2,1)S(1)} %collective-permute-done.4.refs_6_), channel_id=1, source_target_pairs={{0,4},{1,9},{2,6},{3,11},{8,0},{9,17},{10,2},{11,19},{16,8},{17,25... | collective-permute-start | bytes 1572872 | tf_op jit(solution)/shard_map/ppermute | solution.py:360
  20.5 11.9 %collective-permute-start.13 = (bf16[16,128,128]{2,1,0:T(8,128)(2,1)}, bf16[16,128,128]{2,1,0:T(8,128)(2,1)S(1)}, u32[]{:S(2)}, u32[]{:S(2)}) collective-permute-start(bf16[16,128,128]{2,1,0:T(8,128)(2,1)} %refs_2_), channel_id=1, source_target_pairs={{0,2},{1,3},{2,0},{3,1},{4,6},{5,7},{6,4},{7,5},{8,10},{9,11},{10,... | collective-permute-start | bytes 1572872 | tf_op jit(solution)/shard_map/ppermute | solution.py:24
  22.0 11.0 %collective-permute-start.12 = (s32[256]{0:T(256)S(1)}, s32[256]{0:T(256)S(1)}, u32[]{:S(2)}, u32[]{:S(2)}) collective-permute-start(s32[256]{0:T(256)S(1)} %pad_add_fusion.1), channel_id=1, source_target_pairs={{0,16},{4,20},{8,24},{12,28},{16,0},{20,4},{24,8},{28,12},{1,17},{... | collective-permute-start | bytes 3080 | tf_op jit(solution)/shard_map/ppermute | solution.py:24
  30.4 12.4 %collective-permute-start.2 = (bf16[16,128,128]{2,1,0:T(8,128)(2,1)S(1)}, bf16[16,128,128]{2,1,0:T(8,128)(2,1)S(1)}, u32[]{:S(2)}, u32[]{:S(2)}) collective-permute-start(bf16[16,128,128]{2,1,0:T(8,128)(2,1)S(1)} %collective-permute-done.1.refs_10_), channel_id=1, source_target_pairs={{0,8},{1,5},{2,10},{3,7},{8,16},{9,1},{10,18},{11,3},{16,24},{17,9... | collective-permute-start | bytes 1572872 | tf_op jit(solution)/shard_map/ppermute | solution.py:360
  32.2 10.6 %collective-permute-start.6 = (bf16[16,128,128]{2,1,0:T(8,128)(2,1)S(1)}, bf16[16,128,128]{2,1,0:T(8,128)(2,1)S(1)}, u32[]{:S(2)}, u32[]{:S(2)}) collective-permute-start(bf16[16,128,128]{2,1,0:T(8,128)(2,1)S(1)} %collective-permute-done.5.refs_7_), channel_id=1, source_target_pairs={{0,4},{1,9},{2,6},{3,11},{8,0},{9,17},{10,2},{11,19},{16,8},{17,25... | collective-permute-start | bytes 1572872 | tf_op jit(solution)/shard_map/ppermute | solution.py:360
  32.4 10.4 %collective-permute-start.14 = (bf16[16,128,128]{2,1,0:T(8,128)(2,1)S(1)}, bf16[16,128,128]{2,1,0:T(8,128)(2,1)S(1)}, u32[]{:S(2)}, u32[]{:S(2)}) collective-permute-start(bf16[16,128,128]{2,1,0:T(8,128)(2,1)S(1)} %collective-permute-done.13.refs_3_), channel_id=1, source_target_pairs={{0,1},{1,0},{2,3},{3,2},{4,5},{5,4},{6,7},{7,6},{8,9},{9,8},{10,11... | collective-permute-start | bytes 1572872 | tf_op jit(solution)/shard_map/ppermute | solution.py:24
  32.4 10.4 %collective-permute-start.15 = (bf16[16,128,128]{2,1,0:T(8,128)(2,1)S(1)}, bf16[16,128,128]{2,1,0:T(8,128)(2,1)S(1)}, u32[]{:S(2)}, u32[]{:S(2)}) collective-permute-start(bf16[16,128,128]{2,1,0:T(8,128)(2,1)S(1)} %collective-permute-done.4.refs_6_), channel_id=1, source_target_pairs={{0,1},{1,0},{2,3},{3,2},{4,5},{5,4},{6,7},{7,6},{8,9},{9,8},{10,11... | collective-permute-start | bytes 1572872 | tf_op jit(solution)/shard_map/ppermute | solution.py:24
  32.9 9.9 %collective-permute-start.16 = (bf16[16,128,128]{2,1,0:T(8,128)(2,1)S(1)}, bf16[16,128,128]{2,1,0:T(8,128)(2,1)S(1)}, u32[]{:S(2)}, u32[]{:S(2)}) collective-permute-start(bf16[16,128,128]{2,1,0:T(8,128)(2,1)S(1)} %collective-permute-done.refs_11_), channel_id=1, source_target_pairs={{0,1},{1,0},{2,3},{3,2},{4,5},{5,4},{6,7},{7,6},{8,9},{9,8},{10,11... | collective-permute-start | bytes 1572872 | tf_op jit(solution)/shard_map/ppermute | solution.py:24
  42.9 2.8 %collective-permute-start.18 = (bf16[16,128,128]{2,1,0:T(8,128)(2,1)S(1)}, bf16[16,128,128]{2,1,0:T(8,128)(2,1)S(1)}, u32[]{:S(2)}, u32[]{:S(2)}) collective-permute-start(bf16[16,128,128]{2,1,0:T(8,128)(2,1)S(1)} %collective-permute-done.5.refs_7_), channel_id=1, source_target_pairs={{0,1},{1,0},{2,3},{3,2},{4,5},{5,4},{6,7},{7,6},{8,9},{9,8},{10,11... | collective-permute-start | bytes 1572872 | tf_op jit(solution)/shard_map/ppermute | solution.py:24
  42.9 2.7 %collective-permute-start.21 = (bf16[16,128,128]{2,1,0:T(8,128)(2,1)S(1)}, bf16[16,128,128]{2,1,0:T(8,128)(2,1)S(1)}, u32[]{:S(2)}, u32[]{:S(2)}) collective-permute-start(bf16[16,128,128]{2,1,0:T(8,128)(2,1)S(1)} %collective-permute-done.1.refs_10_), channel_id=1, source_target_pairs={{0,1},{1,0},{2,3},{3,2},{4,5},{5,4},{6,7},{7,6},{8,9},{9,8},{10,11... | collective-permute-start | bytes 1572872 | tf_op jit(solution)/shard_map/ppermute | solution.py:24
  43.4 2.9 %collective-permute-start.19 = (bf16[16,128,128]{2,1,0:T(8,128)(2,1)S(1)}, bf16[16,128,128]{2,1,0:T(8,128)(2,1)S(1)}, u32[]{:S(2)}, u32[]{:S(2)}) collective-permute-start(bf16[16,128,128]{2,1,0:T(8,128)(2,1)S(1)} %collective-permute-done.6.refs_8_), channel_id=1, source_target_pairs={{0,1},{1,0},{2,3},{3,2},{4,5},{5,4},{6,7},{7,6},{8,9},{9,8},{10,11... | collective-permute-start | bytes 1572872 | tf_op jit(solution)/shard_map/ppermute | solution.py:24
  43.5 3.6 %collective-permute-start.20 = (bf16[16,128,128]{2,1,0:T(8,128)(2,1)S(1)}, bf16[16,128,128]{2,1,0:T(8,128)(2,1)S(1)}, u32[]{:S(2)}, u32[]{:S(2)}) collective-permute-start(bf16[16,128,128]{2,1,0:T(8,128)(2,1)S(1)} %collective-permute-done.2.refs_9_), channel_id=1, source_target_pairs={{0,1},{1,0},{2,3},{3,2},{4,5},{5,4},{6,7},{7,6},{8,9},{9,8},{10,11... | collective-permute-start | bytes 1572872 | tf_op jit(solution)/shard_map/ppermute | solution.py:24
  43.9 9.2 %collective-permute-start.17 = (bf16[16,128,128]{2,1,0:T(8,128)(2,1)S(1)}, bf16[16,128,128]{2,1,0:T(8,128)(2,1)S(1)}, u32[]{:S(2)}, u32[]{:S(2)}) collective-permute-start(bf16[16,128,128]{2,1,0:T(8,128)(2,1)S(1)} %collective-permute-done.2.refs_9_), channel_id=1, source_target_pairs={{0,8},{1,5},{2,10},{3,7},{8,16},{9,1},{10,18},{11,3},{16,24},{17,9... | collective-permute-start | bytes 1572872 | tf_op jit(solution)/shard_map/ppermute | solution.py:360
  53.1 2.1 %collective-permute-start.22 = (bf16[16,128,128]{2,1,0:T(8,128)(2,1)S(1)}, bf16[16,128,128]{2,1,0:T(8,128)(2,1)S(1)}, u32[]{:S(2)}, u32[]{:S(2)}) collective-permute-start(bf16[16,128,128]{2,1,0:T(8,128)(2,1)S(1)} %collective-permute-done.17.far0), channel_id=1, source_target_pairs={{0,1},{1,0},{2,3},{3,2},{4,5},{5,4},{6,7},{7,6},{8,9},{9,8},{10,11... | collective-permute-start | bytes 1572872 | tf_op jit(solution)/shard_map/ppermute | solution.py:24
  58.9 16.8 %collective-permute-start.23 = (bf16[2,2,2,1,1,336,128]{6,5,2,4,3,1,0:T(8,128)(2,1)S(1)}, bf16[2,2,2,1,1,336,128]{6,5,2,4,3,1,0:T(8,128)(2,1)S(1)}, u32[]{:S(2)}, u32[]{:S(2)}) collective-permute-start(bf16[2,2,2,1,1,336,128]{6,5,2,4,3,1,0:T(8,128)(2,1)S(1)} %bitcast.153), channel_id=1, source_target_pairs={{0,8},{1,3},{2,10},{3,1},{4,12},{5,7},{6,14},{7,5},{8,0},{9,11},{1... | collective-permute-start | bytes 2064392 | tf_op jit(solution)/shard_map/ppermute | solution.py:35
  60.3 17.0 %collective-permute-start.27 = (bf16[2,2,2,1,1,336,128]{6,5,2,4,3,1,0:T(8,128)(2,1)S(1)}, bf16[2,2,2,1,1,336,128]{6,5,2,4,3,1,0:T(8,128)(2,1)S(1)}, u32[]{:S(2)}, u32[]{:S(2)}) collective-permute-start(bf16[2,2,2,1,1,336,128]{6,5,2,4,3,1,0:T(8,128)(2,1)S(1)} %bitcast.152), channel_id=1, source_target_pairs={{0,2},{1,5},{2,0},{3,7},{4,6},{5,1},{6,4},{7,3},{8,10},{9,13},{10,... | collective-permute-start | bytes 2064392 | tf_op jit(solution)/shard_map/ppermute | solution.py:35
  62.1 18.3 %collective-permute-start.31 = (bf16[2,2,2,1,1,352,128]{6,5,2,4,3,1,0:T(8,128)(2,1)S(1)}, bf16[2,2,2,1,1,352,128]{6,5,2,4,3,1,0:T(8,128)(2,1)S(1)}, u32[]{:S(2)}, u32[]{:S(2)}) collective-permute-start(bf16[2,2,2,1,1,352,128]{6,5,2,4,3,1,0:T(8,128)(2,1)S(1)} %bitcast.151), channel_id=1, source_target_pairs={{0,4},{1,17},{2,6},{3,19},{4,0},{5,21},{6,2},{7,23},{8,12},{9,25},... | collective-permute-start | bytes 2162696 | tf_op jit(solution)/shard_map/ppermute | solution.py:35
  75.8 10.1 %collective-permute-start.24 = (bf16[2,2,1,1,336,128]{5,4,3,2,1,0:T(8,128)(2,1)S(1)}, bf16[2,2,1,1,336,128]{5,4,3,2,1,0:T(8,128)(2,1)S(1)}, u32[]{:S(2)}, u32[]{:S(2)}) collective-permute-start(bf16[2,2,1,1,336,128]{5,4,3,2,1,0:T(8,128)(2,1)S(1)} %get-tuple-element.73), channel_id=1, source_target_pairs={{0,2},{1,9},{2,0},{3,11},{4,6},{5,13},{6,4},{7,15},{8,10},{9,1},{1... | collective-permute-start | bytes 1032200 | tf_op jit(solution)/shard_map/ppermute | solution.py:35
  77.5 10.6 %collective-permute-start.28 = (bf16[2,2,1,1,336,128]{5,4,3,2,1,0:T(8,128)(2,1)S(1)}, bf16[2,2,1,1,336,128]{5,4,3,2,1,0:T(8,128)(2,1)S(1)}, u32[]{:S(2)}, u32[]{:S(2)}) collective-permute-start(bf16[2,2,1,1,336,128]{5,4,3,2,1,0:T(8,128)(2,1)S(1)} %get-tuple-element.75), channel_id=1, source_target_pairs={{0,4},{1,3},{2,6},{3,1},{4,0},{5,7},{6,2},{7,5},{8,12},{9,11},{10,... | collective-permute-start | bytes 1032200 | tf_op jit(solution)/shard_map/ppermute | solution.py:35
  80.5 7.8 %collective-permute-start.32 = (bf16[2,2,1,1,352,128]{5,4,1,0,3,2:T(8,128)(2,1)S(1)}, bf16[2,2,1,1,352,128]{5,4,1,0,3,2:T(8,128)(2,1)S(1)}, u32[]{:S(2)}, u32[]{:S(2)}) collective-permute-start(bf16[2,2,1,1,352,128]{5,4,1,0,3,2:T(8,128)(2,1)S(1)} %fusion.3), channel_id=1, source_target_pairs={{0,8},{1,3},{2,10},{3,1},{4,12},{5,7},{6,14},{7,5},{8,0},{9,11},{1... | collective-permute-start | bytes 1081352 | tf_op jit(solution)/shard_map/ppermute | solution.py:35
  86.0 12.7 %collective-permute-start.25 = (bf16[2,1,1,336,128]{4,3,2,1,0:T(8,128)(2,1)S(1)}, bf16[2,1,1,336,128]{4,3,2,1,0:T(8,128)(2,1)S(1)}, u32[]{:S(2)}, u32[]{:S(2)}) collective-permute-start(bf16[2,1,1,336,128]{4,3,2,1,0:T(8,128)(2,1)S(1)} %get-tuple-element.77), channel_id=1, source_target_pairs={{0,16},{1,5},{2,18},{3,7},{4,20},{5,1},{6,22},{7,3},{8,24},{9,13},... | collective-permute-start | bytes 516104 | tf_op jit(solution)/shard_map/ppermute | solution.py:35
  88.2 13.6 %collective-permute-start.29 = (bf16[2,1,1,336,128]{4,3,2,1,0:T(8,128)(2,1)S(1)}, bf16[2,1,1,336,128]{4,3,2,1,0:T(8,128)(2,1)S(1)}, u32[]{:S(2)}, u32[]{:S(2)}) collective-permute-start(bf16[2,1,1,336,128]{4,3,2,1,0:T(8,128)(2,1)S(1)} %get-tuple-element.79), channel_id=1, source_target_pairs={{0,8},{1,17},{2,10},{3,19},{4,12},{5,21},{6,14},{7,23},{8,0},{9,25... | collective-permute-start | bytes 516104 | tf_op jit(solution)/shard_map/ppermute | solution.py:35
  88.3 13.6 %collective-permute-start.33 = (bf16[2,1,1,352,128]{4,3,0,2,1:T(8,128)(2,1)S(1)}, bf16[2,1,1,352,128]{4,3,0,2,1:T(8,128)(2,1)S(1)}, u32[]{:S(2)}, u32[]{:S(2)}) collective-permute-start(bf16[2,1,1,352,128]{4,3,0,2,1:T(8,128)(2,1)S(1)} %fusion.15), channel_id=1, source_target_pairs={{0,2},{1,5},{2,0},{3,7},{4,6},{5,1},{6,4},{7,3},{8,10},{9,13},{10,... | collective-permute-start | bytes 540680 | tf_op jit(solution)/shard_map/ppermute | solution.py:35
  98.7 6.2 %collective-permute-start.26 = (bf16[1,1,336,128]{3,2,1,0:T(8,128)(2,1)S(1)}, bf16[1,1,336,128]{3,2,1,0:T(8,128)(2,1)S(1)}, u32[]{:S(2)}, u32[]{:S(2)}) collective-permute-start(bf16[1,1,336,128]{3,2,1,0:T(8,128)(2,1)S(1)} %fusion.34), channel_id=1, source_target_pairs={{0,4},{1,17},{2,6},{3,19},{4,0},{5,21},{6,2},{7,23},{8,12},{9,25},... | collective-permute-start | bytes 258056 | tf_op jit(solution)/shard_map/ppermute | solution.py:35
  101.8 6.2 %collective-permute-start.30 = (bf16[1,1,336,128]{3,2,1,0:T(8,128)(2,1)S(1)}, bf16[1,1,336,128]{3,2,1,0:T(8,128)(2,1)S(1)}, u32[]{:S(2)}, u32[]{:S(2)}) collective-permute-start(bf16[1,1,336,128]{3,2,1,0:T(8,128)(2,1)S(1)} %fusion.35), channel_id=1, source_target_pairs={{0,16},{1,9},{2,18},{3,11},{4,20},{5,13},{6,22},{7,15},{8,24},{9,1... | collective-permute-start | bytes 258056 | tf_op jit(solution)/shard_map/ppermute | solution.py:35
  101.9 7.1 %collective-permute-start.34 = (bf16[1,1,352,128]{3,2,1,0:T(8,128)(2,1)S(1)}, bf16[1,1,352,128]{3,2,1,0:T(8,128)(2,1)S(1)}, u32[]{:S(2)}, u32[]{:S(2)}) collective-permute-start(bf16[1,1,352,128]{3,2,1,0:T(8,128)(2,1)S(1)} %fusion.33), channel_id=1, source_target_pairs={{0,16},{1,9},{2,18},{3,11},{4,20},{5,13},{6,22},{7,15},{8,24},{9,1... | collective-permute-start | bytes 270344 | tf_op jit(solution)/shard_map/ppermute | solution.py:35

commit v5 on v4

--- a/solution.py
+++ b/solution.py
@@ -11,6 +11,7 @@
 
 OWN = 2
 UNROLL = 8
+LOOK_BITS = 12
 ORDERS = (("1x2y", "x1y2"), ("xy12", "yx21"), ("y1x2", "2xy1"))
 LINKS = {"x": ("col", 2), "y": ("row", 1), "1": ("row", 2), "2": ("row", 4)}
 
@@ -69,7 +70,13 @@
     return (entry >> shift) & mask
 
 
-def plan_kernel(s, cols_ref, aggs_ref, plan_ref, starts_ref, info, counts):
+def column_part(s, j_agg, col):
+    rel_col = (j_agg >> log2(s.width)) ^ col
+    part = ((rel_col >> 1) << log2(s.per)) + (j_agg & (s.width - 1))
+    return (rel_col & 1) == 0, part << s.fields[2][0]
+
+
+def plan_kernel(s, cols_ref, aggs_ref, near_ref, late_ref, meta_ref, info, counts):
     row = lax.axis_index("row")
     col = lax.axis_index("col")
 
@@ -80,56 +87,65 @@
     for b in range(s.buckets):
         counts[b] = 0
 
-    def blank(k, carry):
-        plan_ref[k] = -1
-        return carry
-
-    lax.fori_loop(0, s.slots + 1, blank, 0, unroll=8)
-
     def sort(i, carry):
+        n_near, n_late = carry
         tile = i & (s.slab - 1)
         side = i >> log2(s.slab)
         other = cols_ref[i]
-        other_row = other >> log2(s.slab)
         i_agg = aggs_ref[tile]
-        j_agg = aggs_ref[((other_row ^ row) << log2(s.slab)) + (other & (s.slab - 1))]
-        rel_col = (j_agg >> log2(s.width)) ^ col
         rel_row = (i_agg >> log2(OWN)) ^ row
-        turn = ring_place(other_row) - here
+        turn = ring_place(other >> log2(s.slab)) - here
+        mine = jnp.where((col & 1) == 0, turn, -turn) & (s.rows - 1)
         away = jnp.where(((col ^ side) & 1) == 0, turn, -turn) & (s.rows - 1)
         late = jnp.where(away == s.half, 1, 0)
         order = away - jnp.where(away > s.half, 1, 0) + side * s.early
         piece = jnp.where(late == 1, side, order)
         panel_at = (piece << log2(s.tiles)) + (other & (s.tiles - 1))
-        cell = (rel_row & 7) * (s.cols // 2) + (rel_col >> 1)
-        cell = (cell << log2(OWN)) + (i_agg & (OWN - 1))
-        cell = (cell << log2(s.width)) + (j_agg & (s.width - 1))
+        cell = ((rel_row & 7) << (log2(s.cols // 2) + log2(s.per))) + (
+            (i_agg & (OWN - 1)) << log2(s.width)
+        )
+        entry = i + (panel_at << s.fields[1][0]) + (cell << s.fields[2][0])
+        slab_at = mine - jnp.where(mine > s.half, 1, 0)
+        look = jnp.where(late == 1, 0, slab_at << log2(s.slab)) + (other & (s.slab - 1))
+        look = look + ((rel_row >> 3) << LOOK_BITS)
         bucket = (rel_row >> 3) * 2 + late
-        mine = (rel_col & 1) == 0
+        counts[bucket] = counts[bucket] + 1
+        near_ref[n_near * 2] = entry
+        near_ref[n_near * 2 + 1] = look
+        info[n_late * 2] = entry
+        info[n_late * 2 + 1] = look
+        return n_near + 1 - late, n_late + late
+
+    zero = jnp.int32(0)
+    n_near, n_late = lax.fori_loop(0, s.pairs, sort, (zero, zero), unroll=4)
+    for u in range(4):
+        near_ref[(n_near + u) * 2] = 0
+        near_ref[(n_near + u) * 2 + 1] = 0
+
+    start = zero
+    for b in range(s.buckets):
+        meta_ref[b] = start
+        start = start + ((counts[b] + UNROLL - 1) & ~(UNROLL - 1))
+    meta_ref[s.buckets] = start
+    meta_ref[s.buckets + 1] = n_near
+    for hi in range(s.his):
+        meta_ref[s.buckets + 2 + hi] = counts[2 * hi + 1]
+        for u in range(UNROLL):
+            at = meta_ref[2 * hi + 1] + counts[2 * hi + 1] + u
+            late_ref[jnp.where(at < meta_ref[2 * hi + 2], at, s.slots) * 2] = 0
+        counts[2 * hi + 1] = 0
+
+    def place(n, carry):
+        look = info[n * 2 + 1]
+        bucket = (look >> LOOK_BITS) * 2 + 1
         rank = counts[bucket]
-        counts[bucket] = rank + jnp.where(mine, 1, 0)
-        info[i * 2] = jnp.where(mine, rank * s.buckets + bucket, -1)
-        entry = i
-        for k, value in enumerate((panel_at, cell)):
-            entry = entry + (value << s.fields[k + 1][0])
-        info[i * 2 + 1] = entry
+        counts[bucket] = rank + 1
+        slot = meta_ref[bucket] + rank
+        late_ref[slot * 2] = info[n * 2]
+        late_ref[slot * 2 + 1] = look & ((1 << LOOK_BITS) - 1)
         return carry
 
-    lax.fori_loop(0, s.pairs, sort, 0, unroll=4)
-
-    start = jnp.int32(0)
-    for b in range(s.buckets):
-        starts_ref[b] = start
-        start = start + ((counts[b] + UNROLL - 1) & ~(UNROLL - 1))
-    starts_ref[s.buckets] = start
-
-    def place(i, carry):
-        key = info[i * 2]
-        slot = starts_ref[key & (s.buckets - 1)] + (key >> log2(s.buckets))
-        plan_ref[jnp.where(key >= 0, slot, s.slots)] = info[i * 2 + 1]
-        return carry
-
-    lax.fori_loop(0, s.pairs, place, 0, unroll=4)
+    lax.fori_loop(0, n_late, place, 0)
 
 
 def room(*shapes):
@@ -139,14 +155,12 @@
 
 def make_plan(s, cols, aggs):
     smem = pl.BlockSpec(memory_space=pltpu.SMEM)
+    counts = (s.pairs * 2 + 8, (s.slots + 1) * 2, s.buckets + 2 + s.his)
     return pl.pallas_call(
         functools.partial(plan_kernel, s),
         in_specs=[smem, smem],
-        out_specs=[smem, smem],
-        out_shape=[
-            jax.ShapeDtypeStruct((s.slots + 1,), jnp.int32),
-            jax.ShapeDtypeStruct((s.buckets + 1,), jnp.int32),
-        ],
+        out_specs=[smem, smem, smem],
+        out_shape=[jax.ShapeDtypeStruct((count,), jnp.int32) for count in counts],
         scratch_shapes=[
             pltpu.SMEM((s.pairs * 2,), jnp.int32),
             pltpu.SMEM((s.buckets,), jnp.int32),
@@ -156,44 +170,67 @@
     )(cols, aggs)
 
 
-def product_kernel(s, plan_ref, starts_ref, *refs):
-    slots_ref, rows_ref, a_buf, panel, rows_buf, sems = refs[-6:]
+def product_kernel(s, near_ref, late_ref, meta_ref, aggs_ref, *refs):
+    slots_ref, rows_ref, plan_ref, counts, a_buf, rows_buf, panel, sems = refs[-8:]
+    high = s.tiles * s.side
     copies = []
     for k in range(2):
         copies.append((refs[k], a_buf.at[pl.ds(k * s.slab, s.slab)]))
     for k in range(s.cols):
-        copies.append((refs[2 + k], rows_buf.at[pl.ds(k * s.tiles, s.tiles)]))
+        copies.append((refs[2 + k], rows_buf.at[pl.ds(k * high, high)]))
     for k in range(2 * s.early):
         source = refs[2] if k == 0 else refs[1 + s.cols + k]
-        copies.append((source, panel.at[pl.ds(k * s.tiles, s.tiles)]))
+        copies.append((source.at[pl.ds(0, high)], panel.at[pl.ds(k * high, high)]))
     copies = [pltpu.make_async_copy(src, dst, sems.at[k]) for k, (src, dst) in enumerate(copies)]
     for copy in copies:
         copy.start()
+
+    col = lax.axis_index("col")
+    for hi in range(s.his):
+        counts[hi] = 0
+    n_near = meta_ref[s.buckets + 1]
+
+    def pick(step, carry):
+        for n in range(4):
+            n = step * 4 + n
+            look = near_ref[n * 2 + 1]
+            hi = look >> LOOK_BITS
+            mine, part = column_part(s, aggs_ref[look & ((1 << LOOK_BITS) - 1)], col)
+            mine = mine & (n < n_near)
+            rank = counts[hi]
+            counts[hi] = rank + jnp.where(mine, 1, 0)
+            plan_ref[jnp.where(mine, meta_ref[2 * hi] + rank, s.slots)] = near_ref[n * 2] + part
+        return carry
+
+    lax.fori_loop(0, pl.cdiv(n_near, 4), pick, 0)
+    for hi in range(s.his):
+        for u in range(UNROLL):
+            at = meta_ref[2 * hi] + counts[hi] + u
+            plan_ref[jnp.where(at < meta_ref[2 * hi + 1], at, s.slots)] = -1
     for copy in copies:
         copy.wait()
-
-    col = lax.axis_index("col")
 
     def turn(k, carry):
         part = k >> log2(s.tiles)
         rel = (part & (s.cols // 2 - 1)) * 2 + (part >> log2(s.cols // 2))
-        rows_ref[((rel ^ col) << log2(s.tiles)) + (k & (s.tiles - 1))] = rows_buf[k].T
+        at = pl.ds(pl.multiple_of(k * s.side, s.side), s.side)
+        rows_ref[((rel ^ col) << log2(s.tiles)) + (k & (s.tiles - 1))] = rows_buf[at, :].T
         return carry
 
     lax.fori_loop(0, s.slab, turn, 0, unroll=4)
 
     for hi in range(s.his):
-        begin = starts_ref[2 * hi] // UNROLL
-        middle = starts_ref[2 * hi + 1] // UNROLL
-        end = starts_ref[2 * hi + 2] // UNROLL
+        begin = meta_ref[2 * hi] // UNROLL
+        middle = pl.cdiv(meta_ref[2 * hi] + counts[hi], UNROLL)
 
         def near(group, carry):
             for u in range(UNROLL):
                 n = group * UNROLL + u
                 entry = jnp.maximum(plan_ref[n], 0)
+                at = pl.multiple_of(field(s, entry, 1) * s.side, s.side)
                 slots_ref[n] = jnp.dot(
                     a_buf[field(s, entry, 0)],
-                    panel[field(s, entry, 1)],
+                    panel[pl.ds(at, s.side), :],
                     preferred_element_type=jnp.float32,
                 ).astype(jnp.bfloat16)
             return carry
@@ -201,45 +238,48 @@
         def far(group, carry):
             for u in range(UNROLL):
                 n = group * UNROLL + u
-                slots_ref[n] = a_buf[field(s, jnp.maximum(plan_ref[n], 0), 0)]
+                slots_ref[n] = a_buf[field(s, late_ref[n * 2], 0)]
             return carry
 
         lax.fori_loop(begin, middle, near, 0)
-        lax.fori_loop(middle, end, far, 0)
-
-
-def make_products(s, plan, starts, a_own, a_other, near, rows):
+        lax.fori_loop(meta_ref[2 * hi + 1] // UNROLL, meta_ref[2 * hi + 2] // UNROLL, far, 0)
+
+
+def make_products(s, plan, aggs, a_own, a_other, near, rows):
     smem = pl.BlockSpec(memory_space=pltpu.SMEM)
     vmem = pl.BlockSpec(memory_space=pltpu.VMEM)
+    hbm = pl.BlockSpec(memory_space=pltpu.HBM)
     anywhere = pl.BlockSpec(memory_space=pl.ANY)
-    shapes = [
-        ((count, s.side, s.side), jnp.bfloat16)
-        for count in (s.slots, s.slab, s.pairs, s.near, s.slab)
-    ]
-    hbm = pl.BlockSpec(memory_space=pltpu.HBM)
+    block = (s.side, s.side)
+    shapes = [((count,) + block, jnp.bfloat16) for count in (s.slots, s.slab, s.pairs)]
+    shapes += [((count * s.side, s.side), jnp.bfloat16) for count in (s.slab, s.near)]
     a_own, own = (pltpu.with_memory_space_constraint(x, pltpu.HBM) for x in (a_own, rows[0]))
     operands = [a_own, a_other, own, *rows[1:], *near[1:]]
     return pl.pallas_call(
         functools.partial(product_kernel, s),
-        in_specs=[smem, smem, hbm, anywhere, hbm] + [anywhere] * (len(operands) - 3),
-        out_specs=[vmem, vmem],
-        out_shape=[jax.ShapeDtypeStruct(*shape) for shape in shapes[:2]],
+        in_specs=[smem] * 4 + [hbm, anywhere, hbm] + [anywhere] * (len(operands) - 3),
+        out_specs=[vmem, vmem, smem, smem],
+        out_shape=[jax.ShapeDtypeStruct(*shape) for shape in shapes[:2]]
+        + [jax.ShapeDtypeStruct((count,), jnp.int32) for count in (s.slots + 1, s.his)],
         scratch_shapes=[pltpu.VMEM(*shape) for shape in shapes[2:]]
         + [pltpu.SemaphoreType.DMA((len(operands) + 1,))],
         compiler_params=pltpu.CompilerParams(vmem_limit_bytes=room(*shapes)),
         cost_estimate=pl.CostEstimate(
             flops=s.pairs * s.side**3, bytes_accessed=1 << 20, transcendentals=0
         ),
-    )(plan, starts, *operands)
+    )(*plan, aggs, *operands)
 
 
 def sum_kernel(
-    s, plan_ref, starts_ref, slots_ref, rows_ref, far0, far1,
-    send0, keep0, send1, keep1, send2, keep2, total, far_buf, sems,
+    s, plan_ref, counts, late_ref, meta_ref, aggs_ref, slots_ref, rows_ref, far0, far1,
+    send0, keep0, send1, keep1, send2, keep2, total, far_buf, picked, sems,
 ):
     hi = pl.program_id(0)
+    high = s.tiles * s.side
     copies = [
-        pltpu.make_async_copy(ref, far_buf.at[pl.ds(k * s.tiles, s.tiles)], sems.at[k])
+        pltpu.make_async_copy(
+            ref.at[pl.ds(0, high)], far_buf.at[pl.ds(k * high, high)], sems.at[k]
+        )
         for k, ref in enumerate((far0, far1))
     ]
 
@@ -254,8 +294,7 @@
 
     lax.fori_loop(0, s.blocks, clear, 0)
 
-    def add(n, product):
-        entry = plan_ref[n]
+    def add(entry, product):
         known = jnp.maximum(entry, 0)
         term = jnp.dot(
             rows_ref[known & (s.slab - 1)], product, preferred_element_type=jnp.float32
@@ -267,28 +306,43 @@
     def near(group, carry):
         for u in range(UNROLL):
             n = group * UNROLL + u
-            add(n, slots_ref[n])
+            add(plan_ref[n], slots_ref[n])
         return carry
 
-    def far(group, carry):
-        for u in range(UNROLL):
-            n = group * UNROLL + u
-            piece = far_buf[field(s, jnp.maximum(plan_ref[n], 0), 1)]
-            product = jnp.dot(slots_ref[n], piece, preferred_element_type=jnp.float32)
-            add(n, product.astype(jnp.bfloat16))
-        return carry
-
-    begin = starts_ref[2 * hi] // UNROLL
-    middle = starts_ref[2 * hi + 1] // UNROLL
-    end = starts_ref[2 * hi + 2] // UNROLL
-    lax.fori_loop(begin, middle, near, 0)
+    begin = meta_ref[2 * hi]
+    lax.fori_loop(begin // UNROLL, pl.cdiv(begin + counts[hi], UNROLL), near, 0)
+
+    col = lax.axis_index("col")
+    first = meta_ref[2 * hi + 1]
+
+    def pick(n, n_mine):
+        slot = first + n
+        mine, part = column_part(s, aggs_ref[late_ref[slot * 2 + 1]], col)
+        picked[n_mine * 2] = slot
+        picked[n_mine * 2 + 1] = late_ref[slot * 2] + part
+        return n_mine + jnp.where(mine, 1, 0)
+
+    n_mine = lax.fori_loop(0, meta_ref[s.buckets + 2 + hi], pick, jnp.int32(0))
+    for u in range(UNROLL):
+        picked[(n_mine + u) * 2] = 0
+        picked[(n_mine + u) * 2 + 1] = -1
 
     @pl.when(hi == 0)
     def _():
         for copy in copies:
             copy.wait()
 
-    lax.fori_loop(middle, end, far, 0)
+    def far(group, carry):
+        for u in range(UNROLL):
+            n = group * UNROLL + u
+            slot, entry = picked[n * 2], picked[n * 2 + 1]
+            at = field(s, jnp.maximum(entry, 0), 1) * s.side
+            piece = far_buf[pl.ds(pl.multiple_of(at, s.side), s.side), :]
+            product = jnp.dot(slots_ref[slot], piece, preferred_element_type=jnp.float32)
+            add(entry, product.astype(jnp.bfloat16))
+        return carry
+
+    lax.fori_loop(0, pl.cdiv(n_mine, UNROLL), far, 0)
 
     half = s.cols // 2
     weight = {"x": 1, "y": half, "1": 2 * half, "2": 4 * half}
@@ -308,7 +362,7 @@
                     keep[(*bits[1:], 0, x)] = part
 
 
-def make_sums(s, plan, starts, slots, rows_t, far):
+def make_sums(s, lists, slots, rows_t, far):
     smem = pl.BlockSpec(memory_space=pltpu.SMEM)
     vmem = pl.BlockSpec(memory_space=pltpu.VMEM)
     anywhere = pl.BlockSpec(memory_space=pl.ANY)
@@ -328,19 +382,20 @@
     return pl.pallas_call(
         functools.partial(sum_kernel, s),
         grid=(s.his,),
-        in_specs=[smem, smem, vmem, vmem, anywhere, anywhere],
+        in_specs=[smem] * 5 + [vmem, vmem, anywhere, anywhere],
         out_specs=out_specs,
         out_shape=out_shape,
         scratch_shapes=[
             pltpu.VMEM((s.blocks, s.tall, s.side), jnp.float32),
-            pltpu.VMEM((2 * s.tiles, s.side, s.side), jnp.bfloat16),
+            pltpu.VMEM((2 * s.tiles * s.side, s.side), jnp.bfloat16),
+            pltpu.SMEM(((s.pairs + UNROLL) * 2,), jnp.int32),
             pltpu.SemaphoreType.DMA((2,)),
         ],
         compiler_params=pltpu.CompilerParams(vmem_limit_bytes=room(*shapes)),
         cost_estimate=pl.CostEstimate(
             flops=s.pairs * s.side**3, bytes_accessed=16 << 20, transcendentals=0
         ),
-    )(plan, starts, slots, rows_t, *far)
+    )(*lists, slots, rows_t, *far)
 
 
 def shards(a_blocks, p_tiles, owner, agg_local, a_cols):
@@ -359,30 +414,32 @@
                 moves.append((order[k] * s.cols + c, to * s.cols + c))
         return lax.ppermute(value, ("row", "col"), moves)
 
-    first = ring(p_tiles, 0)
+    high = s.tiles * s.side
+    aggs = owner[:, 0] * OWN + agg_local
+    label = jnp.pad(aggs.astype(jnp.bfloat16)[None], ((0, 15), (0, s.side - s.slab)))
+    mine = p_tiles.reshape(high, s.side)
+    labelled = jnp.concatenate([mine, label], 0)
+
+    def labels(piece):
+        return piece[high, :s.slab].astype(jnp.int32)
+
+    first = ring(labelled, 0)
     cols = a_cols[:, 0]
     cols_other = swap(cols, "col", 1)
-    cols_other, mine = barrier((cols_other, p_tiles))
-    second = ring(mine, 1)
-    a_other, p_other = swap(a_blocks[:, 0], "col", 1), swap(p_tiles, "col", 1)
-
-    aggs = owner[:, 0] * OWN + agg_local
-    came, aggs, a_other, p_other = barrier((first, aggs, a_other, p_other))
+    cols_other, labelled = barrier((cols_other, labelled))
+    second = ring(labelled, 1)
+    a_other, p_other = swap(a_blocks[:, 0], "col", 1), swap(mine, "col", 1)
+    plan = make_plan(s, jnp.concatenate([cols, cols_other], 0), aggs)
+
+    came, a_other, p_other, mine = barrier((first, a_other, p_other, mine))
     first = ring(first, 0)
-    aggs = [aggs] + [swap(aggs, "row", mask) for mask in (1, 2, 3)]
-    own_near, other_near = {0: p_tiles, s.rows - 1: came, 1: second}, {0: p_other}
+    own_near, other_near = {0: labelled, s.rows - 1: came, 1: second}, {0: p_other}
     second = ring(second, 1)
-    aggs, mine = barrier((jnp.concatenate(aggs, 0), p_tiles))
-    bit = 4
-    while bit < s.rows:
-        aggs = jnp.concatenate([aggs, swap(aggs, "row", bit)], 0)
-        bit *= 2
     rows = [mine]
     bit = 2
     while bit < s.cols:
         rows += [swap(piece, "col", bit) for piece in rows]
         bit *= 2
-    plan, starts = make_plan(s, jnp.concatenate([cols, cols_other], 0), aggs)
 
     held = [1, s.rows - 1]
     for step in range(2, s.half - 1):
@@ -396,11 +453,10 @@
         held = [step, s.rows - step]
 
     others = sorted(set(other_near) - {0})
-    tie = (first, second, plan, starts, *rows[s.cols // 2 + 1:])
+    tie = (first, second, *plan)
     tie += (*(own_near[away] for away in held), *(other_near[away] for away in others))
-    first, second, plan, starts, *rest = barrier(tie)
-    rows[s.cols // 2 + 1:] = rest[:s.cols // 2 - 1]
-    rest = rest[s.cols // 2 - 1:]
+    first, second, *rest = barrier(tie)
+    plan, rest = rest[:len(plan)], rest[len(plan):]
     for away, piece in zip(others, rest[len(held):]):
         other_near[away] = piece
     far = ring(first, 0)
@@ -410,11 +466,15 @@
     for away in (s.half + 1, s.half - 1):
         other_near[away] = swap(own_near[away], "col", 1)
     near = [own_near[k] for k in sorted(own_near)]
+    near_aggs = jnp.concatenate([labels(piece) for piece in near], 0)
     near += [other_near[k] for k in sorted(other_near)]
-    slots, rows_t = make_products(s, plan, starts, a_blocks[:, 0], a_other, near, rows)
+    slots, rows_t, picks, counts = make_products(
+        s, plan, near_aggs, a_blocks[:, 0], a_other, near, rows
+    )
     far, slots, rows_t = barrier((far, slots, rows_t))
     far_other = swap(far, "col", 1)
-    parts = make_sums(s, plan, starts, slots, rows_t, [far, far_other])
+    lists = (picks, counts, plan[1], plan[2], labels(far))
+    parts = make_sums(s, lists, slots, rows_t, [far, far_other])
 
     sends, keeps = list(parts[0::2]), list(parts[1::2])
     groups = range(len(ORDERS))

time: 110 us -> 126 us (1.15)
  local copies, waits for them, and re-layouts: 0 us -> 13.2 us
  starting transfers between devices: 43.5 us -> 41.1 us
  other arithmetic: 3.19 us -> 4.82 us
  Pallas kernels: 13.9 us -> 15.5 us
  waiting for transfers between devices: 49.1 us -> 50.5 us
    unnamed x0 -> x24, local copies, waits for them, and re-layouts: none -> 11.1 us
    ppermute x7, waiting for transfers between devices: 15.9 us -> 24.5 us  [ring(): return lax.ppermute(value, ('row', 'col'), moves)]
    ppermute x16 -> x12, starting transfers between devices: 10.6 us -> 4.41 us  [swap(): return lax.ppermute(value, axis, [(i, i ^ bit) for i in range(size)])]
    ppermute x16 -> x12, waiting for transfers between devices: 5.28 us -> 1.11 us  [swap(): return lax.ppermute(value, axis, [(i, i ^ bit) for i in range(size)])]
    ppermute x12, starting transfers between devices: 21.3 us -> 24.6 us  [exchange(): return lax.ppermute(value, ('row', 'col'), moves)]
    ppermute x12, waiting for transfers between devices: 27.9 us -> 24.9 us  [exchange(): return lax.ppermute(value, ('row', 'col'), moves)]
    convert_element_type x0 -> x6, local copies, waits for them, and re-layouts: none -> 2.02 us  [labels(): return piece[high, :s.slab].astype(jnp.int32)]
    pallas_call x1, Pallas kernels: 5.67 us -> 7.46 us  [make_products(): pl.pallas_call(functools.partial(product_kernel, s), in_specs=[smem] * 4...]
  transfers between devices with their start and end apart: 35 -> 31, of which waited for: 16 -> 9; matrix products, arithmetic and copies ran while one was open for 2% -> 5% of each run, Pallas kernels for 9% -> 9%
where the time goes in v5:
time: 126 us; the launch traced here: 125 us
  waiting for transfers between devices  50.5 us (40%)
  starting transfers between devices  41.1 us (33%)
  Pallas kernels  15.5 us (12%)
  local copies, waits for them, and re-layouts  13.2 us (10%)
  other arithmetic  4.82 us (4%)
    ppermute x12, waiting for transfers between devices, exchange(): return lax.ppermute(value, ('row', 'col'), moves)  24.9 us
    ppermute x12, starting transfers between devices, exchange(): return lax.ppermute(value, ('row', 'col'), moves)  24.6 us
    ppermute x7, waiting for transfers between devices, ring(): return lax.ppermute(value, ('row', 'col'), moves)  24.5 us
    ppermute x7, starting transfers between devices, ring(): return lax.ppermute(value, ('row', 'col'), moves)  12.1 us
    unnamed x24, local copies, waits for them, and re-layouts  11.1 us
    pallas_call x1, Pallas kernels, make_products(): pl.pallas_call(functools.partial(product_kernel, s), in_specs=[smem] * 4...  7.46 us
    ppermute x12, starting transfers between devices, swap(): return lax.ppermute(value, axis, [(i, i ^ bit) for i in range(size)])  4.41 us
    pallas_call x1, Pallas kernels, make_plan(): pl.pallas_call(functools.partial(plan_kernel, s), in_specs=[smem, smem],...  4.09 us
  transfers between devices with their start and end apart: 31, of which 9 were waited for; matrix products, arithmetic and copies ran while one was open for 5% of the time, Pallas kernels for 9%

profile of v5, /device:TPU:0, one launch (start us, length us, event | category | flops | bytes accessed | tf_op | source)
XLA Modules:
  0.0 125.3 jit_solution(7364560463378878141)
XLA Ops:
  0.5 0.7 convert_bitcast_fusion
  1.2 1.1 fusion.4
  2.3 3.1 %collective-permute-start = (bf16[2064,128]{1,0:T(8,128)(2,1)S(1)}, bf16[2064,128]{1,0:T(8,128)(2,1)S(1)}, u32[]{:S(2)}, u32[]{:S(2)}) collective-permute-start(bf16[2064,128]{1,0:T(8,128)(2,1)S(1)} %fusion.4), channel_id=1, source_target_pairs={{0,8},{1,5},{2,10},{3,7},{8,16},{9,1},{10,18},{11,3},{16,24},{17,9... | collective-permute-start | bytes 1585160 | tf_op jit(solution)/shard_map/ppermute | solution.py:415
  5.3 2.0 %collective-permute-start.4 = (bf16[2064,128]{1,0:T(8,128)(2,1)S(1)}, bf16[2064,128]{1,0:T(8,128)(2,1)S(1)}, u32[]{:S(2)}, u32[]{:S(2)}) collective-permute-start(bf16[2064,128]{1,0:T(8,128)(2,1)S(1)} %fusion.4), channel_id=1, source_target_pairs={{0,4},{1,9},{2,6},{3,11},{8,0},{9,17},{10,2},{11,19},{16,8},{17,25... | collective-permute-start | bytes 1585160 | tf_op jit(solution)/shard_map/ppermute | solution.py:415
  7.3 9.2 %collective-permute-done.refs_11_ = bf16[2064,128]{1,0:T(8,128)(2,1)S(1)} collective-permute-done((bf16[2064,128]{1,0:T(8,128)(2,1)S(1)}, bf16[2064,128]{1,0:T(8,128)(2,1)S(1)}, u32[]{:S(2)}, u32[]{:S(2)}) %collective-permute-start) | collective-permute-done | bytes 528416 | tf_op jit(solution)/shard_map/ppermute | solution.py:415
  16.6 2.4 %collective-permute-start.1 = (bf16[2064,128]{1,0:T(8,128)(2,1)S(1)}, bf16[2064,128]{1,0:T(8,128)(2,1)}, u32[]{:S(2)}, u32[]{:S(2)}) collective-permute-start(bf16[2064,128]{1,0:T(8,128)(2,1)S(1)} %collective-permute-done.refs_11_), channel_id=1, source_target_pairs={{0,8},{1,5},{2,10},{3,7},{8,16},{9,1},{10,18},{11,3},{16,24},{17,9... | collective-permute-start | bytes 1585160 | tf_op jit(solution)/shard_map/ppermute | solution.py:415
  19.5 1.5 %collective-permute-start.9 = (bf16[2048,128]{1,0:T(8,128)(2,1)}, bf16[2048,128]{1,0:T(8,128)(2,1)S(1)}, u32[]{:S(2)}, u32[]{:S(2)}) collective-permute-start(bf16[2048,128]{1,0:T(8,128)(2,1)} %bitcast.179), channel_id=1, source_target_pairs={{0,2},{1,3},{2,0},{3,1},{4,6},{5,7},{6,4},{7,5},{8,10},{9,11},{10,... | collective-permute-start | bytes 1572872 | tf_op jit(solution)/shard_map/ppermute | solution.py:25
  21.0 10.6 %collective-permute-done.1.refs_10_ = bf16[2064,128]{1,0:T(8,128)(2,1)} collective-permute-done((bf16[2064,128]{1,0:T(8,128)(2,1)S(1)}, bf16[2064,128]{1,0:T(8,128)(2,1)}, u32[]{:S(2)}, u32[]{:S(2)}) %collective-permute-start.1) | collective-permute-done | bytes 528416 | tf_op jit(solution)/shard_map/ppermute | solution.py:415
  31.6 2.3 %collective-permute-start.2 = (bf16[2064,128]{1,0:T(8,128)(2,1)}, bf16[2064,128]{1,0:T(8,128)(2,1)S(1)}, u32[]{:S(2)}, u32[]{:S(2)}) collective-permute-start(bf16[2064,128]{1,0:T(8,128)(2,1)} %collective-permute-done.1.refs_10_), channel_id=1, source_target_pairs={{0,8},{1,5},{2,10},{3,7},{8,16},{9,1},{10,18},{11,3},{16,24},{17,9... | collective-permute-start | bytes 1585160 | tf_op jit(solution)/shard_map/ppermute | solution.py:415
  34.5 0.8 copy-done.8
  35.3 0.7 pad_add_fusion.cols_ref
  36.1 4.1 %shard_map.55 = (s32[264]{0:T(512)S(1)}, s32[290]{0:T(512)S(1)}, s32[5]{0:T(128)S(1)}) custom-call(s32[128]{0:T(128)S(1)} %pad_add_fusion.cols_ref, s32[64]{0:T(128)S(1)} %get-tuple-element.76.aggs_ref), custom_call_target="tpu_custom_call" | custom-call | flops 1048576 | bytes 16777216 | tf_op jit(solution)/shard_map/pallas_call | solution.py:159
  40.2 0.8 copy-done.2
  41.0 0.7 slice_bitcast_fusion.13
  41.6 4.7 %collective-permute-done.2.refs_9_ = bf16[2064,128]{1,0:T(8,128)(2,1)S(1)} collective-permute-done((bf16[2064,128]{1,0:T(8,128)(2,1)}, bf16[2064,128]{1,0:T(8,128)(2,1)S(1)}, u32[]{:S(2)}, u32[]{:S(2)}) %collective-permute-start.2) | collective-permute-done | bytes 528416 | tf_op jit(solution)/shard_map/ppermute | solution.py:415
  46.3 0.8 copy-done.4
  47.1 0.8 copy-done.6
  48.0 1.8 %collective-permute-start.17 = (bf16[2064,128]{1,0:T(8,128)(2,1)S(1)}, bf16[2064,128]{1,0:T(8,128)(2,1)}, u32[]{:S(2)}, u32[]{:S(2)}) collective-permute-start(bf16[2064,128]{1,0:T(8,128)(2,1)S(1)} %collective-permute-done.2.refs_9_), channel_id=1, source_target_pairs={{0,8},{1,5},{2,10},{3,7},{8,16},{9,1},{10,18},{11,3},{16,24},{17,9... | collective-permute-start | bytes 1585160 | tf_op jit(solution)/shard_map/ppermute | solution.py:415
  50.3 0.8 copy-done.10
  51.3 0.8 copy-done
  52.7 0.7 slice_bitcast_fusion.16
  53.5 1.0 copy-done.1
  54.6 1.0 copy-done.3
  55.6 1.0 copy-done.5
  56.7 1.0 copy-done.7
  57.7 1.0 copy-done.9
  58.7 1.0 copy-done.11
  59.8 7.5 %shard_map.56 = (bf16[144,128,128]{2,1,0:T(8,128)(2,1)S(1)}, bf16[64,128,128]{2,1,0:T(8,128)(2,1)S(1)}, s32[145]{0:T(256)S(1)}, s32[1]{0:T(128)}) custom-call(s32[264]{0:T(512)S(1)} %get-tuple-element.50.near_ref, s32[290]{0:T(512)S(1)} %get-tuple-element.51.late_ref, s32[5]{0:T(128)S(1)} %get-tuple-element.52.meta_ref, s32[448]{0:T(512)S(1)} %concatenate.17.aggs_ref, ...), custom_call_target="tpu_custom_call" | custom-call | flops 268435456 | bytes 1048576 | tf_op jit(solution)/shard_map/pallas_call | solution.py:258
  67.3 1.1 collective-permute-start.18
  68.3 0.7 bitcast_convert_fusion.aggs_ref
  69.0 1.1 collective-permute-done.18.far1
  70.1 4.0 %shard_map.57 = (bf16[2,2,2,1,1,336,128]{6,5,4,3,2,1,0:T(8,128)(2,1)S(1)}, f32[2,2,2,1,1,336,128]{6,5,4,3,2,1,0:T(8,128)S(1)}, bf16[2,2,2,1,1,336,128]{6,5,4,3,2...) custom-call(s32[145]{0:T(256)S(1)} %get-tuple-element.62.plan_ref, ...), custom_call_target="tpu_custom_call" | custom-call | flops 268435456 | bytes 16777216 | tf_op jit(solution)/shard_map/pallas_call | solution.py:382
  74.1 2.1 %collective-permute-start.19 = (bf16[2,2,2,1,1,336,128]{6,5,2,4,3,1,0:T(8,128)(2,1)S(1)}, bf16[2,2,2,1,1,336,128]{6,5,2,4,3,1,0:T(8,128)(2,1)S(1)}, u32[]{:S(2)}, u32[]{:S(2)}) collective-permute-start(bf16[2,2,2,1,1,336,128]{6,5,2,4,3,1,0:T(8,128)(2,1)S(1)} %bitcast.174), channel_id=1, source_target_pairs={{0,8},{1,3},{2,10},{3,1},{4,12},{5,7},{6,14},{7,5},{8,0},{9,11},{1... | collective-permute-start | bytes 2064392 | tf_op jit(solution)/shard_map/ppermute | solution.py:36
  76.2 0.8 collective-permute-start.23
  77.0 2.5 %collective-permute-start.27 = (bf16[2,2,2,1,1,352,128]{6,5,2,4,3,1,0:T(8,128)(2,1)S(1)}, bf16[2,2,2,1,1,352,128]{6,5,2,4,3,1,0:T(8,128)(2,1)S(1)}, u32[]{:S(2)}, u32[]{:S(2)}) collective-permute-start(bf16[2,2,2,1,1,352,128]{6,5,2,4,3,1,0:T(8,128)(2,1)S(1)} %bitcast.172), channel_id=1, source_target_pairs={{0,4},{1,17},{2,6},{3,19},{4,0},{5,21},{6,2},{7,23},{8,12},{9,25},... | collective-permute-start | bytes 2162696 | tf_op jit(solution)/shard_map/ppermute | solution.py:36
  79.5 9.8 %collective-permute-done.19 = bf16[2,2,2,1,1,336,128]{6,5,2,4,3,1,0:T(8,128)(2,1)S(1)} collective-permute-done((bf16[2,2,2,1,1,336,128]{6,5,2,4,3,1,0:T(8,128)(2,1)S(1)}, bf16[2,2,2,1,1,336,128]{6,5,2,4,3,1,0:T(8,128)(2,1)S(1)}, u32[]{:S(2)}, u32[]{:S(2)}) %collective-permute-start.19) | collective-permute-done | bytes 688160 | tf_op jit(solution)/shard_map/ppermute | solution.py:36
  89.5 3.8 %collective-permute-start.20 = (bf16[2,2,1,1,336,128]{5,4,3,2,1,0:T(8,128)(2,1)S(1)}, bf16[2,2,1,1,336,128]{5,4,3,2,1,0:T(8,128)(2,1)S(1)}, u32[]{:S(2)}, u32[]{:S(2)}) collective-permute-start(bf16[2,2,1,1,336,128]{5,4,3,2,1,0:T(8,128)(2,1)S(1)} %get-tuple-element.77), channel_id=1, source_target_pairs={{0,2},{1,9},{2,0},{3,11},{4,6},{5,13},{6,4},{7,15},{8,10},{9,1},{1... | collective-permute-start | bytes 1032200 | tf_op jit(solution)/shard_map/ppermute | solution.py:36
  93.4 2.0 %collective-permute-start.24 = (bf16[2,2,1,1,336,128]{5,4,3,2,1,0:T(8,128)(2,1)S(1)}, bf16[2,2,1,1,336,128]{5,4,3,2,1,0:T(8,128)(2,1)S(1)}, u32[]{:S(2)}, u32[]{:S(2)}) collective-permute-start(bf16[2,2,1,1,336,128]{5,4,3,2,1,0:T(8,128)(2,1)S(1)} %get-tuple-element.79), channel_id=1, source_target_pairs={{0,4},{1,3},{2,6},{3,1},{4,0},{5,7},{6,2},{7,5},{8,12},{9,11},{10,... | collective-permute-start | bytes 1032200 | tf_op jit(solution)/shard_map/ppermute | solution.py:36
  95.5 1.4 %collective-permute-start.28 = (bf16[2,2,1,1,352,128]{5,4,1,0,3,2:T(8,128)(2,1)S(1)}, bf16[2,2,1,1,352,128]{5,4,1,0,3,2:T(8,128)(2,1)S(1)}, u32[]{:S(2)}, u32[]{:S(2)}) collective-permute-start(bf16[2,2,1,1,352,128]{5,4,1,0,3,2:T(8,128)(2,1)S(1)} %fusion.5), channel_id=1, source_target_pairs={{0,8},{1,3},{2,10},{3,1},{4,12},{5,7},{6,14},{7,5},{8,0},{9,11},{1... | collective-permute-start | bytes 1081352 | tf_op jit(solution)/shard_map/ppermute | solution.py:36
  97.0 3.8 %collective-permute-done.20 = bf16[2,2,1,1,336,128]{5,4,3,2,1,0:T(8,128)(2,1)S(1)} collective-permute-done((bf16[2,2,1,1,336,128]{5,4,3,2,1,0:T(8,128)(2,1)S(1)}, bf16[2,2,1,1,336,128]{5,4,3,2,1,0:T(8,128)(2,1)S(1)}, u32[]{:S(2)}, u32[]{:S(2)}) %collective-permute-start.20) | collective-permute-done | bytes 344096 | tf_op jit(solution)/shard_map/ppermute | solution.py:36
  100.9 3.0 %collective-permute-start.21 = (bf16[2,1,1,336,128]{4,3,2,1,0:T(8,128)(2,1)S(1)}, bf16[2,1,1,336,128]{4,3,2,1,0:T(8,128)(2,1)S(1)}, u32[]{:S(2)}, u32[]{:S(2)}) collective-permute-start(bf16[2,1,1,336,128]{4,3,2,1,0:T(8,128)(2,1)S(1)} %get-tuple-element.81), channel_id=1, source_target_pairs={{0,16},{1,5},{2,18},{3,7},{4,20},{5,1},{6,22},{7,3},{8,24},{9,13},... | collective-permute-start | bytes 516104 | tf_op jit(solution)/shard_map/ppermute | solution.py:36
  104.6 2.0 %collective-permute-start.29 = (bf16[2,1,1,352,128]{4,3,0,2,1:T(8,128)(2,1)S(1)}, bf16[2,1,1,352,128]{4,3,0,2,1:T(8,128)(2,1)S(1)}, u32[]{:S(2)}, u32[]{:S(2)}) collective-permute-start(bf16[2,1,1,352,128]{4,3,0,2,1:T(8,128)(2,1)S(1)} %fusion.17), channel_id=1, source_target_pairs={{0,2},{1,5},{2,0},{3,7},{4,6},{5,1},{6,4},{7,3},{8,10},{9,13},{10,... | collective-permute-start | bytes 540680 | tf_op jit(solution)/shard_map/ppermute | solution.py:36
  106.7 7.0 %collective-permute-done.21 = bf16[2,1,1,336,128]{4,3,2,1,0:T(8,128)(2,1)S(1)} collective-permute-done((bf16[2,1,1,336,128]{4,3,2,1,0:T(8,128)(2,1)S(1)}, bf16[2,1,1,336,128]{4,3,2,1,0:T(8,128)(2,1)S(1)}, u32[]{:S(2)}, u32[]{:S(2)}) %collective-permute-start.21) | collective-permute-done | bytes 172064 | tf_op jit(solution)/shard_map/ppermute | solution.py:36
  113.7 3.4 %collective-permute-start.22 = (bf16[1,1,336,128]{3,2,1,0:T(8,128)(2,1)S(1)}, bf16[1,1,336,128]{3,2,1,0:T(8,128)(2,1)S(1)}, u32[]{:S(2)}, u32[]{:S(2)}) collective-permute-start(bf16[1,1,336,128]{3,2,1,0:T(8,128)(2,1)S(1)} %fusion.36), channel_id=1, source_target_pairs={{0,4},{1,17},{2,6},{3,19},{4,0},{5,21},{6,2},{7,23},{8,12},{9,25},... | collective-permute-start | bytes 258056 | tf_op jit(solution)/shard_map/ppermute | solution.py:36
  117.2 3.0 %collective-permute-start.30 = (bf16[1,1,352,128]{3,2,1,0:T(8,128)(2,1)S(1)}, bf16[1,1,352,128]{3,2,1,0:T(8,128)(2,1)S(1)}, u32[]{:S(2)}, u32[]{:S(2)}) collective-permute-start(bf16[1,1,352,128]{3,2,1,0:T(8,128)(2,1)S(1)} %fusion.35), channel_id=1, source_target_pairs={{0,16},{1,9},{2,18},{3,11},{4,20},{5,13},{6,22},{7,15},{8,24},{9,1... | collective-permute-start | bytes 270344 | tf_op jit(solution)/shard_map/ppermute | solution.py:36
  120.2 2.3 %collective-permute-done.26 = bf16[1,1,336,128]{3,2,1,0:T(8,128)(2,1)S(1)} collective-permute-done((bf16[1,1,336,128]{3,2,1,0:T(8,128)(2,1)S(1)}, bf16[1,1,336,128]{3,2,1,0:T(8,128)(2,1)S(1)}, u32[]{:S(2)}, u32[]{:S(2)}) %collective-permute-start.26) | collective-permute-done | bytes 86048 | tf_op jit(solution)/shard_map/ppermute | solution.py:36
  122.5 1.9 %collective-permute-done.30 = bf16[1,1,352,128]{3,2,1,0:T(8,128)(2,1)S(1)} collective-permute-done((bf16[1,1,352,128]{3,2,1,0:T(8,128)(2,1)S(1)}, bf16[1,1,352,128]{3,2,1,0:T(8,128)(2,1)S(1)}, u32[]{:S(2)}, u32[]{:S(2)}) %collective-permute-start.30) | collective-permute-done | bytes 90144 | tf_op jit(solution)/shard_map/ppermute | solution.py:36
  124.4 0.8 pad_maximum_fusion
  (68 shorter events, 4.7 us)
Async XLA Ops:
  0.0 19.5 %collective-permute-start.7 = (bf16[64,128,128]{2,1,0:T(8,128)(2,1)}, bf16[64,128,128]{2,1,0:T(8,128)(2,1)S(1)}, u32[]{:S(2)}, u32[]{:S(2)}) collective-permute-start(bf16[64,128,128]{2,1,0:T(8,128)(2,1)} %bitcast.175), channel_id=1, source_target_pairs={{0,1},{1,0},{2,3},{3,2},{4,5},{5,4},{6,7},{7,6},{8,9},{9,8},{10,11... | collective-permute-start | bytes 6291464 | tf_op jit(solution)/shard_map/ppermute | solution.py:25
  0.5 4.9 %collective-permute-start.3 = (s32[64]{0:T(128)}, s32[64]{0:T(128)S(1)}, u32[]{:S(2)}, u32[]{:S(2)}) collective-permute-start(s32[64]{0:T(128)} %bitcast.183), channel_id=1, source_target_pairs={{0,1},{1,0},{2,3},{3,2},{4,5},{5,4},{6,7},{7,6},{8,9},{9,8},{10,11... | collective-permute-start | bytes 776 | tf_op jit(solution)/shard_map/ppermute | solution.py:25
  2.3 14.3 %collective-permute-start = (bf16[2064,128]{1,0:T(8,128)(2,1)S(1)}, bf16[2064,128]{1,0:T(8,128)(2,1)S(1)}, u32[]{:S(2)}, u32[]{:S(2)}) collective-permute-start(bf16[2064,128]{1,0:T(8,128)(2,1)S(1)} %fusion.4), channel_id=1, source_target_pairs={{0,8},{1,5},{2,10},{3,7},{8,16},{9,1},{10,18},{11,3},{16,24},{17,9... | collective-permute-start | bytes 1585160 | tf_op jit(solution)/shard_map/ppermute | solution.py:415
  5.3 13.6 %collective-permute-start.4 = (bf16[2064,128]{1,0:T(8,128)(2,1)S(1)}, bf16[2064,128]{1,0:T(8,128)(2,1)S(1)}, u32[]{:S(2)}, u32[]{:S(2)}) collective-permute-start(bf16[2064,128]{1,0:T(8,128)(2,1)S(1)} %fusion.4), channel_id=1, source_target_pairs={{0,4},{1,9},{2,6},{3,11},{8,0},{9,17},{10,2},{11,19},{16,8},{17,25... | collective-permute-start | bytes 1585160 | tf_op jit(solution)/shard_map/ppermute | solution.py:415
  7.3 12.2 %collective-permute-start.8 = (bf16[2048,128]{1,0:T(8,128)(2,1)}, bf16[2048,128]{1,0:T(8,128)(2,1)S(1)}, u32[]{:S(2)}, u32[]{:S(2)}) collective-permute-start(bf16[2048,128]{1,0:T(8,128)(2,1)} %bitcast.178), channel_id=1, source_target_pairs={{0,1},{1,0},{2,3},{3,2},{4,5},{5,4},{6,7},{7,6},{8,9},{9,8},{10,11... | collective-permute-start | bytes 1572872 | tf_op jit(solution)/shard_map/ppermute | solution.py:25
  16.6 15.0 %collective-permute-start.1 = (bf16[2064,128]{1,0:T(8,128)(2,1)S(1)}, bf16[2064,128]{1,0:T(8,128)(2,1)}, u32[]{:S(2)}, u32[]{:S(2)}) collective-permute-start(bf16[2064,128]{1,0:T(8,128)(2,1)S(1)} %collective-permute-done.refs_11_), channel_id=1, source_target_pairs={{0,8},{1,5},{2,10},{3,7},{8,16},{9,1},{10,18},{11,3},{16,24},{17,9... | collective-permute-start | bytes 1585160 | tf_op jit(solution)/shard_map/ppermute | solution.py:415
  19.0 14.9 %collective-permute-start.5 = (bf16[2064,128]{1,0:T(8,128)(2,1)S(1)}, bf16[2064,128]{1,0:T(8,128)(2,1)}, u32[]{:S(2)}, u32[]{:S(2)}) collective-permute-start(bf16[2064,128]{1,0:T(8,128)(2,1)S(1)} %collective-permute-done.4.refs_6_), channel_id=1, source_target_pairs={{0,4},{1,9},{2,6},{3,11},{8,0},{9,17},{10,2},{11,19},{16,8},{17,25... | collective-permute-start | bytes 1585160 | tf_op jit(solution)/shard_map/ppermute | solution.py:415
  19.5 14.4 %collective-permute-start.9 = (bf16[2048,128]{1,0:T(8,128)(2,1)}, bf16[2048,128]{1,0:T(8,128)(2,1)S(1)}, u32[]{:S(2)}, u32[]{:S(2)}) collective-permute-start(bf16[2048,128]{1,0:T(8,128)(2,1)} %bitcast.179), channel_id=1, source_target_pairs={{0,2},{1,3},{2,0},{3,1},{4,6},{5,7},{6,4},{7,5},{8,10},{9,11},{10,... | collective-permute-start | bytes 1572872 | tf_op jit(solution)/shard_map/ppermute | solution.py:25
  31.6 14.7 %collective-permute-start.2 = (bf16[2064,128]{1,0:T(8,128)(2,1)}, bf16[2064,128]{1,0:T(8,128)(2,1)S(1)}, u32[]{:S(2)}, u32[]{:S(2)}) collective-permute-start(bf16[2064,128]{1,0:T(8,128)(2,1)} %collective-permute-done.1.refs_10_), channel_id=1, source_target_pairs={{0,8},{1,5},{2,10},{3,7},{8,16},{9,1},{10,18},{11,3},{16,24},{17,9... | collective-permute-start | bytes 1585160 | tf_op jit(solution)/shard_map/ppermute | solution.py:415
  33.9 12.4 %collective-permute-start.6 = (bf16[2064,128]{1,0:T(8,128)(2,1)}, bf16[2064,128]{1,0:T(8,128)(2,1)}, u32[]{:S(2)}, u32[]{:S(2)}) collective-permute-start(bf16[2064,128]{1,0:T(8,128)(2,1)} %collective-permute-done.5.refs_7_), channel_id=1, source_target_pairs={{0,4},{1,9},{2,6},{3,11},{8,0},{9,17},{10,2},{11,19},{16,8},{17,25... | collective-permute-start | bytes 1585160 | tf_op jit(solution)/shard_map/ppermute | solution.py:415
  33.9 12.4 %collective-permute-start.10 = (bf16[2064,128]{1,0:T(8,128)(2,1)S(1)}, bf16[2064,128]{1,0:T(8,128)(2,1)S(1)}, u32[]{:S(2)}, u32[]{:S(2)}) collective-permute-start(bf16[2064,128]{1,0:T(8,128)(2,1)S(1)} %collective-permute-done.4.refs_6_), channel_id=1, source_target_pairs={{0,1},{1,0},{2,3},{3,2},{4,5},{5,4},{6,7},{7,6},{8,9},{9,8},{10,11... | collective-permute-start | bytes 1585160 | tf_op jit(solution)/shard_map/ppermute | solution.py:25
  34.0 13.2 %collective-permute-start.11 = (bf16[2064,128]{1,0:T(8,128)(2,1)S(1)}, bf16[2064,128]{1,0:T(8,128)(2,1)S(1)}, u32[]{:S(2)}, u32[]{:S(2)}) collective-permute-start(bf16[2064,128]{1,0:T(8,128)(2,1)S(1)} %collective-permute-done.refs_11_), channel_id=1, source_target_pairs={{0,1},{1,0},{2,3},{3,2},{4,5},{5,4},{6,7},{7,6},{8,9},{9,8},{10,11... | collective-permute-start | bytes 1585160 | tf_op jit(solution)/shard_map/ppermute | solution.py:25
  34.5 15.8 %collective-permute-start.12 = (bf16[2048,128]{1,0:T(8,128)(2,1)S(1)}, bf16[2048,128]{1,0:T(8,128)(2,1)S(1)}, u32[]{:S(2)}, u32[]{:S(2)}) collective-permute-start(bf16[2048,128]{1,0:T(8,128)(2,1)S(1)} %collective-permute-done.9.refs_3_), channel_id=1, source_target_pairs={{0,1},{1,0},{2,3},{3,2},{4,5},{5,4},{6,7},{7,6},{8,9},{9,8},{10,11... | collective-permute-start | bytes 1572872 | tf_op jit(solution)/shard_map/ppermute | solution.py:25
  34.5 0.8 copy-start.8
  40.2 0.8 copy-start.2
  46.3 0.8 copy-start.4
  47.1 0.8 copy-start.6
  47.9 5.6 %collective-permute-start.15 = (bf16[2064,128]{1,0:T(8,128)(2,1)S(1)}, bf16[2064,128]{1,0:T(8,128)(2,1)}, u32[]{:S(2)}, u32[]{:S(2)}) collective-permute-start(bf16[2064,128]{1,0:T(8,128)(2,1)S(1)} %collective-permute-done.2.refs_9_), channel_id=1, source_target_pairs={{0,1},{1,0},{2,3},{3,2},{4,5},{5,4},{6,7},{7,6},{8,9},{9,8},{10,11... | collective-permute-start | bytes 1585160 | tf_op jit(solution)/shard_map/ppermute | solution.py:25
  48.0 19.3 %collective-permute-start.17 = (bf16[2064,128]{1,0:T(8,128)(2,1)S(1)}, bf16[2064,128]{1,0:T(8,128)(2,1)}, u32[]{:S(2)}, u32[]{:S(2)}) collective-permute-start(bf16[2064,128]{1,0:T(8,128)(2,1)S(1)} %collective-permute-done.2.refs_9_), channel_id=1, source_target_pairs={{0,8},{1,5},{2,10},{3,7},{8,16},{9,1},{10,18},{11,3},{16,24},{17,9... | collective-permute-start | bytes 1585160 | tf_op jit(solution)/shard_map/ppermute | solution.py:415
  49.8 3.7 %collective-permute-start.13 = (bf16[2064,128]{1,0:T(8,128)(2,1)}, bf16[2064,128]{1,0:T(8,128)(2,1)}, u32[]{:S(2)}, u32[]{:S(2)}) collective-permute-start(bf16[2064,128]{1,0:T(8,128)(2,1)} %collective-permute-done.5.refs_7_), channel_id=1, source_target_pairs={{0,1},{1,0},{2,3},{3,2},{4,5},{5,4},{6,7},{7,6},{8,9},{9,8},{10,11... | collective-permute-start | bytes 1585160 | tf_op jit(solution)/shard_map/ppermute | solution.py:25
  49.9 3.6 %collective-permute-start.14 = (bf16[2064,128]{1,0:T(8,128)(2,1)}, bf16[2064,128]{1,0:T(8,128)(2,1)}, u32[]{:S(2)}, u32[]{:S(2)}) collective-permute-start(bf16[2064,128]{1,0:T(8,128)(2,1)} %collective-permute-done.6.refs_8_), channel_id=1, source_target_pairs={{0,1},{1,0},{2,3},{3,2},{4,5},{5,4},{6,7},{7,6},{8,9},{9,8},{10,11... | collective-permute-start | bytes 1585160 | tf_op jit(solution)/shard_map/ppermute | solution.py:25
  50.3 0.8 copy-start.10
  51.1 2.4 %collective-permute-start.16 = (bf16[2064,128]{1,0:T(8,128)(2,1)}, bf16[2064,128]{1,0:T(8,128)(2,1)}, u32[]{:S(2)}, u32[]{:S(2)}) collective-permute-start(bf16[2064,128]{1,0:T(8,128)(2,1)} %collective-permute-done.1.refs_10_), channel_id=1, source_target_pairs={{0,1},{1,0},{2,3},{3,2},{4,5},{5,4},{6,7},{7,6},{8,9},{9,8},{10,11... | collective-permute-start | bytes 1585160 | tf_op jit(solution)/shard_map/ppermute | solution.py:25
  51.3 0.8 copy-start
  53.5 1.0 copy-start.1
  54.6 1.0 copy-start.3
  55.6 1.0 copy-start.5
  56.7 1.0 copy-start.7
  57.7 1.0 copy-start.9
  58.7 1.0 copy-start.11
  67.3 2.8 %collective-permute-start.18 = (bf16[2064,128]{1,0:T(8,128)(2,1)}, bf16[2064,128]{1,0:T(8,128)(2,1)S(1)}, u32[]{:S(2)}, u32[]{:S(2)}) collective-permute-start(bf16[2064,128]{1,0:T(8,128)(2,1)} %collective-permute-done.17.far0), channel_id=1, source_target_pairs={{0,1},{1,0},{2,3},{3,2},{4,5},{5,4},{6,7},{7,6},{8,9},{9,8},{10,11... | collective-permute-start | bytes 1585160 | tf_op jit(solution)/shard_map/ppermute | solution.py:25
  74.1 15.3 %collective-permute-start.19 = (bf16[2,2,2,1,1,336,128]{6,5,2,4,3,1,0:T(8,128)(2,1)S(1)}, bf16[2,2,2,1,1,336,128]{6,5,2,4,3,1,0:T(8,128)(2,1)S(1)}, u32[]{:S(2)}, u32[]{:S(2)}) collective-permute-start(bf16[2,2,2,1,1,336,128]{6,5,2,4,3,1,0:T(8,128)(2,1)S(1)} %bitcast.174), channel_id=1, source_target_pairs={{0,8},{1,3},{2,10},{3,1},{4,12},{5,7},{6,14},{7,5},{8,0},{9,11},{1... | collective-permute-start | bytes 2064392 | tf_op jit(solution)/shard_map/ppermute | solution.py:36
  76.2 17.1 %collective-permute-start.23 = (bf16[2,2,2,1,1,336,128]{6,5,2,4,3,1,0:T(8,128)(2,1)S(1)}, bf16[2,2,2,1,1,336,128]{6,5,2,4,3,1,0:T(8,128)(2,1)S(1)}, u32[]{:S(2)}, u32[]{:S(2)}) collective-permute-start(bf16[2,2,2,1,1,336,128]{6,5,2,4,3,1,0:T(8,128)(2,1)S(1)} %bitcast.173), channel_id=1, source_target_pairs={{0,2},{1,5},{2,0},{3,7},{4,6},{5,1},{6,4},{7,3},{8,10},{9,13},{10,... | collective-permute-start | bytes 2064392 | tf_op jit(solution)/shard_map/ppermute | solution.py:36
  77.0 18.4 %collective-permute-start.27 = (bf16[2,2,2,1,1,352,128]{6,5,2,4,3,1,0:T(8,128)(2,1)S(1)}, bf16[2,2,2,1,1,352,128]{6,5,2,4,3,1,0:T(8,128)(2,1)S(1)}, u32[]{:S(2)}, u32[]{:S(2)}) collective-permute-start(bf16[2,2,2,1,1,352,128]{6,5,2,4,3,1,0:T(8,128)(2,1)S(1)} %bitcast.172), channel_id=1, source_target_pairs={{0,4},{1,17},{2,6},{3,19},{4,0},{5,21},{6,2},{7,23},{8,12},{9,25},... | collective-permute-start | bytes 2162696 | tf_op jit(solution)/shard_map/ppermute | solution.py:36
  89.5 11.3 %collective-permute-start.20 = (bf16[2,2,1,1,336,128]{5,4,3,2,1,0:T(8,128)(2,1)S(1)}, bf16[2,2,1,1,336,128]{5,4,3,2,1,0:T(8,128)(2,1)S(1)}, u32[]{:S(2)}, u32[]{:S(2)}) collective-permute-start(bf16[2,2,1,1,336,128]{5,4,3,2,1,0:T(8,128)(2,1)S(1)} %get-tuple-element.77), channel_id=1, source_target_pairs={{0,2},{1,9},{2,0},{3,11},{4,6},{5,13},{6,4},{7,15},{8,10},{9,1},{1... | collective-permute-start | bytes 1032200 | tf_op jit(solution)/shard_map/ppermute | solution.py:36
  93.4 10.5 %collective-permute-start.24 = (bf16[2,2,1,1,336,128]{5,4,3,2,1,0:T(8,128)(2,1)S(1)}, bf16[2,2,1,1,336,128]{5,4,3,2,1,0:T(8,128)(2,1)S(1)}, u32[]{:S(2)}, u32[]{:S(2)}) collective-permute-start(bf16[2,2,1,1,336,128]{5,4,3,2,1,0:T(8,128)(2,1)S(1)} %get-tuple-element.79), channel_id=1, source_target_pairs={{0,4},{1,3},{2,6},{3,1},{4,0},{5,7},{6,2},{7,5},{8,12},{9,11},{10,... | collective-permute-start | bytes 1032200 | tf_op jit(solution)/shard_map/ppermute | solution.py:36
  95.5 9.0 %collective-permute-start.28 = (bf16[2,2,1,1,352,128]{5,4,1,0,3,2:T(8,128)(2,1)S(1)}, bf16[2,2,1,1,352,128]{5,4,1,0,3,2:T(8,128)(2,1)S(1)}, u32[]{:S(2)}, u32[]{:S(2)}) collective-permute-start(bf16[2,2,1,1,352,128]{5,4,1,0,3,2:T(8,128)(2,1)S(1)} %fusion.5), channel_id=1, source_target_pairs={{0,8},{1,3},{2,10},{3,1},{4,12},{5,7},{6,14},{7,5},{8,0},{9,11},{1... | collective-permute-start | bytes 1081352 | tf_op jit(solution)/shard_map/ppermute | solution.py:36
  100.9 12.7 %collective-permute-start.21 = (bf16[2,1,1,336,128]{4,3,2,1,0:T(8,128)(2,1)S(1)}, bf16[2,1,1,336,128]{4,3,2,1,0:T(8,128)(2,1)S(1)}, u32[]{:S(2)}, u32[]{:S(2)}) collective-permute-start(bf16[2,1,1,336,128]{4,3,2,1,0:T(8,128)(2,1)S(1)} %get-tuple-element.81), channel_id=1, source_target_pairs={{0,16},{1,5},{2,18},{3,7},{4,20},{5,1},{6,22},{7,3},{8,24},{9,13},... | collective-permute-start | bytes 516104 | tf_op jit(solution)/shard_map/ppermute | solution.py:36
  103.9 13.1 %collective-permute-start.25 = (bf16[2,1,1,336,128]{4,3,2,1,0:T(8,128)(2,1)S(1)}, bf16[2,1,1,336,128]{4,3,2,1,0:T(8,128)(2,1)S(1)}, u32[]{:S(2)}, u32[]{:S(2)}) collective-permute-start(bf16[2,1,1,336,128]{4,3,2,1,0:T(8,128)(2,1)S(1)} %get-tuple-element.83), channel_id=1, source_target_pairs={{0,8},{1,17},{2,10},{3,19},{4,12},{5,21},{6,14},{7,23},{8,0},{9,25... | collective-permute-start | bytes 516104 | tf_op jit(solution)/shard_map/ppermute | solution.py:36
  104.6 12.5 %collective-permute-start.29 = (bf16[2,1,1,352,128]{4,3,0,2,1:T(8,128)(2,1)S(1)}, bf16[2,1,1,352,128]{4,3,0,2,1:T(8,128)(2,1)S(1)}, u32[]{:S(2)}, u32[]{:S(2)}) collective-permute-start(bf16[2,1,1,352,128]{4,3,0,2,1:T(8,128)(2,1)S(1)} %fusion.17), channel_id=1, source_target_pairs={{0,2},{1,5},{2,0},{3,7},{4,6},{5,1},{6,4},{7,3},{8,10},{9,13},{10,... | collective-permute-start | bytes 540680 | tf_op jit(solution)/shard_map/ppermute | solution.py:36
  113.7 6.5 %collective-permute-start.22 = (bf16[1,1,336,128]{3,2,1,0:T(8,128)(2,1)S(1)}, bf16[1,1,336,128]{3,2,1,0:T(8,128)(2,1)S(1)}, u32[]{:S(2)}, u32[]{:S(2)}) collective-permute-start(bf16[1,1,336,128]{3,2,1,0:T(8,128)(2,1)S(1)} %fusion.36), channel_id=1, source_target_pairs={{0,4},{1,17},{2,6},{3,19},{4,0},{5,21},{6,2},{7,23},{8,12},{9,25},... | collective-permute-start | bytes 258056 | tf_op jit(solution)/shard_map/ppermute | solution.py:36
  117.0 5.4 %collective-permute-start.26 = (bf16[1,1,336,128]{3,2,1,0:T(8,128)(2,1)S(1)}, bf16[1,1,336,128]{3,2,1,0:T(8,128)(2,1)S(1)}, u32[]{:S(2)}, u32[]{:S(2)}) collective-permute-start(bf16[1,1,336,128]{3,2,1,0:T(8,128)(2,1)S(1)} %fusion.37), channel_id=1, source_target_pairs={{0,16},{1,9},{2,18},{3,11},{4,20},{5,13},{6,22},{7,15},{8,24},{9,1... | collective-permute-start | bytes 258056 | tf_op jit(solution)/shard_map/ppermute | solution.py:36
  117.2 7.3 %collective-permute-start.30 = (bf16[1,1,352,128]{3,2,1,0:T(8,128)(2,1)S(1)}, bf16[1,1,352,128]{3,2,1,0:T(8,128)(2,1)S(1)}, u32[]{:S(2)}, u32[]{:S(2)}) collective-permute-start(bf16[1,1,352,128]{3,2,1,0:T(8,128)(2,1)S(1)} %fusion.35), channel_id=1, source_target_pairs={{0,16},{1,9},{2,18},{3,11},{4,20},{5,13},{6,22},{7,15},{8,24},{9,1... | collective-permute-start | bytes 270344 | tf_op jit(solution)/shard_map/ppermute | solution.py:36

commit v6 on v3

--- a/solution.py
+++ b/solution.py
@@ -156,31 +156,54 @@
     )(cols, aggs)
 
 
+def turn_kernel(s, *refs):
+    rows_ref, rows_buf, sems = refs[-3:]
+    copies = [
+        pltpu.make_async_copy(refs[k], rows_buf.at[pl.ds(k * s.tiles, s.tiles)], sems.at[k])
+        for k in range(s.cols)
+    ]
+    for copy in copies:
+        copy.start()
+    for copy in copies:
+        copy.wait()
+    col = lax.axis_index("col")
+
+    def turn(k, carry):
+        part = k >> log2(s.tiles)
+        rel = (part & (s.cols // 2 - 1)) * 2 + (part >> log2(s.cols // 2))
+        rows_ref[((rel ^ col) << log2(s.tiles)) + (k & (s.tiles - 1))] = rows_buf[k].T
+        return carry
+
+    lax.fori_loop(0, s.slab, turn, 0, unroll=4)
+
+
+def turn_rows(s, rows):
+    own = pltpu.with_memory_space_constraint(rows[0], pltpu.HBM)
+    shape = ((s.slab, s.side, s.side), jnp.bfloat16)
+    return pl.pallas_call(
+        functools.partial(turn_kernel, s),
+        in_specs=[pl.BlockSpec(memory_space=pltpu.HBM)]
+        + [pl.BlockSpec(memory_space=pl.ANY)] * (s.cols - 1),
+        out_specs=pl.BlockSpec(memory_space=pltpu.VMEM),
+        out_shape=jax.ShapeDtypeStruct(*shape),
+        scratch_shapes=[pltpu.VMEM(*shape), pltpu.SemaphoreType.DMA((s.cols,))],
+        compiler_params=pltpu.CompilerParams(vmem_limit_bytes=room(shape, shape)),
+        cost_estimate=pl.CostEstimate(flops=1 << 20, bytes_accessed=16 << 20, transcendentals=0),
+    )(own, *rows[1:])
+
+
 def product_kernel(s, plan_ref, starts_ref, *refs):
-    slots_ref, rows_ref, a_buf, panel, rows_buf, sems = refs[-6:]
+    slots_ref, a_buf, panel, sems = refs[-4:]
     copies = []
     for k in range(2):
         copies.append((refs[k], a_buf.at[pl.ds(k * s.slab, s.slab)]))
-    for k in range(s.cols):
-        copies.append((refs[2 + k], rows_buf.at[pl.ds(k * s.tiles, s.tiles)]))
     for k in range(2 * s.early):
-        source = refs[2] if k == 0 else refs[1 + s.cols + k]
-        copies.append((source, panel.at[pl.ds(k * s.tiles, s.tiles)]))
+        copies.append((refs[2 + k], panel.at[pl.ds(k * s.tiles, s.tiles)]))
     copies = [pltpu.make_async_copy(src, dst, sems.at[k]) for k, (src, dst) in enumerate(copies)]
     for copy in copies:
         copy.start()
     for copy in copies:
         copy.wait()
-
-    col = lax.axis_index("col")
-
-    def turn(k, carry):
-        part = k >> log2(s.tiles)
-        rel = (part & (s.cols // 2 - 1)) * 2 + (part >> log2(s.cols // 2))
-        rows_ref[((rel ^ col) << log2(s.tiles)) + (k & (s.tiles - 1))] = rows_buf[k].T
-        return carry
-
-    lax.fori_loop(0, s.slab, turn, 0, unroll=4)
 
     for hi in range(s.his):
         begin = starts_ref[2 * hi] // UNROLL
@@ -208,24 +231,22 @@
         lax.fori_loop(middle, end, far, 0)
 
 
-def make_products(s, plan, starts, a_own, a_other, near, rows):
+def make_products(s, plan, starts, a_own, a_other, near):
     smem = pl.BlockSpec(memory_space=pltpu.SMEM)
-    vmem = pl.BlockSpec(memory_space=pltpu.VMEM)
+    hbm = pl.BlockSpec(memory_space=pltpu.HBM)
     anywhere = pl.BlockSpec(memory_space=pl.ANY)
     shapes = [
-        ((count, s.side, s.side), jnp.bfloat16)
-        for count in (s.slots, s.slab, s.pairs, s.near, s.slab)
+        ((count, s.side, s.side), jnp.bfloat16) for count in (s.slots, s.pairs, s.near)
     ]
-    hbm = pl.BlockSpec(memory_space=pltpu.HBM)
-    a_own, own = (pltpu.with_memory_space_constraint(x, pltpu.HBM) for x in (a_own, rows[0]))
-    operands = [a_own, a_other, own, *rows[1:], *near[1:]]
+    a_own, own = (pltpu.with_memory_space_constraint(x, pltpu.HBM) for x in (a_own, near[0]))
+    operands = [a_own, a_other, own, *near[1:]]
     return pl.pallas_call(
         functools.partial(product_kernel, s),
         in_specs=[smem, smem, hbm, anywhere, hbm] + [anywhere] * (len(operands) - 3),
-        out_specs=[vmem, vmem],
-        out_shape=[jax.ShapeDtypeStruct(*shape) for shape in shapes[:2]],
-        scratch_shapes=[pltpu.VMEM(*shape) for shape in shapes[2:]]
-        + [pltpu.SemaphoreType.DMA((len(operands) + 1,))],
+        out_specs=pl.BlockSpec(memory_space=pltpu.VMEM),
+        out_shape=jax.ShapeDtypeStruct(*shapes[0]),
+        scratch_shapes=[pltpu.VMEM(*shape) for shape in shapes[1:]]
+        + [pltpu.SemaphoreType.DMA((len(operands),))],
         compiler_params=pltpu.CompilerParams(vmem_limit_bytes=room(*shapes)),
         cost_estimate=pl.CostEstimate(
             flops=s.pairs * s.side**3, bytes_accessed=1 << 20, transcendentals=0
@@ -365,20 +386,20 @@
     cols_other, mine = barrier((cols_other, p_tiles))
     second = ring(mine, 1)
     a_other, p_other = swap(a_blocks[:, 0], "col", 1), swap(p_tiles, "col", 1)
-
-    aggs = owner[:, 0] * OWN + agg_local
-    aggs, a_other, p_other, one, two, mine = barrier(
-        (aggs, a_other, p_other, first, second, p_tiles)
-    )
-    own_near, other_near = {0: p_tiles, s.rows - 1: one, 1: two}, {0: p_other}
-    first, second = ring(first, 0), ring(second, 1)
-    aggs = [aggs] + [swap(aggs, "row", mask) for mask in (1, 2, 3)]
-    second, aggs = barrier((second, jnp.concatenate(aggs, 0)))
-    rows = [mine]
+    rows = [p_tiles]
     bit = 2
     while bit < s.cols:
         rows += [swap(piece, "col", bit) for piece in rows]
         bit *= 2
+
+    aggs = owner[:, 0] * OWN + agg_local
+    aggs, a_other, p_other, came, *rows[1:] = barrier(
+        (aggs, a_other, p_other, first, *rows[1:])
+    )
+    own_near, other_near = {0: p_tiles, s.rows - 1: came, 1: second}, {0: p_other}
+    first, second = ring(first, 0), ring(second, 1)
+    aggs = [aggs] + [swap(aggs, "row", mask) for mask in (1, 2, 3)]
+    aggs = jnp.concatenate(aggs, 0)
     bit = 4
     while bit < s.rows:
         aggs = jnp.concatenate([aggs, swap(aggs, "row", bit)], 0)
@@ -397,9 +418,11 @@
         held = [step, s.rows - step]
 
     others = sorted(set(other_near) - {0})
-    tie = (first, second, plan, starts)
+    first, *rest = barrier((first, *rows[1:]))
+    rows_t = turn_rows(s, [p_tiles, *rest])
+    tie = (first, second, plan, starts, rows_t)
     tie += (*(own_near[away] for away in held), *(other_near[away] for away in others))
-    first, second, plan, starts, *rest = barrier(tie)
+    first, second, plan, starts, rows_t, *rest = barrier(tie)
     for away, piece in zip(others, rest[len(held):]):
         other_near[away] = piece
     far = ring(first, 0)
@@ -410,8 +433,8 @@
         other_near[away] = swap(own_near[away], "col", 1)
     near = [own_near[k] for k in sorted(own_near)]
     near += [other_near[k] for k in sorted(other_near)]
-    slots, rows_t = make_products(s, plan, starts, a_blocks[:, 0], a_other, near, rows)
-    far, slots, rows_t = barrier((far, slots, rows_t))
+    slots = make_products(s, plan, starts, a_blocks[:, 0], a_other, near)
+    far, slots = barrier((far, slots))
     far_other = swap(far, "col", 1)
     parts = make_sums(s, plan, starts, slots, rows_t, [far, far_other])
 

time: 115 us -> 115 us (level)
  starting transfers between devices: 46.4 us -> 41.4 us
  Pallas kernels: 14.8 us -> 17.6 us
  waiting for transfers between devices: 50.5 us -> 52.7 us
    ppermute x16, waiting for transfers between devices: 14.6 us -> 7.08 us  [swap(): return lax.ppermute(value, axis, [(i, i ^ bit) for i in range(size)])]
    ppermute x12, waiting for transfers between devices: 28.2 us -> 33.4 us  [exchange(): return lax.ppermute(value, ('row', 'col'), moves)]
    ppermute x12, starting transfers between devices: 20 us -> 15 us  [exchange(): return lax.ppermute(value, ('row', 'col'), moves)]
    ppermute x7, waiting for transfers between devices: 7.71 us -> 12.2 us  [ring(): return lax.ppermute(value, ('row', 'col'), moves)]
    pallas_call x0 -> x1, Pallas kernels: none -> 2.87 us  [turn_rows(): pl.pallas_call(functools.partial(turn_kernel, s), in_specs=[pl.BlockSpec(...]
    ppermute x16, starting transfers between devices: 11.4 us -> 10.1 us  [swap(): return lax.ppermute(value, axis, [(i, i ^ bit) for i in range(size)])]
    ppermute x7, starting transfers between devices: 15 us -> 16.2 us  [ring(): return lax.ppermute(value, ('row', 'col'), moves)]
  transfers between devices with their start and end apart: 35 -> 35, of which waited for: 15 -> 18; matrix products, arithmetic and copies ran while one was open for 2% -> 2% of each run, Pallas kernels for 9% -> 12%
where the time goes in v6:
time: 115 us
  waiting for transfers between devices  52.7 us (46%)
  starting transfers between devices  41.4 us (36%)
  Pallas kernels  17.6 us (15%)
  other arithmetic  3.1 us (3%)
    ppermute x12, waiting for transfers between devices, exchange(): return lax.ppermute(value, ('row', 'col'), moves)  33.4 us
    ppermute x7, starting transfers between devices, ring(): return lax.ppermute(value, ('row', 'col'), moves)  16.2 us
    ppermute x12, starting transfers between devices, exchange(): return lax.ppermute(value, ('row', 'col'), moves)  15 us
    ppermute x7, waiting for transfers between devices, ring(): return lax.ppermute(value, ('row', 'col'), moves)  12.2 us
    ppermute x16, starting transfers between devices, swap(): return lax.ppermute(value, axis, [(i, i ^ bit) for i in range(size)])  10.1 us
    ppermute x16, waiting for transfers between devices, swap(): return lax.ppermute(value, axis, [(i, i ^ bit) for i in range(size)])  7.08 us
    pallas_call x1, Pallas kernels, make_products(): pl.pallas_call(functools.partial(product_kernel, s), in_specs=[smem, smem...  5.97 us
    pallas_call x1, Pallas kernels, make_plan(): pl.pallas_call(functools.partial(plan_kernel, s), in_specs=[smem, smem],...  4.54 us
  transfers between devices with their start and end apart: 35, of which 18 were waited for; matrix products, arithmetic and copies ran while one was open for 2% of the time, Pallas kernels for 12%

profile of v6, /device:TPU:0, one launch (start us, length us, event | category | flops | bytes accessed | tf_op | source)
XLA Modules:
  0.0 115.0 jit_solution(11631773988769511322)
XLA Ops:
  0.0 0.5 collective-permute-start.3
  0.5 3.0 %collective-permute-start = (bf16[16,128,128]{2,1,0:T(8,128)(2,1)}, bf16[16,128,128]{2,1,0:T(8,128)(2,1)S(1)}, u32[]{:S(2)}, u32[]{:S(2)}) collective-permute-start(bf16[16,128,128]{2,1,0:T(8,128)(2,1)} %refs_2_.1), channel_id=1, source_target_pairs={{0,8},{1,5},{2,10},{3,7},{8,16},{9,1},{10,18},{11,3},{16,24},{17,9... | collective-permute-start | bytes 1572872 | tf_op jit(solution)/shard_map/ppermute | solution.py:381
  3.5 0.9 collective-permute-done.6
  4.5 2.9 %collective-permute-start.7 = (bf16[16,128,128]{2,1,0:T(8,128)(2,1)}, bf16[16,128,128]{2,1,0:T(8,128)(2,1)}, u32[]{:S(2)}, u32[]{:S(2)}) collective-permute-start(bf16[16,128,128]{2,1,0:T(8,128)(2,1)} %refs_2_.1), channel_id=1, source_target_pairs={{0,4},{1,9},{2,6},{3,11},{8,0},{9,17},{10,2},{11,19},{16,8},{17,25... | collective-permute-start | bytes 1572872 | tf_op jit(solution)/shard_map/ppermute | solution.py:381
  7.3 1.5 %collective-permute-start.5 = (bf16[16,128,128]{2,1,0:T(8,128)(2,1)}, bf16[16,128,128]{2,1,0:T(8,128)(2,1)}, u32[]{:S(2)}, u32[]{:S(2)}) collective-permute-start(bf16[16,128,128]{2,1,0:T(8,128)(2,1)} %refs_2_.1), channel_id=1, source_target_pairs={{0,2},{1,3},{2,0},{3,1},{4,6},{5,7},{6,4},{7,5},{8,10},{9,11},{10,... | collective-permute-start | bytes 1572872 | tf_op jit(solution)/shard_map/ppermute | solution.py:24
  8.8 4.3 %collective-permute-done.refs_8_ = bf16[16,128,128]{2,1,0:T(8,128)(2,1)S(1)} collective-permute-done((bf16[16,128,128]{2,1,0:T(8,128)(2,1)}, bf16[16,128,128]{2,1,0:T(8,128)(2,1)S(1)}, u32[]{:S(2)}, u32[]{:S(2)}) %collective-permute-start) | collective-permute-done | bytes 524320 | tf_op jit(solution)/shard_map/ppermute | solution.py:381
  13.1 2.4 %collective-permute-start.1 = (bf16[16,128,128]{2,1,0:T(8,128)(2,1)S(1)}, bf16[16,128,128]{2,1,0:T(8,128)(2,1)}, u32[]{:S(2)}, u32[]{:S(2)}) collective-permute-start(bf16[16,128,128]{2,1,0:T(8,128)(2,1)S(1)} %collective-permute-done.refs_8_), channel_id=1, source_target_pairs={{0,8},{1,5},{2,10},{3,7},{8,16},{9,1},{10,18},{11,3},{16,24},{17,9... | collective-permute-start | bytes 1572872 | tf_op jit(solution)/shard_map/ppermute | solution.py:381
  15.5 2.2 %collective-permute-done.7.refs_3_ = bf16[16,128,128]{2,1,0:T(8,128)(2,1)} collective-permute-done((bf16[16,128,128]{2,1,0:T(8,128)(2,1)}, bf16[16,128,128]{2,1,0:T(8,128)(2,1)}, u32[]{:S(2)}, u32[]{:S(2)}) %collective-permute-start.7) | collective-permute-done | bytes 524320 | tf_op jit(solution)/shard_map/ppermute | solution.py:381
  17.7 2.0 %collective-permute-start.8 = (bf16[16,128,128]{2,1,0:T(8,128)(2,1)}, bf16[16,128,128]{2,1,0:T(8,128)(2,1)}, u32[]{:S(2)}, u32[]{:S(2)}) collective-permute-start(bf16[16,128,128]{2,1,0:T(8,128)(2,1)} %collective-permute-done.7.refs_3_), channel_id=1, source_target_pairs={{0,4},{1,9},{2,6},{3,11},{8,0},{9,17},{10,2},{11,19},{16,8},{17,25... | collective-permute-start | bytes 1572872 | tf_op jit(solution)/shard_map/ppermute | solution.py:381
  19.6 0.7 bitcast_add_fusion
  20.3 1.1 collective-permute-done.5.refs_1_
  21.4 1.6 %collective-permute-start.13 = (s32[64]{0:T(128)S(1)}, s32[64]{0:T(128)S(1)}, u32[]{:S(2)}, u32[]{:S(2)}) collective-permute-start(s32[64]{0:T(128)S(1)} %bitcast_add_fusion), channel_id=1, source_target_pairs={{0,12},{4,8},{8,4},{12,0},{16,28},{20,24},{24,20},{28,16},{1,13},{... | collective-permute-start | bytes 776 | tf_op jit(solution)/shard_map/ppermute | solution.py:24
  23.0 0.4 collective-permute-start.12
  23.4 1.5 %collective-permute-start.11 = (s32[64]{0:T(128)S(1)}, s32[64]{0:T(128)S(1)}, u32[]{:S(2)}, u32[]{:S(2)}) collective-permute-start(s32[64]{0:T(128)S(1)} %bitcast_add_fusion), channel_id=1, source_target_pairs={{0,4},{4,0},{8,12},{12,8},{16,20},{20,16},{24,28},{28,24},{1,5},{5... | collective-permute-start | bytes 776 | tf_op jit(solution)/shard_map/ppermute | solution.py:24
  24.9 2.1 %collective-permute-done.13 = s32[64]{0:T(128)S(1)} collective-permute-done((s32[64]{0:T(128)S(1)}, s32[64]{0:T(128)S(1)}, u32[]{:S(2)}, u32[]{:S(2)}) %collective-permute-start.13) | collective-permute-done | bytes 288 | tf_op jit(solution)/shard_map/ppermute | solution.py:24
  27.3 3.0 %collective-permute-start.14 = (s32[256]{0:T(256)S(1)}, s32[256]{0:T(256)S(1)}, u32[]{:S(2)}, u32[]{:S(2)}) collective-permute-start(s32[256]{0:T(256)S(1)} %pad_add_fusion), channel_id=1, source_target_pairs={{0,16},{4,20},{8,24},{12,28},{16,0},{20,4},{24,8},{28,12},{1,17},{... | collective-permute-start | bytes 3080 | tf_op jit(solution)/shard_map/ppermute | solution.py:24
  30.3 2.4 %collective-permute-start.2 = (bf16[16,128,128]{2,1,0:T(8,128)(2,1)}, bf16[16,128,128]{2,1,0:T(8,128)(2,1)}, u32[]{:S(2)}, u32[]{:S(2)}) collective-permute-start(bf16[16,128,128]{2,1,0:T(8,128)(2,1)} %collective-permute-done.1.refs_7_), channel_id=1, source_target_pairs={{0,8},{1,5},{2,10},{3,7},{8,16},{9,1},{10,18},{11,3},{16,24},{17,9... | collective-permute-start | bytes 1572872 | tf_op jit(solution)/shard_map/ppermute | solution.py:381
  32.7 1.1 collective-permute-start.10
  33.8 0.5 collective-permute-start.16
  34.3 0.7 pad_add_fusion.1.cols_ref
  35.2 4.5 %shard_map.55 = (s32[145]{0:T(256)S(1)}, s32[3]{0:T(128)S(1)}) custom-call(s32[128]{0:T(128)S(1)} %pad_add_fusion.1.cols_ref, s32[512]{0:T(512)S(1)} %concatenate.15.aggs_ref), custom_call_target="tpu_custom_call" | custom-call | flops 1048576 | bytes 16777216 | tf_op jit(solution)/shard_map/pallas_call | solution.py:142
  39.7 5.6 %collective-permute-done.2.refs_6_ = bf16[16,128,128]{2,1,0:T(8,128)(2,1)} collective-permute-done((bf16[16,128,128]{2,1,0:T(8,128)(2,1)}, bf16[16,128,128]{2,1,0:T(8,128)(2,1)}, u32[]{:S(2)}, u32[]{:S(2)}) %collective-permute-start.2) | collective-permute-done | bytes 524320 | tf_op jit(solution)/shard_map/ppermute | solution.py:381
  45.3 2.9 %shard_map.56.rows_ref = bf16[64,128,128]{2,1,0:T(8,128)(2,1)S(1)} custom-call(bf16[16,128,128]{2,1,0:T(8,128)(2,1)} %refs_2_.1, bf16[16,128,128]{2,1,0:T(8,128)(2,1)} %collective-permute-done.5.refs_1_, bf16[16,128,128]{2,1,0:T(8,128)(2,1)S(1)} %collective-permute-done.4.refs_2_.refs_9_, bf16[16,128,128]{2,1,0:T(8,128)(2,1)} %collective-permute-done.9.refs_3_), custom_call_target="tpu_custom_call" | custom-call | flops 1048576 | bytes 16777216 | tf_op jit(solution)/shard_map/pallas_call | solution.py:183
  48.2 0.5 collective-permute-start.21
  48.8 0.4 collective-permute-start.20
  49.3 2.5 %collective-permute-start.17 = (bf16[16,128,128]{2,1,0:T(8,128)(2,1)}, bf16[16,128,128]{2,1,0:T(8,128)(2,1)S(1)}, u32[]{:S(2)}, u32[]{:S(2)}) collective-permute-start(bf16[16,128,128]{2,1,0:T(8,128)(2,1)} %collective-permute-done.2.refs_6_), channel_id=1, source_target_pairs={{0,8},{1,5},{2,10},{3,7},{8,16},{9,1},{10,18},{11,3},{16,24},{17,9... | collective-permute-start | bytes 1572872 | tf_op jit(solution)/shard_map/ppermute | solution.py:381
  51.9 0.7 collective-permute-done.20.refs_13_
  52.6 6.0 %shard_map.57.slots_ref = bf16[144,128,128]{2,1,0:T(8,128)(2,1)S(1)} custom-call(s32[145]{0:T(256)S(1)} %get-tuple-element.55.plan_ref, s32[3]{0:T(128)S(1)} %get-tuple-element.56.starts_ref, bf16[64,128,128]{2,1,0:T(8,128)(2,1)} %bitcast.155, bf16[64,128,128]{2,1,0:T(8,128)(2,1)S(1)} %collective-permute-done.3.refs_1_, bf16[16,128,128]{2,1,0:T(8,128)(2,1)} %refs_2_.1, ...), custom_call_target="tpu_custom_call" | custom-call | flops 268435456 | bytes 1048576 | tf_op jit(solution)/shard_map/pallas_call | solution.py:243
  58.8 1.9 %collective-permute-done.22.far1 = bf16[16,128,128]{2,1,0:T(8,128)(2,1)S(1)} collective-permute-done((bf16[16,128,128]{2,1,0:T(8,128)(2,1)S(1)}, bf16[16,128,128]{2,1,0:T(8,128)(2,1)S(1)}, u32[]{:S(2)}, u32[]{:S(2)}) %collective-permute-start.22) | collective-permute-done | bytes 524320 | tf_op jit(solution)/shard_map/ppermute | solution.py:24
  60.7 4.2 %shard_map.58 = (bf16[2,2,2,1,1,336,128]{6,5,4,3,2,1,0:T(8,128)(2,1)S(1)}, f32[2,2,2,1,1,336,128]{6,5,4,3,2,1,0:T(8,128)S(1)}, bf16[2,2,2,1,1,336,128]{6,5,4,3,2...) custom-call(s32[145]{0:T(256)S(1)} %get-tuple-element.55.plan_ref, ...), custom_call_target="tpu_custom_call" | custom-call | flops 268435456 | bytes 16777216 | tf_op jit(solution)/shard_map/pallas_call | solution.py:349
  64.9 2.6 %collective-permute-start.23 = (bf16[2,2,2,1,1,336,128]{6,5,2,4,3,1,0:T(8,128)(2,1)S(1)}, bf16[2,2,2,1,1,336,128]{6,5,2,4,3,1,0:T(8,128)(2,1)S(1)}, u32[]{:S(2)}, u32[]{:S(2)}) collective-permute-start(bf16[2,2,2,1,1,336,128]{6,5,2,4,3,1,0:T(8,128)(2,1)S(1)} %bitcast.153), channel_id=1, source_target_pairs={{0,8},{1,3},{2,10},{3,1},{4,12},{5,7},{6,14},{7,5},{8,0},{9,11},{1... | collective-permute-start | bytes 2064392 | tf_op jit(solution)/shard_map/ppermute | solution.py:35
  67.5 1.8 %collective-permute-start.27 = (bf16[2,2,2,1,1,336,128]{6,5,2,4,3,1,0:T(8,128)(2,1)S(1)}, bf16[2,2,2,1,1,336,128]{6,5,2,4,3,1,0:T(8,128)(2,1)S(1)}, u32[]{:S(2)}, u32[]{:S(2)}) collective-permute-start(bf16[2,2,2,1,1,336,128]{6,5,2,4,3,1,0:T(8,128)(2,1)S(1)} %bitcast.152), channel_id=1, source_target_pairs={{0,2},{1,5},{2,0},{3,7},{4,6},{5,1},{6,4},{7,3},{8,10},{9,13},{10,... | collective-permute-start | bytes 2064392 | tf_op jit(solution)/shard_map/ppermute | solution.py:35
  69.3 1.0 collective-permute-start.31
  70.2 14.7 %collective-permute-done.23 = bf16[2,2,2,1,1,336,128]{6,5,2,4,3,1,0:T(8,128)(2,1)S(1)} collective-permute-done((bf16[2,2,2,1,1,336,128]{6,5,2,4,3,1,0:T(8,128)(2,1)S(1)}, bf16[2,2,2,1,1,336,128]{6,5,2,4,3,1,0:T(8,128)(2,1)S(1)}, u32[]{:S(2)}, u32[]{:S(2)}) %collective-permute-start.23) | collective-permute-done | bytes 688160 | tf_op jit(solution)/shard_map/ppermute | solution.py:35
  85.1 1.9 %collective-permute-start.24 = (bf16[2,2,1,1,336,128]{5,4,3,2,1,0:T(8,128)(2,1)S(1)}, bf16[2,2,1,1,336,128]{5,4,3,2,1,0:T(8,128)(2,1)S(1)}, u32[]{:S(2)}, u32[]{:S(2)}) collective-permute-start(bf16[2,2,1,1,336,128]{5,4,3,2,1,0:T(8,128)(2,1)S(1)} %get-tuple-element.73), channel_id=1, source_target_pairs={{0,2},{1,9},{2,0},{3,11},{4,6},{5,13},{6,4},{7,15},{8,10},{9,1},{1... | collective-permute-start | bytes 1032200 | tf_op jit(solution)/shard_map/ppermute | solution.py:35
  87.4 1.8 %collective-permute-start.32 = (bf16[2,2,1,1,352,128]{5,4,1,0,3,2:T(8,128)(2,1)S(1)}, bf16[2,2,1,1,352,128]{5,4,1,0,3,2:T(8,128)(2,1)S(1)}, u32[]{:S(2)}, u32[]{:S(2)}) collective-permute-start(bf16[2,2,1,1,352,128]{5,4,1,0,3,2:T(8,128)(2,1)S(1)} %fusion.3), channel_id=1, source_target_pairs={{0,8},{1,3},{2,10},{3,1},{4,12},{5,7},{6,14},{7,5},{8,0},{9,11},{1... | collective-permute-start | bytes 1081352 | tf_op jit(solution)/shard_map/ppermute | solution.py:35
  89.2 6.5 %collective-permute-done.24 = bf16[2,2,1,1,336,128]{5,4,3,2,1,0:T(8,128)(2,1)S(1)} collective-permute-done((bf16[2,2,1,1,336,128]{5,4,3,2,1,0:T(8,128)(2,1)S(1)}, bf16[2,2,1,1,336,128]{5,4,3,2,1,0:T(8,128)(2,1)S(1)}, u32[]{:S(2)}, u32[]{:S(2)}) %collective-permute-start.24) | collective-permute-done | bytes 344096 | tf_op jit(solution)/shard_map/ppermute | solution.py:35
  95.8 0.5 collective-permute-start.25
  96.3 0.2 collective-permute-start.29
  96.7 1.4 %collective-permute-start.33 = (bf16[2,1,1,352,128]{4,3,0,2,1:T(8,128)(2,1)S(1)}, bf16[2,1,1,352,128]{4,3,0,2,1:T(8,128)(2,1)S(1)}, u32[]{:S(2)}, u32[]{:S(2)}) collective-permute-start(bf16[2,1,1,352,128]{4,3,0,2,1:T(8,128)(2,1)S(1)} %fusion.15), channel_id=1, source_target_pairs={{0,2},{1,5},{2,0},{3,7},{4,6},{5,1},{6,4},{7,3},{8,10},{9,13},{10,... | collective-permute-start | bytes 540680 | tf_op jit(solution)/shard_map/ppermute | solution.py:35
  98.2 7.8 %collective-permute-done.25 = bf16[2,1,1,336,128]{4,3,2,1,0:T(8,128)(2,1)S(1)} collective-permute-done((bf16[2,1,1,336,128]{4,3,2,1,0:T(8,128)(2,1)S(1)}, bf16[2,1,1,336,128]{4,3,2,1,0:T(8,128)(2,1)S(1)}, u32[]{:S(2)}, u32[]{:S(2)}) %collective-permute-start.25) | collective-permute-done | bytes 172064 | tf_op jit(solution)/shard_map/ppermute | solution.py:35
  105.9 0.7 collective-permute-start.26
  106.7 0.7 collective-permute-start.30
  107.5 2.3 %collective-permute-start.34 = (bf16[1,1,352,128]{3,2,1,0:T(8,128)(2,1)S(1)}, bf16[1,1,352,128]{3,2,1,0:T(8,128)(2,1)S(1)}, u32[]{:S(2)}, u32[]{:S(2)}) collective-permute-start(bf16[1,1,352,128]{3,2,1,0:T(8,128)(2,1)S(1)} %fusion.33), channel_id=1, source_target_pairs={{0,16},{1,9},{2,18},{3,11},{4,20},{5,13},{6,22},{7,15},{8,24},{9,1... | collective-permute-start | bytes 270344 | tf_op jit(solution)/shard_map/ppermute | solution.py:35
  109.8 0.7 collective-permute-done.26
  110.5 1.7 %collective-permute-done.30 = bf16[1,1,336,128]{3,2,1,0:T(8,128)(2,1)S(1)} collective-permute-done((bf16[1,1,336,128]{3,2,1,0:T(8,128)(2,1)S(1)}, bf16[1,1,336,128]{3,2,1,0:T(8,128)(2,1)S(1)}, u32[]{:S(2)}, u32[]{:S(2)}) %collective-permute-start.30) | collective-permute-done | bytes 86048 | tf_op jit(solution)/shard_map/ppermute | solution.py:35
  112.2 1.9 %collective-permute-done.34 = bf16[1,1,352,128]{3,2,1,0:T(8,128)(2,1)S(1)} collective-permute-done((bf16[1,1,352,128]{3,2,1,0:T(8,128)(2,1)S(1)}, bf16[1,1,352,128]{3,2,1,0:T(8,128)(2,1)S(1)}, u32[]{:S(2)}, u32[]{:S(2)}) %collective-permute-start.34) | collective-permute-done | bytes 90144 | tf_op jit(solution)/shard_map/ppermute | solution.py:35
  114.1 0.8 pad_maximum_fusion
  (45 shorter events, 1.9 us)
Async XLA Ops:
  0.0 21.4 %collective-permute-start.3 = (bf16[64,128,128]{2,1,0:T(8,128)(2,1)}, bf16[64,128,128]{2,1,0:T(8,128)(2,1)S(1)}, u32[]{:S(2)}, u32[]{:S(2)}) collective-permute-start(bf16[64,128,128]{2,1,0:T(8,128)(2,1)} %bitcast.154), channel_id=1, source_target_pairs={{0,1},{1,0},{2,3},{3,2},{4,5},{5,4},{6,7},{7,6},{8,9},{9,8},{10,11... | collective-permute-start | bytes 6291464 | tf_op jit(solution)/shard_map/ppermute | solution.py:24
  0.5 4.0 %collective-permute-start.6 = (s32[64]{0:T(128)}, s32[64]{0:T(128)S(1)}, u32[]{:S(2)}, u32[]{:S(2)}) collective-permute-start(s32[64]{0:T(128)} %bitcast.158), channel_id=1, source_target_pairs={{0,1},{1,0},{2,3},{3,2},{4,5},{5,4},{6,7},{7,6},{8,9},{9,8},{10,11... | collective-permute-start | bytes 776 | tf_op jit(solution)/shard_map/ppermute | solution.py:24
  0.5 12.6 %collective-permute-start = (bf16[16,128,128]{2,1,0:T(8,128)(2,1)}, bf16[16,128,128]{2,1,0:T(8,128)(2,1)S(1)}, u32[]{:S(2)}, u32[]{:S(2)}) collective-permute-start(bf16[16,128,128]{2,1,0:T(8,128)(2,1)} %refs_2_.1), channel_id=1, source_target_pairs={{0,8},{1,5},{2,10},{3,7},{8,16},{9,1},{10,18},{11,3},{16,24},{17,9... | collective-permute-start | bytes 1572872 | tf_op jit(solution)/shard_map/ppermute | solution.py:381
  4.5 13.2 %collective-permute-start.7 = (bf16[16,128,128]{2,1,0:T(8,128)(2,1)}, bf16[16,128,128]{2,1,0:T(8,128)(2,1)}, u32[]{:S(2)}, u32[]{:S(2)}) collective-permute-start(bf16[16,128,128]{2,1,0:T(8,128)(2,1)} %refs_2_.1), channel_id=1, source_target_pairs={{0,4},{1,9},{2,6},{3,11},{8,0},{9,17},{10,2},{11,19},{16,8},{17,25... | collective-permute-start | bytes 1572872 | tf_op jit(solution)/shard_map/ppermute | solution.py:381
  7.3 14.1 %collective-permute-start.5 = (bf16[16,128,128]{2,1,0:T(8,128)(2,1)}, bf16[16,128,128]{2,1,0:T(8,128)(2,1)}, u32[]{:S(2)}, u32[]{:S(2)}) collective-permute-start(bf16[16,128,128]{2,1,0:T(8,128)(2,1)} %refs_2_.1), channel_id=1, source_target_pairs={{0,2},{1,3},{2,0},{3,1},{4,6},{5,7},{6,4},{7,5},{8,10},{9,11},{10,... | collective-permute-start | bytes 1572872 | tf_op jit(solution)/shard_map/ppermute | solution.py:24
  8.8 12.6 %collective-permute-start.4 = (bf16[16,128,128]{2,1,0:T(8,128)(2,1)}, bf16[16,128,128]{2,1,0:T(8,128)(2,1)S(1)}, u32[]{:S(2)}, u32[]{:S(2)}) collective-permute-start(bf16[16,128,128]{2,1,0:T(8,128)(2,1)} %refs_2_.1), channel_id=1, source_target_pairs={{0,1},{1,0},{2,3},{3,2},{4,5},{5,4},{6,7},{7,6},{8,9},{9,8},{10,11... | collective-permute-start | bytes 1572872 | tf_op jit(solution)/shard_map/ppermute | solution.py:24
  13.1 17.2 %collective-permute-start.1 = (bf16[16,128,128]{2,1,0:T(8,128)(2,1)S(1)}, bf16[16,128,128]{2,1,0:T(8,128)(2,1)}, u32[]{:S(2)}, u32[]{:S(2)}) collective-permute-start(bf16[16,128,128]{2,1,0:T(8,128)(2,1)S(1)} %collective-permute-done.refs_8_), channel_id=1, source_target_pairs={{0,8},{1,5},{2,10},{3,7},{8,16},{9,1},{10,18},{11,3},{16,24},{17,9... | collective-permute-start | bytes 1572872 | tf_op jit(solution)/shard_map/ppermute | solution.py:381
  17.7 15.0 %collective-permute-start.8 = (bf16[16,128,128]{2,1,0:T(8,128)(2,1)}, bf16[16,128,128]{2,1,0:T(8,128)(2,1)}, u32[]{:S(2)}, u32[]{:S(2)}) collective-permute-start(bf16[16,128,128]{2,1,0:T(8,128)(2,1)} %collective-permute-done.7.refs_3_), channel_id=1, source_target_pairs={{0,4},{1,9},{2,6},{3,11},{8,0},{9,17},{10,2},{11,19},{16,8},{17,25... | collective-permute-start | bytes 1572872 | tf_op jit(solution)/shard_map/ppermute | solution.py:381
  21.4 5.6 %collective-permute-start.13 = (s32[64]{0:T(128)S(1)}, s32[64]{0:T(128)S(1)}, u32[]{:S(2)}, u32[]{:S(2)}) collective-permute-start(s32[64]{0:T(128)S(1)} %bitcast_add_fusion), channel_id=1, source_target_pairs={{0,12},{4,8},{8,4},{12,0},{16,28},{20,24},{24,20},{28,16},{1,13},{... | collective-permute-start | bytes 776 | tf_op jit(solution)/shard_map/ppermute | solution.py:24
  23.0 4.2 %collective-permute-start.12 = (s32[64]{0:T(128)S(1)}, s32[64]{0:T(128)S(1)}, u32[]{:S(2)}, u32[]{:S(2)}) collective-permute-start(s32[64]{0:T(128)S(1)} %bitcast_add_fusion), channel_id=1, source_target_pairs={{0,8},{4,12},{8,0},{12,4},{16,24},{20,28},{24,16},{28,20},{1,9},{5... | collective-permute-start | bytes 776 | tf_op jit(solution)/shard_map/ppermute | solution.py:24
  23.4 3.8 %collective-permute-start.11 = (s32[64]{0:T(128)S(1)}, s32[64]{0:T(128)S(1)}, u32[]{:S(2)}, u32[]{:S(2)}) collective-permute-start(s32[64]{0:T(128)S(1)} %bitcast_add_fusion), channel_id=1, source_target_pairs={{0,4},{4,0},{8,12},{12,8},{16,20},{20,16},{24,28},{28,24},{1,5},{5... | collective-permute-start | bytes 776 | tf_op jit(solution)/shard_map/ppermute | solution.py:24
  27.3 6.6 %collective-permute-start.14 = (s32[256]{0:T(256)S(1)}, s32[256]{0:T(256)S(1)}, u32[]{:S(2)}, u32[]{:S(2)}) collective-permute-start(s32[256]{0:T(256)S(1)} %pad_add_fusion), channel_id=1, source_target_pairs={{0,16},{4,20},{8,24},{12,28},{16,0},{20,4},{24,8},{28,12},{1,17},{... | collective-permute-start | bytes 3080 | tf_op jit(solution)/shard_map/ppermute | solution.py:24
  30.3 15.0 %collective-permute-start.2 = (bf16[16,128,128]{2,1,0:T(8,128)(2,1)}, bf16[16,128,128]{2,1,0:T(8,128)(2,1)}, u32[]{:S(2)}, u32[]{:S(2)}) collective-permute-start(bf16[16,128,128]{2,1,0:T(8,128)(2,1)} %collective-permute-done.1.refs_7_), channel_id=1, source_target_pairs={{0,8},{1,5},{2,10},{3,7},{8,16},{9,1},{10,18},{11,3},{16,24},{17,9... | collective-permute-start | bytes 1572872 | tf_op jit(solution)/shard_map/ppermute | solution.py:381
  32.7 12.5 %collective-permute-start.9 = (bf16[16,128,128]{2,1,0:T(8,128)(2,1)}, bf16[16,128,128]{2,1,0:T(8,128)(2,1)}, u32[]{:S(2)}, u32[]{:S(2)}) collective-permute-start(bf16[16,128,128]{2,1,0:T(8,128)(2,1)} %collective-permute-done.5.refs_1_), channel_id=1, source_target_pairs={{0,1},{1,0},{2,3},{3,2},{4,5},{5,4},{6,7},{7,6},{8,9},{9,8},{10,11... | collective-permute-start | bytes 1572872 | tf_op jit(solution)/shard_map/ppermute | solution.py:24
  32.7 15.4 %collective-permute-start.10 = (bf16[16,128,128]{2,1,0:T(8,128)(2,1)}, bf16[16,128,128]{2,1,0:T(8,128)(2,1)}, u32[]{:S(2)}, u32[]{:S(2)}) collective-permute-start(bf16[16,128,128]{2,1,0:T(8,128)(2,1)} %collective-permute-done.8.refs_4_), channel_id=1, source_target_pairs={{0,4},{1,9},{2,6},{3,11},{8,0},{9,17},{10,2},{11,19},{16,8},{17,25... | collective-permute-start | bytes 1572872 | tf_op jit(solution)/shard_map/ppermute | solution.py:381
  33.8 14.3 %collective-permute-start.15 = (bf16[16,128,128]{2,1,0:T(8,128)(2,1)}, bf16[16,128,128]{2,1,0:T(8,128)(2,1)}, u32[]{:S(2)}, u32[]{:S(2)}) collective-permute-start(bf16[16,128,128]{2,1,0:T(8,128)(2,1)} %collective-permute-done.7.refs_3_), channel_id=1, source_target_pairs={{0,1},{1,0},{2,3},{3,2},{4,5},{5,4},{6,7},{7,6},{8,9},{9,8},{10,11... | collective-permute-start | bytes 1572872 | tf_op jit(solution)/shard_map/ppermute | solution.py:24
  33.8 14.3 %collective-permute-start.16 = (bf16[16,128,128]{2,1,0:T(8,128)(2,1)S(1)}, bf16[16,128,128]{2,1,0:T(8,128)(2,1)}, u32[]{:S(2)}, u32[]{:S(2)}) collective-permute-start(bf16[16,128,128]{2,1,0:T(8,128)(2,1)S(1)} %collective-permute-done.refs_8_), channel_id=1, source_target_pairs={{0,1},{1,0},{2,3},{3,2},{4,5},{5,4},{6,7},{7,6},{8,9},{9,8},{10,11... | collective-permute-start | bytes 1572872 | tf_op jit(solution)/shard_map/ppermute | solution.py:24
  48.2 3.6 %collective-permute-start.18 = (bf16[16,128,128]{2,1,0:T(8,128)(2,1)}, bf16[16,128,128]{2,1,0:T(8,128)(2,1)S(1)}, u32[]{:S(2)}, u32[]{:S(2)}) collective-permute-start(bf16[16,128,128]{2,1,0:T(8,128)(2,1)} %collective-permute-done.8.refs_4_), channel_id=1, source_target_pairs={{0,1},{1,0},{2,3},{3,2},{4,5},{5,4},{6,7},{7,6},{8,9},{9,8},{10,11... | collective-permute-start | bytes 1572872 | tf_op jit(solution)/shard_map/ppermute | solution.py:24
  48.2 3.5 %collective-permute-start.21 = (bf16[16,128,128]{2,1,0:T(8,128)(2,1)}, bf16[16,128,128]{2,1,0:T(8,128)(2,1)S(1)}, u32[]{:S(2)}, u32[]{:S(2)}) collective-permute-start(bf16[16,128,128]{2,1,0:T(8,128)(2,1)} %collective-permute-done.1.refs_7_), channel_id=1, source_target_pairs={{0,1},{1,0},{2,3},{3,2},{4,5},{5,4},{6,7},{7,6},{8,9},{9,8},{10,11... | collective-permute-start | bytes 1572872 | tf_op jit(solution)/shard_map/ppermute | solution.py:24
  48.7 3.1 %collective-permute-start.19 = (bf16[16,128,128]{2,1,0:T(8,128)(2,1)}, bf16[16,128,128]{2,1,0:T(8,128)(2,1)S(1)}, u32[]{:S(2)}, u32[]{:S(2)}) collective-permute-start(bf16[16,128,128]{2,1,0:T(8,128)(2,1)} %collective-permute-done.10.refs_5_), channel_id=1, source_target_pairs={{0,1},{1,0},{2,3},{3,2},{4,5},{5,4},{6,7},{7,6},{8,9},{9,8},{10,11... | collective-permute-start | bytes 1572872 | tf_op jit(solution)/shard_map/ppermute | solution.py:24
  48.8 3.8 %collective-permute-start.20 = (bf16[16,128,128]{2,1,0:T(8,128)(2,1)}, bf16[16,128,128]{2,1,0:T(8,128)(2,1)S(1)}, u32[]{:S(2)}, u32[]{:S(2)}) collective-permute-start(bf16[16,128,128]{2,1,0:T(8,128)(2,1)} %collective-permute-done.2.refs_6_), channel_id=1, source_target_pairs={{0,1},{1,0},{2,3},{3,2},{4,5},{5,4},{6,7},{7,6},{8,9},{9,8},{10,11... | collective-permute-start | bytes 1572872 | tf_op jit(solution)/shard_map/ppermute | solution.py:24
  49.3 9.5 %collective-permute-start.17 = (bf16[16,128,128]{2,1,0:T(8,128)(2,1)}, bf16[16,128,128]{2,1,0:T(8,128)(2,1)S(1)}, u32[]{:S(2)}, u32[]{:S(2)}) collective-permute-start(bf16[16,128,128]{2,1,0:T(8,128)(2,1)} %collective-permute-done.2.refs_6_), channel_id=1, source_target_pairs={{0,8},{1,5},{2,10},{3,7},{8,16},{9,1},{10,18},{11,3},{16,24},{17,9... | collective-permute-start | bytes 1572872 | tf_op jit(solution)/shard_map/ppermute | solution.py:381
  58.8 1.9 %collective-permute-start.22 = (bf16[16,128,128]{2,1,0:T(8,128)(2,1)S(1)}, bf16[16,128,128]{2,1,0:T(8,128)(2,1)S(1)}, u32[]{:S(2)}, u32[]{:S(2)}) collective-permute-start(bf16[16,128,128]{2,1,0:T(8,128)(2,1)S(1)} %collective-permute-done.17.far0), channel_id=1, source_target_pairs={{0,1},{1,0},{2,3},{3,2},{4,5},{5,4},{6,7},{7,6},{8,9},{9,8},{10,11... | collective-permute-start | bytes 1572872 | tf_op jit(solution)/shard_map/ppermute | solution.py:24
  64.9 20.1 %collective-permute-start.23 = (bf16[2,2,2,1,1,336,128]{6,5,2,4,3,1,0:T(8,128)(2,1)S(1)}, bf16[2,2,2,1,1,336,128]{6,5,2,4,3,1,0:T(8,128)(2,1)S(1)}, u32[]{:S(2)}, u32[]{:S(2)}) collective-permute-start(bf16[2,2,2,1,1,336,128]{6,5,2,4,3,1,0:T(8,128)(2,1)S(1)} %bitcast.153), channel_id=1, source_target_pairs={{0,8},{1,3},{2,10},{3,1},{4,12},{5,7},{6,14},{7,5},{8,0},{9,11},{1... | collective-permute-start | bytes 2064392 | tf_op jit(solution)/shard_map/ppermute | solution.py:35
  67.5 19.5 %collective-permute-start.27 = (bf16[2,2,2,1,1,336,128]{6,5,2,4,3,1,0:T(8,128)(2,1)S(1)}, bf16[2,2,2,1,1,336,128]{6,5,2,4,3,1,0:T(8,128)(2,1)S(1)}, u32[]{:S(2)}, u32[]{:S(2)}) collective-permute-start(bf16[2,2,2,1,1,336,128]{6,5,2,4,3,1,0:T(8,128)(2,1)S(1)} %bitcast.152), channel_id=1, source_target_pairs={{0,2},{1,5},{2,0},{3,7},{4,6},{5,1},{6,4},{7,3},{8,10},{9,13},{10,... | collective-permute-start | bytes 2064392 | tf_op jit(solution)/shard_map/ppermute | solution.py:35
  69.3 18.0 %collective-permute-start.31 = (bf16[2,2,2,1,1,352,128]{6,5,2,4,3,1,0:T(8,128)(2,1)S(1)}, bf16[2,2,2,1,1,352,128]{6,5,2,4,3,1,0:T(8,128)(2,1)S(1)}, u32[]{:S(2)}, u32[]{:S(2)}) collective-permute-start(bf16[2,2,2,1,1,352,128]{6,5,2,4,3,1,0:T(8,128)(2,1)S(1)} %bitcast.151), channel_id=1, source_target_pairs={{0,4},{1,17},{2,6},{3,19},{4,0},{5,21},{6,2},{7,23},{8,12},{9,25},... | collective-permute-start | bytes 2162696 | tf_op jit(solution)/shard_map/ppermute | solution.py:35
  85.1 10.6 %collective-permute-start.24 = (bf16[2,2,1,1,336,128]{5,4,3,2,1,0:T(8,128)(2,1)S(1)}, bf16[2,2,1,1,336,128]{5,4,3,2,1,0:T(8,128)(2,1)S(1)}, u32[]{:S(2)}, u32[]{:S(2)}) collective-permute-start(bf16[2,2,1,1,336,128]{5,4,3,2,1,0:T(8,128)(2,1)S(1)} %get-tuple-element.73), channel_id=1, source_target_pairs={{0,2},{1,9},{2,0},{3,11},{4,6},{5,13},{6,4},{7,15},{8,10},{9,1},{1... | collective-permute-start | bytes 1032200 | tf_op jit(solution)/shard_map/ppermute | solution.py:35
  87.2 9.1 %collective-permute-start.28 = (bf16[2,2,1,1,336,128]{5,4,3,2,1,0:T(8,128)(2,1)S(1)}, bf16[2,2,1,1,336,128]{5,4,3,2,1,0:T(8,128)(2,1)S(1)}, u32[]{:S(2)}, u32[]{:S(2)}) collective-permute-start(bf16[2,2,1,1,336,128]{5,4,3,2,1,0:T(8,128)(2,1)S(1)} %get-tuple-element.75), channel_id=1, source_target_pairs={{0,4},{1,3},{2,6},{3,1},{4,0},{5,7},{6,2},{7,5},{8,12},{9,11},{10,... | collective-permute-start | bytes 1032200 | tf_op jit(solution)/shard_map/ppermute | solution.py:35
  87.4 9.3 %collective-permute-start.32 = (bf16[2,2,1,1,352,128]{5,4,1,0,3,2:T(8,128)(2,1)S(1)}, bf16[2,2,1,1,352,128]{5,4,1,0,3,2:T(8,128)(2,1)S(1)}, u32[]{:S(2)}, u32[]{:S(2)}) collective-permute-start(bf16[2,2,1,1,352,128]{5,4,1,0,3,2:T(8,128)(2,1)S(1)} %fusion.3), channel_id=1, source_target_pairs={{0,8},{1,3},{2,10},{3,1},{4,12},{5,7},{6,14},{7,5},{8,0},{9,11},{1... | collective-permute-start | bytes 1081352 | tf_op jit(solution)/shard_map/ppermute | solution.py:35
  95.8 10.1 %collective-permute-start.25 = (bf16[2,1,1,336,128]{4,3,2,1,0:T(8,128)(2,1)S(1)}, bf16[2,1,1,336,128]{4,3,2,1,0:T(8,128)(2,1)S(1)}, u32[]{:S(2)}, u32[]{:S(2)}) collective-permute-start(bf16[2,1,1,336,128]{4,3,2,1,0:T(8,128)(2,1)S(1)} %get-tuple-element.77), channel_id=1, source_target_pairs={{0,16},{1,5},{2,18},{3,7},{4,20},{5,1},{6,22},{7,3},{8,24},{9,13},... | collective-permute-start | bytes 516104 | tf_op jit(solution)/shard_map/ppermute | solution.py:35
  96.3 10.4 %collective-permute-start.29 = (bf16[2,1,1,336,128]{4,3,2,1,0:T(8,128)(2,1)S(1)}, bf16[2,1,1,336,128]{4,3,2,1,0:T(8,128)(2,1)S(1)}, u32[]{:S(2)}, u32[]{:S(2)}) collective-permute-start(bf16[2,1,1,336,128]{4,3,2,1,0:T(8,128)(2,1)S(1)} %get-tuple-element.79), channel_id=1, source_target_pairs={{0,8},{1,17},{2,10},{3,19},{4,12},{5,21},{6,14},{7,23},{8,0},{9,25... | collective-permute-start | bytes 516104 | tf_op jit(solution)/shard_map/ppermute | solution.py:35
  96.7 10.7 %collective-permute-start.33 = (bf16[2,1,1,352,128]{4,3,0,2,1:T(8,128)(2,1)S(1)}, bf16[2,1,1,352,128]{4,3,0,2,1:T(8,128)(2,1)S(1)}, u32[]{:S(2)}, u32[]{:S(2)}) collective-permute-start(bf16[2,1,1,352,128]{4,3,0,2,1:T(8,128)(2,1)S(1)} %fusion.15), channel_id=1, source_target_pairs={{0,2},{1,5},{2,0},{3,7},{4,6},{5,1},{6,4},{7,3},{8,10},{9,13},{10,... | collective-permute-start | bytes 540680 | tf_op jit(solution)/shard_map/ppermute | solution.py:35
  105.9 4.6 %collective-permute-start.26 = (bf16[1,1,336,128]{3,2,1,0:T(8,128)(2,1)S(1)}, bf16[1,1,336,128]{3,2,1,0:T(8,128)(2,1)S(1)}, u32[]{:S(2)}, u32[]{:S(2)}) collective-permute-start(bf16[1,1,336,128]{3,2,1,0:T(8,128)(2,1)S(1)} %fusion.34), channel_id=1, source_target_pairs={{0,4},{1,17},{2,6},{3,19},{4,0},{5,21},{6,2},{7,23},{8,12},{9,25},... | collective-permute-start | bytes 258056 | tf_op jit(solution)/shard_map/ppermute | solution.py:35
  106.7 5.5 %collective-permute-start.30 = (bf16[1,1,336,128]{3,2,1,0:T(8,128)(2,1)S(1)}, bf16[1,1,336,128]{3,2,1,0:T(8,128)(2,1)S(1)}, u32[]{:S(2)}, u32[]{:S(2)}) collective-permute-start(bf16[1,1,336,128]{3,2,1,0:T(8,128)(2,1)S(1)} %fusion.35), channel_id=1, source_target_pairs={{0,16},{1,9},{2,18},{3,11},{4,20},{5,13},{6,22},{7,15},{8,24},{9,1... | collective-permute-start | bytes 258056 | tf_op jit(solution)/shard_map/ppermute | solution.py:35
  107.5 6.6 %collective-permute-start.34 = (bf16[1,1,352,128]{3,2,1,0:T(8,128)(2,1)S(1)}, bf16[1,1,352,128]{3,2,1,0:T(8,128)(2,1)S(1)}, u32[]{:S(2)}, u32[]{:S(2)}) collective-permute-start(bf16[1,1,352,128]{3,2,1,0:T(8,128)(2,1)S(1)} %fusion.33), channel_id=1, source_target_pairs={{0,16},{1,9},{2,18},{3,11},{4,20},{5,13},{6,22},{7,15},{8,24},{9,1... | collective-permute-start | bytes 270344 | tf_op jit(solution)/shard_map/ppermute | solution.py:35

commit v7 on v6

--- a/solution.py
+++ b/solution.py
@@ -11,7 +11,7 @@
 
 OWN = 2
 UNROLL = 8
-ORDERS = (("1x2y", "x1y2"), ("xy12", "yx21"), ("y1x2", "2xy1"))
+ORDERS = (("yx21", "1yx2"), ("xy12", "x1y2"), ("2xy1", "y1x2"))
 LINKS = {"x": ("col", 2), "y": ("row", 1), "1": ("row", 2), "2": ("row", 4)}
 
 
@@ -188,7 +188,7 @@
         out_shape=jax.ShapeDtypeStruct(*shape),
         scratch_shapes=[pltpu.VMEM(*shape), pltpu.SemaphoreType.DMA((s.cols,))],
         compiler_params=pltpu.CompilerParams(vmem_limit_bytes=room(shape, shape)),
-        cost_estimate=pl.CostEstimate(flops=1 << 20, bytes_accessed=16 << 20, transcendentals=0),
+        cost_estimate=pl.CostEstimate(flops=0, bytes_accessed=0, transcendentals=0),
     )(own, *rows[1:])
 
 
@@ -386,23 +386,22 @@
     cols_other, mine = barrier((cols_other, p_tiles))
     second = ring(mine, 1)
     a_other, p_other = swap(a_blocks[:, 0], "col", 1), swap(p_tiles, "col", 1)
-    rows = [p_tiles]
+
+    aggs = owner[:, 0] * OWN + agg_local
+    came, aggs, a_other, p_other = barrier((first, aggs, a_other, p_other))
+    first = ring(first, 0)
+    aggs = [aggs] + [swap(aggs, "row", mask) for mask in (1, 2, 3)]
+    own_near, other_near = {0: p_tiles, s.rows - 1: came, 1: second}, {0: p_other}
+    second = ring(second, 1)
+    aggs, mine = barrier((jnp.concatenate(aggs, 0), p_tiles))
+    bit = 4
+    while bit < s.rows:
+        aggs = jnp.concatenate([aggs, swap(aggs, "row", bit)], 0)
+        bit *= 2
+    rows = [mine]
     bit = 2
     while bit < s.cols:
         rows += [swap(piece, "col", bit) for piece in rows]
-        bit *= 2
-
-    aggs = owner[:, 0] * OWN + agg_local
-    aggs, a_other, p_other, came, *rows[1:] = barrier(
-        (aggs, a_other, p_other, first, *rows[1:])
-    )
-    own_near, other_near = {0: p_tiles, s.rows - 1: came, 1: second}, {0: p_other}
-    first, second = ring(first, 0), ring(second, 1)
-    aggs = [aggs] + [swap(aggs, "row", mask) for mask in (1, 2, 3)]
-    aggs = jnp.concatenate(aggs, 0)
-    bit = 4
-    while bit < s.rows:
-        aggs = jnp.concatenate([aggs, swap(aggs, "row", bit)], 0)
         bit *= 2
     plan, starts = make_plan(s, jnp.concatenate([cols, cols_other], 0), aggs)
 
@@ -418,8 +417,7 @@
         held = [step, s.rows - step]
 
     others = sorted(set(other_near) - {0})
-    first, *rest = barrier((first, *rows[1:]))
-    rows_t = turn_rows(s, [p_tiles, *rest])
+    rows_t = turn_rows(s, rows)
     tie = (first, second, plan, starts, rows_t)
     tie += (*(own_near[away] for away in held), *(other_near[away] for away in others))
     first, second, plan, starts, rows_t, *rest = barrier(tie)

time: 115 us -> 107 us (0.930)
  waiting for transfers between devices: 52.7 us -> 48 us
  Pallas kernels: 17.6 us -> 15.2 us
    ppermute x12, waiting for transfers between devices: 33.4 us -> 27.4 us  [exchange(): return lax.ppermute(value, ('row', 'col'), moves)]
    ppermute x7, starting transfers between devices: 16.2 us -> 11.4 us  [ring(): return lax.ppermute(value, ('row', 'col'), moves)]
    ppermute x7, waiting for transfers between devices: 12.2 us -> 14.9 us  [ring(): return lax.ppermute(value, ('row', 'col'), moves)]
    ppermute x16, starting transfers between devices: 10.1 us -> 12.3 us  [swap(): return lax.ppermute(value, axis, [(i, i ^ bit) for i in range(size)])]
    ppermute x12, starting transfers between devices: 15 us -> 16.8 us  [exchange(): return lax.ppermute(value, ('row', 'col'), moves)]
    pallas_call x1, Pallas kernels: 5.97 us -> 4.21 us  [make_products(): pl.pallas_call(functools.partial(product_kernel, s), in_specs=[smem, smem...]
    ppermute x16, waiting for transfers between devices: 7.08 us -> 5.67 us  [swap(): return lax.ppermute(value, axis, [(i, i ^ bit) for i in range(size)])]
  transfers between devices with their start and end apart: 35 -> 35, of which waited for: 18 -> 18; matrix products, arithmetic and copies ran while one was open for 2% -> 2% of each run, Pallas kernels for 12% -> 11%
where the time goes in v7:
time: 107 us
  waiting for transfers between devices  48 us (45%)
  starting transfers between devices  40.5 us (38%)
  Pallas kernels  15.2 us (14%)
  other arithmetic  3.11 us (3%)
    ppermute x12, waiting for transfers between devices, exchange(): return lax.ppermute(value, ('row', 'col'), moves)  27.4 us
    ppermute x12, starting transfers between devices, exchange(): return lax.ppermute(value, ('row', 'col'), moves)  16.8 us
    ppermute x7, waiting for transfers between devices, ring(): return lax.ppermute(value, ('row', 'col'), moves)  14.9 us
    ppermute x16, starting transfers between devices, swap(): return lax.ppermute(value, axis, [(i, i ^ bit) for i in range(size)])  12.3 us
    ppermute x7, starting transfers between devices, ring(): return lax.ppermute(value, ('row', 'col'), moves)  11.4 us
    ppermute x16, waiting for transfers between devices, swap(): return lax.ppermute(value, axis, [(i, i ^ bit) for i in range(size)])  5.67 us
    pallas_call x1, Pallas kernels, make_plan(): pl.pallas_call(functools.partial(plan_kernel, s), in_specs=[smem, smem],...  4.54 us
    pallas_call x1, Pallas kernels, make_products(): pl.pallas_call(functools.partial(product_kernel, s), in_specs=[smem, smem...  4.21 us
  transfers between devices with their start and end apart: 35, of which 18 were waited for; matrix products, arithmetic and copies ran while one was open for 2% of the time, Pallas kernels for 11%

profile of v7, /device:TPU:0, one launch (start us, length us, event | category | flops | bytes accessed | tf_op | source)
XLA Modules:
  0.0 107.0 jit_solution(8257425500963457073)
XLA Ops:
  0.0 0.5 collective-permute-start.7
  0.5 0.5 collective-permute-start.8
  1.0 2.6 %collective-permute-start = (bf16[16,128,128]{2,1,0:T(8,128)(2,1)}, bf16[16,128,128]{2,1,0:T(8,128)(2,1)S(1)}, u32[]{:S(2)}, u32[]{:S(2)}) collective-permute-start(bf16[16,128,128]{2,1,0:T(8,128)(2,1)} %refs_2_.1), channel_id=1, source_target_pairs={{0,8},{1,5},{2,10},{3,7},{8,16},{9,1},{10,18},{11,3},{16,24},{17,9... | collective-permute-start | bytes 1572872 | tf_op jit(solution)/shard_map/ppermute | solution.py:381
  3.5 0.9 collective-permute-done.3
  4.5 2.9 %collective-permute-start.4 = (bf16[16,128,128]{2,1,0:T(8,128)(2,1)}, bf16[16,128,128]{2,1,0:T(8,128)(2,1)S(1)}, u32[]{:S(2)}, u32[]{:S(2)}) collective-permute-start(bf16[16,128,128]{2,1,0:T(8,128)(2,1)} %refs_2_.1), channel_id=1, source_target_pairs={{0,4},{1,9},{2,6},{3,11},{8,0},{9,17},{10,2},{11,19},{16,8},{17,25... | collective-permute-start | bytes 1572872 | tf_op jit(solution)/shard_map/ppermute | solution.py:381
  7.3 0.7 bitcast_add_fusion
  8.0 5.1 %collective-permute-done.refs_8_ = bf16[16,128,128]{2,1,0:T(8,128)(2,1)S(1)} collective-permute-done((bf16[16,128,128]{2,1,0:T(8,128)(2,1)}, bf16[16,128,128]{2,1,0:T(8,128)(2,1)S(1)}, u32[]{:S(2)}, u32[]{:S(2)}) %collective-permute-start) | collective-permute-done | bytes 524320 | tf_op jit(solution)/shard_map/ppermute | solution.py:381
  13.1 3.3 %collective-permute-start.11 = (s32[64]{0:T(128)S(1)}, s32[64]{0:T(128)S(1)}, u32[]{:S(2)}, u32[]{:S(2)}) collective-permute-start(s32[64]{0:T(128)S(1)} %bitcast_add_fusion), channel_id=1, source_target_pairs={{0,12},{4,8},{8,4},{12,0},{16,28},{20,24},{24,20},{28,16},{1,13},{... | collective-permute-start | bytes 776 | tf_op jit(solution)/shard_map/ppermute | solution.py:24
  16.4 0.4 collective-permute-start.10
  17.0 2.0 %collective-permute-start.1 = (bf16[16,128,128]{2,1,0:T(8,128)(2,1)S(1)}, bf16[16,128,128]{2,1,0:T(8,128)(2,1)S(1)}, u32[]{:S(2)}, u32[]{:S(2)}) collective-permute-start(bf16[16,128,128]{2,1,0:T(8,128)(2,1)S(1)} %collective-permute-done.refs_8_), channel_id=1, source_target_pairs={{0,8},{1,5},{2,10},{3,7},{8,16},{9,1},{10,18},{11,3},{16,24},{17,9... | collective-permute-start | bytes 1572872 | tf_op jit(solution)/shard_map/ppermute | solution.py:381
  19.0 1.0 collective-permute-done.10
  20.0 0.4 collective-permute-done.9
  20.5 1.5 %collective-permute-start.13 = (bf16[16,128,128]{2,1,0:T(8,128)(2,1)}, bf16[16,128,128]{2,1,0:T(8,128)(2,1)S(1)}, u32[]{:S(2)}, u32[]{:S(2)}) collective-permute-start(bf16[16,128,128]{2,1,0:T(8,128)(2,1)} %refs_2_.1), channel_id=1, source_target_pairs={{0,2},{1,3},{2,0},{3,1},{4,6},{5,7},{6,4},{7,5},{8,10},{9,11},{10,... | collective-permute-start | bytes 1572872 | tf_op jit(solution)/shard_map/ppermute | solution.py:24
  22.0 2.6 %collective-permute-start.12 = (s32[256]{0:T(256)S(1)}, s32[256]{0:T(256)S(1)}, u32[]{:S(2)}, u32[]{:S(2)}) collective-permute-start(s32[256]{0:T(256)S(1)} %pad_add_fusion.1), channel_id=1, source_target_pairs={{0,16},{4,20},{8,24},{12,28},{16,0},{20,4},{24,8},{28,12},{1,17},{... | collective-permute-start | bytes 3080 | tf_op jit(solution)/shard_map/ppermute | solution.py:24
  24.6 5.8 %collective-permute-done.1.refs_7_ = bf16[16,128,128]{2,1,0:T(8,128)(2,1)S(1)} collective-permute-done((bf16[16,128,128]{2,1,0:T(8,128)(2,1)S(1)}, bf16[16,128,128]{2,1,0:T(8,128)(2,1)S(1)}, u32[]{:S(2)}, u32[]{:S(2)}) %collective-permute-start.1) | collective-permute-done | bytes 524320 | tf_op jit(solution)/shard_map/ppermute | solution.py:381
  30.4 1.8 %collective-permute-start.2 = (bf16[16,128,128]{2,1,0:T(8,128)(2,1)S(1)}, bf16[16,128,128]{2,1,0:T(8,128)(2,1)S(1)}, u32[]{:S(2)}, u32[]{:S(2)}) collective-permute-start(bf16[16,128,128]{2,1,0:T(8,128)(2,1)S(1)} %collective-permute-done.1.refs_7_), channel_id=1, source_target_pairs={{0,8},{1,5},{2,10},{3,7},{8,16},{9,1},{10,18},{11,3},{16,24},{17,9... | collective-permute-start | bytes 1572872 | tf_op jit(solution)/shard_map/ppermute | solution.py:381
  32.5 1.5 %collective-permute-start.15 = (bf16[16,128,128]{2,1,0:T(8,128)(2,1)S(1)}, bf16[16,128,128]{2,1,0:T(8,128)(2,1)S(1)}, u32[]{:S(2)}, u32[]{:S(2)}) collective-permute-start(bf16[16,128,128]{2,1,0:T(8,128)(2,1)S(1)} %collective-permute-done.4.refs_3_), channel_id=1, source_target_pairs={{0,1},{1,0},{2,3},{3,2},{4,5},{5,4},{6,7},{7,6},{8,9},{9,8},{10,11... | collective-permute-start | bytes 1572872 | tf_op jit(solution)/shard_map/ppermute | solution.py:24
  34.1 0.7 pad_add_fusion.2.cols_ref
  34.8 4.5 %shard_map.55 = (s32[145]{0:T(256)S(1)}, s32[3]{0:T(128)S(1)}) custom-call(s32[128]{0:T(128)S(1)} %pad_add_fusion.2.cols_ref, s32[512]{0:T(512)S(1)} %pad_add_fusion.aggs_ref), custom_call_target="tpu_custom_call" | custom-call | flops 1048576 | bytes 16777216 | tf_op jit(solution)/shard_map/pallas_call | solution.py:142
  39.3 2.6 %shard_map.56.rows_ref = bf16[64,128,128]{2,1,0:T(8,128)(2,1)S(1)} custom-call(bf16[16,128,128]{2,1,0:T(8,128)(2,1)} %refs_2_.1, bf16[16,128,128]{2,1,0:T(8,128)(2,1)S(1)} %collective-permute-done.13.refs_1_, bf16[16,128,128]{2,1,0:T(8,128)(2,1)S(1)} %collective-permute-done.8.refs_2_.refs_9_, bf16[16,128,128]{2,1,0:T(8,128)(2,1)S(1)} %collective-permute-done.14.refs_3_), custom_call_target="tpu_custom_call" | custom-call | tf_op jit(solution)/shard_map/pallas_call | solution.py:183
  41.9 1.9 %collective-permute-done.2.refs_6_ = bf16[16,128,128]{2,1,0:T(8,128)(2,1)S(1)} collective-permute-done((bf16[16,128,128]{2,1,0:T(8,128)(2,1)S(1)}, bf16[16,128,128]{2,1,0:T(8,128)(2,1)S(1)}, u32[]{:S(2)}, u32[]{:S(2)}) %collective-permute-start.2) | collective-permute-done | bytes 524320 | tf_op jit(solution)/shard_map/ppermute | solution.py:381
  43.8 1.2 %collective-permute-start.18 = (bf16[16,128,128]{2,1,0:T(8,128)(2,1)S(1)}, bf16[16,128,128]{2,1,0:T(8,128)(2,1)S(1)}, u32[]{:S(2)}, u32[]{:S(2)}) collective-permute-start(bf16[16,128,128]{2,1,0:T(8,128)(2,1)S(1)} %collective-permute-done.5.refs_4_), channel_id=1, source_target_pairs={{0,1},{1,0},{2,3},{3,2},{4,5},{5,4},{6,7},{7,6},{8,9},{9,8},{10,11... | collective-permute-start | bytes 1572872 | tf_op jit(solution)/shard_map/ppermute | solution.py:24
  45.1 0.4 collective-permute-start.19
  45.6 1.8 %collective-permute-start.17 = (bf16[16,128,128]{2,1,0:T(8,128)(2,1)S(1)}, bf16[16,128,128]{2,1,0:T(8,128)(2,1)S(1)}, u32[]{:S(2)}, u32[]{:S(2)}) collective-permute-start(bf16[16,128,128]{2,1,0:T(8,128)(2,1)S(1)} %collective-permute-done.2.refs_6_), channel_id=1, source_target_pairs={{0,8},{1,5},{2,10},{3,7},{8,16},{9,1},{10,18},{11,3},{16,24},{17,9... | collective-permute-start | bytes 1572872 | tf_op jit(solution)/shard_map/ppermute | solution.py:381
  47.4 0.6 collective-permute-done.19.refs_12_
  48.1 0.7 collective-permute-done.20.refs_13_
  48.8 4.2 %shard_map.57.slots_ref = bf16[144,128,128]{2,1,0:T(8,128)(2,1)S(1)} custom-call(s32[145]{0:T(256)S(1)} %get-tuple-element.49.plan_ref, s32[3]{0:T(128)S(1)} %get-tuple-element.50.starts_ref, bf16[64,128,128]{2,1,0:T(8,128)(2,1)} %bitcast.155, bf16[64,128,128]{2,1,0:T(8,128)(2,1)S(1)} %collective-permute-done.7.refs_1_, bf16[16,128,128]{2,1,0:T(8,128)(2,1)} %refs_2_.1, ...), custom_call_target="tpu_custom_call" | custom-call | flops 268435456 | bytes 1048576 | tf_op jit(solution)/shard_map/pallas_call | solution.py:243
  53.0 2.1 %collective-permute-done.17.far0 = bf16[16,128,128]{2,1,0:T(8,128)(2,1)S(1)} collective-permute-done((bf16[16,128,128]{2,1,0:T(8,128)(2,1)S(1)}, bf16[16,128,128]{2,1,0:T(8,128)(2,1)S(1)}, u32[]{:S(2)}, u32[]{:S(2)}) %collective-permute-start.17) | collective-permute-done | bytes 524320 | tf_op jit(solution)/shard_map/ppermute | solution.py:381
  55.1 1.9 %collective-permute-done.22.far1 = bf16[16,128,128]{2,1,0:T(8,128)(2,1)S(1)} collective-permute-done((bf16[16,128,128]{2,1,0:T(8,128)(2,1)S(1)}, bf16[16,128,128]{2,1,0:T(8,128)(2,1)S(1)}, u32[]{:S(2)}, u32[]{:S(2)}) %collective-permute-start.22) | collective-permute-done | bytes 524320 | tf_op jit(solution)/shard_map/ppermute | solution.py:24
  57.0 3.9 %shard_map.58 = (bf16[2,2,2,1,1,336,128]{6,5,4,3,2,1,0:T(8,128)(2,1)S(1)}, f32[2,2,2,1,1,336,128]{6,5,4,3,2,1,0:T(8,128)S(1)}, bf16[2,2,2,1,1,336,128]{6,5,4,3,2...) custom-call(s32[145]{0:T(256)S(1)} %get-tuple-element.49.plan_ref, ...), custom_call_target="tpu_custom_call" | custom-call | flops 268435456 | bytes 16777216 | tf_op jit(solution)/shard_map/pallas_call | solution.py:349
  61.0 1.5 %collective-permute-start.23 = (bf16[2,2,2,1,1,336,128]{6,5,2,4,3,1,0:T(8,128)(2,1)S(1)}, bf16[2,2,2,1,1,336,128]{6,5,2,4,3,1,0:T(8,128)(2,1)S(1)}, u32[]{:S(2)}, u32[]{:S(2)}) collective-permute-start(bf16[2,2,2,1,1,336,128]{6,5,2,4,3,1,0:T(8,128)(2,1)S(1)} %bitcast.153), channel_id=1, source_target_pairs={{0,4},{1,9},{2,6},{3,11},{4,0},{5,13},{6,2},{7,15},{8,12},{9,1},{1... | collective-permute-start | bytes 2064392 | tf_op jit(solution)/shard_map/ppermute | solution.py:35
  62.4 2.0 %collective-permute-start.27 = (bf16[2,2,2,1,1,336,128]{6,5,2,4,3,1,0:T(8,128)(2,1)S(1)}, bf16[2,2,2,1,1,336,128]{6,5,2,4,3,1,0:T(8,128)(2,1)S(1)}, u32[]{:S(2)}, u32[]{:S(2)}) collective-permute-start(bf16[2,2,2,1,1,336,128]{6,5,2,4,3,1,0:T(8,128)(2,1)S(1)} %bitcast.152), channel_id=1, source_target_pairs={{0,2},{1,3},{2,0},{3,1},{4,6},{5,7},{6,4},{7,5},{8,10},{9,11},{10,... | collective-permute-start | bytes 2064392 | tf_op jit(solution)/shard_map/ppermute | solution.py:35
  64.4 2.2 %collective-permute-start.31 = (bf16[2,2,2,1,1,352,128]{6,5,2,4,3,1,0:T(8,128)(2,1)S(1)}, bf16[2,2,2,1,1,352,128]{6,5,2,4,3,1,0:T(8,128)(2,1)S(1)}, u32[]{:S(2)}, u32[]{:S(2)}) collective-permute-start(bf16[2,2,2,1,1,352,128]{6,5,2,4,3,1,0:T(8,128)(2,1)S(1)} %bitcast.151), channel_id=1, source_target_pairs={{0,16},{1,5},{2,18},{3,7},{4,20},{5,1},{6,22},{7,3},{8,24},{9,13},... | collective-permute-start | bytes 2162696 | tf_op jit(solution)/shard_map/ppermute | solution.py:35
  66.6 10.3 %collective-permute-done.23 = bf16[2,2,2,1,1,336,128]{6,5,2,4,3,1,0:T(8,128)(2,1)S(1)} collective-permute-done((bf16[2,2,2,1,1,336,128]{6,5,2,4,3,1,0:T(8,128)(2,1)S(1)}, bf16[2,2,2,1,1,336,128]{6,5,2,4,3,1,0:T(8,128)(2,1)S(1)}, u32[]{:S(2)}, u32[]{:S(2)}) %collective-permute-start.23) | collective-permute-done | bytes 688160 | tf_op jit(solution)/shard_map/ppermute | solution.py:35
  77.0 1.8 %collective-permute-start.24 = (bf16[2,2,1,1,336,128]{5,4,3,2,1,0:T(8,128)(2,1)S(1)}, bf16[2,2,1,1,336,128]{5,4,3,2,1,0:T(8,128)(2,1)S(1)}, u32[]{:S(2)}, u32[]{:S(2)}) collective-permute-start(bf16[2,2,1,1,336,128]{5,4,3,2,1,0:T(8,128)(2,1)S(1)} %get-tuple-element.67), channel_id=1, source_target_pairs={{0,2},{1,5},{2,0},{3,7},{4,6},{5,1},{6,4},{7,3},{8,10},{9,13},{10,... | collective-permute-start | bytes 1032200 | tf_op jit(solution)/shard_map/ppermute | solution.py:35
  78.8 1.1 %collective-permute-done.27 = bf16[2,2,2,1,1,336,128]{6,5,2,4,3,1,0:T(8,128)(2,1)S(1)} collective-permute-done((bf16[2,2,2,1,1,336,128]{6,5,2,4,3,1,0:T(8,128)(2,1)S(1)}, bf16[2,2,2,1,1,336,128]{6,5,2,4,3,1,0:T(8,128)(2,1)S(1)}, u32[]{:S(2)}, u32[]{:S(2)}) %collective-permute-start.27) | collective-permute-done | bytes 688160 | tf_op jit(solution)/shard_map/ppermute | solution.py:35
  80.1 1.2 %collective-permute-start.28 = (bf16[2,2,1,1,336,128]{5,4,3,2,1,0:T(8,128)(2,1)S(1)}, bf16[2,2,1,1,336,128]{5,4,3,2,1,0:T(8,128)(2,1)S(1)}, u32[]{:S(2)}, u32[]{:S(2)}) collective-permute-start(bf16[2,2,1,1,336,128]{5,4,3,2,1,0:T(8,128)(2,1)S(1)} %get-tuple-element.69), channel_id=1, source_target_pairs={{0,4},{1,9},{2,6},{3,11},{4,0},{5,13},{6,2},{7,15},{8,12},{9,1},{1... | collective-permute-start | bytes 1032200 | tf_op jit(solution)/shard_map/ppermute | solution.py:35
  81.3 3.1 %collective-permute-done.31 = bf16[2,2,2,1,1,352,128]{6,5,2,4,3,1,0:T(8,128)(2,1)S(1)} collective-permute-done((bf16[2,2,2,1,1,352,128]{6,5,2,4,3,1,0:T(8,128)(2,1)S(1)}, bf16[2,2,2,1,1,352,128]{6,5,2,4,3,1,0:T(8,128)(2,1)S(1)}, u32[]{:S(2)}, u32[]{:S(2)}) %collective-permute-start.31) | collective-permute-done | bytes 720928 | tf_op jit(solution)/shard_map/ppermute | solution.py:35
  85.0 2.2 %collective-permute-start.25 = (bf16[2,1,1,336,128]{4,3,2,1,0:T(8,128)(2,1)S(1)}, bf16[2,1,1,336,128]{4,3,2,1,0:T(8,128)(2,1)S(1)}, u32[]{:S(2)}, u32[]{:S(2)}) collective-permute-start(bf16[2,1,1,336,128]{4,3,2,1,0:T(8,128)(2,1)S(1)} %get-tuple-element.71), channel_id=1, source_target_pairs={{0,16},{1,3},{2,18},{3,1},{4,20},{5,7},{6,22},{7,5},{8,24},{9,11},... | collective-permute-start | bytes 516104 | tf_op jit(solution)/shard_map/ppermute | solution.py:35
  87.2 1.6 %collective-permute-done.28 = bf16[2,2,1,1,336,128]{5,4,3,2,1,0:T(8,128)(2,1)S(1)} collective-permute-done((bf16[2,2,1,1,336,128]{5,4,3,2,1,0:T(8,128)(2,1)S(1)}, bf16[2,2,1,1,336,128]{5,4,3,2,1,0:T(8,128)(2,1)S(1)}, u32[]{:S(2)}, u32[]{:S(2)}) %collective-permute-start.28) | collective-permute-done | bytes 344096 | tf_op jit(solution)/shard_map/ppermute | solution.py:35
  88.9 1.8 %collective-permute-start.29 = (bf16[2,1,1,336,128]{4,3,2,1,0:T(8,128)(2,1)S(1)}, bf16[2,1,1,336,128]{4,3,2,1,0:T(8,128)(2,1)S(1)}, u32[]{:S(2)}, u32[]{:S(2)}) collective-permute-start(bf16[2,1,1,336,128]{4,3,2,1,0:T(8,128)(2,1)S(1)} %get-tuple-element.73), channel_id=1, source_target_pairs={{0,8},{1,5},{2,10},{3,7},{4,12},{5,1},{6,14},{7,3},{8,0},{9,13},{1... | collective-permute-start | bytes 516104 | tf_op jit(solution)/shard_map/ppermute | solution.py:35
  90.7 3.2 %collective-permute-done.32 = bf16[2,2,1,1,352,128]{5,4,1,0,3,2:T(8,128)(2,1)S(1)} collective-permute-done((bf16[2,2,1,1,352,128]{5,4,1,0,3,2:T(8,128)(2,1)S(1)}, bf16[2,2,1,1,352,128]{5,4,1,0,3,2:T(8,128)(2,1)S(1)}, u32[]{:S(2)}, u32[]{:S(2)}) %collective-permute-start.32) | collective-permute-done | bytes 360480 | tf_op jit(solution)/shard_map/ppermute | solution.py:35
  94.1 2.2 %collective-permute-start.26 = (bf16[1,1,336,128]{3,2,1,0:T(8,128)(2,1)S(1)}, bf16[1,1,336,128]{3,2,1,0:T(8,128)(2,1)S(1)}, u32[]{:S(2)}, u32[]{:S(2)}) collective-permute-start(bf16[1,1,336,128]{3,2,1,0:T(8,128)(2,1)S(1)} %fusion.34), channel_id=1, source_target_pairs={{0,8},{1,17},{2,10},{3,19},{4,12},{5,21},{6,14},{7,23},{8,0},{9,25... | collective-permute-start | bytes 258056 | tf_op jit(solution)/shard_map/ppermute | solution.py:35
  96.3 1.4 %collective-permute-start.30 = (bf16[1,1,336,128]{3,2,1,0:T(8,128)(2,1)S(1)}, bf16[1,1,336,128]{3,2,1,0:T(8,128)(2,1)S(1)}, u32[]{:S(2)}, u32[]{:S(2)}) collective-permute-start(bf16[1,1,336,128]{3,2,1,0:T(8,128)(2,1)S(1)} %fusion.35), channel_id=1, source_target_pairs={{0,16},{1,17},{2,18},{3,19},{4,20},{5,21},{6,22},{7,23},{8,24},{9,... | collective-permute-start | bytes 258056 | tf_op jit(solution)/shard_map/ppermute | solution.py:35
  97.7 1.8 %collective-permute-done.33 = bf16[2,1,1,352,128]{4,3,0,2,1:T(8,128)(2,1)S(1)} collective-permute-done((bf16[2,1,1,352,128]{4,3,0,2,1:T(8,128)(2,1)S(1)}, bf16[2,1,1,352,128]{4,3,0,2,1:T(8,128)(2,1)S(1)}, u32[]{:S(2)}, u32[]{:S(2)}) %collective-permute-start.33) | collective-permute-done | bytes 180256 | tf_op jit(solution)/shard_map/ppermute | solution.py:35
  99.8 5.5 %collective-permute-done.30 = bf16[1,1,336,128]{3,2,1,0:T(8,128)(2,1)S(1)} collective-permute-done((bf16[1,1,336,128]{3,2,1,0:T(8,128)(2,1)S(1)}, bf16[1,1,336,128]{3,2,1,0:T(8,128)(2,1)S(1)}, u32[]{:S(2)}, u32[]{:S(2)}) %collective-permute-start.30) | collective-permute-done | bytes 86048 | tf_op jit(solution)/shard_map/ppermute | solution.py:35
  105.3 0.8 collective-permute-done.34
  106.1 0.8 pad_maximum_fusion
  (45 shorter events, 2.1 us)
Async XLA Ops:
  0.0 13.1 %collective-permute-start.7 = (bf16[64,128,128]{2,1,0:T(8,128)(2,1)}, bf16[64,128,128]{2,1,0:T(8,128)(2,1)S(1)}, u32[]{:S(2)}, u32[]{:S(2)}) collective-permute-start(bf16[64,128,128]{2,1,0:T(8,128)(2,1)} %bitcast.154), channel_id=1, source_target_pairs={{0,1},{1,0},{2,3},{3,2},{4,5},{5,4},{6,7},{7,6},{8,9},{9,8},{10,11... | collective-permute-start | bytes 6291464 | tf_op jit(solution)/shard_map/ppermute | solution.py:24
  0.5 4.0 %collective-permute-start.3 = (s32[64]{0:T(128)}, s32[64]{0:T(128)S(1)}, u32[]{:S(2)}, u32[]{:S(2)}) collective-permute-start(s32[64]{0:T(128)} %bitcast.158), channel_id=1, source_target_pairs={{0,1},{1,0},{2,3},{3,2},{4,5},{5,4},{6,7},{7,6},{8,9},{9,8},{10,11... | collective-permute-start | bytes 776 | tf_op jit(solution)/shard_map/ppermute | solution.py:24
  0.5 7.5 %collective-permute-start.8 = (bf16[16,128,128]{2,1,0:T(8,128)(2,1)}, bf16[16,128,128]{2,1,0:T(8,128)(2,1)S(1)}, u32[]{:S(2)}, u32[]{:S(2)}) collective-permute-start(bf16[16,128,128]{2,1,0:T(8,128)(2,1)} %refs_2_.1), channel_id=1, source_target_pairs={{0,1},{1,0},{2,3},{3,2},{4,5},{5,4},{6,7},{7,6},{8,9},{9,8},{10,11... | collective-permute-start | bytes 1572872 | tf_op jit(solution)/shard_map/ppermute | solution.py:24
  1.0 12.1 %collective-permute-start = (bf16[16,128,128]{2,1,0:T(8,128)(2,1)}, bf16[16,128,128]{2,1,0:T(8,128)(2,1)S(1)}, u32[]{:S(2)}, u32[]{:S(2)}) collective-permute-start(bf16[16,128,128]{2,1,0:T(8,128)(2,1)} %refs_2_.1), channel_id=1, source_target_pairs={{0,8},{1,5},{2,10},{3,7},{8,16},{9,1},{10,18},{11,3},{16,24},{17,9... | collective-permute-start | bytes 1572872 | tf_op jit(solution)/shard_map/ppermute | solution.py:381
  4.5 14.5 %collective-permute-start.4 = (bf16[16,128,128]{2,1,0:T(8,128)(2,1)}, bf16[16,128,128]{2,1,0:T(8,128)(2,1)S(1)}, u32[]{:S(2)}, u32[]{:S(2)}) collective-permute-start(bf16[16,128,128]{2,1,0:T(8,128)(2,1)} %refs_2_.1), channel_id=1, source_target_pairs={{0,4},{1,9},{2,6},{3,11},{8,0},{9,17},{10,2},{11,19},{16,8},{17,25... | collective-permute-start | bytes 1572872 | tf_op jit(solution)/shard_map/ppermute | solution.py:381
  13.1 5.9 %collective-permute-start.11 = (s32[64]{0:T(128)S(1)}, s32[64]{0:T(128)S(1)}, u32[]{:S(2)}, u32[]{:S(2)}) collective-permute-start(s32[64]{0:T(128)S(1)} %bitcast_add_fusion), channel_id=1, source_target_pairs={{0,12},{4,8},{8,4},{12,0},{16,28},{20,24},{24,20},{28,16},{1,13},{... | collective-permute-start | bytes 776 | tf_op jit(solution)/shard_map/ppermute | solution.py:24
  16.4 3.6 %collective-permute-start.10 = (s32[64]{0:T(128)S(1)}, s32[64]{0:T(128)S(1)}, u32[]{:S(2)}, u32[]{:S(2)}) collective-permute-start(s32[64]{0:T(128)S(1)} %bitcast_add_fusion), channel_id=1, source_target_pairs={{0,8},{4,12},{8,0},{12,4},{16,24},{20,28},{24,16},{28,20},{1,9},{5... | collective-permute-start | bytes 776 | tf_op jit(solution)/shard_map/ppermute | solution.py:24
  16.9 3.6 %collective-permute-start.9 = (s32[64]{0:T(128)S(1)}, s32[64]{0:T(128)S(1)}, u32[]{:S(2)}, u32[]{:S(2)}) collective-permute-start(s32[64]{0:T(128)S(1)} %bitcast_add_fusion), channel_id=1, source_target_pairs={{0,4},{4,0},{8,12},{12,8},{16,20},{20,16},{24,28},{28,24},{1,5},{5... | collective-permute-start | bytes 776 | tf_op jit(solution)/shard_map/ppermute | solution.py:24
  17.0 13.4 %collective-permute-start.1 = (bf16[16,128,128]{2,1,0:T(8,128)(2,1)S(1)}, bf16[16,128,128]{2,1,0:T(8,128)(2,1)S(1)}, u32[]{:S(2)}, u32[]{:S(2)}) collective-permute-start(bf16[16,128,128]{2,1,0:T(8,128)(2,1)S(1)} %collective-permute-done.refs_8_), channel_id=1, source_target_pairs={{0,8},{1,5},{2,10},{3,7},{8,16},{9,1},{10,18},{11,3},{16,24},{17,9... | collective-permute-start | bytes 1572872 | tf_op jit(solution)/shard_map/ppermute | solution.py:381
  19.0 13.3 %collective-permute-start.5 = (bf16[16,128,128]{2,1,0:T(8,128)(2,1)S(1)}, bf16[16,128,128]{2,1,0:T(8,128)(2,1)S(1)}, u32[]{:S(2)}, u32[]{:S(2)}) collective-permute-start(bf16[16,128,128]{2,1,0:T(8,128)(2,1)S(1)} %collective-permute-done.4.refs_3_), channel_id=1, source_target_pairs={{0,4},{1,9},{2,6},{3,11},{8,0},{9,17},{10,2},{11,19},{16,8},{17,25... | collective-permute-start | bytes 1572872 | tf_op jit(solution)/shard_map/ppermute | solution.py:381
  20.5 11.7 %collective-permute-start.13 = (bf16[16,128,128]{2,1,0:T(8,128)(2,1)}, bf16[16,128,128]{2,1,0:T(8,128)(2,1)S(1)}, u32[]{:S(2)}, u32[]{:S(2)}) collective-permute-start(bf16[16,128,128]{2,1,0:T(8,128)(2,1)} %refs_2_.1), channel_id=1, source_target_pairs={{0,2},{1,3},{2,0},{3,1},{4,6},{5,7},{6,4},{7,5},{8,10},{9,11},{10,... | collective-permute-start | bytes 1572872 | tf_op jit(solution)/shard_map/ppermute | solution.py:24
  22.0 12.1 %collective-permute-start.12 = (s32[256]{0:T(256)S(1)}, s32[256]{0:T(256)S(1)}, u32[]{:S(2)}, u32[]{:S(2)}) collective-permute-start(s32[256]{0:T(256)S(1)} %pad_add_fusion.1), channel_id=1, source_target_pairs={{0,16},{4,20},{8,24},{12,28},{16,0},{20,4},{24,8},{28,12},{1,17},{... | collective-permute-start | bytes 3080 | tf_op jit(solution)/shard_map/ppermute | solution.py:24
  30.4 13.4 %collective-permute-start.2 = (bf16[16,128,128]{2,1,0:T(8,128)(2,1)S(1)}, bf16[16,128,128]{2,1,0:T(8,128)(2,1)S(1)}, u32[]{:S(2)}, u32[]{:S(2)}) collective-permute-start(bf16[16,128,128]{2,1,0:T(8,128)(2,1)S(1)} %collective-permute-done.1.refs_7_), channel_id=1, source_target_pairs={{0,8},{1,5},{2,10},{3,7},{8,16},{9,1},{10,18},{11,3},{16,24},{17,9... | collective-permute-start | bytes 1572872 | tf_op jit(solution)/shard_map/ppermute | solution.py:381
  32.2 7.1 %collective-permute-start.14 = (bf16[16,128,128]{2,1,0:T(8,128)(2,1)S(1)}, bf16[16,128,128]{2,1,0:T(8,128)(2,1)S(1)}, u32[]{:S(2)}, u32[]{:S(2)}) collective-permute-start(bf16[16,128,128]{2,1,0:T(8,128)(2,1)S(1)} %collective-permute-done.13.refs_1_), channel_id=1, source_target_pairs={{0,1},{1,0},{2,3},{3,2},{4,5},{5,4},{6,7},{7,6},{8,9},{9,8},{10,11... | collective-permute-start | bytes 1572872 | tf_op jit(solution)/shard_map/ppermute | solution.py:24
  32.2 11.6 %collective-permute-start.6 = (bf16[16,128,128]{2,1,0:T(8,128)(2,1)S(1)}, bf16[16,128,128]{2,1,0:T(8,128)(2,1)S(1)}, u32[]{:S(2)}, u32[]{:S(2)}) collective-permute-start(bf16[16,128,128]{2,1,0:T(8,128)(2,1)S(1)} %collective-permute-done.5.refs_4_), channel_id=1, source_target_pairs={{0,4},{1,9},{2,6},{3,11},{8,0},{9,17},{10,2},{11,19},{16,8},{17,25... | collective-permute-start | bytes 1572872 | tf_op jit(solution)/shard_map/ppermute | solution.py:381
  32.5 11.3 %collective-permute-start.15 = (bf16[16,128,128]{2,1,0:T(8,128)(2,1)S(1)}, bf16[16,128,128]{2,1,0:T(8,128)(2,1)S(1)}, u32[]{:S(2)}, u32[]{:S(2)}) collective-permute-start(bf16[16,128,128]{2,1,0:T(8,128)(2,1)S(1)} %collective-permute-done.4.refs_3_), channel_id=1, source_target_pairs={{0,1},{1,0},{2,3},{3,2},{4,5},{5,4},{6,7},{7,6},{8,9},{9,8},{10,11... | collective-permute-start | bytes 1572872 | tf_op jit(solution)/shard_map/ppermute | solution.py:24
  34.1 9.7 %collective-permute-start.16 = (bf16[16,128,128]{2,1,0:T(8,128)(2,1)S(1)}, bf16[16,128,128]{2,1,0:T(8,128)(2,1)S(1)}, u32[]{:S(2)}, u32[]{:S(2)}) collective-permute-start(bf16[16,128,128]{2,1,0:T(8,128)(2,1)S(1)} %collective-permute-done.refs_8_), channel_id=1, source_target_pairs={{0,1},{1,0},{2,3},{3,2},{4,5},{5,4},{6,7},{7,6},{8,9},{9,8},{10,11... | collective-permute-start | bytes 1572872 | tf_op jit(solution)/shard_map/ppermute | solution.py:24
  43.8 3.6 %collective-permute-start.18 = (bf16[16,128,128]{2,1,0:T(8,128)(2,1)S(1)}, bf16[16,128,128]{2,1,0:T(8,128)(2,1)S(1)}, u32[]{:S(2)}, u32[]{:S(2)}) collective-permute-start(bf16[16,128,128]{2,1,0:T(8,128)(2,1)S(1)} %collective-permute-done.5.refs_4_), channel_id=1, source_target_pairs={{0,1},{1,0},{2,3},{3,2},{4,5},{5,4},{6,7},{7,6},{8,9},{9,8},{10,11... | collective-permute-start | bytes 1572872 | tf_op jit(solution)/shard_map/ppermute | solution.py:24
  45.0 2.4 %collective-permute-start.21 = (bf16[16,128,128]{2,1,0:T(8,128)(2,1)S(1)}, bf16[16,128,128]{2,1,0:T(8,128)(2,1)S(1)}, u32[]{:S(2)}, u32[]{:S(2)}) collective-permute-start(bf16[16,128,128]{2,1,0:T(8,128)(2,1)S(1)} %collective-permute-done.1.refs_7_), channel_id=1, source_target_pairs={{0,1},{1,0},{2,3},{3,2},{4,5},{5,4},{6,7},{7,6},{8,9},{9,8},{10,11... | collective-permute-start | bytes 1572872 | tf_op jit(solution)/shard_map/ppermute | solution.py:24
  45.1 3.0 %collective-permute-start.19 = (bf16[16,128,128]{2,1,0:T(8,128)(2,1)S(1)}, bf16[16,128,128]{2,1,0:T(8,128)(2,1)S(1)}, u32[]{:S(2)}, u32[]{:S(2)}) collective-permute-start(bf16[16,128,128]{2,1,0:T(8,128)(2,1)S(1)} %collective-permute-done.6.refs_5_), channel_id=1, source_target_pairs={{0,1},{1,0},{2,3},{3,2},{4,5},{5,4},{6,7},{7,6},{8,9},{9,8},{10,11... | collective-permute-start | bytes 1572872 | tf_op jit(solution)/shard_map/ppermute | solution.py:24
  45.5 3.3 %collective-permute-start.20 = (bf16[16,128,128]{2,1,0:T(8,128)(2,1)S(1)}, bf16[16,128,128]{2,1,0:T(8,128)(2,1)S(1)}, u32[]{:S(2)}, u32[]{:S(2)}) collective-permute-start(bf16[16,128,128]{2,1,0:T(8,128)(2,1)S(1)} %collective-permute-done.2.refs_6_), channel_id=1, source_target_pairs={{0,1},{1,0},{2,3},{3,2},{4,5},{5,4},{6,7},{7,6},{8,9},{9,8},{10,11... | collective-permute-start | bytes 1572872 | tf_op jit(solution)/shard_map/ppermute | solution.py:24
  45.6 9.5 %collective-permute-start.17 = (bf16[16,128,128]{2,1,0:T(8,128)(2,1)S(1)}, bf16[16,128,128]{2,1,0:T(8,128)(2,1)S(1)}, u32[]{:S(2)}, u32[]{:S(2)}) collective-permute-start(bf16[16,128,128]{2,1,0:T(8,128)(2,1)S(1)} %collective-permute-done.2.refs_6_), channel_id=1, source_target_pairs={{0,8},{1,5},{2,10},{3,7},{8,16},{9,1},{10,18},{11,3},{16,24},{17,9... | collective-permute-start | bytes 1572872 | tf_op jit(solution)/shard_map/ppermute | solution.py:381
  55.1 1.9 %collective-permute-start.22 = (bf16[16,128,128]{2,1,0:T(8,128)(2,1)S(1)}, bf16[16,128,128]{2,1,0:T(8,128)(2,1)S(1)}, u32[]{:S(2)}, u32[]{:S(2)}) collective-permute-start(bf16[16,128,128]{2,1,0:T(8,128)(2,1)S(1)} %collective-permute-done.17.far0), channel_id=1, source_target_pairs={{0,1},{1,0},{2,3},{3,2},{4,5},{5,4},{6,7},{7,6},{8,9},{9,8},{10,11... | collective-permute-start | bytes 1572872 | tf_op jit(solution)/shard_map/ppermute | solution.py:24
  61.0 15.9 %collective-permute-start.23 = (bf16[2,2,2,1,1,336,128]{6,5,2,4,3,1,0:T(8,128)(2,1)S(1)}, bf16[2,2,2,1,1,336,128]{6,5,2,4,3,1,0:T(8,128)(2,1)S(1)}, u32[]{:S(2)}, u32[]{:S(2)}) collective-permute-start(bf16[2,2,2,1,1,336,128]{6,5,2,4,3,1,0:T(8,128)(2,1)S(1)} %bitcast.153), channel_id=1, source_target_pairs={{0,4},{1,9},{2,6},{3,11},{4,0},{5,13},{6,2},{7,15},{8,12},{9,1},{1... | collective-permute-start | bytes 2064392 | tf_op jit(solution)/shard_map/ppermute | solution.py:35
  62.4 17.5 %collective-permute-start.27 = (bf16[2,2,2,1,1,336,128]{6,5,2,4,3,1,0:T(8,128)(2,1)S(1)}, bf16[2,2,2,1,1,336,128]{6,5,2,4,3,1,0:T(8,128)(2,1)S(1)}, u32[]{:S(2)}, u32[]{:S(2)}) collective-permute-start(bf16[2,2,2,1,1,336,128]{6,5,2,4,3,1,0:T(8,128)(2,1)S(1)} %bitcast.152), channel_id=1, source_target_pairs={{0,2},{1,3},{2,0},{3,1},{4,6},{5,7},{6,4},{7,5},{8,10},{9,11},{10,... | collective-permute-start | bytes 2064392 | tf_op jit(solution)/shard_map/ppermute | solution.py:35
  64.4 20.1 %collective-permute-start.31 = (bf16[2,2,2,1,1,352,128]{6,5,2,4,3,1,0:T(8,128)(2,1)S(1)}, bf16[2,2,2,1,1,352,128]{6,5,2,4,3,1,0:T(8,128)(2,1)S(1)}, u32[]{:S(2)}, u32[]{:S(2)}) collective-permute-start(bf16[2,2,2,1,1,352,128]{6,5,2,4,3,1,0:T(8,128)(2,1)S(1)} %bitcast.151), channel_id=1, source_target_pairs={{0,16},{1,5},{2,18},{3,7},{4,20},{5,1},{6,22},{7,3},{8,24},{9,13},... | collective-permute-start | bytes 2162696 | tf_op jit(solution)/shard_map/ppermute | solution.py:35
  77.0 7.9 %collective-permute-start.24 = (bf16[2,2,1,1,336,128]{5,4,3,2,1,0:T(8,128)(2,1)S(1)}, bf16[2,2,1,1,336,128]{5,4,3,2,1,0:T(8,128)(2,1)S(1)}, u32[]{:S(2)}, u32[]{:S(2)}) collective-permute-start(bf16[2,2,1,1,336,128]{5,4,3,2,1,0:T(8,128)(2,1)S(1)} %get-tuple-element.67), channel_id=1, source_target_pairs={{0,2},{1,5},{2,0},{3,7},{4,6},{5,1},{6,4},{7,3},{8,10},{9,13},{10,... | collective-permute-start | bytes 1032200 | tf_op jit(solution)/shard_map/ppermute | solution.py:35
  80.1 8.7 %collective-permute-start.28 = (bf16[2,2,1,1,336,128]{5,4,3,2,1,0:T(8,128)(2,1)S(1)}, bf16[2,2,1,1,336,128]{5,4,3,2,1,0:T(8,128)(2,1)S(1)}, u32[]{:S(2)}, u32[]{:S(2)}) collective-permute-start(bf16[2,2,1,1,336,128]{5,4,3,2,1,0:T(8,128)(2,1)S(1)} %get-tuple-element.69), channel_id=1, source_target_pairs={{0,4},{1,9},{2,6},{3,11},{4,0},{5,13},{6,2},{7,15},{8,12},{9,1},{1... | collective-permute-start | bytes 1032200 | tf_op jit(solution)/shard_map/ppermute | solution.py:35
  84.6 9.3 %collective-permute-start.32 = (bf16[2,2,1,1,352,128]{5,4,1,0,3,2:T(8,128)(2,1)S(1)}, bf16[2,2,1,1,352,128]{5,4,1,0,3,2:T(8,128)(2,1)S(1)}, u32[]{:S(2)}, u32[]{:S(2)}) collective-permute-start(bf16[2,2,1,1,352,128]{5,4,1,0,3,2:T(8,128)(2,1)S(1)} %fusion.3), channel_id=1, source_target_pairs={{0,2},{1,9},{2,0},{3,11},{4,6},{5,13},{6,4},{7,15},{8,10},{9,1},{1... | collective-permute-start | bytes 1081352 | tf_op jit(solution)/shard_map/ppermute | solution.py:35
  85.0 9.1 %collective-permute-start.25 = (bf16[2,1,1,336,128]{4,3,2,1,0:T(8,128)(2,1)S(1)}, bf16[2,1,1,336,128]{4,3,2,1,0:T(8,128)(2,1)S(1)}, u32[]{:S(2)}, u32[]{:S(2)}) collective-permute-start(bf16[2,1,1,336,128]{4,3,2,1,0:T(8,128)(2,1)S(1)} %get-tuple-element.71), channel_id=1, source_target_pairs={{0,16},{1,3},{2,18},{3,1},{4,20},{5,7},{6,22},{7,5},{8,24},{9,11},... | collective-permute-start | bytes 516104 | tf_op jit(solution)/shard_map/ppermute | solution.py:35
  88.9 7.4 %collective-permute-start.29 = (bf16[2,1,1,336,128]{4,3,2,1,0:T(8,128)(2,1)S(1)}, bf16[2,1,1,336,128]{4,3,2,1,0:T(8,128)(2,1)S(1)}, u32[]{:S(2)}, u32[]{:S(2)}) collective-permute-start(bf16[2,1,1,336,128]{4,3,2,1,0:T(8,128)(2,1)S(1)} %get-tuple-element.73), channel_id=1, source_target_pairs={{0,8},{1,5},{2,10},{3,7},{4,12},{5,1},{6,14},{7,3},{8,0},{9,13},{1... | collective-permute-start | bytes 516104 | tf_op jit(solution)/shard_map/ppermute | solution.py:35
  93.9 5.6 %collective-permute-start.33 = (bf16[2,1,1,352,128]{4,3,0,2,1:T(8,128)(2,1)S(1)}, bf16[2,1,1,352,128]{4,3,0,2,1:T(8,128)(2,1)S(1)}, u32[]{:S(2)}, u32[]{:S(2)}) collective-permute-start(bf16[2,1,1,352,128]{4,3,0,2,1:T(8,128)(2,1)S(1)} %fusion.15), channel_id=1, source_target_pairs={{0,4},{1,3},{2,6},{3,1},{4,0},{5,7},{6,2},{7,5},{8,12},{9,11},{10,... | collective-permute-start | bytes 540680 | tf_op jit(solution)/shard_map/ppermute | solution.py:35
  94.1 5.6 %collective-permute-start.26 = (bf16[1,1,336,128]{3,2,1,0:T(8,128)(2,1)S(1)}, bf16[1,1,336,128]{3,2,1,0:T(8,128)(2,1)S(1)}, u32[]{:S(2)}, u32[]{:S(2)}) collective-permute-start(bf16[1,1,336,128]{3,2,1,0:T(8,128)(2,1)S(1)} %fusion.34), channel_id=1, source_target_pairs={{0,8},{1,17},{2,10},{3,19},{4,12},{5,21},{6,14},{7,23},{8,0},{9,25... | collective-permute-start | bytes 258056 | tf_op jit(solution)/shard_map/ppermute | solution.py:35
  96.3 8.9 %collective-permute-start.30 = (bf16[1,1,336,128]{3,2,1,0:T(8,128)(2,1)S(1)}, bf16[1,1,336,128]{3,2,1,0:T(8,128)(2,1)S(1)}, u32[]{:S(2)}, u32[]{:S(2)}) collective-permute-start(bf16[1,1,336,128]{3,2,1,0:T(8,128)(2,1)S(1)} %fusion.35), channel_id=1, source_target_pairs={{0,16},{1,17},{2,18},{3,19},{4,20},{5,21},{6,22},{7,23},{8,24},{9,... | collective-permute-start | bytes 258056 | tf_op jit(solution)/shard_map/ppermute | solution.py:35
  99.5 6.6 %collective-permute-start.34 = (bf16[1,1,352,128]{3,2,1,0:T(8,128)(2,1)S(1)}, bf16[1,1,352,128]{3,2,1,0:T(8,128)(2,1)S(1)}, u32[]{:S(2)}, u32[]{:S(2)}) collective-permute-start(bf16[1,1,352,128]{3,2,1,0:T(8,128)(2,1)S(1)} %fusion.33), channel_id=1, source_target_pairs={{0,8},{1,17},{2,10},{3,19},{4,12},{5,21},{6,14},{7,23},{8,0},{9,25... | collective-permute-start | bytes 270344 | tf_op jit(solution)/shard_map/ppermute | solution.py:35

commit v8 on v7

--- a/solution.py
+++ b/solution.py
@@ -11,7 +11,7 @@
 
 OWN = 2
 UNROLL = 8
-ORDERS = (("yx21", "1yx2"), ("xy12", "x1y2"), ("2xy1", "y1x2"))
+ORDERS = (("xy12", "1yx2"), ("yx12", "2yx1"))
 LINKS = {"x": ("col", 2), "y": ("row", 1), "1": ("row", 2), "2": ("row", 4)}
 
 
@@ -50,8 +50,8 @@
         self.per = OWN * self.width
         self.his = rows // 8
         self.blocks, self.tall = 4 * cols, self.per * side
-        third = self.tall // 16 // 3 * 16
-        self.splits = (0, third, 2 * third, self.tall)
+        share = self.tall // 16 // len(ORDERS) * 16
+        self.splits = tuple(share * k for k in range(len(ORDERS))) + (self.tall,)
         self.buckets = 2 * self.his
         self.slots = self.pairs + self.buckets * UNROLL
         self.half = rows // 2
@@ -254,10 +254,8 @@
     )(plan, starts, *operands)
 
 
-def sum_kernel(
-    s, plan_ref, starts_ref, slots_ref, rows_ref, far0, far1,
-    send0, keep0, send1, keep1, send2, keep2, total, far_buf, sems,
-):
+def sum_kernel(s, plan_ref, starts_ref, slots_ref, rows_ref, far0, far1, *refs):
+    outs, (total, far_buf, sems) = refs[:-3], refs[-3:]
     hi = pl.program_id(0)
     copies = [
         pltpu.make_async_copy(ref, far_buf.at[pl.ds(k * s.tiles, s.tiles)], sems.at[k])
@@ -314,8 +312,7 @@
     half = s.cols // 2
     weight = {"x": 1, "y": half, "1": 2 * half, "2": 4 * half}
     core = lax.axis_index("col") & 1
-    outs = ((send0, keep0), (send1, keep1), (send2, keep2))
-    for k, (send, keep) in enumerate(outs):
+    for k, (send, keep) in enumerate(zip(outs[0::2], outs[1::2])):
         for bits in itertools.product(range(2), repeat=4):
             base = [
                 sum(weight[link] * bit for link, bit in zip(order, bits)) for order in ORDERS[k]

time: 107 us -> 110 us (1.028)
  the two profiles are of different devices: /device:TPU:0 before, /device:TPU:1 now
where the time goes in v8:
time: 110 us; the launch traced here: 111 us
  waiting for transfers between devices  55.9 us (51%)
  starting transfers between devices  35.6 us (32%)
  Pallas kernels  15.7 us (14%)
  other arithmetic  3.18 us (3%)
    ppermute x8, waiting for transfers between devices, exchange(): return lax.ppermute(value, ('row', 'col'), moves)  38.4 us
    ppermute x7, waiting for transfers between devices, ring(): return lax.ppermute(value, ('row', 'col'), moves)  13.3 us
    ppermute x16, starting transfers between devices, swap(): return lax.ppermute(value, axis, [(i, i ^ bit) for i in range(size)])  13.1 us
    ppermute x7, starting transfers between devices, ring(): return lax.ppermute(value, ('row', 'col'), moves)  13.1 us
    ppermute x8, starting transfers between devices, exchange(): return lax.ppermute(value, ('row', 'col'), moves)  9.46 us
    pallas_call x1, Pallas kernels, make_plan(): pl.pallas_call(functools.partial(plan_kernel, s), in_specs=[smem, smem],...  4.54 us
    pallas_call x1, Pallas kernels, make_products(): pl.pallas_call(functools.partial(product_kernel, s), in_specs=[smem, smem...  4.44 us
    pallas_call x1, Pallas kernels, make_sums(): pl.pallas_call(functools.partial(sum_kernel, s), grid=(s.his,), in_specs=...  4.18 us
  transfers between devices with their start and end apart: 31, of which 16 were waited for; matrix products, arithmetic and copies ran while one was open for 2% of the time, Pallas kernels for 10%

profile of v8, /device:TPU:1, one launch (start us, length us, event | category | flops | bytes accessed | tf_op | source)
XLA Modules:
  0.0 110.5 jit_solution(7177409830620636561)
XLA Ops:
  0.1 0.5 collective-permute-start.3
  0.6 2.7 %collective-permute-start = (bf16[16,128,128]{2,1,0:T(8,128)(2,1)}, bf16[16,128,128]{2,1,0:T(8,128)(2,1)S(1)}, u32[]{:S(2)}, u32[]{:S(2)}) collective-permute-start(bf16[16,128,128]{2,1,0:T(8,128)(2,1)} %refs_2_.1), channel_id=1, source_target_pairs={{0,8},{1,5},{2,10},{3,7},{8,16},{9,1},{10,18},{11,3},{16,24},{17,9... | collective-permute-start | bytes 1572872 | tf_op jit(solution)/shard_map/ppermute | solution.py:378
  3.3 1.1 %collective-permute-done.3 = s32[64]{0:T(128)S(1)} collective-permute-done((s32[64]{0:T(128)}, s32[64]{0:T(128)S(1)}, u32[]{:S(2)}, u32[]{:S(2)}) %collective-permute-start.3) | collective-permute-done | bytes 288 | tf_op jit(solution)/shard_map/ppermute | solution.py:24
  4.4 2.4 %collective-permute-start.4 = (bf16[16,128,128]{2,1,0:T(8,128)(2,1)}, bf16[16,128,128]{2,1,0:T(8,128)(2,1)S(1)}, u32[]{:S(2)}, u32[]{:S(2)}) collective-permute-start(bf16[16,128,128]{2,1,0:T(8,128)(2,1)} %refs_2_.1), channel_id=1, source_target_pairs={{0,4},{1,9},{2,6},{3,11},{8,0},{9,17},{10,2},{11,19},{16,8},{17,25... | collective-permute-start | bytes 1572872 | tf_op jit(solution)/shard_map/ppermute | solution.py:378
  6.8 0.7 bitcast_add_fusion
  7.5 4.4 %collective-permute-done.refs_8_ = bf16[16,128,128]{2,1,0:T(8,128)(2,1)S(1)} collective-permute-done((bf16[16,128,128]{2,1,0:T(8,128)(2,1)}, bf16[16,128,128]{2,1,0:T(8,128)(2,1)S(1)}, u32[]{:S(2)}, u32[]{:S(2)}) %collective-permute-start) | collective-permute-done | bytes 524320 | tf_op jit(solution)/shard_map/ppermute | solution.py:378
  11.9 2.1 %collective-permute-start.11 = (s32[64]{0:T(128)S(1)}, s32[64]{0:T(128)S(1)}, u32[]{:S(2)}, u32[]{:S(2)}) collective-permute-start(s32[64]{0:T(128)S(1)} %bitcast_add_fusion), channel_id=1, source_target_pairs={{0,12},{4,8},{8,4},{12,0},{16,28},{20,24},{24,20},{28,16},{1,13},{... | collective-permute-start | bytes 776 | tf_op jit(solution)/shard_map/ppermute | solution.py:24
  14.0 0.2 collective-permute-start.10
  14.2 0.3 collective-permute-start.9
  14.6 1.1 %collective-permute-start.1 = (bf16[16,128,128]{2,1,0:T(8,128)(2,1)S(1)}, bf16[16,128,128]{2,1,0:T(8,128)(2,1)S(1)}, u32[]{:S(2)}, u32[]{:S(2)}) collective-permute-start(bf16[16,128,128]{2,1,0:T(8,128)(2,1)S(1)} %collective-permute-done.refs_8_), channel_id=1, source_target_pairs={{0,8},{1,5},{2,10},{3,7},{8,16},{9,1},{10,18},{11,3},{16,24},{17,9... | collective-permute-start | bytes 1572872 | tf_op jit(solution)/shard_map/ppermute | solution.py:378
  15.7 0.3 collective-permute-done.4.refs_3_
  16.0 1.6 %collective-permute-start.5 = (bf16[16,128,128]{2,1,0:T(8,128)(2,1)S(1)}, bf16[16,128,128]{2,1,0:T(8,128)(2,1)S(1)}, u32[]{:S(2)}, u32[]{:S(2)}) collective-permute-start(bf16[16,128,128]{2,1,0:T(8,128)(2,1)S(1)} %collective-permute-done.4.refs_3_), channel_id=1, source_target_pairs={{0,4},{1,9},{2,6},{3,11},{8,0},{9,17},{10,2},{11,19},{16,8},{17,25... | collective-permute-start | bytes 1572872 | tf_op jit(solution)/shard_map/ppermute | solution.py:378
  17.7 1.2 %collective-permute-start.13 = (bf16[16,128,128]{2,1,0:T(8,128)(2,1)}, bf16[16,128,128]{2,1,0:T(8,128)(2,1)S(1)}, u32[]{:S(2)}, u32[]{:S(2)}) collective-permute-start(bf16[16,128,128]{2,1,0:T(8,128)(2,1)} %refs_2_.1), channel_id=1, source_target_pairs={{0,2},{1,3},{2,0},{3,1},{4,6},{5,7},{6,4},{7,5},{8,10},{9,11},{10,... | collective-permute-start | bytes 1572872 | tf_op jit(solution)/shard_map/ppermute | solution.py:24
  18.9 2.3 %collective-permute-start.12 = (s32[256]{0:T(256)S(1)}, s32[256]{0:T(256)S(1)}, u32[]{:S(2)}, u32[]{:S(2)}) collective-permute-start(s32[256]{0:T(256)S(1)} %pad_add_fusion.1), channel_id=1, source_target_pairs={{0,16},{4,20},{8,24},{12,28},{16,0},{20,4},{24,8},{28,12},{1,17},{... | collective-permute-start | bytes 3080 | tf_op jit(solution)/shard_map/ppermute | solution.py:24
  21.3 2.5 %collective-permute-done.1.refs_7_ = bf16[16,128,128]{2,1,0:T(8,128)(2,1)S(1)} collective-permute-done((bf16[16,128,128]{2,1,0:T(8,128)(2,1)S(1)}, bf16[16,128,128]{2,1,0:T(8,128)(2,1)S(1)}, u32[]{:S(2)}, u32[]{:S(2)}) %collective-permute-start.1) | collective-permute-done | bytes 524320 | tf_op jit(solution)/shard_map/ppermute | solution.py:378
  23.8 2.2 %collective-permute-start.2 = (bf16[16,128,128]{2,1,0:T(8,128)(2,1)S(1)}, bf16[16,128,128]{2,1,0:T(8,128)(2,1)S(1)}, u32[]{:S(2)}, u32[]{:S(2)}) collective-permute-start(bf16[16,128,128]{2,1,0:T(8,128)(2,1)S(1)} %collective-permute-done.1.refs_7_), channel_id=1, source_target_pairs={{0,8},{1,5},{2,10},{3,7},{8,16},{9,1},{10,18},{11,3},{16,24},{17,9... | collective-permute-start | bytes 1572872 | tf_op jit(solution)/shard_map/ppermute | solution.py:378
  26.0 2.6 %collective-permute-done.5.refs_4_ = bf16[16,128,128]{2,1,0:T(8,128)(2,1)S(1)} collective-permute-done((bf16[16,128,128]{2,1,0:T(8,128)(2,1)S(1)}, bf16[16,128,128]{2,1,0:T(8,128)(2,1)S(1)}, u32[]{:S(2)}, u32[]{:S(2)}) %collective-permute-start.5) | collective-permute-done | bytes 524320 | tf_op jit(solution)/shard_map/ppermute | solution.py:378
  28.6 3.6 %collective-permute-start.14 = (bf16[16,128,128]{2,1,0:T(8,128)(2,1)S(1)}, bf16[16,128,128]{2,1,0:T(8,128)(2,1)S(1)}, u32[]{:S(2)}, u32[]{:S(2)}) collective-permute-start(bf16[16,128,128]{2,1,0:T(8,128)(2,1)S(1)} %collective-permute-done.13.refs_1_), channel_id=1, source_target_pairs={{0,1},{1,0},{2,3},{3,2},{4,5},{5,4},{6,7},{7,6},{8,9},{9,8},{10,11... | collective-permute-start | bytes 1572872 | tf_op jit(solution)/shard_map/ppermute | solution.py:24
  32.3 1.3 %collective-permute-start.6 = (bf16[16,128,128]{2,1,0:T(8,128)(2,1)S(1)}, bf16[16,128,128]{2,1,0:T(8,128)(2,1)S(1)}, u32[]{:S(2)}, u32[]{:S(2)}) collective-permute-start(bf16[16,128,128]{2,1,0:T(8,128)(2,1)S(1)} %collective-permute-done.5.refs_4_), channel_id=1, source_target_pairs={{0,4},{1,9},{2,6},{3,11},{8,0},{9,17},{10,2},{11,19},{16,8},{17,25... | collective-permute-start | bytes 1572872 | tf_op jit(solution)/shard_map/ppermute | solution.py:378
  33.6 0.5 collective-permute-start.16
  34.1 0.7 pad_add_fusion.2.cols_ref
  34.8 4.5 %shard_map.55 = (s32[145]{0:T(256)S(1)}, s32[3]{0:T(128)S(1)}) custom-call(s32[128]{0:T(128)S(1)} %pad_add_fusion.2.cols_ref, s32[512]{0:T(512)S(1)} %pad_add_fusion.aggs_ref), custom_call_target="tpu_custom_call" | custom-call | flops 1048576 | bytes 16777216 | tf_op jit(solution)/shard_map/pallas_call | solution.py:142
  39.4 2.6 %shard_map.56.rows_ref = bf16[64,128,128]{2,1,0:T(8,128)(2,1)S(1)} custom-call(bf16[16,128,128]{2,1,0:T(8,128)(2,1)} %refs_2_.1, bf16[16,128,128]{2,1,0:T(8,128)(2,1)S(1)} %collective-permute-done.13.refs_1_, bf16[16,128,128]{2,1,0:T(8,128)(2,1)S(1)} %collective-permute-done.8.refs_2_.refs_9_, bf16[16,128,128]{2,1,0:T(8,128)(2,1)S(1)} %collective-permute-done.14.refs_3_), custom_call_target="tpu_custom_call" | custom-call | tf_op jit(solution)/shard_map/pallas_call | solution.py:183
  42.0 2.6 %collective-permute-done.6.refs_5_ = bf16[16,128,128]{2,1,0:T(8,128)(2,1)S(1)} collective-permute-done((bf16[16,128,128]{2,1,0:T(8,128)(2,1)S(1)}, bf16[16,128,128]{2,1,0:T(8,128)(2,1)S(1)}, u32[]{:S(2)}, u32[]{:S(2)}) %collective-permute-start.6) | collective-permute-done | bytes 524320 | tf_op jit(solution)/shard_map/ppermute | solution.py:378
  44.6 0.5 collective-permute-start.21
  45.2 0.4 collective-permute-start.20
  45.6 1.7 %collective-permute-start.17 = (bf16[16,128,128]{2,1,0:T(8,128)(2,1)S(1)}, bf16[16,128,128]{2,1,0:T(8,128)(2,1)S(1)}, u32[]{:S(2)}, u32[]{:S(2)}) collective-permute-start(bf16[16,128,128]{2,1,0:T(8,128)(2,1)S(1)} %collective-permute-done.2.refs_6_), channel_id=1, source_target_pairs={{0,8},{1,5},{2,10},{3,7},{8,16},{9,1},{10,18},{11,3},{16,24},{17,9... | collective-permute-start | bytes 1572872 | tf_op jit(solution)/shard_map/ppermute | solution.py:378
  47.3 0.7 collective-permute-done.19.refs_12_
  48.0 0.7 collective-permute-done.20.refs_13_
  48.7 4.4 %shard_map.57.slots_ref = bf16[144,128,128]{2,1,0:T(8,128)(2,1)S(1)} custom-call(s32[145]{0:T(256)S(1)} %get-tuple-element.47.plan_ref, s32[3]{0:T(128)S(1)} %get-tuple-element.48.starts_ref, bf16[64,128,128]{2,1,0:T(8,128)(2,1)} %bitcast.107, bf16[64,128,128]{2,1,0:T(8,128)(2,1)S(1)} %collective-permute-done.7.refs_1_, bf16[16,128,128]{2,1,0:T(8,128)(2,1)} %refs_2_.1, ...), custom_call_target="tpu_custom_call" | custom-call | flops 268435456 | bytes 1048576 | tf_op jit(solution)/shard_map/pallas_call | solution.py:243
  53.2 0.8 collective-permute-done.17.far0
  54.0 1.2 %collective-permute-start.22 = (bf16[16,128,128]{2,1,0:T(8,128)(2,1)S(1)}, bf16[16,128,128]{2,1,0:T(8,128)(2,1)S(1)}, u32[]{:S(2)}, u32[]{:S(2)}) collective-permute-start(bf16[16,128,128]{2,1,0:T(8,128)(2,1)S(1)} %collective-permute-done.17.far0), channel_id=1, source_target_pairs={{0,1},{1,0},{2,3},{3,2},{4,5},{5,4},{6,7},{7,6},{8,9},{9,8},{10,11... | collective-permute-start | bytes 1572872 | tf_op jit(solution)/shard_map/ppermute | solution.py:24
  55.2 1.5 %collective-permute-done.22.far1 = bf16[16,128,128]{2,1,0:T(8,128)(2,1)S(1)} collective-permute-done((bf16[16,128,128]{2,1,0:T(8,128)(2,1)S(1)}, bf16[16,128,128]{2,1,0:T(8,128)(2,1)S(1)}, u32[]{:S(2)}, u32[]{:S(2)}) %collective-permute-start.22) | collective-permute-done | bytes 524320 | tf_op jit(solution)/shard_map/ppermute | solution.py:24
  56.7 4.2 %shard_map.58 = (bf16[2,2,2,1,1,512,128]{6,5,4,3,2,1,0:T(8,128)(2,1)S(1)}, f32[2,2,2,1,1,512,128]{6,5,4,3,2,1,0:T(8,128)S(1)}, bf16[2,2,2,1,1,512,128]{6,5,4,3,2...) custom-call(s32[145]{0:T(256)S(1)} %get-tuple-element.47.plan_ref, s32[3]{0:T(128)S(1)} %get-tuple-element.48.starts_ref, ...), custom_call_target="tpu_custom_call" | custom-call | flops 268435456 | bytes 16777216 | tf_op jit(solution)/shard_map/pallas_call | solution.py:346
  60.9 0.6 collective-permute-start.23
  61.5 2.3 %collective-permute-start.27 = (bf16[2,2,2,1,1,512,128]{6,5,2,4,3,1,0:T(8,128)(2,1)S(1)}, bf16[2,2,2,1,1,512,128]{6,5,2,4,3,1,0:T(8,128)(2,1)S(1)}, u32[]{:S(2)}, u32[]{:S(2)}) collective-permute-start(bf16[2,2,2,1,1,512,128]{6,5,2,4,3,1,0:T(8,128)(2,1)S(1)} %bitcast.104), channel_id=1, source_target_pairs={{0,4},{1,17},{2,6},{3,19},{4,0},{5,21},{6,2},{7,23},{8,12},{9,25},... | collective-permute-start | bytes 3145736 | tf_op jit(solution)/shard_map/ppermute | solution.py:35
  63.8 22.3 %collective-permute-done.23 = bf16[2,2,2,1,1,512,128]{6,5,2,4,3,1,0:T(8,128)(2,1)S(1)} collective-permute-done((bf16[2,2,2,1,1,512,128]{6,5,2,4,3,1,0:T(8,128)(2,1)S(1)}, bf16[2,2,2,1,1,512,128]{6,5,2,4,3,1,0:T(8,128)(2,1)S(1)}, u32[]{:S(2)}, u32[]{:S(2)}) %collective-permute-start.23) | collective-permute-done | bytes 1048608 | tf_op jit(solution)/shard_map/ppermute | solution.py:35
  86.1 0.2 fusion.3
  86.4 1.5 %collective-permute-start.24 = (bf16[2,2,1,1,512,128]{5,4,3,2,1,0:T(8,128)(2,1)S(1)}, bf16[2,2,1,1,512,128]{5,4,3,2,1,0:T(8,128)(2,1)S(1)}, u32[]{:S(2)}, u32[]{:S(2)}) collective-permute-start(bf16[2,2,1,1,512,128]{5,4,3,2,1,0:T(8,128)(2,1)S(1)} %get-tuple-element.63), channel_id=1, source_target_pairs={{0,4},{1,5},{2,6},{3,7},{4,0},{5,1},{6,2},{7,3},{8,12},{9,13},{10,... | collective-permute-start | bytes 1572872 | tf_op jit(solution)/shard_map/ppermute | solution.py:35
  88.0 2.3 %collective-permute-start.28 = (bf16[2,2,1,1,512,128]{5,4,1,0,3,2:T(8,128)(2,1)S(1)}, bf16[2,2,1,1,512,128]{5,4,1,0,3,2:T(8,128)(2,1)S(1)}, u32[]{:S(2)}, u32[]{:S(2)}) collective-permute-start(bf16[2,2,1,1,512,128]{5,4,1,0,3,2:T(8,128)(2,1)S(1)} %fusion.2), channel_id=1, source_target_pairs={{0,2},{1,5},{2,0},{3,7},{4,6},{5,1},{6,4},{7,3},{8,10},{9,13},{10,... | collective-permute-start | bytes 1572872 | tf_op jit(solution)/shard_map/ppermute | solution.py:35
  90.4 4.2 %collective-permute-done.24 = bf16[2,2,1,1,512,128]{5,4,3,2,1,0:T(8,128)(2,1)S(1)} collective-permute-done((bf16[2,2,1,1,512,128]{5,4,3,2,1,0:T(8,128)(2,1)S(1)}, bf16[2,2,1,1,512,128]{5,4,3,2,1,0:T(8,128)(2,1)S(1)}, u32[]{:S(2)}, u32[]{:S(2)}) %collective-permute-start.24) | collective-permute-done | bytes 524320 | tf_op jit(solution)/shard_map/ppermute | solution.py:35
  94.7 1.3 %collective-permute-start.25 = (bf16[2,1,1,512,128]{4,3,2,1,0:T(8,128)(2,1)S(1)}, bf16[2,1,1,512,128]{4,3,2,1,0:T(8,128)(2,1)S(1)}, u32[]{:S(2)}, u32[]{:S(2)}) collective-permute-start(bf16[2,1,1,512,128]{4,3,2,1,0:T(8,128)(2,1)S(1)} %get-tuple-element.65), channel_id=1, source_target_pairs={{0,8},{1,3},{2,10},{3,1},{4,12},{5,7},{6,14},{7,5},{8,0},{9,11},{1... | collective-permute-start | bytes 786440 | tf_op jit(solution)/shard_map/ppermute | solution.py:35
  96.0 4.4 %collective-permute-done.28 = bf16[2,2,1,1,512,128]{5,4,1,0,3,2:T(8,128)(2,1)S(1)} collective-permute-done((bf16[2,2,1,1,512,128]{5,4,1,0,3,2:T(8,128)(2,1)S(1)}, bf16[2,2,1,1,512,128]{5,4,1,0,3,2:T(8,128)(2,1)S(1)}, u32[]{:S(2)}, u32[]{:S(2)}) %collective-permute-start.28) | collective-permute-done | bytes 524320 | tf_op jit(solution)/shard_map/ppermute | solution.py:35
  100.4 1.3 %collective-permute-start.29 = (bf16[2,1,1,512,128]{4,3,0,2,1:T(8,128)(2,1)S(1)}, bf16[2,1,1,512,128]{4,3,0,2,1:T(8,128)(2,1)S(1)}, u32[]{:S(2)}, u32[]{:S(2)}) collective-permute-start(bf16[2,1,1,512,128]{4,3,0,2,1:T(8,128)(2,1)S(1)} %fusion.11), channel_id=1, source_target_pairs={{0,8},{1,3},{2,10},{3,1},{4,12},{5,7},{6,14},{7,5},{8,0},{9,11},{1... | collective-permute-start | bytes 786440 | tf_op jit(solution)/shard_map/ppermute | solution.py:35
  102.0 3.8 %collective-permute-done.29 = bf16[2,1,1,512,128]{4,3,0,2,1:T(8,128)(2,1)S(1)} collective-permute-done((bf16[2,1,1,512,128]{4,3,0,2,1:T(8,128)(2,1)S(1)}, bf16[2,1,1,512,128]{4,3,0,2,1:T(8,128)(2,1)S(1)}, u32[]{:S(2)}, u32[]{:S(2)}) %collective-permute-start.29) | collective-permute-done | bytes 262176 | tf_op jit(solution)/shard_map/ppermute | solution.py:35
  105.8 2.1 %collective-permute-done.26 = bf16[1,1,512,128]{3,2,1,0:T(8,128)(2,1)S(1)} collective-permute-done((bf16[1,1,512,128]{3,2,1,0:T(8,128)(2,1)S(1)}, bf16[1,1,512,128]{3,2,1,0:T(8,128)(2,1)S(1)}, u32[]{:S(2)}, u32[]{:S(2)}) %collective-permute-start.26) | collective-permute-done | bytes 131104 | tf_op jit(solution)/shard_map/ppermute | solution.py:35
  108.0 1.7 %collective-permute-done.30 = bf16[1,1,512,128]{3,2,1,0:T(8,128)(2,1)S(1)} collective-permute-done((bf16[1,1,512,128]{3,2,1,0:T(8,128)(2,1)S(1)}, bf16[1,1,512,128]{3,2,1,0:T(8,128)(2,1)S(1)}, u32[]{:S(2)}, u32[]{:S(2)}) %collective-permute-start.30) | collective-permute-done | bytes 131104 | tf_op jit(solution)/shard_map/ppermute | solution.py:35
  109.7 0.8 pad_maximum_fusion
  (33 shorter events, 1.1 us)
Async XLA Ops:
  0.0 11.9 %collective-permute-start.7 = (bf16[64,128,128]{2,1,0:T(8,128)(2,1)}, bf16[64,128,128]{2,1,0:T(8,128)(2,1)S(1)}, u32[]{:S(2)}, u32[]{:S(2)}) collective-permute-start(bf16[64,128,128]{2,1,0:T(8,128)(2,1)} %bitcast.106), channel_id=1, source_target_pairs={{0,1},{1,0},{2,3},{3,2},{4,5},{5,4},{6,7},{7,6},{8,9},{9,8},{10,11... | collective-permute-start | bytes 6291464 | tf_op jit(solution)/shard_map/ppermute | solution.py:24
  0.1 4.3 %collective-permute-start.3 = (s32[64]{0:T(128)}, s32[64]{0:T(128)S(1)}, u32[]{:S(2)}, u32[]{:S(2)}) collective-permute-start(s32[64]{0:T(128)} %bitcast.110), channel_id=1, source_target_pairs={{0,1},{1,0},{2,3},{3,2},{4,5},{5,4},{6,7},{7,6},{8,9},{9,8},{10,11... | collective-permute-start | bytes 776 | tf_op jit(solution)/shard_map/ppermute | solution.py:24
  0.5 7.0 %collective-permute-start.8 = (bf16[16,128,128]{2,1,0:T(8,128)(2,1)}, bf16[16,128,128]{2,1,0:T(8,128)(2,1)S(1)}, u32[]{:S(2)}, u32[]{:S(2)}) collective-permute-start(bf16[16,128,128]{2,1,0:T(8,128)(2,1)} %refs_2_.1), channel_id=1, source_target_pairs={{0,1},{1,0},{2,3},{3,2},{4,5},{5,4},{6,7},{7,6},{8,9},{9,8},{10,11... | collective-permute-start | bytes 1572872 | tf_op jit(solution)/shard_map/ppermute | solution.py:24
  0.6 11.3 %collective-permute-start = (bf16[16,128,128]{2,1,0:T(8,128)(2,1)}, bf16[16,128,128]{2,1,0:T(8,128)(2,1)S(1)}, u32[]{:S(2)}, u32[]{:S(2)}) collective-permute-start(bf16[16,128,128]{2,1,0:T(8,128)(2,1)} %refs_2_.1), channel_id=1, source_target_pairs={{0,8},{1,5},{2,10},{3,7},{8,16},{9,1},{10,18},{11,3},{16,24},{17,9... | collective-permute-start | bytes 1572872 | tf_op jit(solution)/shard_map/ppermute | solution.py:378
  4.4 11.6 %collective-permute-start.4 = (bf16[16,128,128]{2,1,0:T(8,128)(2,1)}, bf16[16,128,128]{2,1,0:T(8,128)(2,1)S(1)}, u32[]{:S(2)}, u32[]{:S(2)}) collective-permute-start(bf16[16,128,128]{2,1,0:T(8,128)(2,1)} %refs_2_.1), channel_id=1, source_target_pairs={{0,4},{1,9},{2,6},{3,11},{8,0},{9,17},{10,2},{11,19},{16,8},{17,25... | collective-permute-start | bytes 1572872 | tf_op jit(solution)/shard_map/ppermute | solution.py:378
  11.9 5.7 %collective-permute-start.11 = (s32[64]{0:T(128)S(1)}, s32[64]{0:T(128)S(1)}, u32[]{:S(2)}, u32[]{:S(2)}) collective-permute-start(s32[64]{0:T(128)S(1)} %bitcast_add_fusion), channel_id=1, source_target_pairs={{0,12},{4,8},{8,4},{12,0},{16,28},{20,24},{24,20},{28,16},{1,13},{... | collective-permute-start | bytes 776 | tf_op jit(solution)/shard_map/ppermute | solution.py:24
  14.0 3.6 %collective-permute-start.10 = (s32[64]{0:T(128)S(1)}, s32[64]{0:T(128)S(1)}, u32[]{:S(2)}, u32[]{:S(2)}) collective-permute-start(s32[64]{0:T(128)S(1)} %bitcast_add_fusion), channel_id=1, source_target_pairs={{0,8},{4,12},{8,0},{12,4},{16,24},{20,28},{24,16},{28,20},{1,9},{5... | collective-permute-start | bytes 776 | tf_op jit(solution)/shard_map/ppermute | solution.py:24
  14.2 3.4 %collective-permute-start.9 = (s32[64]{0:T(128)S(1)}, s32[64]{0:T(128)S(1)}, u32[]{:S(2)}, u32[]{:S(2)}) collective-permute-start(s32[64]{0:T(128)S(1)} %bitcast_add_fusion), channel_id=1, source_target_pairs={{0,4},{4,0},{8,12},{12,8},{16,20},{20,16},{24,28},{28,24},{1,5},{5... | collective-permute-start | bytes 776 | tf_op jit(solution)/shard_map/ppermute | solution.py:24
  14.6 9.2 %collective-permute-start.1 = (bf16[16,128,128]{2,1,0:T(8,128)(2,1)S(1)}, bf16[16,128,128]{2,1,0:T(8,128)(2,1)S(1)}, u32[]{:S(2)}, u32[]{:S(2)}) collective-permute-start(bf16[16,128,128]{2,1,0:T(8,128)(2,1)S(1)} %collective-permute-done.refs_8_), channel_id=1, source_target_pairs={{0,8},{1,5},{2,10},{3,7},{8,16},{9,1},{10,18},{11,3},{16,24},{17,9... | collective-permute-start | bytes 1572872 | tf_op jit(solution)/shard_map/ppermute | solution.py:378
  16.0 12.6 %collective-permute-start.5 = (bf16[16,128,128]{2,1,0:T(8,128)(2,1)S(1)}, bf16[16,128,128]{2,1,0:T(8,128)(2,1)S(1)}, u32[]{:S(2)}, u32[]{:S(2)}) collective-permute-start(bf16[16,128,128]{2,1,0:T(8,128)(2,1)S(1)} %collective-permute-done.4.refs_3_), channel_id=1, source_target_pairs={{0,4},{1,9},{2,6},{3,11},{8,0},{9,17},{10,2},{11,19},{16,8},{17,25... | collective-permute-start | bytes 1572872 | tf_op jit(solution)/shard_map/ppermute | solution.py:378
  17.7 10.9 %collective-permute-start.13 = (bf16[16,128,128]{2,1,0:T(8,128)(2,1)}, bf16[16,128,128]{2,1,0:T(8,128)(2,1)S(1)}, u32[]{:S(2)}, u32[]{:S(2)}) collective-permute-start(bf16[16,128,128]{2,1,0:T(8,128)(2,1)} %refs_2_.1), channel_id=1, source_target_pairs={{0,2},{1,3},{2,0},{3,1},{4,6},{5,7},{6,4},{7,5},{8,10},{9,11},{10,... | collective-permute-start | bytes 1572872 | tf_op jit(solution)/shard_map/ppermute | solution.py:24
  18.9 14.7 %collective-permute-start.12 = (s32[256]{0:T(256)S(1)}, s32[256]{0:T(256)S(1)}, u32[]{:S(2)}, u32[]{:S(2)}) collective-permute-start(s32[256]{0:T(256)S(1)} %pad_add_fusion.1), channel_id=1, source_target_pairs={{0,16},{4,20},{8,24},{12,28},{16,0},{20,4},{24,8},{28,12},{1,17},{... | collective-permute-start | bytes 3080 | tf_op jit(solution)/shard_map/ppermute | solution.py:24
  23.8 18.2 %collective-permute-start.2 = (bf16[16,128,128]{2,1,0:T(8,128)(2,1)S(1)}, bf16[16,128,128]{2,1,0:T(8,128)(2,1)S(1)}, u32[]{:S(2)}, u32[]{:S(2)}) collective-permute-start(bf16[16,128,128]{2,1,0:T(8,128)(2,1)S(1)} %collective-permute-done.1.refs_7_), channel_id=1, source_target_pairs={{0,8},{1,5},{2,10},{3,7},{8,16},{9,1},{10,18},{11,3},{16,24},{17,9... | collective-permute-start | bytes 1572872 | tf_op jit(solution)/shard_map/ppermute | solution.py:378
  28.6 10.8 %collective-permute-start.14 = (bf16[16,128,128]{2,1,0:T(8,128)(2,1)S(1)}, bf16[16,128,128]{2,1,0:T(8,128)(2,1)S(1)}, u32[]{:S(2)}, u32[]{:S(2)}) collective-permute-start(bf16[16,128,128]{2,1,0:T(8,128)(2,1)S(1)} %collective-permute-done.13.refs_1_), channel_id=1, source_target_pairs={{0,1},{1,0},{2,3},{3,2},{4,5},{5,4},{6,7},{7,6},{8,9},{9,8},{10,11... | collective-permute-start | bytes 1572872 | tf_op jit(solution)/shard_map/ppermute | solution.py:24
  32.3 12.3 %collective-permute-start.6 = (bf16[16,128,128]{2,1,0:T(8,128)(2,1)S(1)}, bf16[16,128,128]{2,1,0:T(8,128)(2,1)S(1)}, u32[]{:S(2)}, u32[]{:S(2)}) collective-permute-start(bf16[16,128,128]{2,1,0:T(8,128)(2,1)S(1)} %collective-permute-done.5.refs_4_), channel_id=1, source_target_pairs={{0,4},{1,9},{2,6},{3,11},{8,0},{9,17},{10,2},{11,19},{16,8},{17,25... | collective-permute-start | bytes 1572872 | tf_op jit(solution)/shard_map/ppermute | solution.py:378
  33.6 11.0 %collective-permute-start.15 = (bf16[16,128,128]{2,1,0:T(8,128)(2,1)S(1)}, bf16[16,128,128]{2,1,0:T(8,128)(2,1)S(1)}, u32[]{:S(2)}, u32[]{:S(2)}) collective-permute-start(bf16[16,128,128]{2,1,0:T(8,128)(2,1)S(1)} %collective-permute-done.4.refs_3_), channel_id=1, source_target_pairs={{0,1},{1,0},{2,3},{3,2},{4,5},{5,4},{6,7},{7,6},{8,9},{9,8},{10,11... | collective-permute-start | bytes 1572872 | tf_op jit(solution)/shard_map/ppermute | solution.py:24
  33.6 11.0 %collective-permute-start.16 = (bf16[16,128,128]{2,1,0:T(8,128)(2,1)S(1)}, bf16[16,128,128]{2,1,0:T(8,128)(2,1)S(1)}, u32[]{:S(2)}, u32[]{:S(2)}) collective-permute-start(bf16[16,128,128]{2,1,0:T(8,128)(2,1)S(1)} %collective-permute-done.refs_8_), channel_id=1, source_target_pairs={{0,1},{1,0},{2,3},{3,2},{4,5},{5,4},{6,7},{7,6},{8,9},{9,8},{10,11... | collective-permute-start | bytes 1572872 | tf_op jit(solution)/shard_map/ppermute | solution.py:24
  44.6 2.7 %collective-permute-start.18 = (bf16[16,128,128]{2,1,0:T(8,128)(2,1)S(1)}, bf16[16,128,128]{2,1,0:T(8,128)(2,1)S(1)}, u32[]{:S(2)}, u32[]{:S(2)}) collective-permute-start(bf16[16,128,128]{2,1,0:T(8,128)(2,1)S(1)} %collective-permute-done.5.refs_4_), channel_id=1, source_target_pairs={{0,1},{1,0},{2,3},{3,2},{4,5},{5,4},{6,7},{7,6},{8,9},{9,8},{10,11... | collective-permute-start | bytes 1572872 | tf_op jit(solution)/shard_map/ppermute | solution.py:24
  44.6 2.7 %collective-permute-start.21 = (bf16[16,128,128]{2,1,0:T(8,128)(2,1)S(1)}, bf16[16,128,128]{2,1,0:T(8,128)(2,1)S(1)}, u32[]{:S(2)}, u32[]{:S(2)}) collective-permute-start(bf16[16,128,128]{2,1,0:T(8,128)(2,1)S(1)} %collective-permute-done.1.refs_7_), channel_id=1, source_target_pairs={{0,1},{1,0},{2,3},{3,2},{4,5},{5,4},{6,7},{7,6},{8,9},{9,8},{10,11... | collective-permute-start | bytes 1572872 | tf_op jit(solution)/shard_map/ppermute | solution.py:24
  45.1 2.9 %collective-permute-start.19 = (bf16[16,128,128]{2,1,0:T(8,128)(2,1)S(1)}, bf16[16,128,128]{2,1,0:T(8,128)(2,1)S(1)}, u32[]{:S(2)}, u32[]{:S(2)}) collective-permute-start(bf16[16,128,128]{2,1,0:T(8,128)(2,1)S(1)} %collective-permute-done.6.refs_5_), channel_id=1, source_target_pairs={{0,1},{1,0},{2,3},{3,2},{4,5},{5,4},{6,7},{7,6},{8,9},{9,8},{10,11... | collective-permute-start | bytes 1572872 | tf_op jit(solution)/shard_map/ppermute | solution.py:24
  45.2 3.6 %collective-permute-start.20 = (bf16[16,128,128]{2,1,0:T(8,128)(2,1)S(1)}, bf16[16,128,128]{2,1,0:T(8,128)(2,1)S(1)}, u32[]{:S(2)}, u32[]{:S(2)}) collective-permute-start(bf16[16,128,128]{2,1,0:T(8,128)(2,1)S(1)} %collective-permute-done.2.refs_6_), channel_id=1, source_target_pairs={{0,1},{1,0},{2,3},{3,2},{4,5},{5,4},{6,7},{7,6},{8,9},{9,8},{10,11... | collective-permute-start | bytes 1572872 | tf_op jit(solution)/shard_map/ppermute | solution.py:24
  45.6 8.4 %collective-permute-start.17 = (bf16[16,128,128]{2,1,0:T(8,128)(2,1)S(1)}, bf16[16,128,128]{2,1,0:T(8,128)(2,1)S(1)}, u32[]{:S(2)}, u32[]{:S(2)}) collective-permute-start(bf16[16,128,128]{2,1,0:T(8,128)(2,1)S(1)} %collective-permute-done.2.refs_6_), channel_id=1, source_target_pairs={{0,8},{1,5},{2,10},{3,7},{8,16},{9,1},{10,18},{11,3},{16,24},{17,9... | collective-permute-start | bytes 1572872 | tf_op jit(solution)/shard_map/ppermute | solution.py:378
  54.0 2.7 %collective-permute-start.22 = (bf16[16,128,128]{2,1,0:T(8,128)(2,1)S(1)}, bf16[16,128,128]{2,1,0:T(8,128)(2,1)S(1)}, u32[]{:S(2)}, u32[]{:S(2)}) collective-permute-start(bf16[16,128,128]{2,1,0:T(8,128)(2,1)S(1)} %collective-permute-done.17.far0), channel_id=1, source_target_pairs={{0,1},{1,0},{2,3},{3,2},{4,5},{5,4},{6,7},{7,6},{8,9},{9,8},{10,11... | collective-permute-start | bytes 1572872 | tf_op jit(solution)/shard_map/ppermute | solution.py:24
  60.9 25.2 %collective-permute-start.23 = (bf16[2,2,2,1,1,512,128]{6,5,2,4,3,1,0:T(8,128)(2,1)S(1)}, bf16[2,2,2,1,1,512,128]{6,5,2,4,3,1,0:T(8,128)(2,1)S(1)}, u32[]{:S(2)}, u32[]{:S(2)}) collective-permute-start(bf16[2,2,2,1,1,512,128]{6,5,2,4,3,1,0:T(8,128)(2,1)S(1)} %bitcast.105), channel_id=1, source_target_pairs={{0,2},{1,9},{2,0},{3,11},{4,6},{5,13},{6,4},{7,15},{8,10},{9,1},{1... | collective-permute-start | bytes 3145736 | tf_op jit(solution)/shard_map/ppermute | solution.py:35
  61.5 26.3 %collective-permute-start.27 = (bf16[2,2,2,1,1,512,128]{6,5,2,4,3,1,0:T(8,128)(2,1)S(1)}, bf16[2,2,2,1,1,512,128]{6,5,2,4,3,1,0:T(8,128)(2,1)S(1)}, u32[]{:S(2)}, u32[]{:S(2)}) collective-permute-start(bf16[2,2,2,1,1,512,128]{6,5,2,4,3,1,0:T(8,128)(2,1)S(1)} %bitcast.104), channel_id=1, source_target_pairs={{0,4},{1,17},{2,6},{3,19},{4,0},{5,21},{6,2},{7,23},{8,12},{9,25},... | collective-permute-start | bytes 3145736 | tf_op jit(solution)/shard_map/ppermute | solution.py:35
  86.4 8.2 %collective-permute-start.24 = (bf16[2,2,1,1,512,128]{5,4,3,2,1,0:T(8,128)(2,1)S(1)}, bf16[2,2,1,1,512,128]{5,4,3,2,1,0:T(8,128)(2,1)S(1)}, u32[]{:S(2)}, u32[]{:S(2)}) collective-permute-start(bf16[2,2,1,1,512,128]{5,4,3,2,1,0:T(8,128)(2,1)S(1)} %get-tuple-element.63), channel_id=1, source_target_pairs={{0,4},{1,5},{2,6},{3,7},{4,0},{5,1},{6,2},{7,3},{8,12},{9,13},{10,... | collective-permute-start | bytes 1572872 | tf_op jit(solution)/shard_map/ppermute | solution.py:35
  88.0 12.4 %collective-permute-start.28 = (bf16[2,2,1,1,512,128]{5,4,1,0,3,2:T(8,128)(2,1)S(1)}, bf16[2,2,1,1,512,128]{5,4,1,0,3,2:T(8,128)(2,1)S(1)}, u32[]{:S(2)}, u32[]{:S(2)}) collective-permute-start(bf16[2,2,1,1,512,128]{5,4,1,0,3,2:T(8,128)(2,1)S(1)} %fusion.2), channel_id=1, source_target_pairs={{0,2},{1,5},{2,0},{3,7},{4,6},{5,1},{6,4},{7,3},{8,10},{9,13},{10,... | collective-permute-start | bytes 1572872 | tf_op jit(solution)/shard_map/ppermute | solution.py:35
  94.7 7.1 %collective-permute-start.25 = (bf16[2,1,1,512,128]{4,3,2,1,0:T(8,128)(2,1)S(1)}, bf16[2,1,1,512,128]{4,3,2,1,0:T(8,128)(2,1)S(1)}, u32[]{:S(2)}, u32[]{:S(2)}) collective-permute-start(bf16[2,1,1,512,128]{4,3,2,1,0:T(8,128)(2,1)S(1)} %get-tuple-element.65), channel_id=1, source_target_pairs={{0,8},{1,3},{2,10},{3,1},{4,12},{5,7},{6,14},{7,5},{8,0},{9,11},{1... | collective-permute-start | bytes 786440 | tf_op jit(solution)/shard_map/ppermute | solution.py:35
  100.4 5.3 %collective-permute-start.29 = (bf16[2,1,1,512,128]{4,3,0,2,1:T(8,128)(2,1)S(1)}, bf16[2,1,1,512,128]{4,3,0,2,1:T(8,128)(2,1)S(1)}, u32[]{:S(2)}, u32[]{:S(2)}) collective-permute-start(bf16[2,1,1,512,128]{4,3,0,2,1:T(8,128)(2,1)S(1)} %fusion.11), channel_id=1, source_target_pairs={{0,8},{1,3},{2,10},{3,1},{4,12},{5,7},{6,14},{7,5},{8,0},{9,11},{1... | collective-permute-start | bytes 786440 | tf_op jit(solution)/shard_map/ppermute | solution.py:35
  101.9 6.1 %collective-permute-start.26 = (bf16[1,1,512,128]{3,2,1,0:T(8,128)(2,1)S(1)}, bf16[1,1,512,128]{3,2,1,0:T(8,128)(2,1)S(1)}, u32[]{:S(2)}, u32[]{:S(2)}) collective-permute-start(bf16[1,1,512,128]{3,2,1,0:T(8,128)(2,1)S(1)} %fusion.22), channel_id=1, source_target_pairs={{0,16},{1,17},{2,18},{3,19},{4,20},{5,21},{6,22},{7,23},{8,24},{9,... | collective-permute-start | bytes 393224 | tf_op jit(solution)/shard_map/ppermute | solution.py:35
  105.8 3.9 %collective-permute-start.30 = (bf16[1,1,512,128]{3,2,1,0:T(8,128)(2,1)S(1)}, bf16[1,1,512,128]{3,2,1,0:T(8,128)(2,1)S(1)}, u32[]{:S(2)}, u32[]{:S(2)}) collective-permute-start(bf16[1,1,512,128]{3,2,1,0:T(8,128)(2,1)S(1)} %fusion.23), channel_id=1, source_target_pairs={{0,16},{1,9},{2,18},{3,11},{4,20},{5,13},{6,22},{7,15},{8,24},{9,1... | collective-permute-start | bytes 393224 | tf_op jit(solution)/shard_map/ppermute | solution.py:35

commit v9 on v7

--- a/solution.py
+++ b/solution.py
@@ -11,7 +11,7 @@
 
 OWN = 2
 UNROLL = 8
-ORDERS = (("yx21", "1yx2"), ("xy12", "x1y2"), ("2xy1", "y1x2"))
+ORDERS = (("xy12", "y1x2"), ("yx21", "12yx"), ("xy12", "2x1y"))
 LINKS = {"x": ("col", 2), "y": ("row", 1), "1": ("row", 2), "2": ("row", 4)}
 
 

time: 107 us -> 109 us (1.019)
  starting transfers between devices: 40.5 us -> 42 us
    ppermute x12, starting transfers between devices: 16.8 us -> 18.3 us  [exchange(): return lax.ppermute(value, ('row', 'col'), moves)]
  transfers between devices with their start and end apart: 35 -> 35, of which waited for: 18 -> 18; matrix products, arithmetic and copies ran while one was open for 2% -> 2% of each run, Pallas kernels for 11% -> 10%
where the time goes in v9:
time: 109 us
  waiting for transfers between devices  48.8 us (45%)
  starting transfers between devices  42 us (39%)
  Pallas kernels  14.8 us (14%)
  other arithmetic  3.11 us (3%)
    ppermute x12, waiting for transfers between devices, exchange(): return lax.ppermute(value, ('row', 'col'), moves)  28 us
    ppermute x12, starting transfers between devices, exchange(): return lax.ppermute(value, ('row', 'col'), moves)  18.3 us
    ppermute x7, waiting for transfers between devices, ring(): return lax.ppermute(value, ('row', 'col'), moves)  15.1 us
    ppermute x16, starting transfers between devices, swap(): return lax.ppermute(value, axis, [(i, i ^ bit) for i in range(size)])  12.3 us
    ppermute x7, starting transfers between devices, ring(): return lax.ppermute(value, ('row', 'col'), moves)  11.4 us
    ppermute x16, waiting for transfers between devices, swap(): return lax.ppermute(value, axis, [(i, i ^ bit) for i in range(size)])  5.67 us
    pallas_call x1, Pallas kernels, make_plan(): pl.pallas_call(functools.partial(plan_kernel, s), in_specs=[smem, smem],...  4.54 us
    pallas_call x1, Pallas kernels, make_products(): pl.pallas_call(functools.partial(product_kernel, s), in_specs=[smem, smem...  3.99 us
  transfers between devices with their start and end apart: 35, of which 18 were waited for; matrix products, arithmetic and copies ran while one was open for 2% of the time, Pallas kernels for 10%

profile of v9, /device:TPU:0, one launch (start us, length us, event | category | flops | bytes accessed | tf_op | source)
XLA Modules:
  0.0 108.8 jit_solution(10828224302193729566)
XLA Ops:
  0.0 0.5 collective-permute-start.7
  0.5 0.5 collective-permute-start.8
  1.0 2.6 %collective-permute-start = (bf16[16,128,128]{2,1,0:T(8,128)(2,1)}, bf16[16,128,128]{2,1,0:T(8,128)(2,1)S(1)}, u32[]{:S(2)}, u32[]{:S(2)}) collective-permute-start(bf16[16,128,128]{2,1,0:T(8,128)(2,1)} %refs_2_.1), channel_id=1, source_target_pairs={{0,8},{1,5},{2,10},{3,7},{8,16},{9,1},{10,18},{11,3},{16,24},{17,9... | collective-permute-start | bytes 1572872 | tf_op jit(solution)/shard_map/ppermute | solution.py:381
  3.5 0.9 collective-permute-done.3
  4.5 2.9 %collective-permute-start.4 = (bf16[16,128,128]{2,1,0:T(8,128)(2,1)}, bf16[16,128,128]{2,1,0:T(8,128)(2,1)S(1)}, u32[]{:S(2)}, u32[]{:S(2)}) collective-permute-start(bf16[16,128,128]{2,1,0:T(8,128)(2,1)} %refs_2_.1), channel_id=1, source_target_pairs={{0,4},{1,9},{2,6},{3,11},{8,0},{9,17},{10,2},{11,19},{16,8},{17,25... | collective-permute-start | bytes 1572872 | tf_op jit(solution)/shard_map/ppermute | solution.py:381
  7.3 0.7 bitcast_add_fusion
  8.0 5.1 %collective-permute-done.refs_8_ = bf16[16,128,128]{2,1,0:T(8,128)(2,1)S(1)} collective-permute-done((bf16[16,128,128]{2,1,0:T(8,128)(2,1)}, bf16[16,128,128]{2,1,0:T(8,128)(2,1)S(1)}, u32[]{:S(2)}, u32[]{:S(2)}) %collective-permute-start) | collective-permute-done | bytes 524320 | tf_op jit(solution)/shard_map/ppermute | solution.py:381
  13.1 3.3 %collective-permute-start.11 = (s32[64]{0:T(128)S(1)}, s32[64]{0:T(128)S(1)}, u32[]{:S(2)}, u32[]{:S(2)}) collective-permute-start(s32[64]{0:T(128)S(1)} %bitcast_add_fusion), channel_id=1, source_target_pairs={{0,12},{4,8},{8,4},{12,0},{16,28},{20,24},{24,20},{28,16},{1,13},{... | collective-permute-start | bytes 776 | tf_op jit(solution)/shard_map/ppermute | solution.py:24
  16.4 0.4 collective-permute-start.10
  17.0 2.0 %collective-permute-start.1 = (bf16[16,128,128]{2,1,0:T(8,128)(2,1)S(1)}, bf16[16,128,128]{2,1,0:T(8,128)(2,1)S(1)}, u32[]{:S(2)}, u32[]{:S(2)}) collective-permute-start(bf16[16,128,128]{2,1,0:T(8,128)(2,1)S(1)} %collective-permute-done.refs_8_), channel_id=1, source_target_pairs={{0,8},{1,5},{2,10},{3,7},{8,16},{9,1},{10,18},{11,3},{16,24},{17,9... | collective-permute-start | bytes 1572872 | tf_op jit(solution)/shard_map/ppermute | solution.py:381
  19.0 1.0 collective-permute-done.10
  20.0 0.4 collective-permute-done.9
  20.5 1.5 %collective-permute-start.13 = (bf16[16,128,128]{2,1,0:T(8,128)(2,1)}, bf16[16,128,128]{2,1,0:T(8,128)(2,1)S(1)}, u32[]{:S(2)}, u32[]{:S(2)}) collective-permute-start(bf16[16,128,128]{2,1,0:T(8,128)(2,1)} %refs_2_.1), channel_id=1, source_target_pairs={{0,2},{1,3},{2,0},{3,1},{4,6},{5,7},{6,4},{7,5},{8,10},{9,11},{10,... | collective-permute-start | bytes 1572872 | tf_op jit(solution)/shard_map/ppermute | solution.py:24
  22.0 2.6 %collective-permute-start.12 = (s32[256]{0:T(256)S(1)}, s32[256]{0:T(256)S(1)}, u32[]{:S(2)}, u32[]{:S(2)}) collective-permute-start(s32[256]{0:T(256)S(1)} %pad_add_fusion.1), channel_id=1, source_target_pairs={{0,16},{4,20},{8,24},{12,28},{16,0},{20,4},{24,8},{28,12},{1,17},{... | collective-permute-start | bytes 3080 | tf_op jit(solution)/shard_map/ppermute | solution.py:24
  24.6 5.8 %collective-permute-done.1.refs_7_ = bf16[16,128,128]{2,1,0:T(8,128)(2,1)S(1)} collective-permute-done((bf16[16,128,128]{2,1,0:T(8,128)(2,1)S(1)}, bf16[16,128,128]{2,1,0:T(8,128)(2,1)S(1)}, u32[]{:S(2)}, u32[]{:S(2)}) %collective-permute-start.1) | collective-permute-done | bytes 524320 | tf_op jit(solution)/shard_map/ppermute | solution.py:381
  30.4 1.8 %collective-permute-start.2 = (bf16[16,128,128]{2,1,0:T(8,128)(2,1)S(1)}, bf16[16,128,128]{2,1,0:T(8,128)(2,1)S(1)}, u32[]{:S(2)}, u32[]{:S(2)}) collective-permute-start(bf16[16,128,128]{2,1,0:T(8,128)(2,1)S(1)} %collective-permute-done.1.refs_7_), channel_id=1, source_target_pairs={{0,8},{1,5},{2,10},{3,7},{8,16},{9,1},{10,18},{11,3},{16,24},{17,9... | collective-permute-start | bytes 1572872 | tf_op jit(solution)/shard_map/ppermute | solution.py:381
  32.5 1.5 %collective-permute-start.15 = (bf16[16,128,128]{2,1,0:T(8,128)(2,1)S(1)}, bf16[16,128,128]{2,1,0:T(8,128)(2,1)S(1)}, u32[]{:S(2)}, u32[]{:S(2)}) collective-permute-start(bf16[16,128,128]{2,1,0:T(8,128)(2,1)S(1)} %collective-permute-done.4.refs_3_), channel_id=1, source_target_pairs={{0,1},{1,0},{2,3},{3,2},{4,5},{5,4},{6,7},{7,6},{8,9},{9,8},{10,11... | collective-permute-start | bytes 1572872 | tf_op jit(solution)/shard_map/ppermute | solution.py:24
  34.1 0.7 pad_add_fusion.2.cols_ref
  34.8 4.5 %shard_map.55 = (s32[145]{0:T(256)S(1)}, s32[3]{0:T(128)S(1)}) custom-call(s32[128]{0:T(128)S(1)} %pad_add_fusion.2.cols_ref, s32[512]{0:T(512)S(1)} %pad_add_fusion.aggs_ref), custom_call_target="tpu_custom_call" | custom-call | flops 1048576 | bytes 16777216 | tf_op jit(solution)/shard_map/pallas_call | solution.py:142
  39.3 2.6 %shard_map.56.rows_ref = bf16[64,128,128]{2,1,0:T(8,128)(2,1)S(1)} custom-call(bf16[16,128,128]{2,1,0:T(8,128)(2,1)} %refs_2_.1, bf16[16,128,128]{2,1,0:T(8,128)(2,1)S(1)} %collective-permute-done.13.refs_1_, bf16[16,128,128]{2,1,0:T(8,128)(2,1)S(1)} %collective-permute-done.8.refs_2_.refs_9_, bf16[16,128,128]{2,1,0:T(8,128)(2,1)S(1)} %collective-permute-done.14.refs_3_), custom_call_target="tpu_custom_call" | custom-call | tf_op jit(solution)/shard_map/pallas_call | solution.py:183
  41.9 1.9 %collective-permute-done.2.refs_6_ = bf16[16,128,128]{2,1,0:T(8,128)(2,1)S(1)} collective-permute-done((bf16[16,128,128]{2,1,0:T(8,128)(2,1)S(1)}, bf16[16,128,128]{2,1,0:T(8,128)(2,1)S(1)}, u32[]{:S(2)}, u32[]{:S(2)}) %collective-permute-start.2) | collective-permute-done | bytes 524320 | tf_op jit(solution)/shard_map/ppermute | solution.py:381
  43.8 1.2 %collective-permute-start.18 = (bf16[16,128,128]{2,1,0:T(8,128)(2,1)S(1)}, bf16[16,128,128]{2,1,0:T(8,128)(2,1)S(1)}, u32[]{:S(2)}, u32[]{:S(2)}) collective-permute-start(bf16[16,128,128]{2,1,0:T(8,128)(2,1)S(1)} %collective-permute-done.5.refs_4_), channel_id=1, source_target_pairs={{0,1},{1,0},{2,3},{3,2},{4,5},{5,4},{6,7},{7,6},{8,9},{9,8},{10,11... | collective-permute-start | bytes 1572872 | tf_op jit(solution)/shard_map/ppermute | solution.py:24
  45.1 0.4 collective-permute-start.19
  45.6 1.8 %collective-permute-start.17 = (bf16[16,128,128]{2,1,0:T(8,128)(2,1)S(1)}, bf16[16,128,128]{2,1,0:T(8,128)(2,1)S(1)}, u32[]{:S(2)}, u32[]{:S(2)}) collective-permute-start(bf16[16,128,128]{2,1,0:T(8,128)(2,1)S(1)} %collective-permute-done.2.refs_6_), channel_id=1, source_target_pairs={{0,8},{1,5},{2,10},{3,7},{8,16},{9,1},{10,18},{11,3},{16,24},{17,9... | collective-permute-start | bytes 1572872 | tf_op jit(solution)/shard_map/ppermute | solution.py:381
  47.4 0.6 collective-permute-done.19.refs_12_
  48.1 0.7 collective-permute-done.20.refs_13_
  48.8 4.0 %shard_map.57.slots_ref = bf16[144,128,128]{2,1,0:T(8,128)(2,1)S(1)} custom-call(s32[145]{0:T(256)S(1)} %get-tuple-element.49.plan_ref, s32[3]{0:T(128)S(1)} %get-tuple-element.50.starts_ref, bf16[64,128,128]{2,1,0:T(8,128)(2,1)} %bitcast.155, bf16[64,128,128]{2,1,0:T(8,128)(2,1)S(1)} %collective-permute-done.7.refs_1_, bf16[16,128,128]{2,1,0:T(8,128)(2,1)} %refs_2_.1, ...), custom_call_target="tpu_custom_call" | custom-call | flops 268435456 | bytes 1048576 | tf_op jit(solution)/shard_map/pallas_call | solution.py:243
  52.8 2.3 %collective-permute-done.17.far0 = bf16[16,128,128]{2,1,0:T(8,128)(2,1)S(1)} collective-permute-done((bf16[16,128,128]{2,1,0:T(8,128)(2,1)S(1)}, bf16[16,128,128]{2,1,0:T(8,128)(2,1)S(1)}, u32[]{:S(2)}, u32[]{:S(2)}) %collective-permute-start.17) | collective-permute-done | bytes 524320 | tf_op jit(solution)/shard_map/ppermute | solution.py:381
  55.1 1.9 %collective-permute-done.22.far1 = bf16[16,128,128]{2,1,0:T(8,128)(2,1)S(1)} collective-permute-done((bf16[16,128,128]{2,1,0:T(8,128)(2,1)S(1)}, bf16[16,128,128]{2,1,0:T(8,128)(2,1)S(1)}, u32[]{:S(2)}, u32[]{:S(2)}) %collective-permute-start.22) | collective-permute-done | bytes 524320 | tf_op jit(solution)/shard_map/ppermute | solution.py:24
  57.0 3.7 %shard_map.58 = (bf16[2,2,2,1,1,336,128]{6,5,4,3,2,1,0:T(8,128)(2,1)S(1)}, f32[2,2,2,1,1,336,128]{6,5,4,3,2,1,0:T(8,128)S(1)}, bf16[2,2,2,1,1,336,128]{6,5,4,3,2...) custom-call(s32[145]{0:T(256)S(1)} %get-tuple-element.49.plan_ref, ...), custom_call_target="tpu_custom_call" | custom-call | flops 268435456 | bytes 16777216 | tf_op jit(solution)/shard_map/pallas_call | solution.py:349
  60.7 1.8 %collective-permute-start.23 = (bf16[2,2,2,1,1,336,128]{6,5,2,4,3,1,0:T(8,128)(2,1)S(1)}, bf16[2,2,2,1,1,336,128]{6,5,2,4,3,1,0:T(8,128)(2,1)S(1)}, u32[]{:S(2)}, u32[]{:S(2)}) collective-permute-start(bf16[2,2,2,1,1,336,128]{6,5,2,4,3,1,0:T(8,128)(2,1)S(1)} %bitcast.153), channel_id=1, source_target_pairs={{0,2},{1,5},{2,0},{3,7},{4,6},{5,1},{6,4},{7,3},{8,10},{9,13},{10,... | collective-permute-start | bytes 2064392 | tf_op jit(solution)/shard_map/ppermute | solution.py:35
  62.6 1.8 %collective-permute-start.27 = (bf16[2,2,2,1,1,336,128]{6,5,2,4,3,1,0:T(8,128)(2,1)S(1)}, bf16[2,2,2,1,1,336,128]{6,5,2,4,3,1,0:T(8,128)(2,1)S(1)}, u32[]{:S(2)}, u32[]{:S(2)}) collective-permute-start(bf16[2,2,2,1,1,336,128]{6,5,2,4,3,1,0:T(8,128)(2,1)S(1)} %bitcast.152), channel_id=1, source_target_pairs={{0,4},{1,9},{2,6},{3,11},{4,0},{5,13},{6,2},{7,15},{8,12},{9,1},{1... | collective-permute-start | bytes 2064392 | tf_op jit(solution)/shard_map/ppermute | solution.py:35
  64.4 0.5 collective-permute-start.31
  64.8 6.9 %collective-permute-done.23 = bf16[2,2,2,1,1,336,128]{6,5,2,4,3,1,0:T(8,128)(2,1)S(1)} collective-permute-done((bf16[2,2,2,1,1,336,128]{6,5,2,4,3,1,0:T(8,128)(2,1)S(1)}, bf16[2,2,2,1,1,336,128]{6,5,2,4,3,1,0:T(8,128)(2,1)S(1)}, u32[]{:S(2)}, u32[]{:S(2)}) %collective-permute-start.23) | collective-permute-done | bytes 688160 | tf_op jit(solution)/shard_map/ppermute | solution.py:35
  71.9 2.1 %collective-permute-start.24 = (bf16[2,2,1,1,336,128]{5,4,3,2,1,0:T(8,128)(2,1)S(1)}, bf16[2,2,1,1,336,128]{5,4,3,2,1,0:T(8,128)(2,1)S(1)}, u32[]{:S(2)}, u32[]{:S(2)}) collective-permute-start(bf16[2,2,1,1,336,128]{5,4,3,2,1,0:T(8,128)(2,1)S(1)} %get-tuple-element.67), channel_id=1, source_target_pairs={{0,4},{1,9},{2,6},{3,11},{4,0},{5,13},{6,2},{7,15},{8,12},{9,1},{1... | collective-permute-start | bytes 1032200 | tf_op jit(solution)/shard_map/ppermute | solution.py:35
  74.0 5.1 %collective-permute-done.27 = bf16[2,2,2,1,1,336,128]{6,5,2,4,3,1,0:T(8,128)(2,1)S(1)} collective-permute-done((bf16[2,2,2,1,1,336,128]{6,5,2,4,3,1,0:T(8,128)(2,1)S(1)}, bf16[2,2,2,1,1,336,128]{6,5,2,4,3,1,0:T(8,128)(2,1)S(1)}, u32[]{:S(2)}, u32[]{:S(2)}) %collective-permute-start.27) | collective-permute-done | bytes 688160 | tf_op jit(solution)/shard_map/ppermute | solution.py:35
  79.2 1.2 %collective-permute-start.28 = (bf16[2,2,1,1,336,128]{5,4,3,2,1,0:T(8,128)(2,1)S(1)}, bf16[2,2,1,1,336,128]{5,4,3,2,1,0:T(8,128)(2,1)S(1)}, u32[]{:S(2)}, u32[]{:S(2)}) collective-permute-start(bf16[2,2,1,1,336,128]{5,4,3,2,1,0:T(8,128)(2,1)S(1)} %get-tuple-element.69), channel_id=1, source_target_pairs={{0,2},{1,17},{2,0},{3,19},{4,6},{5,21},{6,4},{7,23},{8,10},{9,25},... | collective-permute-start | bytes 1032200 | tf_op jit(solution)/shard_map/ppermute | solution.py:35
  80.4 1.8 %collective-permute-start.32 = (bf16[2,2,1,1,352,128]{5,4,1,0,3,2:T(8,128)(2,1)S(1)}, bf16[2,2,1,1,352,128]{5,4,1,0,3,2:T(8,128)(2,1)S(1)}, u32[]{:S(2)}, u32[]{:S(2)}) collective-permute-start(bf16[2,2,1,1,352,128]{5,4,1,0,3,2:T(8,128)(2,1)S(1)} %fusion.3), channel_id=1, source_target_pairs={{0,4},{1,3},{2,6},{3,1},{4,0},{5,7},{6,2},{7,5},{8,12},{9,11},{10,... | collective-permute-start | bytes 1081352 | tf_op jit(solution)/shard_map/ppermute | solution.py:35
  82.3 0.4 collective-permute-done.24
  82.8 2.1 %collective-permute-start.25 = (bf16[2,1,1,336,128]{4,3,2,1,0:T(8,128)(2,1)S(1)}, bf16[2,1,1,336,128]{4,3,2,1,0:T(8,128)(2,1)S(1)}, u32[]{:S(2)}, u32[]{:S(2)}) collective-permute-start(bf16[2,1,1,336,128]{4,3,2,1,0:T(8,128)(2,1)S(1)} %get-tuple-element.71), channel_id=1, source_target_pairs={{0,8},{1,3},{2,10},{3,1},{4,12},{5,7},{6,14},{7,5},{8,0},{9,11},{1... | collective-permute-start | bytes 516104 | tf_op jit(solution)/shard_map/ppermute | solution.py:35
  84.9 1.6 %collective-permute-done.28 = bf16[2,2,1,1,336,128]{5,4,3,2,1,0:T(8,128)(2,1)S(1)} collective-permute-done((bf16[2,2,1,1,336,128]{5,4,3,2,1,0:T(8,128)(2,1)S(1)}, bf16[2,2,1,1,336,128]{5,4,3,2,1,0:T(8,128)(2,1)S(1)}, u32[]{:S(2)}, u32[]{:S(2)}) %collective-permute-start.28) | collective-permute-done | bytes 344096 | tf_op jit(solution)/shard_map/ppermute | solution.py:35
  86.5 5.7 %collective-permute-start.29 = (bf16[2,1,1,336,128]{4,3,2,1,0:T(8,128)(2,1)S(1)}, bf16[2,1,1,336,128]{4,3,2,1,0:T(8,128)(2,1)S(1)}, u32[]{:S(2)}, u32[]{:S(2)}) collective-permute-start(bf16[2,1,1,336,128]{4,3,2,1,0:T(8,128)(2,1)S(1)} %get-tuple-element.73), channel_id=1, source_target_pairs={{0,16},{1,5},{2,18},{3,7},{4,20},{5,1},{6,22},{7,3},{8,24},{9,13},... | collective-permute-start | bytes 516104 | tf_op jit(solution)/shard_map/ppermute | solution.py:35
  92.4 1.1 %collective-permute-start.26 = (bf16[1,1,336,128]{3,2,1,0:T(8,128)(2,1)S(1)}, bf16[1,1,336,128]{3,2,1,0:T(8,128)(2,1)S(1)}, u32[]{:S(2)}, u32[]{:S(2)}) collective-permute-start(bf16[1,1,336,128]{3,2,1,0:T(8,128)(2,1)S(1)} %fusion.34), channel_id=1, source_target_pairs={{0,16},{1,17},{2,18},{3,19},{4,20},{5,21},{6,22},{7,23},{8,24},{9,... | collective-permute-start | bytes 258056 | tf_op jit(solution)/shard_map/ppermute | solution.py:35
  93.6 4.0 %collective-permute-done.29 = bf16[2,1,1,336,128]{4,3,2,1,0:T(8,128)(2,1)S(1)} collective-permute-done((bf16[2,1,1,336,128]{4,3,2,1,0:T(8,128)(2,1)S(1)}, bf16[2,1,1,336,128]{4,3,2,1,0:T(8,128)(2,1)S(1)}, u32[]{:S(2)}, u32[]{:S(2)}) %collective-permute-start.29) | collective-permute-done | bytes 172064 | tf_op jit(solution)/shard_map/ppermute | solution.py:35
  97.7 4.8 %collective-permute-done.33 = bf16[2,1,1,352,128]{4,3,0,2,1:T(8,128)(2,1)S(1)} collective-permute-done((bf16[2,1,1,352,128]{4,3,0,2,1:T(8,128)(2,1)S(1)}, bf16[2,1,1,352,128]{4,3,0,2,1:T(8,128)(2,1)S(1)}, u32[]{:S(2)}, u32[]{:S(2)}) %collective-permute-start.33) | collective-permute-done | bytes 180256 | tf_op jit(solution)/shard_map/ppermute | solution.py:35
  102.6 1.2 %collective-permute-done.30 = bf16[1,1,336,128]{3,2,1,0:T(8,128)(2,1)S(1)} collective-permute-done((bf16[1,1,336,128]{3,2,1,0:T(8,128)(2,1)S(1)}, bf16[1,1,336,128]{3,2,1,0:T(8,128)(2,1)S(1)}, u32[]{:S(2)}, u32[]{:S(2)}) %collective-permute-start.30) | collective-permute-done | bytes 86048 | tf_op jit(solution)/shard_map/ppermute | solution.py:35
  103.8 4.1 %collective-permute-done.34 = bf16[1,1,352,128]{3,2,1,0:T(8,128)(2,1)S(1)} collective-permute-done((bf16[1,1,352,128]{3,2,1,0:T(8,128)(2,1)S(1)}, bf16[1,1,352,128]{3,2,1,0:T(8,128)(2,1)S(1)}, u32[]{:S(2)}, u32[]{:S(2)}) %collective-permute-start.34) | collective-permute-done | bytes 90144 | tf_op jit(solution)/shard_map/ppermute | solution.py:35
  108.0 0.8 pad_maximum_fusion
  (45 shorter events, 1.8 us)
Async XLA Ops:
  0.0 13.1 %collective-permute-start.7 = (bf16[64,128,128]{2,1,0:T(8,128)(2,1)}, bf16[64,128,128]{2,1,0:T(8,128)(2,1)S(1)}, u32[]{:S(2)}, u32[]{:S(2)}) collective-permute-start(bf16[64,128,128]{2,1,0:T(8,128)(2,1)} %bitcast.154), channel_id=1, source_target_pairs={{0,1},{1,0},{2,3},{3,2},{4,5},{5,4},{6,7},{7,6},{8,9},{9,8},{10,11... | collective-permute-start | bytes 6291464 | tf_op jit(solution)/shard_map/ppermute | solution.py:24
  0.5 4.0 %collective-permute-start.3 = (s32[64]{0:T(128)}, s32[64]{0:T(128)S(1)}, u32[]{:S(2)}, u32[]{:S(2)}) collective-permute-start(s32[64]{0:T(128)} %bitcast.158), channel_id=1, source_target_pairs={{0,1},{1,0},{2,3},{3,2},{4,5},{5,4},{6,7},{7,6},{8,9},{9,8},{10,11... | collective-permute-start | bytes 776 | tf_op jit(solution)/shard_map/ppermute | solution.py:24
  0.5 7.5 %collective-permute-start.8 = (bf16[16,128,128]{2,1,0:T(8,128)(2,1)}, bf16[16,128,128]{2,1,0:T(8,128)(2,1)S(1)}, u32[]{:S(2)}, u32[]{:S(2)}) collective-permute-start(bf16[16,128,128]{2,1,0:T(8,128)(2,1)} %refs_2_.1), channel_id=1, source_target_pairs={{0,1},{1,0},{2,3},{3,2},{4,5},{5,4},{6,7},{7,6},{8,9},{9,8},{10,11... | collective-permute-start | bytes 1572872 | tf_op jit(solution)/shard_map/ppermute | solution.py:24
  1.0 12.1 %collective-permute-start = (bf16[16,128,128]{2,1,0:T(8,128)(2,1)}, bf16[16,128,128]{2,1,0:T(8,128)(2,1)S(1)}, u32[]{:S(2)}, u32[]{:S(2)}) collective-permute-start(bf16[16,128,128]{2,1,0:T(8,128)(2,1)} %refs_2_.1), channel_id=1, source_target_pairs={{0,8},{1,5},{2,10},{3,7},{8,16},{9,1},{10,18},{11,3},{16,24},{17,9... | collective-permute-start | bytes 1572872 | tf_op jit(solution)/shard_map/ppermute | solution.py:381
  4.5 14.5 %collective-permute-start.4 = (bf16[16,128,128]{2,1,0:T(8,128)(2,1)}, bf16[16,128,128]{2,1,0:T(8,128)(2,1)S(1)}, u32[]{:S(2)}, u32[]{:S(2)}) collective-permute-start(bf16[16,128,128]{2,1,0:T(8,128)(2,1)} %refs_2_.1), channel_id=1, source_target_pairs={{0,4},{1,9},{2,6},{3,11},{8,0},{9,17},{10,2},{11,19},{16,8},{17,25... | collective-permute-start | bytes 1572872 | tf_op jit(solution)/shard_map/ppermute | solution.py:381
  13.1 5.9 %collective-permute-start.11 = (s32[64]{0:T(128)S(1)}, s32[64]{0:T(128)S(1)}, u32[]{:S(2)}, u32[]{:S(2)}) collective-permute-start(s32[64]{0:T(128)S(1)} %bitcast_add_fusion), channel_id=1, source_target_pairs={{0,12},{4,8},{8,4},{12,0},{16,28},{20,24},{24,20},{28,16},{1,13},{... | collective-permute-start | bytes 776 | tf_op jit(solution)/shard_map/ppermute | solution.py:24
  16.4 3.6 %collective-permute-start.10 = (s32[64]{0:T(128)S(1)}, s32[64]{0:T(128)S(1)}, u32[]{:S(2)}, u32[]{:S(2)}) collective-permute-start(s32[64]{0:T(128)S(1)} %bitcast_add_fusion), channel_id=1, source_target_pairs={{0,8},{4,12},{8,0},{12,4},{16,24},{20,28},{24,16},{28,20},{1,9},{5... | collective-permute-start | bytes 776 | tf_op jit(solution)/shard_map/ppermute | solution.py:24
  16.9 3.6 %collective-permute-start.9 = (s32[64]{0:T(128)S(1)}, s32[64]{0:T(128)S(1)}, u32[]{:S(2)}, u32[]{:S(2)}) collective-permute-start(s32[64]{0:T(128)S(1)} %bitcast_add_fusion), channel_id=1, source_target_pairs={{0,4},{4,0},{8,12},{12,8},{16,20},{20,16},{24,28},{28,24},{1,5},{5... | collective-permute-start | bytes 776 | tf_op jit(solution)/shard_map/ppermute | solution.py:24
  17.0 13.4 %collective-permute-start.1 = (bf16[16,128,128]{2,1,0:T(8,128)(2,1)S(1)}, bf16[16,128,128]{2,1,0:T(8,128)(2,1)S(1)}, u32[]{:S(2)}, u32[]{:S(2)}) collective-permute-start(bf16[16,128,128]{2,1,0:T(8,128)(2,1)S(1)} %collective-permute-done.refs_8_), channel_id=1, source_target_pairs={{0,8},{1,5},{2,10},{3,7},{8,16},{9,1},{10,18},{11,3},{16,24},{17,9... | collective-permute-start | bytes 1572872 | tf_op jit(solution)/shard_map/ppermute | solution.py:381
  19.0 13.3 %collective-permute-start.5 = (bf16[16,128,128]{2,1,0:T(8,128)(2,1)S(1)}, bf16[16,128,128]{2,1,0:T(8,128)(2,1)S(1)}, u32[]{:S(2)}, u32[]{:S(2)}) collective-permute-start(bf16[16,128,128]{2,1,0:T(8,128)(2,1)S(1)} %collective-permute-done.4.refs_3_), channel_id=1, source_target_pairs={{0,4},{1,9},{2,6},{3,11},{8,0},{9,17},{10,2},{11,19},{16,8},{17,25... | collective-permute-start | bytes 1572872 | tf_op jit(solution)/shard_map/ppermute | solution.py:381
  20.5 11.7 %collective-permute-start.13 = (bf16[16,128,128]{2,1,0:T(8,128)(2,1)}, bf16[16,128,128]{2,1,0:T(8,128)(2,1)S(1)}, u32[]{:S(2)}, u32[]{:S(2)}) collective-permute-start(bf16[16,128,128]{2,1,0:T(8,128)(2,1)} %refs_2_.1), channel_id=1, source_target_pairs={{0,2},{1,3},{2,0},{3,1},{4,6},{5,7},{6,4},{7,5},{8,10},{9,11},{10,... | collective-permute-start | bytes 1572872 | tf_op jit(solution)/shard_map/ppermute | solution.py:24
  22.0 12.1 %collective-permute-start.12 = (s32[256]{0:T(256)S(1)}, s32[256]{0:T(256)S(1)}, u32[]{:S(2)}, u32[]{:S(2)}) collective-permute-start(s32[256]{0:T(256)S(1)} %pad_add_fusion.1), channel_id=1, source_target_pairs={{0,16},{4,20},{8,24},{12,28},{16,0},{20,4},{24,8},{28,12},{1,17},{... | collective-permute-start | bytes 3080 | tf_op jit(solution)/shard_map/ppermute | solution.py:24
  30.4 13.4 %collective-permute-start.2 = (bf16[16,128,128]{2,1,0:T(8,128)(2,1)S(1)}, bf16[16,128,128]{2,1,0:T(8,128)(2,1)S(1)}, u32[]{:S(2)}, u32[]{:S(2)}) collective-permute-start(bf16[16,128,128]{2,1,0:T(8,128)(2,1)S(1)} %collective-permute-done.1.refs_7_), channel_id=1, source_target_pairs={{0,8},{1,5},{2,10},{3,7},{8,16},{9,1},{10,18},{11,3},{16,24},{17,9... | collective-permute-start | bytes 1572872 | tf_op jit(solution)/shard_map/ppermute | solution.py:381
  32.2 7.1 %collective-permute-start.14 = (bf16[16,128,128]{2,1,0:T(8,128)(2,1)S(1)}, bf16[16,128,128]{2,1,0:T(8,128)(2,1)S(1)}, u32[]{:S(2)}, u32[]{:S(2)}) collective-permute-start(bf16[16,128,128]{2,1,0:T(8,128)(2,1)S(1)} %collective-permute-done.13.refs_1_), channel_id=1, source_target_pairs={{0,1},{1,0},{2,3},{3,2},{4,5},{5,4},{6,7},{7,6},{8,9},{9,8},{10,11... | collective-permute-start | bytes 1572872 | tf_op jit(solution)/shard_map/ppermute | solution.py:24
  32.2 11.6 %collective-permute-start.6 = (bf16[16,128,128]{2,1,0:T(8,128)(2,1)S(1)}, bf16[16,128,128]{2,1,0:T(8,128)(2,1)S(1)}, u32[]{:S(2)}, u32[]{:S(2)}) collective-permute-start(bf16[16,128,128]{2,1,0:T(8,128)(2,1)S(1)} %collective-permute-done.5.refs_4_), channel_id=1, source_target_pairs={{0,4},{1,9},{2,6},{3,11},{8,0},{9,17},{10,2},{11,19},{16,8},{17,25... | collective-permute-start | bytes 1572872 | tf_op jit(solution)/shard_map/ppermute | solution.py:381
  32.5 11.3 %collective-permute-start.15 = (bf16[16,128,128]{2,1,0:T(8,128)(2,1)S(1)}, bf16[16,128,128]{2,1,0:T(8,128)(2,1)S(1)}, u32[]{:S(2)}, u32[]{:S(2)}) collective-permute-start(bf16[16,128,128]{2,1,0:T(8,128)(2,1)S(1)} %collective-permute-done.4.refs_3_), channel_id=1, source_target_pairs={{0,1},{1,0},{2,3},{3,2},{4,5},{5,4},{6,7},{7,6},{8,9},{9,8},{10,11... | collective-permute-start | bytes 1572872 | tf_op jit(solution)/shard_map/ppermute | solution.py:24
  34.1 9.7 %collective-permute-start.16 = (bf16[16,128,128]{2,1,0:T(8,128)(2,1)S(1)}, bf16[16,128,128]{2,1,0:T(8,128)(2,1)S(1)}, u32[]{:S(2)}, u32[]{:S(2)}) collective-permute-start(bf16[16,128,128]{2,1,0:T(8,128)(2,1)S(1)} %collective-permute-done.refs_8_), channel_id=1, source_target_pairs={{0,1},{1,0},{2,3},{3,2},{4,5},{5,4},{6,7},{7,6},{8,9},{9,8},{10,11... | collective-permute-start | bytes 1572872 | tf_op jit(solution)/shard_map/ppermute | solution.py:24
  43.8 3.6 %collective-permute-start.18 = (bf16[16,128,128]{2,1,0:T(8,128)(2,1)S(1)}, bf16[16,128,128]{2,1,0:T(8,128)(2,1)S(1)}, u32[]{:S(2)}, u32[]{:S(2)}) collective-permute-start(bf16[16,128,128]{2,1,0:T(8,128)(2,1)S(1)} %collective-permute-done.5.refs_4_), channel_id=1, source_target_pairs={{0,1},{1,0},{2,3},{3,2},{4,5},{5,4},{6,7},{7,6},{8,9},{9,8},{10,11... | collective-permute-start | bytes 1572872 | tf_op jit(solution)/shard_map/ppermute | solution.py:24
  45.0 2.4 %collective-permute-start.21 = (bf16[16,128,128]{2,1,0:T(8,128)(2,1)S(1)}, bf16[16,128,128]{2,1,0:T(8,128)(2,1)S(1)}, u32[]{:S(2)}, u32[]{:S(2)}) collective-permute-start(bf16[16,128,128]{2,1,0:T(8,128)(2,1)S(1)} %collective-permute-done.1.refs_7_), channel_id=1, source_target_pairs={{0,1},{1,0},{2,3},{3,2},{4,5},{5,4},{6,7},{7,6},{8,9},{9,8},{10,11... | collective-permute-start | bytes 1572872 | tf_op jit(solution)/shard_map/ppermute | solution.py:24
  45.1 3.0 %collective-permute-start.19 = (bf16[16,128,128]{2,1,0:T(8,128)(2,1)S(1)}, bf16[16,128,128]{2,1,0:T(8,128)(2,1)S(1)}, u32[]{:S(2)}, u32[]{:S(2)}) collective-permute-start(bf16[16,128,128]{2,1,0:T(8,128)(2,1)S(1)} %collective-permute-done.6.refs_5_), channel_id=1, source_target_pairs={{0,1},{1,0},{2,3},{3,2},{4,5},{5,4},{6,7},{7,6},{8,9},{9,8},{10,11... | collective-permute-start | bytes 1572872 | tf_op jit(solution)/shard_map/ppermute | solution.py:24
  45.5 3.3 %collective-permute-start.20 = (bf16[16,128,128]{2,1,0:T(8,128)(2,1)S(1)}, bf16[16,128,128]{2,1,0:T(8,128)(2,1)S(1)}, u32[]{:S(2)}, u32[]{:S(2)}) collective-permute-start(bf16[16,128,128]{2,1,0:T(8,128)(2,1)S(1)} %collective-permute-done.2.refs_6_), channel_id=1, source_target_pairs={{0,1},{1,0},{2,3},{3,2},{4,5},{5,4},{6,7},{7,6},{8,9},{9,8},{10,11... | collective-permute-start | bytes 1572872 | tf_op jit(solution)/shard_map/ppermute | solution.py:24
  45.6 9.5 %collective-permute-start.17 = (bf16[16,128,128]{2,1,0:T(8,128)(2,1)S(1)}, bf16[16,128,128]{2,1,0:T(8,128)(2,1)S(1)}, u32[]{:S(2)}, u32[]{:S(2)}) collective-permute-start(bf16[16,128,128]{2,1,0:T(8,128)(2,1)S(1)} %collective-permute-done.2.refs_6_), channel_id=1, source_target_pairs={{0,8},{1,5},{2,10},{3,7},{8,16},{9,1},{10,18},{11,3},{16,24},{17,9... | collective-permute-start | bytes 1572872 | tf_op jit(solution)/shard_map/ppermute | solution.py:381
  55.1 1.9 %collective-permute-start.22 = (bf16[16,128,128]{2,1,0:T(8,128)(2,1)S(1)}, bf16[16,128,128]{2,1,0:T(8,128)(2,1)S(1)}, u32[]{:S(2)}, u32[]{:S(2)}) collective-permute-start(bf16[16,128,128]{2,1,0:T(8,128)(2,1)S(1)} %collective-permute-done.17.far0), channel_id=1, source_target_pairs={{0,1},{1,0},{2,3},{3,2},{4,5},{5,4},{6,7},{7,6},{8,9},{9,8},{10,11... | collective-permute-start | bytes 1572872 | tf_op jit(solution)/shard_map/ppermute | solution.py:24
  60.7 11.0 %collective-permute-start.23 = (bf16[2,2,2,1,1,336,128]{6,5,2,4,3,1,0:T(8,128)(2,1)S(1)}, bf16[2,2,2,1,1,336,128]{6,5,2,4,3,1,0:T(8,128)(2,1)S(1)}, u32[]{:S(2)}, u32[]{:S(2)}) collective-permute-start(bf16[2,2,2,1,1,336,128]{6,5,2,4,3,1,0:T(8,128)(2,1)S(1)} %bitcast.153), channel_id=1, source_target_pairs={{0,2},{1,5},{2,0},{3,7},{4,6},{5,1},{6,4},{7,3},{8,10},{9,13},{10,... | collective-permute-start | bytes 2064392 | tf_op jit(solution)/shard_map/ppermute | solution.py:35
  62.6 16.5 %collective-permute-start.27 = (bf16[2,2,2,1,1,336,128]{6,5,2,4,3,1,0:T(8,128)(2,1)S(1)}, bf16[2,2,2,1,1,336,128]{6,5,2,4,3,1,0:T(8,128)(2,1)S(1)}, u32[]{:S(2)}, u32[]{:S(2)}) collective-permute-start(bf16[2,2,2,1,1,336,128]{6,5,2,4,3,1,0:T(8,128)(2,1)S(1)} %bitcast.152), channel_id=1, source_target_pairs={{0,4},{1,9},{2,6},{3,11},{4,0},{5,13},{6,2},{7,15},{8,12},{9,1},{1... | collective-permute-start | bytes 2064392 | tf_op jit(solution)/shard_map/ppermute | solution.py:35
  64.4 16.0 %collective-permute-start.31 = (bf16[2,2,2,1,1,352,128]{6,5,2,4,3,1,0:T(8,128)(2,1)S(1)}, bf16[2,2,2,1,1,352,128]{6,5,2,4,3,1,0:T(8,128)(2,1)S(1)}, u32[]{:S(2)}, u32[]{:S(2)}) collective-permute-start(bf16[2,2,2,1,1,352,128]{6,5,2,4,3,1,0:T(8,128)(2,1)S(1)} %bitcast.151), channel_id=1, source_target_pairs={{0,2},{1,17},{2,0},{3,19},{4,6},{5,21},{6,4},{7,23},{8,10},{9,25},... | collective-permute-start | bytes 2162696 | tf_op jit(solution)/shard_map/ppermute | solution.py:35
  71.9 10.8 %collective-permute-start.24 = (bf16[2,2,1,1,336,128]{5,4,3,2,1,0:T(8,128)(2,1)S(1)}, bf16[2,2,1,1,336,128]{5,4,3,2,1,0:T(8,128)(2,1)S(1)}, u32[]{:S(2)}, u32[]{:S(2)}) collective-permute-start(bf16[2,2,1,1,336,128]{5,4,3,2,1,0:T(8,128)(2,1)S(1)} %get-tuple-element.67), channel_id=1, source_target_pairs={{0,4},{1,9},{2,6},{3,11},{4,0},{5,13},{6,2},{7,15},{8,12},{9,1},{1... | collective-permute-start | bytes 1032200 | tf_op jit(solution)/shard_map/ppermute | solution.py:35
  79.2 7.3 %collective-permute-start.28 = (bf16[2,2,1,1,336,128]{5,4,3,2,1,0:T(8,128)(2,1)S(1)}, bf16[2,2,1,1,336,128]{5,4,3,2,1,0:T(8,128)(2,1)S(1)}, u32[]{:S(2)}, u32[]{:S(2)}) collective-permute-start(bf16[2,2,1,1,336,128]{5,4,3,2,1,0:T(8,128)(2,1)S(1)} %get-tuple-element.69), channel_id=1, source_target_pairs={{0,2},{1,17},{2,0},{3,19},{4,6},{5,21},{6,4},{7,23},{8,10},{9,25},... | collective-permute-start | bytes 1032200 | tf_op jit(solution)/shard_map/ppermute | solution.py:35
  80.4 11.8 %collective-permute-start.32 = (bf16[2,2,1,1,352,128]{5,4,1,0,3,2:T(8,128)(2,1)S(1)}, bf16[2,2,1,1,352,128]{5,4,1,0,3,2:T(8,128)(2,1)S(1)}, u32[]{:S(2)}, u32[]{:S(2)}) collective-permute-start(bf16[2,2,1,1,352,128]{5,4,1,0,3,2:T(8,128)(2,1)S(1)} %fusion.3), channel_id=1, source_target_pairs={{0,4},{1,3},{2,6},{3,1},{4,0},{5,7},{6,2},{7,5},{8,12},{9,11},{10,... | collective-permute-start | bytes 1081352 | tf_op jit(solution)/shard_map/ppermute | solution.py:35
  82.8 9.6 %collective-permute-start.25 = (bf16[2,1,1,336,128]{4,3,2,1,0:T(8,128)(2,1)S(1)}, bf16[2,1,1,336,128]{4,3,2,1,0:T(8,128)(2,1)S(1)}, u32[]{:S(2)}, u32[]{:S(2)}) collective-permute-start(bf16[2,1,1,336,128]{4,3,2,1,0:T(8,128)(2,1)S(1)} %get-tuple-element.71), channel_id=1, source_target_pairs={{0,8},{1,3},{2,10},{3,1},{4,12},{5,7},{6,14},{7,5},{8,0},{9,11},{1... | collective-permute-start | bytes 516104 | tf_op jit(solution)/shard_map/ppermute | solution.py:35
  86.5 11.0 %collective-permute-start.29 = (bf16[2,1,1,336,128]{4,3,2,1,0:T(8,128)(2,1)S(1)}, bf16[2,1,1,336,128]{4,3,2,1,0:T(8,128)(2,1)S(1)}, u32[]{:S(2)}, u32[]{:S(2)}) collective-permute-start(bf16[2,1,1,336,128]{4,3,2,1,0:T(8,128)(2,1)S(1)} %get-tuple-element.73), channel_id=1, source_target_pairs={{0,16},{1,5},{2,18},{3,7},{4,20},{5,1},{6,22},{7,3},{8,24},{9,13},... | collective-permute-start | bytes 516104 | tf_op jit(solution)/shard_map/ppermute | solution.py:35
  92.3 10.2 %collective-permute-start.33 = (bf16[2,1,1,352,128]{4,3,0,2,1:T(8,128)(2,1)S(1)}, bf16[2,1,1,352,128]{4,3,0,2,1:T(8,128)(2,1)S(1)}, u32[]{:S(2)}, u32[]{:S(2)}) collective-permute-start(bf16[2,1,1,352,128]{4,3,0,2,1:T(8,128)(2,1)S(1)} %fusion.15), channel_id=1, source_target_pairs={{0,8},{1,9},{2,10},{3,11},{4,12},{5,13},{6,14},{7,15},{8,0},{9,1},... | collective-permute-start | bytes 540680 | tf_op jit(solution)/shard_map/ppermute | solution.py:35
  92.4 10.1 %collective-permute-start.26 = (bf16[1,1,336,128]{3,2,1,0:T(8,128)(2,1)S(1)}, bf16[1,1,336,128]{3,2,1,0:T(8,128)(2,1)S(1)}, u32[]{:S(2)}, u32[]{:S(2)}) collective-permute-start(bf16[1,1,336,128]{3,2,1,0:T(8,128)(2,1)S(1)} %fusion.34), channel_id=1, source_target_pairs={{0,16},{1,17},{2,18},{3,19},{4,20},{5,21},{6,22},{7,23},{8,24},{9,... | collective-permute-start | bytes 258056 | tf_op jit(solution)/shard_map/ppermute | solution.py:35
  97.6 6.2 %collective-permute-start.30 = (bf16[1,1,336,128]{3,2,1,0:T(8,128)(2,1)S(1)}, bf16[1,1,336,128]{3,2,1,0:T(8,128)(2,1)S(1)}, u32[]{:S(2)}, u32[]{:S(2)}) collective-permute-start(bf16[1,1,336,128]{3,2,1,0:T(8,128)(2,1)S(1)} %fusion.35), channel_id=1, source_target_pairs={{0,8},{1,3},{2,10},{3,1},{4,12},{5,7},{6,14},{7,5},{8,0},{9,11},{1... | collective-permute-start | bytes 258056 | tf_op jit(solution)/shard_map/ppermute | solution.py:35
  102.5 5.5 %collective-permute-start.34 = (bf16[1,1,352,128]{3,2,1,0:T(8,128)(2,1)S(1)}, bf16[1,1,352,128]{3,2,1,0:T(8,128)(2,1)S(1)}, u32[]{:S(2)}, u32[]{:S(2)}) collective-permute-start(bf16[1,1,352,128]{3,2,1,0:T(8,128)(2,1)S(1)} %fusion.33), channel_id=1, source_target_pairs={{0,16},{1,5},{2,18},{3,7},{4,20},{5,1},{6,22},{7,3},{8,24},{9,13},... | collective-permute-start | bytes 270344 | tf_op jit(solution)/shard_map/ppermute | solution.py:35
